TPU v7x, 512 devices: a whole 4x4x16 slice. The times are simulated.
512 devices in a mesh: shot: 8 (over x, core), gx: 8 (over z_lo), gy: 8 (over y, z_hi).
Axes of the slice: x: 4, y: 4, z: 16 (z_hi: 2, z_lo: 8; z = z_hi * 8 + z_lo), core: 2. Of those that a mesh axis runs over, the one named last changes fastest.
Arguments:
- features: bfloat16 [32, 256, 128, 128], P('shot', 'gx', 'gy'), may hold values from -6 to 6
- conv_weight: float32 [32, 27], P('shot'), may hold values from -0.21875 to 0.21875
- fwd_prev: float32 [8, 256, 128, 128], P('shot', 'gx', 'gy'), may hold values from -6 to 6
- fwd_now: float32 [8, 256, 128, 128], P('shot', 'gx', 'gy'), may hold values from -6 to 6
- back_prev: float32 [8, 256, 128, 128], P('shot', 'gx', 'gy'), may hold values from -96 to 96
- back_now: float32 [8, 256, 128, 128], P('shot', 'gx', 'gy'), may hold values from -96 to 96
- sources: int32 [8], P('shot'), may hold values from 0 to 4194303
- wavelet: float32 [8, 2], P('shot'), may hold values from -24 to 24
- receivers: int32 [8, 512], P('shot'), may hold values from 0 to 32767
- residual: float32 [8, 2, 512], P('shot'), may hold values from -96 to 96
- damping: float32 [1], replicated, may hold values from 100 to 1000
Outputs:
- fwd_last: float32 [8, 256, 128, 128], P('shot', 'gx', 'gy')
- back_last: float32 [8, 256, 128, 128], P('shot', 'gx', 'gy')
- traces: float32 [8, 2, 512], P('shot')
- update: float32 [256, 128, 128], P('gx', 'gy')
- weight_grad: float32 [32, 27], P('shot')
All inputs are finite; a program needn't handle non-finite values.
Results may differ from a plain program's by a relative error of at most 0.0003.
Values may be sent and summed in bfloat16 or wider, within the bound.
No kernel may reach another device: no remote copies, remote signals or barrier semaphores. Data moves between devices by JAX's collectives and lax.ppermute only.
A program may use at most 64 MiB of HBM per device.

v0:
```python
import jax
import jax.numpy as jnp
from jax import lax
from jax.sharding import PartitionSpec as P

RDEPTH = 3


COEFFICIENTS = (-205.0 / 72.0, 8.0 / 5.0, -1.0 / 5.0, 8.0 / 315.0, -1.0 / 560.0)


def padded_2(cells, sides, width):
    for axis, dim in sides:
        count = lax.axis_size(axis)
        ends = count - 1
        head = lax.slice_in_dim(cells, 0, width, axis=dim)
        tail = lax.slice_in_dim(cells, cells.shape[dim] - width, cells.shape[dim], axis=dim)
        cells = jnp.concatenate(
            [
                lax.ppermute(tail, axis, [(i, (i + 1) % count) for i in range(ends)]),
                cells,
                lax.ppermute(head, axis, [((i + 1) % count, i) for i in range(ends)]),
            ],
            axis=dim,
        )
    return cells


def laplace_inner(extended):
    size_x = extended.shape[-3] - 8
    size_y = extended.shape[-2] - 8
    depth = extended.shape[-1]
    inner = extended[..., 4 : 4 + size_x, 4 : 4 + size_y, :]
    deep_pad = jnp.pad(inner, [(0, 0)] * (extended.ndim - 1) + [(4, 4)])
    total = 3.0 * COEFFICIENTS[0] * inner
    for reach in range(1, 5):
        along_x = (
            extended[..., 4 + reach : 4 + reach + size_x, 4 : 4 + size_y, :]
            + extended[..., 4 - reach : 4 - reach + size_x, 4 : 4 + size_y, :]
        )
        along_y = (
            extended[..., 4 : 4 + size_x, 4 + reach : 4 + reach + size_y, :]
            + extended[..., 4 : 4 + size_x, 4 - reach : 4 - reach + size_y, :]
        )
        along_z = (
            deep_pad[..., 4 + reach : 4 + reach + depth]
            + deep_pad[..., 4 - reach : 4 - reach + depth]
        )
        total = total + COEFFICIENTS[reach] * (along_x + along_y + along_z)
    return total


def receiver_places(receivers, anchor_x, anchor_y, size_x, size_y, plane_y):
    local_x = receivers // plane_y - anchor_x
    local_y = receivers % plane_y - anchor_y
    inside = (local_x >= 0) & (local_x < size_x) & (local_y >= 0) & (local_y < size_y)
    return (jnp.clip(local_x, 0, size_x - 1), jnp.clip(local_y, 0, size_y - 1), inside)


def source_field(region_courant, amplitude, sources, anchor_x, anchor_y, plane_y):
    size_x, size_y, depth = region_courant.shape
    shots_here = sources.shape[0]
    spot_x = sources // (plane_y * depth)
    spot_y = sources // depth % plane_y
    spot_z = sources % depth
    hit_x = (
        lax.broadcasted_iota(jnp.int32, (shots_here, size_x), 1) + anchor_x == spot_x[:, None]
    ).astype(jnp.float32)
    hit_y = (
        lax.broadcasted_iota(jnp.int32, (shots_here, size_y), 1) + anchor_y == spot_y[:, None]
    ).astype(jnp.float32)
    hit_z = (lax.broadcasted_iota(jnp.int32, (shots_here, depth), 1) == spot_z[:, None]).astype(
        jnp.float32
    )
    scaled = amplitude[:, None, None, None] * region_courant[None]
    return scaled * (hit_x[:, :, None, None] * hit_y[:, None, :, None] * hit_z[:, None, None, :])


def advance(
    fwd_ext,
    back_ext,
    fwd_old,
    back_old,
    region_courant,
    amplitude,
    sources,
    receivers,
    injected,
    anchor_x,
    anchor_y,
    plane_y,
):
    size_x, size_y, depth = region_courant.shape
    lap_fwd = laplace_inner(fwd_ext)
    lap_back = laplace_inner(back_ext)
    new_fwd = (
        2.0 * fwd_ext[:, 4 : 4 + size_x, 4 : 4 + size_y, :]
        - fwd_old
        + region_courant[None] * lap_fwd
    )
    new_fwd = new_fwd + source_field(
        region_courant, amplitude, sources, anchor_x, anchor_y, plane_y
    )
    new_back = (
        2.0 * back_ext[:, 4 : 4 + size_x, 4 : 4 + size_y, :]
        - back_old
        + region_courant[None] * lap_back
    )
    place_x, place_y, inside = receiver_places(
        receivers, anchor_x, anchor_y, size_x, size_y, plane_y
    )
    shot_rows = lax.broadcasted_iota(jnp.int32, receivers.shape, 0)
    plane = jnp.zeros((receivers.shape[0], size_x, size_y), jnp.float32)
    plane = plane.at[shot_rows, place_x, place_y].add(jnp.where(inside, injected, 0.0))
    new_back = new_back.at[:, :, :, RDEPTH].add(region_courant[None, :, :, RDEPTH] * plane)
    return (new_fwd, new_back, lap_fwd)


def sample(field, receivers, anchor_x, anchor_y, plane_y):
    place_x, place_y, inside = receiver_places(
        receivers, anchor_x, anchor_y, field.shape[1], field.shape[2], plane_y
    )
    shot_rows = lax.broadcasted_iota(jnp.int32, receivers.shape, 0)
    return jnp.where(inside, field[shot_rows, place_x, place_y, RDEPTH], 0.0)


def per_device(
    features,
    conv_weight,
    fwd_prev,
    fwd_now,
    back_prev,
    back_now,
    sources,
    wavelet,
    receivers,
    residual,
    damping,
):
    channels, size_x, size_y, depth = features.shape
    start_x = lax.axis_index("gx") * size_x
    start_y = lax.axis_index("gy") * size_y
    plane_y = size_y * lax.axis_size("gy")
    rimmed = padded_2(features, (("gx", 1), ("gy", 2)), 1)
    padded = jnp.pad(rimmed, ((0, 0), (0, 0), (0, 0), (1, 1)))
    partial_value = jnp.zeros((size_x, size_y, depth), jnp.float32)
    for offset_x in range(3):
        for offset_y in range(3):
            for offset_z in range(3):
                window = padded[
                    :,
                    offset_x : offset_x + size_x,
                    offset_y : offset_y + size_y,
                    offset_z : offset_z + depth,
                ].astype(jnp.float32)
                tap_weights = conv_weight[:, 9 * offset_x + 3 * offset_y + offset_z]
                partial_value = partial_value + jnp.sum(
                    tap_weights[:, None, None, None] * window, axis=0
                )
    raw_field = lax.psum(partial_value, "shot")
    squashed = jax.nn.sigmoid(raw_field)
    courant = 0.02 + 0.16 * squashed
    derivative = 0.16 * squashed * (1.0 - squashed)
    older_fwd, older_back = (fwd_prev, back_prev)
    current_fwd, current_back = (fwd_now, back_now)
    forward_list, backward_list, laplacians = ([], [], [])
    for moment in range(2):
        ext_fwd, ext_back = (
            padded_2(current_fwd, (("gx", 1), ("gy", 2)), 4),
            padded_2(current_back, (("gx", 1), ("gy", 2)), 4),
        )
        new_fwd, new_back, lap_fwd = advance(
            ext_fwd,
            ext_back,
            older_fwd,
            older_back,
            courant,
            wavelet[:, moment],
            sources,
            receivers,
            residual[:, moment],
            start_x,
            start_y,
            plane_y,
        )
        forward_list.append(new_fwd)
        backward_list.append(new_back)
        laplacians.append(lap_fwd)
        older_fwd, current_fwd = (current_fwd, new_fwd)
        older_back, current_back = (current_back, new_back)
    trace_part = jnp.stack(
        [sample(forward_list[moment], receivers, start_x, start_y, plane_y) for moment in range(2)],
        axis=1,
    )
    traces = lax.psum(trace_part, ("gx", "gy"))
    image_part = jnp.zeros((size_x, size_y, depth), jnp.float32)
    light_part = jnp.zeros((size_x, size_y, depth), jnp.float32)
    for moment in range(2):
        image_part = image_part + jnp.sum(laplacians[moment] * backward_list[moment], axis=0)
        light_part = light_part + jnp.sum(laplacians[moment] * laplacians[moment], axis=0)
    image_total, light_total = lax.psum((image_part, light_part), "shot")
    update = image_total / (light_total + damping[0])
    pulled = update * derivative
    columns = []
    for offset_x in range(3):
        for offset_y in range(3):
            for offset_z in range(3):
                window = padded[
                    :,
                    offset_x : offset_x + size_x,
                    offset_y : offset_y + size_y,
                    offset_z : offset_z + depth,
                ].astype(jnp.float32)
                columns.append(jnp.sum(window * pulled[None], axis=(1, 2, 3)))
    weight_part = jnp.stack(columns, axis=1)
    weight_grad = lax.psum(weight_part, ("gx", "gy"))
    return (forward_list[1], backward_list[1], traces, update, weight_grad)


def solution(mesh):
    in_specs = (
        P("shot", "gx", "gy", None),
        P("shot", None),
        P("shot", "gx", "gy", None),
        P("shot", "gx", "gy", None),
        P("shot", "gx", "gy", None),
        P("shot", "gx", "gy", None),
        P("shot"),
        P("shot", None),
        P("shot", None),
        P("shot", None, None),
        P(),
    )
    out_specs = (
        P("shot", "gx", "gy", None),
        P("shot", "gx", "gy", None),
        P("shot", None, None),
        P("gx", "gy", None),
        P("shot", None),
    )
    return jax.shard_map(
        per_device, mesh=mesh, in_specs=in_specs, out_specs=out_specs, check_vma=False
    )
```

profile of v0, /device:TPU:64, one launch (start us, length us, event | category | flops | bytes accessed | tf_op | source)
XLA Modules:
  0.0 649.6 jit_solution(1115533157219635614)
XLA Ops:
  7.2 0.8 fusion.213
  8.0 3.8 collective-permute-start
  11.8 2.1 collective-permute-start.1
  14.0 0.8 fusion.219
  14.8 4.9 collective-permute-start.5
  19.7 1.9 collective-permute-start.4
  21.6 0.8 fusion.217
  22.4 5.1 collective-permute-start.13
  27.6 2.4 slice_reduce_fusion.25
  30.0 1.9 slice_reduce_fusion.26
  32.6 1.3 fusion.220
  33.9 1.3 fusion.198
  35.4 0.7 broadcast_multiply_fusion
  36.7 1.9 collective-permute-start.12
  38.7 1.1 constant_dynamic-update-slice_fusion.1
  39.9 11.7 %collective-permute-start.2 = (bf16[4,34,1,128]{3,2,1,0:T(2,128)(2,1)S(1)}, bf16[4,34,1,128]{3,2,1,0:T(2,128)(2,1)S(1)}, u32[]{:S(2)}, u32[]{:S(2)}) collective-permute-start(bf16[4,34,1,128]{3,2,1,0:T(2,128)(2,1)S(1)} %get-tuple-element.165), channel_id=1, source_target_pairs={{0,1},{1,2},{2,3},{3,4},{4,5},{5,6},{6,7},{8,9},{9,10},{10,11},{11... | collective-permute-start | bytes 104456 | tf_op jit(solution)/shard_map/ppermute | solution.py:20
  52.0 1.3 collective-permute-start.3
  53.4 0.8 fusion.215
  54.2 1.3 collective-permute-start.6
  55.5 14.5 %collective-permute-start.7 = (f32[1,40,4,128]{3,2,1,0:T(4,128)}, f32[1,40,4,128]{3,2,1,0:T(4,128)}, u32[]{:S(2)}, u32[]{:S(2)}) collective-permute-start(f32[1,40,4,128]{3,2,1,0:T(4,128)} %get-tuple-element.180), channel_id=1, source_target_pairs={{0,1},{1,2},{2,3},{3,4},{4,5},{5,6},{6,7},{8,9},{9,10},{10,11},{11... | collective-permute-start | bytes 245768 | tf_op jit(solution)/shard_map/ppermute | solution.py:20
  70.3 0.7 copy-done.4
  70.9 1.4 fusion.5
  72.5 1.8 fusion.6
  74.5 2.1 fusion.10
  76.7 2.4 fusion.8
  79.1 1.2 add_add_fusion
  80.3 0.7 fusion.214
  81.0 1.3 collective-permute-start.14
  82.3 14.2 %collective-permute-start.15 = (f32[1,40,4,128]{3,2,1,0:T(4,128)}, f32[1,40,4,128]{3,2,1,0:T(4,128)}, u32[]{:S(2)}, u32[]{:S(2)}) collective-permute-start(f32[1,40,4,128]{3,2,1,0:T(4,128)} %get-tuple-element.174), channel_id=1, source_target_pairs={{0,1},{1,2},{2,3},{3,4},{4,5},{5,6},{6,7},{8,9},{9,10},{10,11},{11... | collective-permute-start | bytes 245768 | tf_op jit(solution)/shard_map/ppermute | solution.py:20
  96.5 62.5 %all-reduce.10.cloned.1.call-done = f32[32,16,128]{2,1,0:T(8,128)} async-done(((f32[32,16,128]{2,1,0:T(8,128)}), f32[32,16,128]{2,1,0:T(8,128)}) %all-reduce.10.cloned.1.call-update) | async-done | bytes 262160 | tf_op jit(solution)/shard_map/psum | solution.py:160
  158.9 1.0 multiply_add_fusion
  160.3 5.3 fusion.111
  165.6 4.6 gather_fusion
  170.8 25.2 %scatter_fusion = f32[32,16]{0,1:T(8,128)S(1)} fusion(f32[32,16]{0,1:T(8,128)S(1)} %broadcast.269.clone.1, s32[512]{0:T(512)S(1)} %bitcast.97, f32[512]{0:T(512)S(1)} %bitcast.102), kind=kCustom, calls=%fused_computation.2 | custom fusion | flops 512 | bytes 10240 | tf_op jit(solution)/shard_map/scatter-add | solution.py:114
  196.1 25.2 %scatter_fusion.1 = f32[32,16]{0,1:T(8,128)S(1)} fusion(f32[32,16]{0,1:T(8,128)S(1)} %broadcast.269.clone, s32[512]{0:T(512)S(1)} %bitcast.98, f32[512]{0:T(512)S(1)} %bitcast.101), kind=kCustom, calls=%fused_computation.3 | custom fusion | flops 512 | bytes 10240 | tf_op jit(solution)/shard_map/scatter-add | solution.py:114
  221.3 0.9 copy.570
  222.2 3.9 fusion.122
  226.2 0.8 slice_add_fusion.5
  227.0 3.3 scatter-add.25
  230.4 0.6 fusion.216
  231.0 2.4 collective-permute-start.16
  233.4 3.5 collective-permute-start.17
  236.8 0.6 fusion.218
  237.5 0.9 copy.571
  238.3 2.4 collective-permute-start.8
  240.7 4.2 collective-permute-start.9
  245.0 1.3 collective-permute-start.18
  246.3 13.3 %collective-permute-start.19 = (f32[1,40,4,128]{3,2,1,0:T(4,128)S(1)}, f32[1,40,4,128]{3,2,1,0:T(4,128)S(1)}, u32[]{:S(2)}, u32[]{:S(2)}) collective-permute-start(f32[1,40,4,128]{3,2,1,0:T(4,128)S(1)} %get-tuple-element.172), channel_id=1, source_target_pairs={{0,1},{1,2},{2,3},{3,4},{4,5},{5,6},{6,7},{8,9},{9,10},{10,11},{11... | collective-permute-start | bytes 245768 | tf_op jit(solution)/shard_map/ppermute | solution.py:20
  259.6 0.7 pad_maximum_fusion.19
  260.3 1.3 collective-permute-start.10
  261.6 13.9 %collective-permute-start.11 = (f32[1,40,4,128]{3,2,1,0:T(4,128)}, f32[1,40,4,128]{3,2,1,0:T(4,128)}, u32[]{:S(2)}, u32[]{:S(2)}) collective-permute-start(f32[1,40,4,128]{3,2,1,0:T(4,128)} %get-tuple-element.178), channel_id=1, source_target_pairs={{0,1},{1,2},{2,3},{3,4},{4,5},{5,6},{6,7},{8,9},{9,10},{10,11},{11... | collective-permute-start | bytes 245768 | tf_op jit(solution)/shard_map/ppermute | solution.py:20
  275.6 0.6 fusion.72
  276.2 0.7 copy-done.11
  276.9 0.8 slice_add_fusion
  277.7 4.1 scatter-add.27
  281.9 1.0 pad_maximum_fusion.4
  282.9 1.3 add_bitcast_fusion
  284.3 1.5 add_bitcast_fusion.1
  285.8 4.6 gather_fusion.1
  290.4 80.2 %all-reduce.12.cloned.1.call-done = (f32[32,16,128]{2,1,0:T(8,128)}, f32[32,16,128]{2,1,0:T(8,128)}) async-done(((f32[32,16,128]{2,1,0:T(8,128)}, f32[32,16,128]{2,1,0:T(8,128)}), (f32[32,16,128]{2,1,0:T(8,128)}, f32[32,16,128]{2,1,0:T(8,128)})) %all-reduce.12.cloned.1.call-update) | async-done | bytes 524304 | tf_op jit(solution)/shard_map/psum | solution.py:201
  370.6 1.9 multiply_multiply_fusion.2
  372.4 4.8 fusion.59
  377.2 2.4 fusion.57
  382.3 260.5 %all-reduce.5 = (f32[1,2,512]{2,1,0:T(2,128)}, f32[4,27]{1,0:T(4,128)}) all-reduce(f32[1,2,512]{2,1,0:T(2,128)S(1)} %pad_maximum_fusion.20, f32[4,27]{1,0:T(4,128)S(1)} %stack.123), channel_id=1, replica_groups=mesh['shot'=8,'gx'=8,'gy'=8] {'gx','gy'}, use_global_device_ids=true, to_apply=%region_30.31 | all-reduce | flops 1132 | bytes 9056 | tf_op jit(solution)/shard_map/psum | solution.py:195
  (180 shorter events, 4.8 us)
Async XLA Ops:
  7.2 44.5 %copy-start.2 = (bf16[4,32,16,128]{3,2,1,0:T(8,128)(2,1)S(1)}, bf16[4,32,16,128]{3,2,1,0:T(8,128)(2,1)}, u32[]{:S(2)}) copy-start(bf16[4,32,16,128]{3,2,1,0:T(8,128)(2,1)} %param.15) | copy-start | bytes 1572868
  7.2 151.8 %all-reduce.10.cloned.1.call-start = ((), (), s32[]{:S(2)}) async-start(), calls=%async_computation | async-start | bytes 524288 | tf_op jit(solution)/shard_map/psum | solution.py:160
  8.0 28.7 %collective-permute-start = (bf16[4,1,16,128]{3,2,1,0:T(8,128)(2,1)S(1)}, bf16[4,1,16,128]{3,2,1,0:T(8,128)(2,1)S(1)}, u32[]{:S(2)}, u32[]{:S(2)}) collective-permute-start(bf16[4,1,16,128]{3,2,1,0:T(8,128)(2,1)S(1)} %get-tuple-element.168), channel_id=1, source_target_pairs={{0,8},{8,16},{16,24},{24,32},{32,40},{40,48},{48,56},{1,9},{9,17},... | collective-permute-start | bytes 49160 | tf_op jit(solution)/shard_map/ppermute | solution.py:20
  11.8 41.5 %copy-start.7 = (f32[1,32,16,128]{3,2,1,0:T(8,128)S(1)}, f32[1,32,16,128]{3,2,1,0:T(8,128)}, u32[]{:S(2)}) copy-start(f32[1,32,16,128]{3,2,1,0:T(8,128)} %param.18) | copy-start | bytes 786436
  11.8 28.0 %collective-permute-start.1 = (bf16[4,1,16,128]{3,2,1,0:T(8,128)(2,1)S(1)}, bf16[4,1,16,128]{3,2,1,0:T(8,128)(2,1)S(1)}, u32[]{:S(2)}, u32[]{:S(2)}) collective-permute-start(bf16[4,1,16,128]{3,2,1,0:T(8,128)(2,1)S(1)} %get-tuple-element.167), channel_id=1, source_target_pairs={{8,0},{16,8},{24,16},{32,24},{40,32},{48,40},{56,48},{9,1},{17,9},... | collective-permute-start | bytes 49160 | tf_op jit(solution)/shard_map/ppermute | solution.py:22
  14.8 37.2 %collective-permute-start.5 = (f32[1,4,16,128]{3,2,1,0:T(8,128)S(1)}, f32[1,4,16,128]{3,2,1,0:T(8,128)S(1)}, u32[]{:S(2)}, u32[]{:S(2)}) collective-permute-start(f32[1,4,16,128]{3,2,1,0:T(8,128)S(1)} %get-tuple-element.196), channel_id=1, source_target_pairs={{0,8},{8,16},{16,24},{24,32},{32,40},{40,48},{48,56},{1,9},{9,17},... | collective-permute-start | bytes 98312 | tf_op jit(solution)/shard_map/ppermute | solution.py:20
  19.7 33.7 %collective-permute-start.4 = (f32[1,4,16,128]{3,2,1,0:T(8,128)S(1)}, f32[1,4,16,128]{3,2,1,0:T(8,128)S(1)}, u32[]{:S(2)}, u32[]{:S(2)}) collective-permute-start(f32[1,4,16,128]{3,2,1,0:T(8,128)S(1)} %get-tuple-element.195), channel_id=1, source_target_pairs={{8,0},{16,8},{24,16},{32,24},{40,32},{48,40},{56,48},{9,1},{17,9},... | collective-permute-start | bytes 98312 | tf_op jit(solution)/shard_map/ppermute | solution.py:22
  22.4 33.1 %collective-permute-start.13 = (f32[1,4,16,128]{3,2,1,0:T(8,128)S(1)}, f32[1,4,16,128]{3,2,1,0:T(8,128)S(1)}, u32[]{:S(2)}, u32[]{:S(2)}) collective-permute-start(f32[1,4,16,128]{3,2,1,0:T(8,128)S(1)} %get-tuple-element.189), channel_id=1, source_target_pairs={{0,8},{8,16},{16,24},{24,32},{32,40},{40,48},{48,56},{1,9},{9,17},... | collective-permute-start | bytes 98312 | tf_op jit(solution)/shard_map/ppermute | solution.py:20
  36.1 124.2 %copy-start.24 = (f32[128]{0:T(128)}, f32[128]{0:T(128)S(1)}, u32[]{:S(2)}) copy-start(f32[128]{0:T(128)S(1)} %compare_convert_fusion) | copy-start | bytes 1540
  36.7 33.5 %collective-permute-start.12 = (f32[1,4,16,128]{3,2,1,0:T(8,128)S(1)}, f32[1,4,16,128]{3,2,1,0:T(8,128)S(1)}, u32[]{:S(2)}, u32[]{:S(2)}) collective-permute-start(f32[1,4,16,128]{3,2,1,0:T(8,128)S(1)} %get-tuple-element.188), channel_id=1, source_target_pairs={{8,0},{16,8},{24,16},{32,24},{40,32},{48,40},{56,48},{9,1},{17,9},... | collective-permute-start | bytes 98312 | tf_op jit(solution)/shard_map/ppermute | solution.py:22
  39.8 30.3 %copy-start.5 = (f32[1,32,16,128]{3,2,1,0:T(8,128)S(1)}, f32[1,32,16,128]{3,2,1,0:T(8,128)}, u32[]{:S(2)}) copy-start(f32[1,32,16,128]{3,2,1,0:T(8,128)} %param.20) | copy-start | bytes 786436
  39.9 30.3 %collective-permute-start.2 = (bf16[4,34,1,128]{3,2,1,0:T(2,128)(2,1)S(1)}, bf16[4,34,1,128]{3,2,1,0:T(2,128)(2,1)S(1)}, u32[]{:S(2)}, u32[]{:S(2)}) collective-permute-start(bf16[4,34,1,128]{3,2,1,0:T(2,128)(2,1)S(1)} %get-tuple-element.165), channel_id=1, source_target_pairs={{0,1},{1,2},{2,3},{3,4},{4,5},{5,6},{6,7},{8,9},{9,10},{10,11},{11... | collective-permute-start | bytes 104456 | tf_op jit(solution)/shard_map/ppermute | solution.py:20
  52.0 18.9 %collective-permute-start.3 = (bf16[4,34,1,128]{3,2,1,0:T(2,128)(2,1)S(1)}, bf16[4,34,1,128]{3,2,1,0:T(2,128)(2,1)S(1)}, u32[]{:S(2)}, u32[]{:S(2)}) collective-permute-start(bf16[4,34,1,128]{3,2,1,0:T(2,128)(2,1)S(1)} %get-tuple-element.166), channel_id=1, source_target_pairs={{1,0},{2,1},{3,2},{4,3},{5,4},{6,5},{7,6},{9,8},{10,9},{11,10},{12... | collective-permute-start | bytes 104456 | tf_op jit(solution)/shard_map/ppermute | solution.py:22
  53.4 2.1 copy-start.15
  54.2 106.1 %collective-permute-start.6 = (f32[1,40,4,128]{3,2,1,0:T(4,128)}, f32[1,40,4,128]{3,2,1,0:T(4,128)}, u32[]{:S(2)}, u32[]{:S(2)}) collective-permute-start(f32[1,40,4,128]{3,2,1,0:T(4,128)} %get-tuple-element.179), channel_id=1, source_target_pairs={{1,0},{2,1},{3,2},{4,3},{5,4},{6,5},{7,6},{9,8},{10,9},{11,10},{12... | collective-permute-start | bytes 245768 | tf_op jit(solution)/shard_map/ppermute | solution.py:22
  55.5 104.8 %collective-permute-start.7 = (f32[1,40,4,128]{3,2,1,0:T(4,128)}, f32[1,40,4,128]{3,2,1,0:T(4,128)}, u32[]{:S(2)}, u32[]{:S(2)}) collective-permute-start(f32[1,40,4,128]{3,2,1,0:T(4,128)} %get-tuple-element.180), channel_id=1, source_target_pairs={{0,1},{1,2},{2,3},{3,4},{4,5},{5,6},{6,7},{8,9},{9,10},{10,11},{11... | collective-permute-start | bytes 245768 | tf_op jit(solution)/shard_map/ppermute | solution.py:20
  70.1 2.3 copy-start.35
  70.1 2.3 copy-start.36
  70.1 2.3 copy-start.37
  70.1 2.3 copy-start.38
  70.1 2.3 copy-start.39
  70.1 2.3 copy-start.40
  70.1 2.3 copy-start.41
  70.1 2.3 copy-start.42
  70.1 2.3 copy-start.49
  70.2 10.1 %copy-start.16 = (f32[1,40,16,128]{3,2,1,0:T(8,128)}, f32[1,40,16,128]{3,2,1,0:T(8,128)S(1)}, u32[]{:S(2)}) copy-start(f32[1,40,16,128]{3,2,1,0:T(8,128)S(1)} %get-tuple-element.198) | copy-start | bytes 983044
  70.9 5.7 copy-start.17
  72.5 1.9 copy-start.31
  72.5 1.9 copy-start.32
  72.5 1.9 copy-start.33
  72.5 1.9 copy-start.34
  72.5 1.9 copy-start.44
  72.5 1.9 copy-start.45
  72.5 1.9 copy-start.46
  72.5 1.9 copy-start.47
  72.5 1.9 copy-start.48
  74.4 2.2 copy-start.26
  74.4 2.2 copy-start.27
  74.4 2.2 copy-start.28
  74.4 2.2 copy-start.29
  74.5 2.2 copy-start.30
  74.5 2.2 copy-start.43
  80.3 290.3 %all-reduce.12.cloned.1.call-start = ((), (), s32[]{:S(2)}) async-start(), calls=%async_computation.1 | async-start | bytes 1048576 | tf_op jit(solution)/shard_map/psum | solution.py:201
  81.0 141.2 %collective-permute-start.14 = (f32[1,40,4,128]{3,2,1,0:T(4,128)}, f32[1,40,4,128]{3,2,1,0:T(4,128)}, u32[]{:S(2)}, u32[]{:S(2)}) collective-permute-start(f32[1,40,4,128]{3,2,1,0:T(4,128)} %get-tuple-element.173), channel_id=1, source_target_pairs={{1,0},{2,1},{3,2},{4,3},{5,4},{6,5},{7,6},{9,8},{10,9},{11,10},{12... | collective-permute-start | bytes 245768 | tf_op jit(solution)/shard_map/ppermute | solution.py:22
  82.3 139.9 %collective-permute-start.15 = (f32[1,40,4,128]{3,2,1,0:T(4,128)}, f32[1,40,4,128]{3,2,1,0:T(4,128)}, u32[]{:S(2)}, u32[]{:S(2)}) collective-permute-start(f32[1,40,4,128]{3,2,1,0:T(4,128)} %get-tuple-element.174), channel_id=1, source_target_pairs={{0,1},{1,2},{2,3},{3,4},{4,5},{5,6},{6,7},{8,9},{9,10},{10,11},{11... | collective-permute-start | bytes 245768 | tf_op jit(solution)/shard_map/ppermute | solution.py:20
  165.6 4.6 copy-start.20
  165.6 4.6 copy-start.21
  165.6 5.2 copy-start.23
  196.1 26.1 %copy-start.1 = (f32[32,16,128]{2,1,0:T(8,128)S(1)}, f32[32,16,128]{2,1,0:T(8,128)}, u32[]{:S(2)}) copy-start(f32[32,16,128]{2,1,0:T(8,128)} %all-reduce.10.cloned.1.call-done) | copy-start | bytes 786436
  222.2 4.0 copy-start.14
  227.0 48.5 %copy-start.6 = (f32[1,32,16,128]{3,2,1,0:T(8,128)S(1)}, f32[1,32,16,128]{3,2,1,0:T(8,128)}, u32[]{:S(2)}) copy-start(f32[1,32,16,128]{3,2,1,0:T(8,128)} %param.20) | copy-start | bytes 786436
  231.0 13.9 %collective-permute-start.16 = (f32[1,4,16,128]{3,2,1,0:T(8,128)}, f32[1,4,16,128]{3,2,1,0:T(8,128)S(1)}, u32[]{:S(2)}, u32[]{:S(2)}) collective-permute-start(f32[1,4,16,128]{3,2,1,0:T(8,128)} %get-tuple-element.183), channel_id=1, source_target_pairs={{8,0},{16,8},{24,16},{32,24},{40,32},{48,40},{56,48},{9,1},{17,9},... | collective-permute-start | bytes 98312 | tf_op jit(solution)/shard_map/ppermute | solution.py:22
  233.4 11.6 %collective-permute-start.17 = (f32[1,4,16,128]{3,2,1,0:T(8,128)}, f32[1,4,16,128]{3,2,1,0:T(8,128)S(1)}, u32[]{:S(2)}, u32[]{:S(2)}) collective-permute-start(f32[1,4,16,128]{3,2,1,0:T(8,128)} %get-tuple-element.184), channel_id=1, source_target_pairs={{0,8},{8,16},{16,24},{24,32},{32,40},{40,48},{48,56},{1,9},{9,17},... | collective-permute-start | bytes 98312 | tf_op jit(solution)/shard_map/ppermute | solution.py:20
  238.3 21.2 %collective-permute-start.8 = (f32[1,4,16,128]{3,2,1,0:T(8,128)}, f32[1,4,16,128]{3,2,1,0:T(8,128)S(1)}, u32[]{:S(2)}, u32[]{:S(2)}) collective-permute-start(f32[1,4,16,128]{3,2,1,0:T(8,128)} %get-tuple-element.191), channel_id=1, source_target_pairs={{8,0},{16,8},{24,16},{32,24},{40,32},{48,40},{56,48},{9,1},{17,9},... | collective-permute-start | bytes 98312 | tf_op jit(solution)/shard_map/ppermute | solution.py:22
  240.7 18.9 %collective-permute-start.9 = (f32[1,4,16,128]{3,2,1,0:T(8,128)S(1)}, f32[1,4,16,128]{3,2,1,0:T(8,128)S(1)}, u32[]{:S(2)}, u32[]{:S(2)}) collective-permute-start(f32[1,4,16,128]{3,2,1,0:T(8,128)S(1)} %get-tuple-element.190), channel_id=1, source_target_pairs={{0,8},{8,16},{16,24},{24,32},{32,40},{40,48},{48,56},{1,9},{9,17},... | collective-permute-start | bytes 98312 | tf_op jit(solution)/shard_map/ppermute | solution.py:20
  245.0 30.5 %collective-permute-start.18 = (f32[1,40,4,128]{3,2,1,0:T(4,128)S(1)}, f32[1,40,4,128]{3,2,1,0:T(4,128)S(1)}, u32[]{:S(2)}, u32[]{:S(2)}) collective-permute-start(f32[1,40,4,128]{3,2,1,0:T(4,128)S(1)} %get-tuple-element.171), channel_id=1, source_target_pairs={{1,0},{2,1},{3,2},{4,3},{5,4},{6,5},{7,6},{9,8},{10,9},{11,10},{12... | collective-permute-start | bytes 245768 | tf_op jit(solution)/shard_map/ppermute | solution.py:22
  246.3 29.2 %collective-permute-start.19 = (f32[1,40,4,128]{3,2,1,0:T(4,128)S(1)}, f32[1,40,4,128]{3,2,1,0:T(4,128)S(1)}, u32[]{:S(2)}, u32[]{:S(2)}) collective-permute-start(f32[1,40,4,128]{3,2,1,0:T(4,128)S(1)} %get-tuple-element.172), channel_id=1, source_target_pairs={{0,1},{1,2},{2,3},{3,4},{4,5},{5,6},{6,7},{8,9},{9,10},{10,11},{11... | collective-permute-start | bytes 245768 | tf_op jit(solution)/shard_map/ppermute | solution.py:20
  260.3 21.6 %collective-permute-start.10 = (f32[1,40,4,128]{3,2,1,0:T(4,128)}, f32[1,40,4,128]{3,2,1,0:T(4,128)}, u32[]{:S(2)}, u32[]{:S(2)}) collective-permute-start(f32[1,40,4,128]{3,2,1,0:T(4,128)} %get-tuple-element.177), channel_id=1, source_target_pairs={{1,0},{2,1},{3,2},{4,3},{5,4},{6,5},{7,6},{9,8},{10,9},{11,10},{12... | collective-permute-start | bytes 245768 | tf_op jit(solution)/shard_map/ppermute | solution.py:22
  261.6 20.3 %collective-permute-start.11 = (f32[1,40,4,128]{3,2,1,0:T(4,128)}, f32[1,40,4,128]{3,2,1,0:T(4,128)}, u32[]{:S(2)}, u32[]{:S(2)}) collective-permute-start(f32[1,40,4,128]{3,2,1,0:T(4,128)} %get-tuple-element.178), channel_id=1, source_target_pairs={{0,1},{1,2},{2,3},{3,4},{4,5},{5,6},{6,7},{8,9},{9,10},{10,11},{11... | collective-permute-start | bytes 245768 | tf_op jit(solution)/shard_map/ppermute | solution.py:20
  276.9 6.0 copy-start.9
  285.8 86.7 %copy-start = (f32[1,32,16,128]{3,2,1,0:T(8,128)}, f32[1,32,16,128]{3,2,1,0:T(8,128)S(1)}, u32[]{:S(2)}) copy-start(f32[1,32,16,128]{3,2,1,0:T(8,128)S(1)} %get-tuple-element.182) | copy-start | bytes 786436
  285.8 4.6 copy-start.22
  372.4 4.8 copy-start.3
  372.4 4.8 copy-start.18
  (8 other events, 9.6 us)
Sparse Core Ops, SparseCore 0:
  80.4 78.5 all-reduce.9
  290.5 80.0 all-reduce.11
where the time goes:
time: 651 us; the launch traced here: 650 us
  blocking collectives  260 us (40%)
  waiting for transfers between devices  143 us (22%)
  starting transfers between devices  106 us (16%)
  other arithmetic  88.6 us (14%)
  local copies, waits for them, and re-layouts  35 us (5%)
  between operations  16.5 us (3%)
    psum x1, blocking collectives, per_device(): traces = lax.psum(trace_part, ('gx', 'gy'))  260 us
    ppermute x10, starting transfers between devices, padded_2(): lax.ppermute(tail, axis, [(i, (i + 1) % count) for i in range(ends)])  89.1 us
    psum x1, waiting for transfers between devices, per_device(): image_total, light_total = lax.psum((image_part, light_part), 'shot')  80.2 us
    psum x1, waiting for transfers between devices, per_device(): raw_field = lax.psum(partial_value, 'shot')  62.5 us
    scatter-add x2, other arithmetic, advance(): plane.at[shot_rows, place_x, place_y].add(jnp.where(inside, injected, 0.0))  50.4 us
    ppermute x10, starting transfers between devices, padded_2(): lax.ppermute(head, axis, [((i + 1) % count, i) for i in range(ends)])  17.1 us
  transfers between devices with their start and end apart: 22, of which 2 were waited for; matrix products, arithmetic and copies ran while one was open for 14% of the time, Pallas kernels for 0%

commit v1 on v0

v1 whole, which is shorter than its diff:
```python
import functools

import jax
import jax.numpy as jnp
from jax import lax
from jax.experimental import pallas as pl
from jax.experimental.pallas import tpu as pltpu
from jax.sharding import PartitionSpec as P

RDEPTH = 3
COEFFICIENTS = (-205.0 / 72.0, 8.0 / 5.0, -1.0 / 5.0, 8.0 / 315.0, -1.0 / 560.0)
F32 = jnp.float32
BF16 = jnp.bfloat16
VMEM_LIMIT = 48 * 1024 * 1024

VM = pl.BlockSpec(memory_space=pltpu.VMEM)
SM = pl.BlockSpec(memory_space=pltpu.SMEM)


def call(body, outs, ins, specs, scratch=(), flops=1_000_000, name=None):
    moved = sum(a.size * a.dtype.itemsize for a in ins) + sum(
        o.size * jnp.dtype(o.dtype).itemsize for o in outs
    )
    single = len(outs) == 1
    return pl.pallas_call(
        body,
        out_shape=outs[0] if single else tuple(outs),
        in_specs=specs,
        out_specs=VM if single else tuple(VM for _ in outs),
        scratch_shapes=list(scratch),
        compiler_params=pltpu.CompilerParams(vmem_limit_bytes=VMEM_LIMIT),
        cost_estimate=pl.CostEstimate(flops=flops, bytes_accessed=moved, transcendentals=0),
        name=name,
    )(*ins)


def shape(*dims, dtype=F32):
    return jax.ShapeDtypeStruct(dims, dtype)


def split3(value):
    top = value.astype(BF16)
    rest = value - top.astype(F32)
    middle = rest.astype(BF16)
    low = (rest - middle.astype(F32)).astype(BF16)
    return (top, middle, low)


def shifted_lanes(value, by):
    depth = value.shape[1]
    lane = lax.broadcasted_iota(jnp.int32, value.shape, 1)
    if by > 0:
        return jnp.where(lane < depth - by, pltpu.roll(value, depth - by, 1), 0.0)
    return jnp.where(lane >= -by, pltpu.roll(value, -by, 1), 0.0)


def shifted_rows(value, by):
    count = value.shape[0]
    row = lax.broadcasted_iota(jnp.int32, value.shape, 0)
    if by > 0:
        return jnp.where(row < count - by, pltpu.roll(value, count - by, 0), 0.0)
    return jnp.where(row >= -by, pltpu.roll(value, -by, 0), 0.0)


def pack_x_body(feat_ref, fwd_ref, back_ref, up_ref, down_ref):
    channels, size_x = feat_ref.shape[:2]
    up_ref[0:4] = fwd_ref[size_x - 4 : size_x]
    up_ref[4:8] = back_ref[size_x - 4 : size_x]
    down_ref[0:4] = fwd_ref[0:4]
    down_ref[4:8] = back_ref[0:4]
    for c in range(channels):
        up_ref[8 + c] = feat_ref[c, size_x - 1].astype(F32)
        down_ref[8 + c] = feat_ref[c, 0].astype(F32)


def pack_y_body(feat_ref, fwd_ref, back_ref, low_ref, high_ref, up_ref, down_ref, plane_ref):
    channels, size_x, size_y, depth = feat_ref.shape
    groups = size_x // 8 + 1
    up_ref[0:size_x, 0:4] = fwd_ref[:, size_y - 4 : size_y]
    up_ref[0:size_x, 4:8] = back_ref[:, size_y - 4 : size_y]
    down_ref[0:size_x, 0:4] = fwd_ref[:, 0:4]
    down_ref[0:size_x, 4:8] = back_ref[:, 0:4]
    row = lax.broadcasted_iota(jnp.int32, (8, depth), 0)
    for c in range(channels):
        plane_ref[...] = feat_ref[c].astype(F32)
        for out_ref, y in ((up_ref, size_y - 1), (down_ref, 0)):
            own = plane_ref[:, y, :]
            first = size_x + c * groups
            out_ref[first : first + groups - 1] = own.reshape(groups - 1, 8, depth)
            low = low_ref[8 + c, y : y + 1, :]
            high = high_ref[8 + c, y : y + 1, :]
            tail = jnp.where(row == 0, low, jnp.where(row == 1, high, 0.0))
            out_ref[first + groups - 1] = tail


def fill_features(ext_ref, feat_ref, low_ref, high_ref):
    channels, size_x = feat_ref.shape[:2]
    for c in range(channels):
        ext_ref[c, 0] = low_ref[8 + c]
        ext_ref[c, 1 : 1 + size_x] = feat_ref[c].astype(F32)
        ext_ref[c, 1 + size_x] = high_ref[8 + c]


def conv_body(feat_ref, low_ref, high_ref, weight_ref, out_ref, ext_ref):
    channels, size_x = feat_ref.shape[:2]
    fill_features(ext_ref, feat_ref, low_ref, high_ref)

    def one_row(i, carry):
        terms = [[None] * 3 for _ in range(3)]
        for c in range(channels):
            for dx in range(3):
                row = ext_ref[c, i + dx]
                for dy in range(3):
                    for dz in range(3):
                        part = weight_ref[c, 9 * dx + 3 * dy + dz] * row
                        old = terms[dy][dz]
                        terms[dy][dz] = part if old is None else old + part
        total = None
        for dy in range(3):
            part = (
                terms[dy][1]
                + shifted_lanes(terms[dy][0], -1)
                + shifted_lanes(terms[dy][2], 1)
            )
            if dy != 1:
                part = shifted_rows(part, dy - 1)
            total = part if total is None else total + part
        out_ref[i] = total
        return carry

    lax.fori_loop(0, size_x, one_row, 0)


def load_plane(plane_ref, buffer_ref, c, size_x):
    groups = size_x // 8 + 1
    depth = plane_ref.shape[1]
    first = size_x + c * groups
    plane_ref[8 : 8 + size_x] = buffer_ref[first : first + groups - 1].reshape(size_x, depth)
    plane_ref[7:8] = buffer_ref[first + groups - 1, 0:1, :]
    plane_ref[8 + size_x : 9 + size_x] = buffer_ref[first + groups - 1, 1:2, :]


def conv_edge_body(main_ref, low_ref, high_ref, weight_ref, out_ref, plane_ref):
    size_x, size_y, depth = main_ref.shape
    channels = weight_ref.shape[0]
    out_ref[...] = main_ref[...]
    for buffer_ref, dy, y in ((low_ref, 0, 0), (high_ref, 2, size_y - 1)):
        terms = [None] * 3
        for c in range(channels):
            load_plane(plane_ref, buffer_ref, c, size_x)
            for dx in range(3):
                rows = plane_ref[7 + dx : 7 + dx + size_x]
                for dz in range(3):
                    part = weight_ref[c, 9 * dx + 3 * dy + dz] * rows
                    terms[dz] = part if terms[dz] is None else terms[dz] + part
        total = terms[1] + shifted_lanes(terms[0], -1) + shifted_lanes(terms[2], 1)
        out_ref[:, y : y + 1, :] += total.reshape(size_x, 1, depth)


def squash_body(parts_ref, out_ref):
    count = parts_ref.shape[0]
    total = parts_ref[0]
    for n in range(1, count):
        total = total + parts_ref[n]
    squashed = jax.nn.sigmoid(total)
    for n in range(count):
        out_ref[n] = squashed


def update_body(parts_ref, damping_ref, out_ref):
    count, rows = parts_ref.shape[:2]
    half = rows // 2
    total = parts_ref[0]
    for n in range(1, count):
        total = total + parts_ref[n]
    update = total[:half] / (total[half:] + damping_ref[0])
    for n in range(count):
        out_ref[n] = update


def step_body(moment, plane_y, rows, refs):
    (
        fwd_ref,
        back_ref,
        fwd_old_ref,
        back_old_ref,
        squashed_ref,
        x_low_ref,
        x_high_ref,
        y_low_ref,
        y_high_ref,
        place_ref,
        wavelet_ref,
        receivers_ref,
        residual_ref,
        *rest,
    ) = refs
    if moment == 0:
        (fwd_new_ref, back_new_ref, lap_ref, trace_ref) = rest[:4]
        (x_up_ref, x_down_ref, y_up_ref, y_down_ref) = rest[4:8]
        scratch = rest[8:]
    else:
        lap_old_ref = rest[0]
        (fwd_new_ref, back_new_ref, sums_ref, trace_ref) = rest[1:5]
        scratch = rest[5:]
    fwd_x_ref, back_x_ref, fwd_y_ref, back_y_ref, inject_ref = scratch
    size_x, size_y, depth = fwd_ref.shape
    cells = size_x * size_y
    count = receivers_ref.shape[1]
    for first, ref, x_ref, y_ref in (
        (0, fwd_ref, fwd_x_ref, fwd_y_ref),
        (4, back_ref, back_x_ref, back_y_ref),
    ):
        x_ref[0:4] = x_low_ref[first : first + 4]
        x_ref[4 : 4 + size_x] = ref[...]
        x_ref[4 + size_x : 8 + size_x] = x_high_ref[first : first + 4]
        y_ref[:, 4:8] = y_low_ref[0:size_x, first : first + 4]
        y_ref[:, 8 : 8 + size_y] = ref[...]
        y_ref[:, 8 + size_y : 12 + size_y] = y_high_ref[0:size_x, first : first + 4]

    anchor_x, anchor_y, source = place_ref[0], place_ref[1], place_ref[2]
    shift_y = plane_y.bit_length() - 1
    shift_z = depth.bit_length() - 1
    column = lax.shift_right_logical(source, shift_z)
    source_x = lax.shift_right_logical(column, shift_y) - anchor_x
    source_y = (column & (plane_y - 1)) - anchor_y
    source_z = source & (depth - 1)
    here = (source_x >= 0) & (source_x < size_x) & (source_y >= 0) & (source_y < size_y)
    spot = jnp.where(here, (source_x * size_y + source_y) * depth + source_z, -1)
    amplitude = wavelet_ref[0, moment]

    receivers = receivers_ref[...]
    place_x = lax.shift_right_logical(receivers, shift_y) - anchor_x
    place_y = (receivers & (plane_y - 1)) - anchor_y
    inside = (place_x >= 0) & (place_x < size_x) & (place_y >= 0) & (place_y < size_y)
    cell = jnp.where(inside, place_x * size_y + place_y, -1)
    hit = (
        (lax.broadcasted_iota(jnp.int32, (cells, count), 0) == cell).astype(F32).astype(BF16)
    )
    injected = jnp.where(
        lax.broadcasted_iota(jnp.int32, (depth, count), 0) == RDEPTH,
        residual_ref[0, moment : moment + 1, :],
        0.0,
    )
    total = None
    for part in split3(injected):
        product = lax.dot_general(
            hit, part, (((1,), (1,)), ((), ())), preferred_element_type=F32
        )
        total = product if total is None else total + product
    inject_ref[...] = total.reshape(size_x, size_y, depth)

    def laplacian(x_ref, y_ref, start):
        centre = x_ref[pl.ds(start + 4, rows)]
        flat = centre.reshape(rows * size_y, depth)
        result = (3.0 * COEFFICIENTS[0]) * centre
        for k in range(1, 5):
            along_x = x_ref[pl.ds(start + 4 + k, rows)] + x_ref[pl.ds(start + 4 - k, rows)]
            along_y = (
                y_ref[pl.ds(start, rows), 8 + k : 8 + k + size_y, :]
                + y_ref[pl.ds(start, rows), 8 - k : 8 - k + size_y, :]
            )
            along_z = (shifted_lanes(flat, k) + shifted_lanes(flat, -k)).reshape(centre.shape)
            result = result + COEFFICIENTS[k] * (along_x + along_y + along_z)
        return centre, result

    def one_block(i, carry):
        start = i * rows
        here = pl.ds(start, rows)
        courant = 0.02 + 0.16 * squashed_ref[here]
        fwd, lap_fwd = laplacian(fwd_x_ref, fwd_y_ref, start)
        back, lap_back = laplacian(back_x_ref, back_y_ref, start)
        index = (
            lax.broadcasted_iota(jnp.int32, fwd.shape, 0) * (size_y * depth)
            + lax.broadcasted_iota(jnp.int32, fwd.shape, 1) * depth
            + lax.broadcasted_iota(jnp.int32, fwd.shape, 2)
        )
        added = jnp.where(index == spot - start * (size_y * depth), amplitude, 0.0)
        fwd_new = 2.0 * fwd - fwd_old_ref[here] + courant * lap_fwd + courant * added
        back_new = (
            2.0 * back - back_old_ref[here] + courant * lap_back + courant * inject_ref[here]
        )
        fwd_new_ref[here] = fwd_new
        back_new_ref[here] = back_new
        if moment == 0:
            lap_ref[here] = lap_fwd
        else:
            lap_old = lap_old_ref[here]
            sums_ref[i, 0:rows] = lap_old * back + lap_fwd * back_new
            sums_ref[i, rows : 2 * rows] = lap_old * lap_old + lap_fwd * lap_fwd
        return carry

    lax.fori_loop(0, size_x // rows, one_block, 0)

    total = None
    for part in split3(fwd_new_ref[...].reshape(cells, depth)):
        product = lax.dot_general(
            part, hit, (((0,), (0,)), ((), ())), preferred_element_type=F32
        )
        total = product if total is None else total + product
    trace_ref[...] = total[RDEPTH : RDEPTH + 1, :]

    if moment == 0:
        x_up_ref[0:4] = fwd_new_ref[size_x - 4 : size_x]
        x_up_ref[4:8] = back_new_ref[size_x - 4 : size_x]
        x_down_ref[0:4] = fwd_new_ref[0:4]
        x_down_ref[4:8] = back_new_ref[0:4]
        y_up_ref[:, 0:4] = fwd_new_ref[:, size_y - 4 : size_y]
        y_up_ref[:, 4:8] = back_new_ref[:, size_y - 4 : size_y]
        y_down_ref[:, 0:4] = fwd_new_ref[:, 0:4]
        y_down_ref[:, 4:8] = back_new_ref[:, 0:4]


def gradient_body(
    update_ref,
    squashed_ref,
    feat_ref,
    x_low_ref,
    x_high_ref,
    y_low_ref,
    y_high_ref,
    first_ref,
    second_ref,
    out_ref,
    ext_ref,
    moved_ref,
    plane_ref,
    rows_ref,
):
    size_x, size_y, depth = update_ref.shape
    channels = feat_ref.shape[0]
    copies = out_ref.shape[0]
    fill_features(ext_ref, feat_ref, x_low_ref, x_high_ref)

    def one_row(i, carry):
        squashed = squashed_ref[i]
        pulled = update_ref[i] * (0.16 * squashed * (1.0 - squashed))
        for dz in range(3):
            along = pulled if dz == 1 else shifted_lanes(pulled, 1 - dz)
            for dy in range(3):
                moved_ref[3 * dy + dz, i] = along if dy == 1 else shifted_rows(along, 1 - dy)
        edge = pulled[0:1, :], pulled[size_y - 1 : size_y, :]
        plane_ref[1, pl.ds(i, 1)] = edge[0]
        plane_ref[2, pl.ds(i, 1)] = edge[1]
        return carry

    lax.fori_loop(0, size_x, one_row, 0)
    rows_ref[...] = jnp.zeros_like(rows_ref)

    for c in range(channels):

        def add_row(i, totals):
            features = [ext_ref[c, i + dx] for dx in range(3)]
            new = []
            for dx in range(3):
                for dy in range(3):
                    for dz in range(3):
                        product = features[dx] * moved_ref[3 * dy + dz, i]
                        folded = product[0:8]
                        for y in range(8, size_y, 8):
                            folded = folded + product[y : y + 8]
                        new.append(totals[9 * dx + 3 * dy + dz] + folded)
            return tuple(new)

        zero = jnp.zeros((8, depth), F32)
        totals = lax.fori_loop(0, size_x, add_row, (zero,) * 27)
        for o in range(27):
            at = c * 27 + o
            rows_ref[at : at + 1] = jnp.sum(totals[o], axis=0, keepdims=True)

    for buffer_ref, dy, which in ((y_low_ref, 0, 1), (y_high_ref, 2, 2)):
        pulled = plane_ref[which, 0:size_x]
        along = [pulled if dz == 1 else shifted_lanes(pulled, 1 - dz) for dz in range(3)]
        for c in range(channels):
            load_plane(plane_ref.at[0], buffer_ref, c, size_x)
            for dx in range(3):
                features = plane_ref[0, 7 + dx : 7 + dx + size_x]
                for dz in range(3):
                    at = c * 27 + 9 * dx + 3 * dy + dz
                    rows_ref[at : at + 1] += jnp.sum(
                        features * along[dz], axis=0, keepdims=True
                    )

    ones = jnp.ones((8, depth), BF16)
    sums = None
    for part in split3(rows_ref[...]):
        product = lax.dot_general(
            ones, part, (((1,), (1,)), ((), ())), preferred_element_type=F32
        )
        sums = product if sums is None else sums + product
    row = lax.broadcasted_iota(jnp.int32, (8, depth), 0)
    lines = jnp.zeros((8, depth), F32)
    for moment, ref in enumerate((first_ref, second_ref)):
        pieces = ref.shape[1] // depth
        for q in range(pieces):
            piece = ref[0:1, q * depth : (q + 1) * depth]
            lines = jnp.where(row == moment * pieces + q, piece, lines)
    for n in range(copies):
        out_ref[n, 0:8] = lines
        out_ref[n, 8:16] = sums


def neighbours(up, down, axis):
    count = lax.axis_size(axis)
    low = lax.ppermute(up, axis, [(i, i + 1) for i in range(count - 1)])
    high = lax.ppermute(down, axis, [(i + 1, i) for i in range(count - 1)])
    return low, high


def per_device(
    features,
    conv_weight,
    fwd_prev,
    fwd_now,
    back_prev,
    back_now,
    sources,
    wavelet,
    receivers,
    residual,
    damping,
):
    channels, size_x, size_y, depth = features.shape
    shots = lax.axis_size("shot")
    rows = size_x // shots
    count = receivers.shape[1]
    plane_y = size_y * lax.axis_size("gy")
    blocks = lax.axis_size("gx") * lax.axis_size("gy")
    groups = size_x // 8 + 1
    grid = (size_x, size_y, depth)
    fwd_prev, fwd_now, back_prev, back_now = (
        a.reshape(grid) for a in (fwd_prev, fwd_now, back_prev, back_now)
    )
    place = jnp.stack(
        [lax.axis_index("gx") * size_x, lax.axis_index("gy") * size_y, sources[0]]
    ).astype(jnp.int32)

    x_shape = shape(8 + channels, size_y, depth)
    with jax.named_scope("pack_x"):
        x_up, x_down = call(
            pack_x_body, [x_shape, x_shape], (features, fwd_now, back_now), [VM] * 3, name="pack_x"
        )
    with jax.named_scope("halo_x"):
        x_low, x_high = neighbours(x_up, x_down, "gx")
    y_shape = shape(size_x + channels * groups, 8, depth)
    with jax.named_scope("pack_y"):
        y_up, y_down = call(
            pack_y_body,
            [y_shape, y_shape],
            (features, fwd_now, back_now, x_low, x_high),
            [VM] * 5,
            scratch=[pltpu.VMEM(grid, F32)],
            name="pack_y",
        )
    with jax.named_scope("halo_y"):
        y_low, y_high = neighbours(y_up, y_down, "gy")
    ext = pltpu.VMEM((channels, size_x + 2, size_y, depth), F32)
    with jax.named_scope("conv"):
        main = call(
            conv_body,
            [shape(*grid)],
            (features, x_low, x_high, conv_weight),
            [VM, VM, VM, SM],
            scratch=[ext],
            flops=54 * channels * size_x * size_y * depth,
            name="conv",
        )
        part = call(
            conv_edge_body,
            [shape(*grid)],
            (main, y_low, y_high, conv_weight),
            [VM, VM, VM, SM],
            scratch=[pltpu.VMEM((size_x + 16, depth), F32)],
            name="conv_edge",
        )
    with jax.named_scope("squash"):
        parts = lax.all_to_all(part, "shot", 0, 0, tiled=True)
        squashed = call(
            squash_body,
            [shape(shots, rows, size_y, depth)],
            (parts.reshape(shots, rows, size_y, depth),),
            [VM],
            name="squash",
        )
        squashed = lax.all_to_all(squashed.reshape(grid), "shot", 0, 0, tiled=True)

    scratch = [
        pltpu.VMEM((size_x + 8, size_y, depth), F32),
        pltpu.VMEM((size_x + 8, size_y, depth), F32),
        pltpu.VMEM((size_x, size_y + 16, depth), F32),
        pltpu.VMEM((size_x, size_y + 16, depth), F32),
        pltpu.VMEM(grid, F32),
    ]
    full = shape(*grid)
    specs = [VM] * 9 + [SM, SM, VM, VM]

    def step_1(*refs):
        step_body(0, plane_y, rows, refs)

    def step_2(*refs):
        step_body(1, plane_y, rows, refs)

    with jax.named_scope("step_1"):
        fwd_1, back_1, lap_1, trace_1, x_up, x_down, y_up, y_down = call(
            step_1,
            [full, full, full, shape(1, count)]
            + [shape(8, size_y, depth)] * 2
            + [shape(size_x, 8, depth)] * 2,
            (
                fwd_now,
                back_now,
                fwd_prev,
                back_prev,
                squashed,
                x_low,
                x_high,
                y_low,
                y_high,
                place,
                wavelet,
                receivers,
                residual,
            ),
            specs,
            scratch=scratch,
            name="step_1",
        )
    with jax.named_scope("halo_2"):
        y_low_2, y_high_2 = neighbours(y_up, y_down, "gy")
        x_low_2, x_high_2 = neighbours(x_up, x_down, "gx")
    with jax.named_scope("step_2"):
        fwd_2, back_2, sums, trace_2 = call(
            step_2,
            [full, full, shape(shots, 2 * rows, size_y, depth), shape(1, count)],
            (
                fwd_1,
                back_1,
                fwd_now,
                back_now,
                squashed,
                x_low_2,
                x_high_2,
                y_low_2,
                y_high_2,
                place,
                wavelet,
                receivers,
                residual,
                lap_1,
            ),
            specs + [VM],
            scratch=scratch,
            name="step_2",
        )
    with jax.named_scope("update"):
        sums = lax.all_to_all(
            sums.reshape(shots * 2 * rows, size_y, depth), "shot", 0, 0, tiled=True
        )
        update = call(
            update_body,
            [shape(shots, rows, size_y, depth)],
            (sums.reshape(shots, 2 * rows, size_y, depth), damping),
            [VM, SM],
            name="update",
        )
        update = lax.all_to_all(update.reshape(grid), "shot", 0, 0, tiled=True)
    with jax.named_scope("gradient"):
        share = call(
            gradient_body,
            [shape(blocks, 16, depth)],
            (update, squashed, features, x_low, x_high, y_low, y_high, trace_1, trace_2),
            [VM] * 9,
            scratch=[
                ext,
                pltpu.VMEM((9,) + grid, F32),
                pltpu.VMEM((3, size_x + 16, depth), F32),
                pltpu.VMEM((128, depth), F32),
            ],
            flops=54 * channels * size_x * size_y * depth,
            name="gradient",
        )
        shares = lax.all_to_all(
            share.reshape(blocks * 16, depth), ("gx", "gy"), 0, 0, tiled=True
        )
        total = jnp.sum(shares.reshape(blocks, 16, depth), axis=0)
    traces = total[:8].reshape(-1)[: 2 * count].reshape(1, 2, count)
    weight_grad = total[8, : 27 * channels].reshape(channels, 27)
    return (fwd_2[None], back_2[None], traces, update, weight_grad)


def solution(mesh):
    in_specs = (
        P("shot", "gx", "gy", None),
        P("shot", None),
        P("shot", "gx", "gy", None),
        P("shot", "gx", "gy", None),
        P("shot", "gx", "gy", None),
        P("shot", "gx", "gy", None),
        P("shot"),
        P("shot", None),
        P("shot", None),
        P("shot", None, None),
        P(),
    )
    out_specs = (
        P("shot", "gx", "gy", None),
        P("shot", "gx", "gy", None),
        P("shot", None, None),
        P("gx", "gy", None),
        P("shot", None),
    )
    return jax.shard_map(
        per_device, mesh=mesh, in_specs=in_specs, out_specs=out_specs, check_vma=False
    )
```

time: 651 us -> 207 us (0.32)
  the two profiles are of different devices: /device:TPU:64 before, /device:TPU:32 now
where the time goes in v1:
time: 207 us; the launch traced here: 206 us
  blocking collectives  65.7 us (32%)
  waiting for transfers between devices  63.2 us (31%)
  starting transfers between devices  48.9 us (24%)
  Pallas kernels  20.2 us (10%)
  local copies, waits for them, and re-layouts  5.57 us (3%)
  between operations  2.13 us (1%)
    all_to_all x1, blocking collectives, per_device(): lax.all_to_all(share.reshape(blocks * 16, depth), ('gx', 'gy'), 0, 0, til...  44 us
    ppermute x4, waiting for transfers between devices, neighbours(): high = lax.ppermute(down, axis, [(i + 1, i) for i in range(count - 1)])  35 us
    ppermute x4, starting transfers between devices, neighbours(): low = lax.ppermute(up, axis, [(i, i + 1) for i in range(count - 1)])  30.5 us
    pallas_call x9, Pallas kernels, call(): pl.pallas_call(body, out_shape=outs[0] if single else tuple(outs), in_spe...  20.2 us
    ppermute x4, waiting for transfers between devices, neighbours(): low = lax.ppermute(up, axis, [(i, i + 1) for i in range(count - 1)])  11.8 us
    all_to_all x1, blocking collectives, per_device(): parts = lax.all_to_all(part, 'shot', 0, 0, tiled=True)  11.6 us
    ppermute x4, starting transfers between devices, neighbours(): high = lax.ppermute(down, axis, [(i + 1, i) for i in range(count - 1)])  11.4 us
    all_to_all x1, blocking collectives, per_device(): update = lax.all_to_all(update.reshape(grid), 'shot', 0, 0, tiled=True)  10.1 us
  transfers between devices with their start and end apart: 10, of which 8 were waited for; matrix products, arithmetic and copies ran while one was open for 0% of the time, Pallas kernels for 2%

profile of v1, /device:TPU:32, one launch (start us, length us, event | category | flops | bytes accessed | tf_op | source)
XLA Modules:
  0.0 205.9 jit_solution(14018613236528558149)
XLA Ops:
  0.6 0.0 copy-start
  0.6 1.0 copy-done
  1.7 0.0 copy-start.2
  1.7 0.9 copy-done.2
  2.6 0.0 copy-start.4
  2.6 0.9 copy-done.4
  3.6 3.8 %collective-permute-start = (f32[12,16,128]{2,1,0:T(8,128)S(1)}, f32[12,16,128]{2,1,0:T(8,128)S(1)}, u32[]{:S(2)}, u32[]{:S(2)}) collective-permute-start(f32[12,16,128]{2,1,0:T(8,128)S(1)} %get-tuple-element.21), channel_id=1, source_target_pairs={{0,8},{8,16},{16,24},{24,32},{32,40},{40,48},{48,56},{1,9},{9,17},... | collective-permute-start | bytes 294920 | tf_op jit(solution)/shard_map/halo_x/ppermute | solution.py:405
  7.4 4.9 %collective-permute-start.1 = (f32[12,16,128]{2,1,0:T(8,128)S(1)}, f32[12,16,128]{2,1,0:T(8,128)S(1)}, u32[]{:S(2)}, u32[]{:S(2)}) collective-permute-start(f32[12,16,128]{2,1,0:T(8,128)S(1)} %get-tuple-element.22), channel_id=1, source_target_pairs={{8,0},{16,8},{24,16},{32,24},{40,32},{48,40},{56,48},{9,1},{17,9},... | collective-permute-start | bytes 294920 | tf_op jit(solution)/shard_map/halo_x/ppermute | solution.py:406
  12.3 0.7 collective-permute-done.low_ref.refs_5_.x_low_ref
  12.9 1.5 collective-permute-done.1.high_ref.refs_6_.x_high_ref
  14.5 0.2 pack_y.1
  14.7 0.0 copy-start.9
  14.7 13.4 %collective-permute-start.2 = (f32[52,8,128]{2,1,0:T(8,128)S(1)}, f32[52,8,128]{2,1,0:T(8,128)S(1)}, u32[]{:S(2)}, u32[]{:S(2)}) collective-permute-start(f32[52,8,128]{2,1,0:T(8,128)S(1)} %get-tuple-element.23), channel_id=1, source_target_pairs={{0,1},{1,2},{2,3},{3,4},{4,5},{5,6},{6,7},{8,9},{9,10},{10,11},{11... | collective-permute-start | bytes 638984 | tf_op jit(solution)/shard_map/halo_y/ppermute | solution.py:405
  28.1 1.3 collective-permute-start.3
  29.4 0.0 copy-done.9
  29.4 4.6 %conv.1.main_ref = f32[32,16,128]{2,1,0:T(8,128)S(1)} custom-call(bf16[4,32,16,128]{3,2,1,0:T(8,128)(2,1)S(1)} %copy-done, f32[12,16,128]{2,1,0:T(8,128)S(1)} %collective-permute-done.low_ref.refs_5_.x_low_ref, f32[12,16,128]{2,1,0:T(8,128)S(1)} %collective-permute-done.1.high_ref.refs_6_.x_high_ref, f32[4,27]{1,0:T(4,128)S(1)} %copy-done.9), custom_call_target="tpu_custom_call" | custom-call | flops 14155776 | bytes 983472 | tf_op jit(solution)/shard_map/conv/conv/pallas_call | solution.py:25
  34.0 4.9 %collective-permute-done.2.low_ref.refs_7_.y_low_ref = f32[52,8,128]{2,1,0:T(8,128)S(1)} collective-permute-done((f32[52,8,128]{2,1,0:T(8,128)S(1)}, f32[52,8,128]{2,1,0:T(8,128)S(1)}, u32[]{:S(2)}, u32[]{:S(2)}) %collective-permute-start.2) | collective-permute-done | bytes 213024 | tf_op jit(solution)/shard_map/halo_y/ppermute | solution.py:405
  38.9 26.9 %collective-permute-done.3.high_ref.refs_8_.y_high_ref = f32[52,8,128]{2,1,0:T(8,128)S(1)} collective-permute-done((f32[52,8,128]{2,1,0:T(8,128)S(1)}, f32[52,8,128]{2,1,0:T(8,128)S(1)}, u32[]{:S(2)}, u32[]{:S(2)}) %collective-permute-start.3) | collective-permute-done | bytes 213024 | tf_op jit(solution)/shard_map/halo_y/ppermute | solution.py:406
  65.8 0.7 conv_edge.1
  66.6 11.6 %all_to_all.26 = f32[32,16,128]{2,1,0:T(8,128)S(1)} all-to-all(f32[32,16,128]{2,1,0:T(8,128)S(1)} %conv_edge.1), channel_id=1, replica_groups=mesh['shot'=8,'gx'=8,'gy'=8] {'shot'}, dimensions={0} | all-to-all | bytes 524288 | tf_op jit(solution)/shard_map/squash/all_to_all | solution.py:477
  78.2 0.0 copy-start.6
  78.2 0.0 copy-start.7
  78.2 0.7 squash.1
  79.0 0.0 copy-start.3
  79.0 0.0 copy-start.5
  79.0 3.5 %all-to-all-start.1 = ((f32[32,16,128]{2,1,0:T(8,128)}), f32[32,16,128]{2,1,0:T(8,128)S(1)}, u32[]{:S(2)}, u32[]{:S(2)}) async-start(f32[32,16,128]{2,1,0:T(8,128)} %bitcast.5), calls=%async_computation.1 | async-start | bytes 524288 | tf_op jit(solution)/shard_map/squash/all_to_all | solution.py:485
  83.2 0.0 copy-start.8
  83.2 0.1 pad_add_fusion.refs_9_
  83.3 0.0 copy-start.10
  83.3 6.7 %all-to-all-done.1.refs_4_.squashed_ref = f32[32,16,128]{2,1,0:T(8,128)S(1)} async-done(((f32[32,16,128]{2,1,0:T(8,128)}), f32[32,16,128]{2,1,0:T(8,128)S(1)}, u32[]{:S(2)}, u32[]{:S(2)}) %all-to-all-start.1) | async-done | bytes 262176 | tf_op jit(solution)/shard_map/squash/all_to_all | solution.py:485
  90.0 0.0 copy-start.11
  90.0 0.0 copy-done.6
  90.0 0.0 copy-done.7
  90.0 0.0 copy-done.3
  90.0 0.0 copy-done.5
  90.0 0.0 copy-done.8
  90.0 0.0 copy-done.10
  90.0 0.6 copy-done.11
  90.6 3.6 %step_1.1 = (f32[32,16,128]{2,1,0:T(8,128)S(1)}, f32[32,16,128]{2,1,0:T(8,128)S(1)}, f32[32,16,128]{2,1,0:T(8,128)S(1)}, f32[1,512]{1,0:T(1,128)S(1)}, f32[8,16,...) custom-call(f32[32,16,128]{2,1,0:T(8,128)S(1)} %bitcast.15, ...), custom_call_target="tpu_custom_call" | custom-call | flops 1000000 | bytes 3121172 | tf_op jit(solution)/shard_map/step_1/step_1/pallas_call | solution.py:25
  94.3 11.4 %collective-permute-start.6 = (f32[32,8,128]{2,1,0:T(8,128)S(1)}, f32[32,8,128]{2,1,0:T(8,128)S(1)}, u32[]{:S(2)}, u32[]{:S(2)}) collective-permute-start(f32[32,8,128]{2,1,0:T(8,128)S(1)} %get-tuple-element.29), channel_id=1, source_target_pairs={{0,1},{1,2},{2,3},{3,4},{4,5},{5,6},{6,7},{8,9},{9,10},{10,11},{11... | collective-permute-start | bytes 393224 | tf_op jit(solution)/shard_map/halo_2/ppermute | solution.py:405
  105.7 1.3 collective-permute-start.7
  107.0 1.9 collective-permute-start.4
  108.9 3.9 %collective-permute-start.5 = (f32[8,16,128]{2,1,0:T(8,128)S(1)}, f32[8,16,128]{2,1,0:T(8,128)S(1)}, u32[]{:S(2)}, u32[]{:S(2)}) collective-permute-start(f32[8,16,128]{2,1,0:T(8,128)S(1)} %get-tuple-element.28), channel_id=1, source_target_pairs={{8,0},{16,8},{24,16},{32,24},{40,32},{48,40},{56,48},{9,1},{17,9},... | collective-permute-start | bytes 196616 | tf_op jit(solution)/shard_map/halo_2/ppermute | solution.py:406
  112.8 6.3 %collective-permute-done.4.refs_5_ = f32[8,16,128]{2,1,0:T(8,128)S(1)} collective-permute-done((f32[8,16,128]{2,1,0:T(8,128)S(1)}, f32[8,16,128]{2,1,0:T(8,128)S(1)}, u32[]{:S(2)}, u32[]{:S(2)}) %collective-permute-start.4) | collective-permute-done | bytes 65568 | tf_op jit(solution)/shard_map/halo_2/ppermute | solution.py:405
  119.1 0.0 collective-permute-done.5.refs_6_
  119.1 0.0 collective-permute-done.6.refs_7_
  119.1 6.6 %collective-permute-done.7.refs_8_ = f32[32,8,128]{2,1,0:T(8,128)S(1)} collective-permute-done((f32[32,8,128]{2,1,0:T(8,128)S(1)}, f32[32,8,128]{2,1,0:T(8,128)S(1)}, u32[]{:S(2)}, u32[]{:S(2)}) %collective-permute-start.7) | collective-permute-done | bytes 131104 | tf_op jit(solution)/shard_map/halo_2/ppermute | solution.py:406
  125.7 4.0 %step_2.1 = (f32[32,16,128]{2,1,0:T(8,128)}, f32[32,16,128]{2,1,0:T(8,128)}, f32[8,8,16,128]{3,2,1,0:T(8,128)}, f32[1,512]{1,0:T(1,128)S(1)}) custom-call(f32[32,16,128]{2,1,0:T(8,128)S(1)} %get-tuple-element.25.refs_0_, f32[32,16,128]{2,1,0:T(8,128)S(1)} %get-tuple-element.26.refs_1_, f32[32,16,128]{2,1,0:T(8,128)S(1)} %bitcast.16, ...), custom_call_target="tpu_custom_call" | custom-call | flops 1000000 | bytes 3022868 | tf_op jit(solution)/shard_map/step_2/step_2/pallas_call | solution.py:25
  129.7 3.5 %all-to-all-start.2 = ((f32[64,16,128]{2,1,0:T(8,128)}), f32[64,16,128]{2,1,0:T(8,128)S(1)}, u32[]{:S(2)}, u32[]{:S(2)}) async-start(f32[64,16,128]{2,1,0:T(8,128)} %bitcast.10), calls=%async_computation.2 | async-start | bytes 1048576 | tf_op jit(solution)/shard_map/update/all_to_all | solution.py:556
  133.8 9.6 %all-to-all-done.2 = f32[64,16,128]{2,1,0:T(8,128)S(1)} async-done(((f32[64,16,128]{2,1,0:T(8,128)}), f32[64,16,128]{2,1,0:T(8,128)S(1)}, u32[]{:S(2)}, u32[]{:S(2)}) %all-to-all-start.2) | async-done | bytes 524320 | tf_op jit(solution)/shard_map/update/all_to_all | solution.py:556
  143.5 0.0 copy-start.1
  143.5 10.1 %all_to_all.27.update_ref = f32[32,16,128]{2,1,0:T(8,128)S(1)} all-to-all(f32[32,16,128]{2,1,0:T(8,128)S(1)} %bitcast.23), channel_id=1, replica_groups=mesh['shot'=8,'gx'=8,'gy'=8] {'shot'}, dimensions={0} | all-to-all | bytes 524288 | tf_op jit(solution)/shard_map/update/all_to_all | solution.py:566
  153.6 0.0 copy-done.1
  153.6 6.3 %gradient.1 = f32[64,16,128]{2,1,0:T(8,128)S(1)} custom-call(f32[32,16,128]{2,1,0:T(8,128)S(1)} %all_to_all.27.update_ref, f32[32,16,128]{2,1,0:T(8,128)S(1)} %all-to-all-done.1.refs_4_.squashed_ref, bf16[4,32,16,128]{3,2,1,0:T(8,128)(2,1)S(1)} %copy-done.1, f32[12,16,128]{2,1,0:T(8,128)S(1)} %collective-permute-done.low_ref.refs_5_.x_low_ref, ...), custom_call_target="tpu_custom_call" | custom-call | flops 14155776 | bytes 2199552 | tf_op jit(solution)/shard_map/gradient/gradient/pallas_call | solution.py:25
  159.8 44.0 %all_to_all.28 = f32[64,16,128]{2,1,0:T(8,128)S(1)} all-to-all(f32[64,16,128]{2,1,0:T(8,128)S(1)} %gradient.1), channel_id=1, replica_groups=mesh['shot'=8,'gx'=8,'gy'=8] {'gx','gy'}, dimensions={0} | all-to-all | bytes 1048576 | tf_op jit(solution)/shard_map/gradient/all_to_all | solution.py:582
  203.9 0.1 reduce_sum.9
  204.0 0.6 reshape_reshape.3
  204.6 0.7 reshape_squeeze.3
  205.2 0.7 copy.19
  (4 shorter events, 0.1 us)
Async XLA Ops:
  0.6 1.0 copy-start
  1.7 0.9 copy-start.2
  2.6 0.9 copy-start.4
  3.6 9.4 %collective-permute-start = (f32[12,16,128]{2,1,0:T(8,128)S(1)}, f32[12,16,128]{2,1,0:T(8,128)S(1)}, u32[]{:S(2)}, u32[]{:S(2)}) collective-permute-start(f32[12,16,128]{2,1,0:T(8,128)S(1)} %get-tuple-element.21), channel_id=1, source_target_pairs={{0,8},{8,16},{16,24},{24,32},{32,40},{40,48},{48,56},{1,9},{9,17},... | collective-permute-start | bytes 294920 | tf_op jit(solution)/shard_map/halo_x/ppermute | solution.py:405
  7.4 7.1 %collective-permute-start.1 = (f32[12,16,128]{2,1,0:T(8,128)S(1)}, f32[12,16,128]{2,1,0:T(8,128)S(1)}, u32[]{:S(2)}, u32[]{:S(2)}) collective-permute-start(f32[12,16,128]{2,1,0:T(8,128)S(1)} %get-tuple-element.22), channel_id=1, source_target_pairs={{8,0},{16,8},{24,16},{32,24},{40,32},{48,40},{56,48},{9,1},{17,9},... | collective-permute-start | bytes 294920 | tf_op jit(solution)/shard_map/halo_x/ppermute | solution.py:406
  14.7 14.7 %copy-start.9 = (f32[4,27]{1,0:T(4,128)S(1)}, f32[4,27]{1,0:T(4,128)}, u32[]{:S(2)}) copy-start(f32[4,27]{1,0:T(4,128)} %weight_ref.3) | copy-start | bytes 1300
  14.7 24.2 %collective-permute-start.2 = (f32[52,8,128]{2,1,0:T(8,128)S(1)}, f32[52,8,128]{2,1,0:T(8,128)S(1)}, u32[]{:S(2)}, u32[]{:S(2)}) collective-permute-start(f32[52,8,128]{2,1,0:T(8,128)S(1)} %get-tuple-element.23), channel_id=1, source_target_pairs={{0,1},{1,2},{2,3},{3,4},{4,5},{5,6},{6,7},{8,9},{9,10},{10,11},{11... | collective-permute-start | bytes 638984 | tf_op jit(solution)/shard_map/halo_y/ppermute | solution.py:405
  28.1 37.8 %collective-permute-start.3 = (f32[52,8,128]{2,1,0:T(8,128)S(1)}, f32[52,8,128]{2,1,0:T(8,128)S(1)}, u32[]{:S(2)}, u32[]{:S(2)}) collective-permute-start(f32[52,8,128]{2,1,0:T(8,128)S(1)} %get-tuple-element.24), channel_id=1, source_target_pairs={{1,0},{2,1},{3,2},{4,3},{5,4},{6,5},{7,6},{9,8},{10,9},{11,10},{12... | collective-permute-start | bytes 638984 | tf_op jit(solution)/shard_map/halo_y/ppermute | solution.py:406
  78.2 11.8 %copy-start.6 = (f32[1,32,16,128]{3,2,1,0:T(8,128)S(1)}, f32[1,32,16,128]{3,2,1,0:T(8,128)}, u32[]{:S(2)}) copy-start(f32[1,32,16,128]{3,2,1,0:T(8,128)} %param.13) | copy-start | bytes 786436
  78.2 11.8 %copy-start.7 = (f32[1,32,16,128]{3,2,1,0:T(8,128)S(1)}, f32[1,32,16,128]{3,2,1,0:T(8,128)}, u32[]{:S(2)}) copy-start(f32[1,32,16,128]{3,2,1,0:T(8,128)} %param.15) | copy-start | bytes 786436
  79.0 11.0 %copy-start.3 = (f32[1,32,16,128]{3,2,1,0:T(8,128)S(1)}, f32[1,32,16,128]{3,2,1,0:T(8,128)}, u32[]{:S(2)}) copy-start(f32[1,32,16,128]{3,2,1,0:T(8,128)} %param.14) | copy-start | bytes 786436
  79.0 11.0 %copy-start.5 = (f32[1,32,16,128]{3,2,1,0:T(8,128)S(1)}, f32[1,32,16,128]{3,2,1,0:T(8,128)}, u32[]{:S(2)}) copy-start(f32[1,32,16,128]{3,2,1,0:T(8,128)} %param.16) | copy-start | bytes 786436
  79.0 11.0 %all-to-all-start.1 = ((f32[32,16,128]{2,1,0:T(8,128)}), f32[32,16,128]{2,1,0:T(8,128)S(1)}, u32[]{:S(2)}, u32[]{:S(2)}) async-start(f32[32,16,128]{2,1,0:T(8,128)} %bitcast.5), calls=%async_computation.1 | async-start | bytes 524288 | tf_op jit(solution)/shard_map/squash/all_to_all | solution.py:485
  83.2 6.8 %copy-start.8 = (f32[1,2,512]{2,1,0:T(2,128)S(1)}, f32[1,2,512]{2,1,0:T(2,128)}, u32[]{:S(2)}) copy-start(f32[1,2,512]{2,1,0:T(2,128)} %refs_12_.3) | copy-start | bytes 12292
  83.3 6.8 %copy-start.10 = (s32[1,512]{1,0:T(1,128)S(1)}, s32[1,512]{1,0:T(1,128)}, u32[]{:S(2)}) copy-start(s32[1,512]{1,0:T(1,128)} %refs_11_.3) | copy-start | bytes 6148
  90.0 0.7 copy-start.11
  94.3 24.9 %collective-permute-start.6 = (f32[32,8,128]{2,1,0:T(8,128)S(1)}, f32[32,8,128]{2,1,0:T(8,128)S(1)}, u32[]{:S(2)}, u32[]{:S(2)}) collective-permute-start(f32[32,8,128]{2,1,0:T(8,128)S(1)} %get-tuple-element.29), channel_id=1, source_target_pairs={{0,1},{1,2},{2,3},{3,4},{4,5},{5,6},{6,7},{8,9},{9,10},{10,11},{11... | collective-permute-start | bytes 393224 | tf_op jit(solution)/shard_map/halo_2/ppermute | solution.py:405
  105.7 20.0 %collective-permute-start.7 = (f32[32,8,128]{2,1,0:T(8,128)S(1)}, f32[32,8,128]{2,1,0:T(8,128)S(1)}, u32[]{:S(2)}, u32[]{:S(2)}) collective-permute-start(f32[32,8,128]{2,1,0:T(8,128)S(1)} %get-tuple-element.30), channel_id=1, source_target_pairs={{1,0},{2,1},{3,2},{4,3},{5,4},{6,5},{7,6},{9,8},{10,9},{11,10},{12... | collective-permute-start | bytes 393224 | tf_op jit(solution)/shard_map/halo_2/ppermute | solution.py:406
  107.0 12.2 %collective-permute-start.4 = (f32[8,16,128]{2,1,0:T(8,128)S(1)}, f32[8,16,128]{2,1,0:T(8,128)S(1)}, u32[]{:S(2)}, u32[]{:S(2)}) collective-permute-start(f32[8,16,128]{2,1,0:T(8,128)S(1)} %get-tuple-element.27), channel_id=1, source_target_pairs={{0,8},{8,16},{16,24},{24,32},{32,40},{40,48},{48,56},{1,9},{9,17},... | collective-permute-start | bytes 196616 | tf_op jit(solution)/shard_map/halo_2/ppermute | solution.py:405
  108.9 10.2 %collective-permute-start.5 = (f32[8,16,128]{2,1,0:T(8,128)S(1)}, f32[8,16,128]{2,1,0:T(8,128)S(1)}, u32[]{:S(2)}, u32[]{:S(2)}) collective-permute-start(f32[8,16,128]{2,1,0:T(8,128)S(1)} %get-tuple-element.28), channel_id=1, source_target_pairs={{8,0},{16,8},{24,16},{32,24},{40,32},{48,40},{56,48},{9,1},{17,9},... | collective-permute-start | bytes 196616 | tf_op jit(solution)/shard_map/halo_2/ppermute | solution.py:406
  129.7 13.8 %all-to-all-start.2 = ((f32[64,16,128]{2,1,0:T(8,128)}), f32[64,16,128]{2,1,0:T(8,128)S(1)}, u32[]{:S(2)}, u32[]{:S(2)}) async-start(f32[64,16,128]{2,1,0:T(8,128)} %bitcast.10), calls=%async_computation.2 | async-start | bytes 1048576 | tf_op jit(solution)/shard_map/update/all_to_all | solution.py:556
  143.5 10.1 %copy-start.1 = (bf16[4,32,16,128]{3,2,1,0:T(8,128)(2,1)S(1)}, bf16[4,32,16,128]{3,2,1,0:T(8,128)(2,1)}, u32[]{:S(2)}) copy-start(bf16[4,32,16,128]{3,2,1,0:T(8,128)(2,1)} %feat_ref.7) | copy-start | bytes 1572868

commit v2 on v1

--- a/solution.py
+++ b/solution.py
@@ -17,13 +17,14 @@
 SM = pl.BlockSpec(memory_space=pltpu.SMEM)
 
 
-def call(body, outs, ins, specs, scratch=(), flops=1_000_000, name=None):
+def call(body, outs, ins, specs, scratch=(), flops=1_000_000, name=None, grid=()):
     moved = sum(a.size * a.dtype.itemsize for a in ins) + sum(
         o.size * jnp.dtype(o.dtype).itemsize for o in outs
     )
     single = len(outs) == 1
     return pl.pallas_call(
         body,
+        grid=grid,
         out_shape=outs[0] if single else tuple(outs),
         in_specs=specs,
         out_specs=VM if single else tuple(VM for _ in outs),
@@ -62,35 +63,46 @@
     return jnp.where(row >= -by, pltpu.roll(value, -by, 0), 0.0)
 
 
-def pack_x_body(feat_ref, fwd_ref, back_ref, up_ref, down_ref):
-    channels, size_x = feat_ref.shape[:2]
-    up_ref[0:4] = fwd_ref[size_x - 4 : size_x]
-    up_ref[4:8] = back_ref[size_x - 4 : size_x]
-    down_ref[0:4] = fwd_ref[0:4]
-    down_ref[4:8] = back_ref[0:4]
+def pack_x_body(
+    feat_first_ref,
+    feat_last_ref,
+    fwd_first_ref,
+    fwd_last_ref,
+    back_first_ref,
+    back_last_ref,
+    up_ref,
+    down_ref,
+):
+    channels = feat_first_ref.shape[0]
+    up_ref[0:4] = fwd_last_ref[...]
+    up_ref[4:8] = back_last_ref[...]
+    down_ref[0:4] = fwd_first_ref[...]
+    down_ref[4:8] = back_first_ref[...]
     for c in range(channels):
-        up_ref[8 + c] = feat_ref[c, size_x - 1].astype(F32)
-        down_ref[8 + c] = feat_ref[c, 0].astype(F32)
-
-
-def pack_y_body(feat_ref, fwd_ref, back_ref, low_ref, high_ref, up_ref, down_ref, plane_ref):
+        up_ref[8 + c] = feat_last_ref[c, 0].astype(F32)
+        down_ref[8 + c] = feat_first_ref[c, 0].astype(F32)
+
+
+def pack_y_body(feat_ref, low_ref, high_ref, up_ref, down_ref, plane_ref):
     channels, size_x, size_y, depth = feat_ref.shape
-    groups = size_x // 8 + 1
-    up_ref[0:size_x, 0:4] = fwd_ref[:, size_y - 4 : size_y]
-    up_ref[0:size_x, 4:8] = back_ref[:, size_y - 4 : size_y]
-    down_ref[0:size_x, 0:4] = fwd_ref[:, 0:4]
-    down_ref[0:size_x, 4:8] = back_ref[:, 0:4]
-    row = lax.broadcasted_iota(jnp.int32, (8, depth), 0)
+    row = lax.broadcasted_iota(jnp.int32, (16, depth), 0)
+    tails = [jnp.zeros((16, depth), F32), jnp.zeros((16, depth), F32)]
     for c in range(channels):
         plane_ref[...] = feat_ref[c].astype(F32)
-        for out_ref, y in ((up_ref, size_y - 1), (down_ref, 0)):
-            own = plane_ref[:, y, :]
-            first = size_x + c * groups
-            out_ref[first : first + groups - 1] = own.reshape(groups - 1, 8, depth)
-            low = low_ref[8 + c, y : y + 1, :]
-            high = high_ref[8 + c, y : y + 1, :]
-            tail = jnp.where(row == 0, low, jnp.where(row == 1, high, 0.0))
-            out_ref[first + groups - 1] = tail
+        for n, (out_ref, y) in enumerate(((up_ref, size_y - 1), (down_ref, 0))):
+            out_ref[c * size_x : (c + 1) * size_x] = plane_ref[:, y, :].astype(BF16)
+            tails[n] = jnp.where(row == 2 * c, low_ref[8 + c, y : y + 1, :], tails[n])
+            tails[n] = jnp.where(row == 2 * c + 1, high_ref[8 + c, y : y + 1, :], tails[n])
+    for tail, out_ref in zip(tails, (up_ref, down_ref)):
+        out_ref[channels * size_x : channels * size_x + 16] = tail.astype(BF16)
+
+
+def pack_waves_body(fwd_ref, back_ref, up_ref, down_ref):
+    size_y = fwd_ref.shape[1]
+    up_ref[:, 0:4] = fwd_ref[:, size_y - 4 : size_y]
+    up_ref[:, 4:8] = back_ref[:, size_y - 4 : size_y]
+    down_ref[:, 0:4] = fwd_ref[:, 0:4]
+    down_ref[:, 4:8] = back_ref[:, 0:4]
 
 
 def fill_features(ext_ref, feat_ref, low_ref, high_ref):
@@ -131,13 +143,11 @@
     lax.fori_loop(0, size_x, one_row, 0)
 
 
-def load_plane(plane_ref, buffer_ref, c, size_x):
-    groups = size_x // 8 + 1
-    depth = plane_ref.shape[1]
-    first = size_x + c * groups
-    plane_ref[8 : 8 + size_x] = buffer_ref[first : first + groups - 1].reshape(size_x, depth)
-    plane_ref[7:8] = buffer_ref[first + groups - 1, 0:1, :]
-    plane_ref[8 + size_x : 9 + size_x] = buffer_ref[first + groups - 1, 1:2, :]
+def load_plane(plane_ref, buffer_ref, c, size_x, channels):
+    plane_ref[8 : 8 + size_x] = buffer_ref[c * size_x : (c + 1) * size_x].astype(F32)
+    tail = buffer_ref[channels * size_x : channels * size_x + 16].astype(F32)
+    plane_ref[7:8] = tail[2 * c : 2 * c + 1]
+    plane_ref[8 + size_x : 9 + size_x] = tail[2 * c + 1 : 2 * c + 2]
 
 
 def conv_edge_body(main_ref, low_ref, high_ref, weight_ref, out_ref, plane_ref):
@@ -147,7 +157,7 @@
     for buffer_ref, dy, y in ((low_ref, 0, 0), (high_ref, 2, size_y - 1)):
         terms = [None] * 3
         for c in range(channels):
-            load_plane(plane_ref, buffer_ref, c, size_x)
+            load_plane(plane_ref, buffer_ref, c, size_x, channels)
             for dx in range(3):
                 rows = plane_ref[7 + dx : 7 + dx + size_x]
                 for dz in range(3):
@@ -372,7 +382,7 @@
         pulled = plane_ref[which, 0:size_x]
         along = [pulled if dz == 1 else shifted_lanes(pulled, 1 - dz) for dz in range(3)]
         for c in range(channels):
-            load_plane(plane_ref.at[0], buffer_ref, c, size_x)
+            load_plane(plane_ref.at[0], buffer_ref, c, size_x, channels)
             for dx in range(3):
                 features = plane_ref[0, 7 + dx : 7 + dx + size_x]
                 for dz in range(3):
@@ -388,16 +398,28 @@
             ones, part, (((1,), (1,)), ((), ())), preferred_element_type=F32
         )
         sums = product if sums is None else sums + product
-    row = lax.broadcasted_iota(jnp.int32, (8, depth), 0)
-    lines = jnp.zeros((8, depth), F32)
-    for moment, ref in enumerate((first_ref, second_ref)):
-        pieces = ref.shape[1] // depth
-        for q in range(pieces):
-            piece = ref[0:1, q * depth : (q + 1) * depth]
-            lines = jnp.where(row == moment * pieces + q, piece, lines)
+    count = first_ref.shape[1]
     for n in range(copies):
-        out_ref[n, 0:8] = lines
-        out_ref[n, 8:16] = sums
+        out_ref[n, :, 0:count] = first_ref[...]
+        out_ref[n, :, count : 2 * count] = second_ref[...]
+        out_ref[n, :, 2 * count : 2 * count + depth] = sums[0:1]
+
+
+def total_body(shares_ref, trace_ref, grad_ref):
+    copies = shares_ref.shape[0]
+    count = trace_ref.shape[2]
+    channels, offsets = grad_ref.shape
+    total = shares_ref[0]
+    for n in range(1, copies):
+        total = total + shares_ref[n]
+    trace_ref[0, 0:1, :] = total[:, 0:count]
+    trace_ref[0, 1:2, :] = total[:, count : 2 * count]
+    last = total[:, 2 * count :]
+    lanes = last.shape[1]
+    last = jnp.broadcast_to(last, (8, lanes))
+    for c in range(channels):
+        turned = last if c == 0 else pltpu.roll(last, lanes - c * offsets, 1)
+        grad_ref[c : c + 1, :] = turned[0:1, 0:offsets]
 
 
 def neighbours(up, down, axis):
@@ -426,7 +448,6 @@
     count = receivers.shape[1]
     plane_y = size_y * lax.axis_size("gy")
     blocks = lax.axis_size("gx") * lax.axis_size("gy")
-    groups = size_x // 8 + 1
     grid = (size_x, size_y, depth)
     fwd_prev, fwd_now, back_prev, back_now = (
         a.reshape(grid) for a in (fwd_prev, fwd_now, back_prev, back_now)
@@ -435,20 +456,33 @@
         [lax.axis_index("gx") * size_x, lax.axis_index("gy") * size_y, sources[0]]
     ).astype(jnp.int32)
 
+    def edge(last):
+        return pl.BlockSpec((4, size_y, depth), lambda i: ((size_x // 4 - 1) * last, 0, 0))
+
+    def feature_edge(last):
+        return pl.BlockSpec(
+            (channels, 1, size_y, depth), lambda i: (0, (size_x - 1) * last, 0, 0)
+        )
+
     x_shape = shape(8 + channels, size_y, depth)
     with jax.named_scope("pack_x"):
         x_up, x_down = call(
-            pack_x_body, [x_shape, x_shape], (features, fwd_now, back_now), [VM] * 3, name="pack_x"
+            pack_x_body,
+            [x_shape, x_shape],
+            (features, features, fwd_now, fwd_now, back_now, back_now),
+            [feature_edge(0), feature_edge(1), edge(0), edge(1), edge(0), edge(1)],
+            name="pack_x",
+            grid=(1,),
         )
     with jax.named_scope("halo_x"):
         x_low, x_high = neighbours(x_up, x_down, "gx")
-    y_shape = shape(size_x + channels * groups, 8, depth)
+    y_shape = shape(channels * size_x + 16, depth, dtype=BF16)
     with jax.named_scope("pack_y"):
         y_up, y_down = call(
             pack_y_body,
             [y_shape, y_shape],
-            (features, fwd_now, back_now, x_low, x_high),
-            [VM] * 5,
+            (features, x_low, x_high),
+            [VM] * 3,
             scratch=[pltpu.VMEM(grid, F32)],
             name="pack_y",
         )
@@ -473,8 +507,19 @@
             scratch=[pltpu.VMEM((size_x + 16, depth), F32)],
             name="conv_edge",
         )
+    wave_shape = shape(size_x, 8, depth)
+    with jax.named_scope("pack_waves"):
+        wave_up, wave_down = call(
+            pack_waves_body,
+            [wave_shape, wave_shape],
+            (fwd_now, back_now),
+            [VM] * 2,
+            name="pack_waves",
+        )
+        part, wave_up, wave_down = lax.optimization_barrier((part, wave_up, wave_down))
     with jax.named_scope("squash"):
         parts = lax.all_to_all(part, "shot", 0, 0, tiled=True)
+        wave_low, wave_high = neighbours(wave_up, wave_down, "gy")
         squashed = call(
             squash_body,
             [shape(shots, rows, size_y, depth)],
@@ -514,8 +559,8 @@
                 squashed,
                 x_low,
                 x_high,
-                y_low,
-                y_high,
+                wave_low,
+                wave_high,
                 place,
                 wavelet,
                 receivers,
@@ -526,8 +571,8 @@
             name="step_1",
         )
     with jax.named_scope("halo_2"):
+        x_low_2, x_high_2 = neighbours(x_up, x_down, "gx")
         y_low_2, y_high_2 = neighbours(y_up, y_down, "gy")
-        x_low_2, x_high_2 = neighbours(x_up, x_down, "gx")
     with jax.named_scope("step_2"):
         fwd_2, back_2, sums, trace_2 = call(
             step_2,
@@ -567,7 +612,7 @@
     with jax.named_scope("gradient"):
         share = call(
             gradient_body,
-            [shape(blocks, 16, depth)],
+            [shape(blocks, 1, 2 * count + depth)],
             (update, squashed, features, x_low, x_high, y_low, y_high, trace_1, trace_2),
             [VM] * 9,
             scratch=[
@@ -579,12 +624,15 @@
             flops=54 * channels * size_x * size_y * depth,
             name="gradient",
         )
-        shares = lax.all_to_all(
-            share.reshape(blocks * 16, depth), ("gx", "gy"), 0, 0, tiled=True
-        )
-        total = jnp.sum(shares.reshape(blocks, 16, depth), axis=0)
-    traces = total[:8].reshape(-1)[: 2 * count].reshape(1, 2, count)
-    weight_grad = total[8, : 27 * channels].reshape(channels, 27)
+        shares = lax.all_to_all(share, ("gx", "gy"), 0, 0, tiled=True)
+        shares = shares.reshape(blocks, 1, 2 * count + depth)
+        traces, weight_grad = call(
+            total_body,
+            [shape(1, 2, count), shape(channels, 27)],
+            (shares,),
+            [VM],
+            name="total",
+        )
     return (fwd_2[None], back_2[None], traces, update, weight_grad)
 
 

time: 207 us -> 202 us (0.976)
  blocking collectives: 65.7 us -> 54.1 us
  waiting for transfers between devices: 63.2 us -> 68.2 us
  starting transfers between devices: 48.9 us -> 51.2 us
    ppermute x4 -> x5, waiting for transfers between devices: 35 us -> 50.5 us  [neighbours(): high = lax.ppermute(down, axis, [(i + 1, i) for i in range(count - 1)])]
    all_to_all x1, blocking collectives: 44 us -> 32.5 us  [per_device(): shares = lax.all_to_all(share, ('gx', 'gy'), 0, 0, tiled=True)]
    all_to_all x1, waiting for transfers between devices: 6.71 us -> 0.01 us  [per_device(): squashed = lax.all_to_all(squashed.reshape(grid), 'shot', 0, 0, tiled=True)]
    ppermute x4 -> x5, waiting for transfers between devices: 11.8 us -> 7.95 us  [neighbours(): low = lax.ppermute(up, axis, [(i, i + 1) for i in range(count - 1)])]
    ppermute x4 -> x5, starting transfers between devices: 11.4 us -> 15.1 us  [neighbours(): high = lax.ppermute(down, axis, [(i + 1, i) for i in range(count - 1)])]
    ppermute x4 -> x5, starting transfers between devices: 30.5 us -> 28.1 us  [neighbours(): low = lax.ppermute(up, axis, [(i, i + 1) for i in range(count - 1)])]
    pallas_call x9 -> x11, Pallas kernels: 20.2 us -> 21 us  [call(): pl.pallas_call(body, grid=grid, out_shape=outs[0] if single else tuple(ou...]
  transfers between devices with their start and end apart: 10 -> 12, of which waited for: 8 -> 8; matrix products, arithmetic and copies ran while one was open for 0% -> 0% of each run, Pallas kernels for 2% -> 2%
where the time goes in v2:
time: 202 us; the launch traced here: 201 us
  waiting for transfers between devices  68.2 us (34%)
  blocking collectives  54.1 us (27%)
  starting transfers between devices  51.2 us (25%)
  Pallas kernels  21 us (10%)
  local copies, waits for them, and re-layouts  4.3 us (2%)
  between operations  2.18 us (1%)
    ppermute x5, waiting for transfers between devices, neighbours(): high = lax.ppermute(down, axis, [(i + 1, i) for i in range(count - 1)])  50.5 us
    all_to_all x1, blocking collectives, per_device(): shares = lax.all_to_all(share, ('gx', 'gy'), 0, 0, tiled=True)  32.5 us
    ppermute x5, starting transfers between devices, neighbours(): low = lax.ppermute(up, axis, [(i, i + 1) for i in range(count - 1)])  28.1 us
    pallas_call x11, Pallas kernels, call(): pl.pallas_call(body, grid=grid, out_shape=outs[0] if single else tuple(ou...  21 us
    ppermute x5, starting transfers between devices, neighbours(): high = lax.ppermute(down, axis, [(i + 1, i) for i in range(count - 1)])  15.1 us
    all_to_all x1, blocking collectives, per_device(): parts = lax.all_to_all(part, 'shot', 0, 0, tiled=True)  11.6 us
    all_to_all x1, blocking collectives, per_device(): update = lax.all_to_all(update.reshape(grid), 'shot', 0, 0, tiled=True)  9.95 us
    all_to_all x1, waiting for transfers between devices, per_device(): lax.all_to_all(sums.reshape(shots * 2 * rows, size_y, depth), 'shot', 0,...  9.7 us
  transfers between devices with their start and end apart: 12, of which 8 were waited for; matrix products, arithmetic and copies ran while one was open for 0% of the time, Pallas kernels for 2%

profile of v2, /device:TPU:32, one launch (start us, length us, event | category | flops | bytes accessed | tf_op | source)
XLA Modules:
  0.0 201.1 jit_solution(7550977498907438701)
XLA Ops:
  0.6 0.0 copy-start
  0.6 1.0 copy-done
  1.7 0.0 copy-start.2
  1.7 0.9 copy-done.2
  2.6 0.0 copy-start.4
  2.6 0.9 copy-done.4
  3.6 3.8 %collective-permute-start = (f32[12,16,128]{2,1,0:T(8,128)S(1)}, f32[12,16,128]{2,1,0:T(8,128)S(1)}, u32[]{:S(2)}, u32[]{:S(2)}) collective-permute-start(f32[12,16,128]{2,1,0:T(8,128)S(1)} %get-tuple-element.28), channel_id=1, source_target_pairs={{0,8},{8,16},{16,24},{24,32},{32,40},{40,48},{48,56},{1,9},{9,17},... | collective-permute-start | bytes 294920 | tf_op jit(solution)/shard_map/halo_x/ppermute | solution.py:427
  7.4 0.0 copy-start.3
  7.4 0.0 copy-start.5
  7.5 0.0 copy-start.1
  7.5 5.0 %collective-permute-start.1 = (f32[12,16,128]{2,1,0:T(8,128)S(1)}, f32[12,16,128]{2,1,0:T(8,128)S(1)}, u32[]{:S(2)}, u32[]{:S(2)}) collective-permute-start(f32[12,16,128]{2,1,0:T(8,128)S(1)} %get-tuple-element.29), channel_id=1, source_target_pairs={{8,0},{16,8},{24,16},{32,24},{40,32},{48,40},{56,48},{9,1},{17,9},... | collective-permute-start | bytes 294920 | tf_op jit(solution)/shard_map/halo_x/ppermute | solution.py:428
  12.5 0.5 collective-permute-done.low_ref.refs_5_.x_low_ref
  12.9 1.7 collective-permute-done.1.high_ref.refs_6_.x_high_ref
  14.7 0.2 pack_y.1
  14.9 13.4 %collective-permute-start.2 = (bf16[144,128]{1,0:T(8,128)(2,1)S(1)}, bf16[144,128]{1,0:T(8,128)(2,1)S(1)}, u32[]{:S(2)}, u32[]{:S(2)}) collective-permute-start(bf16[144,128]{1,0:T(8,128)(2,1)S(1)} %get-tuple-element.30), channel_id=1, source_target_pairs={{0,1},{1,2},{2,3},{3,4},{4,5},{5,6},{6,7},{8,9},{9,10},{10,11},{11... | collective-permute-start | bytes 110600 | tf_op jit(solution)/shard_map/halo_y/ppermute | solution.py:427
  28.3 0.0 copy-start.9
  28.3 1.3 collective-permute-start.3
  29.6 0.0 copy-done.3
  29.6 0.0 copy-done.5
  29.6 0.0 copy-done.1
  29.7 0.0 copy-done.9
  29.7 4.6 %conv.1.main_ref = f32[32,16,128]{2,1,0:T(8,128)S(1)} custom-call(bf16[4,32,16,128]{3,2,1,0:T(8,128)(2,1)S(1)} %copy-done.1, f32[12,16,128]{2,1,0:T(8,128)S(1)} %collective-permute-done.low_ref.refs_5_.x_low_ref, f32[12,16,128]{2,1,0:T(8,128)S(1)} %collective-permute-done.1.high_ref.refs_6_.x_high_ref, f32[4,27]{1,0:T(4,128)S(1)} %copy-done.9), custom_call_target="tpu_custom_call" | custom-call | flops 14155776 | bytes 983472 | tf_op jit(solution)/shard_map/conv/conv/pallas_call | solution.py:25
  34.3 0.0 collective-permute-done.2.low_ref.y_low_ref
  34.3 8.5 %collective-permute-done.3.high_ref.y_high_ref = bf16[144,128]{1,0:T(8,128)(2,1)S(1)} collective-permute-done((bf16[144,128]{1,0:T(8,128)(2,1)S(1)}, bf16[144,128]{1,0:T(8,128)(2,1)S(1)}, u32[]{:S(2)}, u32[]{:S(2)}) %collective-permute-start.3) | collective-permute-done | bytes 36896 | tf_op jit(solution)/shard_map/halo_y/ppermute | solution.py:428
  42.8 0.7 conv_edge.1
  43.6 11.6 %all_to_all.25 = f32[32,16,128]{2,1,0:T(8,128)S(1)} all-to-all(f32[32,16,128]{2,1,0:T(8,128)S(1)} %conv_edge.1), channel_id=1, replica_groups=mesh['shot'=8,'gx'=8,'gy'=8] {'shot'}, dimensions={0} | all-to-all | bytes 524288 | tf_op jit(solution)/shard_map/squash/all_to_all | solution.py:521
  55.2 0.7 squash.1
  55.9 0.0 copy-start.6
  56.0 0.0 copy-start.7
  56.0 3.5 %all-to-all-start.1 = ((f32[32,16,128]{2,1,0:T(8,128)}), f32[32,16,128]{2,1,0:T(8,128)S(1)}, u32[]{:S(2)}, u32[]{:S(2)}) async-start(f32[32,16,128]{2,1,0:T(8,128)} %bitcast.5), calls=%async_computation.1 | async-start | bytes 524288 | tf_op jit(solution)/shard_map/squash/all_to_all | solution.py:530
  59.5 4.8 %collective-permute-start.4 = (f32[32,8,128]{2,1,0:T(8,128)S(1)}, f32[32,8,128]{2,1,0:T(8,128)S(1)}, u32[]{:S(2)}, u32[]{:S(2)}) collective-permute-start(f32[32,8,128]{2,1,0:T(8,128)S(1)} %get-tuple-element.35), channel_id=1, source_target_pairs={{0,1},{1,2},{2,3},{3,4},{4,5},{5,6},{6,7},{8,9},{9,10},{10,11},{11... | collective-permute-start | bytes 393224 | tf_op jit(solution)/shard_map/squash/ppermute | solution.py:427
  64.3 1.3 collective-permute-start.5
  66.2 0.0 copy-start.8
  66.3 0.1 pad_add_fusion.refs_9_
  66.3 0.0 copy-start.10
  66.3 1.2 collective-permute-done.4.refs_7_
  67.6 29.4 %collective-permute-done.5.refs_8_ = f32[32,8,128]{2,1,0:T(8,128)S(1)} collective-permute-done((f32[32,8,128]{2,1,0:T(8,128)S(1)}, f32[32,8,128]{2,1,0:T(8,128)S(1)}, u32[]{:S(2)}, u32[]{:S(2)}) %collective-permute-start.5) | collective-permute-done | bytes 131104 | tf_op jit(solution)/shard_map/squash/ppermute | solution.py:428
  96.9 0.0 all-to-all-done.1.refs_4_.squashed_ref
  97.0 0.0 copy-start.11
  97.0 0.0 copy-done.6
  97.0 0.0 copy-done.7
  97.0 0.0 copy-done.8
  97.0 0.0 copy-done.10
  97.0 0.6 copy-done.11
  97.6 3.6 %step_1.1 = (f32[32,16,128]{2,1,0:T(8,128)S(1)}, f32[32,16,128]{2,1,0:T(8,128)S(1)}, f32[32,16,128]{2,1,0:T(8,128)S(1)}, f32[1,512]{1,0:T(1,128)S(1)}, f32[8,16,...) custom-call(f32[32,16,128]{2,1,0:T(8,128)S(1)} %bitcast.16, ...), custom_call_target="tpu_custom_call" | custom-call | flops 1000000 | bytes 2957332 | tf_op jit(solution)/shard_map/step_1/step_1/pallas_call | solution.py:25
  101.3 4.2 %collective-permute-start.8 = (f32[32,8,128]{2,1,0:T(8,128)S(1)}, f32[32,8,128]{2,1,0:T(8,128)S(1)}, u32[]{:S(2)}, u32[]{:S(2)}) collective-permute-start(f32[32,8,128]{2,1,0:T(8,128)S(1)} %get-tuple-element.41), channel_id=1, source_target_pairs={{0,1},{1,2},{2,3},{3,4},{4,5},{5,6},{6,7},{8,9},{9,10},{10,11},{11... | collective-permute-start | bytes 393224 | tf_op jit(solution)/shard_map/halo_2/ppermute | solution.py:427
  105.4 1.3 collective-permute-start.9
  106.7 1.9 collective-permute-start.6
  108.7 6.3 %collective-permute-start.7 = (f32[8,16,128]{2,1,0:T(8,128)S(1)}, f32[8,16,128]{2,1,0:T(8,128)S(1)}, u32[]{:S(2)}, u32[]{:S(2)}) collective-permute-start(f32[8,16,128]{2,1,0:T(8,128)S(1)} %get-tuple-element.40), channel_id=1, source_target_pairs={{8,0},{16,8},{24,16},{32,24},{40,32},{48,40},{56,48},{9,1},{17,9},... | collective-permute-start | bytes 196616 | tf_op jit(solution)/shard_map/halo_2/ppermute | solution.py:428
  114.9 6.3 %collective-permute-done.6.refs_5_ = f32[8,16,128]{2,1,0:T(8,128)S(1)} collective-permute-done((f32[8,16,128]{2,1,0:T(8,128)S(1)}, f32[8,16,128]{2,1,0:T(8,128)S(1)}, u32[]{:S(2)}, u32[]{:S(2)}) %collective-permute-start.6) | collective-permute-done | bytes 65568 | tf_op jit(solution)/shard_map/halo_2/ppermute | solution.py:427
  121.2 0.0 collective-permute-done.7.refs_6_
  121.2 0.0 collective-permute-done.8.refs_7_
  121.2 10.9 %collective-permute-done.9.refs_8_ = f32[32,8,128]{2,1,0:T(8,128)S(1)} collective-permute-done((f32[32,8,128]{2,1,0:T(8,128)S(1)}, f32[32,8,128]{2,1,0:T(8,128)S(1)}, u32[]{:S(2)}, u32[]{:S(2)}) %collective-permute-start.9) | collective-permute-done | bytes 131104 | tf_op jit(solution)/shard_map/halo_2/ppermute | solution.py:428
  132.1 4.0 %step_2.1 = (f32[32,16,128]{2,1,0:T(8,128)}, f32[32,16,128]{2,1,0:T(8,128)}, f32[8,8,16,128]{3,2,1,0:T(8,128)}, f32[1,512]{1,0:T(1,128)S(1)}) custom-call(f32[32,16,128]{2,1,0:T(8,128)S(1)} %get-tuple-element.37.refs_0_, f32[32,16,128]{2,1,0:T(8,128)S(1)} %get-tuple-element.38.refs_1_, f32[32,16,128]{2,1,0:T(8,128)S(1)} %bitcast.17, ...), custom_call_target="tpu_custom_call" | custom-call | flops 1000000 | bytes 3022868 | tf_op jit(solution)/shard_map/step_2/step_2/pallas_call | solution.py:25
  136.1 4.4 %all-to-all-start.2 = ((f32[64,16,128]{2,1,0:T(8,128)}), f32[64,16,128]{2,1,0:T(8,128)S(1)}, u32[]{:S(2)}, u32[]{:S(2)}) async-start(f32[64,16,128]{2,1,0:T(8,128)} %bitcast.10), calls=%async_computation.2 | async-start | bytes 1048576 | tf_op jit(solution)/shard_map/update/all_to_all | solution.py:601
  141.2 9.7 %all-to-all-done.2 = f32[64,16,128]{2,1,0:T(8,128)S(1)} async-done(((f32[64,16,128]{2,1,0:T(8,128)}), f32[64,16,128]{2,1,0:T(8,128)S(1)}, u32[]{:S(2)}, u32[]{:S(2)}) %all-to-all-start.2) | async-done | bytes 524320 | tf_op jit(solution)/shard_map/update/all_to_all | solution.py:601
  150.9 9.9 %all_to_all.26.update_ref = f32[32,16,128]{2,1,0:T(8,128)S(1)} all-to-all(f32[32,16,128]{2,1,0:T(8,128)S(1)} %bitcast.25), channel_id=1, replica_groups=mesh['shot'=8,'gx'=8,'gy'=8] {'shot'}, dimensions={0} | all-to-all | bytes 524288 | tf_op jit(solution)/shard_map/update/all_to_all | solution.py:611
  160.9 6.3 %gradient.1 = f32[64,1,1152]{2,1,0:T(1,128)S(1)} custom-call(f32[32,16,128]{2,1,0:T(8,128)S(1)} %all_to_all.26.update_ref, f32[32,16,128]{2,1,0:T(8,128)S(1)} %all-to-all-done.1.refs_4_.squashed_ref, bf16[4,32,16,128]{3,2,1,0:T(8,128)(2,1)S(1)} %copy-done.1, f32[12,16,128]{2,1,0:T(8,128)S(1)} %collective-permute-done.low_ref.refs_5_.x_low_ref, ...), custom_call_target="tpu_custom_call" | custom-call | flops 14155776 | bytes 1617920 | tf_op jit(solution)/shard_map/gradient/gradient/pallas_call | solution.py:25
  167.1 32.5 %all_to_all.27.shares_ref = f32[64,1,1152]{2,1,0:T(1,128)S(1)} all-to-all(f32[64,1,1152]{2,1,0:T(1,128)S(1)} %gradient.1), channel_id=1, replica_groups=mesh['shot'=8,'gx'=8,'gy'=8] {'gx','gy'}, dimensions={0} | all-to-all | bytes 589824 | tf_op jit(solution)/shard_map/gradient/all_to_all | solution.py:627
  199.6 0.7 total.1
  200.4 0.7 copy.19
  (3 shorter events, 0.1 us)
Async XLA Ops:
  0.6 1.0 copy-start
  1.7 0.9 copy-start.2
  2.6 0.9 copy-start.4
  3.6 9.4 %collective-permute-start = (f32[12,16,128]{2,1,0:T(8,128)S(1)}, f32[12,16,128]{2,1,0:T(8,128)S(1)}, u32[]{:S(2)}, u32[]{:S(2)}) collective-permute-start(f32[12,16,128]{2,1,0:T(8,128)S(1)} %get-tuple-element.28), channel_id=1, source_target_pairs={{0,8},{8,16},{16,24},{24,32},{32,40},{40,48},{48,56},{1,9},{9,17},... | collective-permute-start | bytes 294920 | tf_op jit(solution)/shard_map/halo_x/ppermute | solution.py:427
  7.4 22.1 %copy-start.3 = (f32[1,32,16,128]{3,2,1,0:T(8,128)S(1)}, f32[1,32,16,128]{3,2,1,0:T(8,128)}, u32[]{:S(2)}) copy-start(f32[1,32,16,128]{3,2,1,0:T(8,128)} %param.14) | copy-start | bytes 786436
  7.4 22.1 %copy-start.5 = (f32[1,32,16,128]{3,2,1,0:T(8,128)S(1)}, f32[1,32,16,128]{3,2,1,0:T(8,128)}, u32[]{:S(2)}) copy-start(f32[1,32,16,128]{3,2,1,0:T(8,128)} %param.16) | copy-start | bytes 786436
  7.5 22.2 %copy-start.1 = (bf16[4,32,16,128]{3,2,1,0:T(8,128)(2,1)S(1)}, bf16[4,32,16,128]{3,2,1,0:T(8,128)(2,1)}, u32[]{:S(2)}) copy-start(bf16[4,32,16,128]{3,2,1,0:T(8,128)(2,1)} %feat_ref.5) | copy-start | bytes 1572868
  7.5 7.2 %collective-permute-start.1 = (f32[12,16,128]{2,1,0:T(8,128)S(1)}, f32[12,16,128]{2,1,0:T(8,128)S(1)}, u32[]{:S(2)}, u32[]{:S(2)}) collective-permute-start(f32[12,16,128]{2,1,0:T(8,128)S(1)} %get-tuple-element.29), channel_id=1, source_target_pairs={{8,0},{16,8},{24,16},{32,24},{40,32},{48,40},{56,48},{9,1},{17,9},... | collective-permute-start | bytes 294920 | tf_op jit(solution)/shard_map/halo_x/ppermute | solution.py:428
  14.9 19.4 %collective-permute-start.2 = (bf16[144,128]{1,0:T(8,128)(2,1)S(1)}, bf16[144,128]{1,0:T(8,128)(2,1)S(1)}, u32[]{:S(2)}, u32[]{:S(2)}) collective-permute-start(bf16[144,128]{1,0:T(8,128)(2,1)S(1)} %get-tuple-element.30), channel_id=1, source_target_pairs={{0,1},{1,2},{2,3},{3,4},{4,5},{5,6},{6,7},{8,9},{9,10},{10,11},{11... | collective-permute-start | bytes 110600 | tf_op jit(solution)/shard_map/halo_y/ppermute | solution.py:427
  28.3 1.4 copy-start.9
  28.3 14.6 %collective-permute-start.3 = (bf16[144,128]{1,0:T(8,128)(2,1)S(1)}, bf16[144,128]{1,0:T(8,128)(2,1)S(1)}, u32[]{:S(2)}, u32[]{:S(2)}) collective-permute-start(bf16[144,128]{1,0:T(8,128)(2,1)S(1)} %get-tuple-element.31), channel_id=1, source_target_pairs={{1,0},{2,1},{3,2},{4,3},{5,4},{6,5},{7,6},{9,8},{10,9},{11,10},{12... | collective-permute-start | bytes 110600 | tf_op jit(solution)/shard_map/halo_y/ppermute | solution.py:428
  55.9 41.0 %copy-start.6 = (f32[1,32,16,128]{3,2,1,0:T(8,128)S(1)}, f32[1,32,16,128]{3,2,1,0:T(8,128)}, u32[]{:S(2)}) copy-start(f32[1,32,16,128]{3,2,1,0:T(8,128)} %param.13) | copy-start | bytes 786436
  56.0 41.0 %copy-start.7 = (f32[1,32,16,128]{3,2,1,0:T(8,128)S(1)}, f32[1,32,16,128]{3,2,1,0:T(8,128)}, u32[]{:S(2)}) copy-start(f32[1,32,16,128]{3,2,1,0:T(8,128)} %param.15) | copy-start | bytes 786436
  56.0 41.0 %all-to-all-start.1 = ((f32[32,16,128]{2,1,0:T(8,128)}), f32[32,16,128]{2,1,0:T(8,128)S(1)}, u32[]{:S(2)}, u32[]{:S(2)}) async-start(f32[32,16,128]{2,1,0:T(8,128)} %bitcast.5), calls=%async_computation.1 | async-start | bytes 524288 | tf_op jit(solution)/shard_map/squash/all_to_all | solution.py:530
  59.5 8.0 %collective-permute-start.4 = (f32[32,8,128]{2,1,0:T(8,128)S(1)}, f32[32,8,128]{2,1,0:T(8,128)S(1)}, u32[]{:S(2)}, u32[]{:S(2)}) collective-permute-start(f32[32,8,128]{2,1,0:T(8,128)S(1)} %get-tuple-element.35), channel_id=1, source_target_pairs={{0,1},{1,2},{2,3},{3,4},{4,5},{5,6},{6,7},{8,9},{9,10},{10,11},{11... | collective-permute-start | bytes 393224 | tf_op jit(solution)/shard_map/squash/ppermute | solution.py:427
  64.3 32.7 %collective-permute-start.5 = (f32[32,8,128]{2,1,0:T(8,128)S(1)}, f32[32,8,128]{2,1,0:T(8,128)S(1)}, u32[]{:S(2)}, u32[]{:S(2)}) collective-permute-start(f32[32,8,128]{2,1,0:T(8,128)S(1)} %get-tuple-element.36), channel_id=1, source_target_pairs={{1,0},{2,1},{3,2},{4,3},{5,4},{6,5},{7,6},{9,8},{10,9},{11,10},{12... | collective-permute-start | bytes 393224 | tf_op jit(solution)/shard_map/squash/ppermute | solution.py:428
  66.2 30.7 %copy-start.8 = (f32[1,2,512]{2,1,0:T(2,128)S(1)}, f32[1,2,512]{2,1,0:T(2,128)}, u32[]{:S(2)}) copy-start(f32[1,2,512]{2,1,0:T(2,128)} %refs_12_.3) | copy-start | bytes 12292
  66.3 30.6 %copy-start.10 = (s32[1,512]{1,0:T(1,128)S(1)}, s32[1,512]{1,0:T(1,128)}, u32[]{:S(2)}) copy-start(s32[1,512]{1,0:T(1,128)} %refs_11_.3) | copy-start | bytes 6148
  97.0 0.7 copy-start.11
  101.3 19.9 %collective-permute-start.8 = (f32[32,8,128]{2,1,0:T(8,128)S(1)}, f32[32,8,128]{2,1,0:T(8,128)S(1)}, u32[]{:S(2)}, u32[]{:S(2)}) collective-permute-start(f32[32,8,128]{2,1,0:T(8,128)S(1)} %get-tuple-element.41), channel_id=1, source_target_pairs={{0,1},{1,2},{2,3},{3,4},{4,5},{5,6},{6,7},{8,9},{9,10},{10,11},{11... | collective-permute-start | bytes 393224 | tf_op jit(solution)/shard_map/halo_2/ppermute | solution.py:427
  105.4 26.6 %collective-permute-start.9 = (f32[32,8,128]{2,1,0:T(8,128)S(1)}, f32[32,8,128]{2,1,0:T(8,128)S(1)}, u32[]{:S(2)}, u32[]{:S(2)}) collective-permute-start(f32[32,8,128]{2,1,0:T(8,128)S(1)} %get-tuple-element.42), channel_id=1, source_target_pairs={{1,0},{2,1},{3,2},{4,3},{5,4},{6,5},{7,6},{9,8},{10,9},{11,10},{12... | collective-permute-start | bytes 393224 | tf_op jit(solution)/shard_map/halo_2/ppermute | solution.py:428
  106.7 14.4 %collective-permute-start.6 = (f32[8,16,128]{2,1,0:T(8,128)S(1)}, f32[8,16,128]{2,1,0:T(8,128)S(1)}, u32[]{:S(2)}, u32[]{:S(2)}) collective-permute-start(f32[8,16,128]{2,1,0:T(8,128)S(1)} %get-tuple-element.39), channel_id=1, source_target_pairs={{0,8},{8,16},{16,24},{24,32},{32,40},{40,48},{48,56},{1,9},{9,17},... | collective-permute-start | bytes 196616 | tf_op jit(solution)/shard_map/halo_2/ppermute | solution.py:427
  108.7 12.5 %collective-permute-start.7 = (f32[8,16,128]{2,1,0:T(8,128)S(1)}, f32[8,16,128]{2,1,0:T(8,128)S(1)}, u32[]{:S(2)}, u32[]{:S(2)}) collective-permute-start(f32[8,16,128]{2,1,0:T(8,128)S(1)} %get-tuple-element.40), channel_id=1, source_target_pairs={{8,0},{16,8},{24,16},{32,24},{40,32},{48,40},{56,48},{9,1},{17,9},... | collective-permute-start | bytes 196616 | tf_op jit(solution)/shard_map/halo_2/ppermute | solution.py:428
  136.1 14.8 %all-to-all-start.2 = ((f32[64,16,128]{2,1,0:T(8,128)}), f32[64,16,128]{2,1,0:T(8,128)S(1)}, u32[]{:S(2)}, u32[]{:S(2)}) async-start(f32[64,16,128]{2,1,0:T(8,128)} %bitcast.10), calls=%async_computation.2 | async-start | bytes 1048576 | tf_op jit(solution)/shard_map/update/all_to_all | solution.py:601

commit v3 on v2

--- a/solution.py
+++ b/solution.py
@@ -63,27 +63,75 @@
     return jnp.where(row >= -by, pltpu.roll(value, -by, 0), 0.0)
 
 
-def pack_x_body(
-    feat_first_ref,
-    feat_last_ref,
-    fwd_first_ref,
-    fwd_last_ref,
-    back_first_ref,
-    back_last_ref,
-    up_ref,
-    down_ref,
+def pack_x_body(feat_ref, fwd_ref, back_ref, up_ref, down_ref, edge_ref, sems):
+    channels, size_x = feat_ref.shape[:2]
+    copies = []
+    for n, (out_ref, start, row) in enumerate(
+        ((up_ref, size_x - 4, size_x - 1), (down_ref, 0, 0))
+    ):
+        pairs = [
+            (fwd_ref.at[pl.ds(start, 4)], out_ref.at[pl.ds(0, 4)]),
+            (back_ref.at[pl.ds(start, 4)], out_ref.at[pl.ds(4, 4)]),
+        ]
+        for c in range(channels):
+            pairs.append((feat_ref.at[c, row], edge_ref.at[n * channels + c]))
+        for m, (source, target) in enumerate(pairs):
+            copies.append(
+                pltpu.make_async_copy(source, target, sems.at[n * (2 + channels) + m])
+            )
+    for copy in copies:
+        copy.start()
+    for copy in copies:
+        copy.wait()
+    for c in range(channels):
+        up_ref[8 + c] = edge_ref[c].astype(F32)
+        down_ref[8 + c] = edge_ref[channels + c].astype(F32)
+
+
+def wave_rows(size_x):
+    return size_x * 12
+
+
+def pack_waves(fwd_ref, back_ref, upward, out_ref, first, edge_ref, low_ref):
+    size_x, size_y, depth = fwd_ref.shape
+    start, near = (size_y - 4, 2) if upward else (0, 0)
+    edge_ref[:, 0:4] = fwd_ref[:, start : start + 4]
+    edge_ref[:, 4:8] = back_ref[:, start : start + 4]
+    value = edge_ref[...].reshape(size_x * 8, depth)
+    high = value.astype(BF16)
+    out_ref[first : first + size_x * 8] = high
+    edge_ref[...] = (value - high.astype(F32)).reshape(size_x, 8, depth)
+    quarter = size_x // 4
+    for q in range(4):
+        part = slice(q * quarter, (q + 1) * quarter)
+        low_ref[:, 4 * q : 4 * q + 2] = edge_ref[part, near : near + 2]
+        low_ref[:, 4 * q + 2 : 4 * q + 4] = edge_ref[part, 4 + near : 6 + near]
+    out_ref[first + size_x * 8 : first + size_x * 12] = (
+        low_ref[...].reshape(size_x * 4, depth).astype(BF16)
+    )
+
+
+def unpack_waves(buffer_ref, upward, first, size_x, edge_ref, low_ref):
+    depth = buffer_ref.shape[1]
+    near = 2 if upward else 0
+    quarter = size_x // 4
+    edge_ref[...] = (
+        buffer_ref[first : first + size_x * 8].astype(F32).reshape(size_x, 8, depth)
+    )
+    low_ref[...] = (
+        buffer_ref[first + size_x * 8 : first + size_x * 12]
+        .astype(F32)
+        .reshape(quarter, 16, depth)
+    )
+    for q in range(4):
+        part = slice(q * quarter, (q + 1) * quarter)
+        edge_ref[part, near : near + 2] += low_ref[:, 4 * q : 4 * q + 2]
+        edge_ref[part, 4 + near : 6 + near] += low_ref[:, 4 * q + 2 : 4 * q + 4]
+
+
+def pack_y_body(
+    feat_ref, fwd_ref, back_ref, low_ref, high_ref, up_ref, down_ref, plane_ref, edge_ref, rest_ref
 ):
-    channels = feat_first_ref.shape[0]
-    up_ref[0:4] = fwd_last_ref[...]
-    up_ref[4:8] = back_last_ref[...]
-    down_ref[0:4] = fwd_first_ref[...]
-    down_ref[4:8] = back_first_ref[...]
-    for c in range(channels):
-        up_ref[8 + c] = feat_last_ref[c, 0].astype(F32)
-        down_ref[8 + c] = feat_first_ref[c, 0].astype(F32)
-
-
-def pack_y_body(feat_ref, low_ref, high_ref, up_ref, down_ref, plane_ref):
     channels, size_x, size_y, depth = feat_ref.shape
     row = lax.broadcasted_iota(jnp.int32, (16, depth), 0)
     tails = [jnp.zeros((16, depth), F32), jnp.zeros((16, depth), F32)]
@@ -93,16 +141,11 @@
             out_ref[c * size_x : (c + 1) * size_x] = plane_ref[:, y, :].astype(BF16)
             tails[n] = jnp.where(row == 2 * c, low_ref[8 + c, y : y + 1, :], tails[n])
             tails[n] = jnp.where(row == 2 * c + 1, high_ref[8 + c, y : y + 1, :], tails[n])
+    first = channels * size_x
     for tail, out_ref in zip(tails, (up_ref, down_ref)):
-        out_ref[channels * size_x : channels * size_x + 16] = tail.astype(BF16)
-
-
-def pack_waves_body(fwd_ref, back_ref, up_ref, down_ref):
-    size_y = fwd_ref.shape[1]
-    up_ref[:, 0:4] = fwd_ref[:, size_y - 4 : size_y]
-    up_ref[:, 4:8] = back_ref[:, size_y - 4 : size_y]
-    down_ref[:, 0:4] = fwd_ref[:, 0:4]
-    down_ref[:, 4:8] = back_ref[:, 0:4]
+        out_ref[first : first + 16] = tail.astype(BF16)
+    pack_waves(fwd_ref, back_ref, True, up_ref, first + 16, edge_ref, rest_ref)
+    pack_waves(fwd_ref, back_ref, False, down_ref, first + 16, edge_ref, rest_ref)
 
 
 def fill_features(ext_ref, feat_ref, low_ref, high_ref):
@@ -188,45 +231,124 @@
         out_ref[n] = update
 
 
-def step_body(moment, plane_y, rows, refs):
-    (
-        fwd_ref,
-        back_ref,
-        fwd_old_ref,
-        back_old_ref,
-        squashed_ref,
-        x_low_ref,
-        x_high_ref,
-        y_low_ref,
-        y_high_ref,
-        place_ref,
-        wavelet_ref,
-        receivers_ref,
-        residual_ref,
-        *rest,
-    ) = refs
+def receiver_hits(receivers_ref, place_ref, plane_y, size_x, size_y):
+    shift_y = plane_y.bit_length() - 1
+    receivers = receivers_ref[...]
+    place_x = lax.shift_right_logical(receivers, shift_y) - place_ref[0]
+    place_y = (receivers & (plane_y - 1)) - place_ref[1]
+    inside = (place_x >= 0) & (place_x < size_x) & (place_y >= 0) & (place_y < size_y)
+    cell = jnp.where(inside, place_x * size_y + place_y, -1)
+    cells = lax.broadcasted_iota(jnp.int32, (size_x * size_y, receivers.shape[1]), 0)
+    return (cells == cell).astype(F32).astype(BF16)
+
+
+def exact_product(parts, other, contract, parts_first):
+    total = None
+    for part in parts:
+        pair = (part, other) if parts_first else (other, part)
+        product = lax.dot_general(
+            *pair, (contract, ((), ())), preferred_element_type=F32
+        )
+        total = product if total is None else total + product
+    return total
+
+
+def sample(fwd_ref, hit, trace_ref):
+    size_x, size_y, depth = fwd_ref.shape
+    field = fwd_ref[...].reshape(size_x * size_y, depth)
+    total = exact_product(split3(field), hit, ((0,), (0,)), True)
+    trace_ref[...] = total[RDEPTH : RDEPTH + 1, :]
+
+
+def trace_body(plane_y, fwd_ref, place_ref, receivers_ref, trace_ref):
+    size_x, size_y, _ = fwd_ref.shape
+    sample(fwd_ref, receiver_hits(receivers_ref, place_ref, plane_y, size_x, size_y), trace_ref)
+
+
+def inner_body(moment, plane_y, *refs):
+    fwd_ref, back_ref, fwd_old_ref, back_old_ref = refs[:4]
+    place_ref, receivers_ref, residual_ref = refs[4:7]
+    refs = refs[7:]
     if moment == 0:
-        (fwd_new_ref, back_new_ref, lap_ref, trace_ref) = rest[:4]
-        (x_up_ref, x_down_ref, y_up_ref, y_down_ref) = rest[4:8]
-        scratch = rest[8:]
+        x_low_ref, x_high_ref = refs[:2]
+        refs = refs[2:]
+    fwd_ahead_ref, back_ahead_ref, lap_fwd_ref, lap_back_ref = refs[:4]
+    refs = refs[4:]
+    if moment == 1:
+        trace_ref = refs[0]
+        refs = refs[1:]
+    x_ref, y_ref, inject_ref = refs
+    size_x, size_y, depth = fwd_ref.shape
+    rows = 4
+    hit = receiver_hits(receivers_ref, place_ref, plane_y, size_x, size_y)
+    injected = jnp.where(
+        lax.broadcasted_iota(jnp.int32, (depth, hit.shape[1]), 0) == RDEPTH,
+        residual_ref[0, moment : moment + 1, :],
+        0.0,
+    )
+    inject_ref[...] = exact_product(split3(injected), hit, ((1,), (1,)), False).reshape(
+        size_x, size_y, depth
+    )
+    if moment == 1:
+        sample(fwd_ref, hit, trace_ref)
+    zero_x = jnp.zeros((4, size_y, depth), F32)
+    y_ref[:, 0:8] = jnp.zeros((size_x, 8, depth), F32)
+    y_ref[:, 8 + size_y : 16 + size_y] = jnp.zeros((size_x, 8, depth), F32)
+    for first, ref, old_ref, ahead_ref, lap_ref in (
+        (0, fwd_ref, fwd_old_ref, fwd_ahead_ref, lap_fwd_ref),
+        (4, back_ref, back_old_ref, back_ahead_ref, lap_back_ref),
+    ):
+        x_ref[0:4] = zero_x if moment else x_low_ref[first : first + 4]
+        x_ref[4 : 4 + size_x] = ref[...]
+        x_ref[4 + size_x : 8 + size_x] = zero_x if moment else x_high_ref[first : first + 4]
+        y_ref[:, 8 : 8 + size_y] = ref[...]
+
+        def one_block(i, carry):
+            start = i * rows
+            here = pl.ds(start, rows)
+            centre = ref[here]
+            flat = centre.reshape(rows * size_y, depth)
+            result = (3.0 * COEFFICIENTS[0]) * centre
+            for k in range(1, 5):
+                along_x = x_ref[pl.ds(start + 4 + k, rows)] + x_ref[pl.ds(start + 4 - k, rows)]
+                along_y = (
+                    y_ref[here, 8 + k : 8 + k + size_y, :] + y_ref[here, 8 - k : 8 - k + size_y, :]
+                )
+                along_z = shifted_lanes(flat, k) + shifted_lanes(flat, -k)
+                result = result + COEFFICIENTS[k] * (
+                    along_x + along_y + along_z.reshape(centre.shape)
+                )
+            if first:
+                result = result + inject_ref[here]
+            lap_ref[here] = result
+            ahead_ref[here] = 2.0 * centre - old_ref[here]
+            return carry
+
+        lax.fori_loop(0, size_x // rows, one_block, 0)
+
+
+def step_body(moment, plane_y, *refs):
+    fwd_ahead_ref, back_ahead_ref, lap_fwd_ref, lap_back_ref, squashed_ref = refs[:5]
+    y_low_ref, y_high_ref, place_ref, wavelet_ref = refs[5:9]
+    refs = refs[9:]
+    if moment == 0:
+        (fwd_new_ref, back_new_ref, lap_ref) = refs[:3]
+        (x_up_ref, x_down_ref, y_up_ref, y_down_ref) = refs[3:7]
+        refs = refs[7:]
     else:
-        lap_old_ref = rest[0]
-        (fwd_new_ref, back_new_ref, sums_ref, trace_ref) = rest[1:5]
-        scratch = rest[5:]
-    fwd_x_ref, back_x_ref, fwd_y_ref, back_y_ref, inject_ref = scratch
-    size_x, size_y, depth = fwd_ref.shape
-    cells = size_x * size_y
-    count = receivers_ref.shape[1]
-    for first, ref, x_ref, y_ref in (
-        (0, fwd_ref, fwd_x_ref, fwd_y_ref),
-        (4, back_ref, back_x_ref, back_y_ref),
-    ):
-        x_ref[0:4] = x_low_ref[first : first + 4]
-        x_ref[4 : 4 + size_x] = ref[...]
-        x_ref[4 + size_x : 8 + size_x] = x_high_ref[first : first + 4]
-        y_ref[:, 4:8] = y_low_ref[0:size_x, first : first + 4]
-        y_ref[:, 8 : 8 + size_y] = ref[...]
-        y_ref[:, 8 + size_y : 12 + size_y] = y_high_ref[0:size_x, first : first + 4]
+        x_low_ref, x_high_ref, lap_old_ref, back_ref = refs[:4]
+        (fwd_new_ref, back_new_ref, sums_ref) = refs[4:7]
+        refs = refs[7:]
+    edge_ref, rest_ref, *sides = refs
+    size_x, size_y, depth = fwd_ahead_ref.shape
+    start_row = y_low_ref.shape[0] - wave_rows(size_x)
+    for n, (buffer_ref, upward) in enumerate(((y_low_ref, True), (y_high_ref, False))):
+        unpack_waves(buffer_ref, upward, start_row, size_x, edge_ref, rest_ref)
+        for m in range(2):
+            side_ref = sides[2 * m + n]
+            at, empty = (4, 8) if upward else (8, 0)
+            side_ref[:, empty : empty + 8] = jnp.zeros((size_x, 8, depth), F32)
+            side_ref[:, at : at + 4] = edge_ref[:, 4 * m : 4 * m + 4]
 
     anchor_x, anchor_y, source = place_ref[0], place_ref[1], place_ref[2]
     shift_y = plane_y.bit_length() - 1
@@ -239,86 +361,63 @@
     spot = jnp.where(here, (source_x * size_y + source_y) * depth + source_z, -1)
     amplitude = wavelet_ref[0, moment]
 
-    receivers = receivers_ref[...]
-    place_x = lax.shift_right_logical(receivers, shift_y) - anchor_x
-    place_y = (receivers & (plane_y - 1)) - anchor_y
-    inside = (place_x >= 0) & (place_x < size_x) & (place_y >= 0) & (place_y < size_y)
-    cell = jnp.where(inside, place_x * size_y + place_y, -1)
-    hit = (
-        (lax.broadcasted_iota(jnp.int32, (cells, count), 0) == cell).astype(F32).astype(BF16)
-    )
-    injected = jnp.where(
-        lax.broadcasted_iota(jnp.int32, (depth, count), 0) == RDEPTH,
-        residual_ref[0, moment : moment + 1, :],
-        0.0,
-    )
-    total = None
-    for part in split3(injected):
-        product = lax.dot_general(
-            hit, part, (((1,), (1,)), ((), ())), preferred_element_type=F32
-        )
-        total = product if total is None else total + product
-    inject_ref[...] = total.reshape(size_x, size_y, depth)
-
-    def laplacian(x_ref, y_ref, start):
-        centre = x_ref[pl.ds(start + 4, rows)]
-        flat = centre.reshape(rows * size_y, depth)
-        result = (3.0 * COEFFICIENTS[0]) * centre
+    def edges(lap, m, start):
+        block = slice(start, start + 4)
+        low = high = None
         for k in range(1, 5):
-            along_x = x_ref[pl.ds(start + 4 + k, rows)] + x_ref[pl.ds(start + 4 - k, rows)]
-            along_y = (
-                y_ref[pl.ds(start, rows), 8 + k : 8 + k + size_y, :]
-                + y_ref[pl.ds(start, rows), 8 - k : 8 - k + size_y, :]
-            )
-            along_z = (shifted_lanes(flat, k) + shifted_lanes(flat, -k)).reshape(centre.shape)
-            result = result + COEFFICIENTS[k] * (along_x + along_y + along_z)
-        return centre, result
-
-    def one_block(i, carry):
-        start = i * rows
-        here = pl.ds(start, rows)
+            a = COEFFICIENTS[k] * sides[2 * m][block, 8 - k : 16 - k, :]
+            b = COEFFICIENTS[k] * sides[2 * m + 1][block, k : 8 + k, :]
+            low, high = (a, b) if low is None else (low + a, high + b)
+        parts = [low, high]
+        if size_y > 16:
+            parts.insert(1, jnp.zeros((4, size_y - 16, depth), F32))
+        lap = lap + jnp.concatenate(parts, axis=1)
+        if moment == 0 or start not in (0, size_x - 4):
+            return lap
+        parts = []
+        for j in range(4):
+            total = None
+            if start == 0:
+                picks = [(k, x_low_ref, 4 * m + 4 + j - k) for k in range(j + 1, 5)]
+            else:
+                picks = [(k, x_high_ref, 4 * m + j + k - 4) for k in range(4 - j, 5)]
+            for k, ref, row in picks:
+                part = COEFFICIENTS[k] * ref[row]
+                total = part if total is None else total + part
+            parts.append(total)
+        return lap + jnp.stack(parts)
+
+    for start in range(0, size_x, 4):
+        here = slice(start, start + 4)
         courant = 0.02 + 0.16 * squashed_ref[here]
-        fwd, lap_fwd = laplacian(fwd_x_ref, fwd_y_ref, start)
-        back, lap_back = laplacian(back_x_ref, back_y_ref, start)
+        lap_fwd = edges(lap_fwd_ref[here], 0, start)
+        lap_back = edges(lap_back_ref[here], 1, start)
+        dims = lap_fwd.shape
         index = (
-            lax.broadcasted_iota(jnp.int32, fwd.shape, 0) * (size_y * depth)
-            + lax.broadcasted_iota(jnp.int32, fwd.shape, 1) * depth
-            + lax.broadcasted_iota(jnp.int32, fwd.shape, 2)
+            lax.broadcasted_iota(jnp.int32, dims, 0) * (size_y * depth)
+            + lax.broadcasted_iota(jnp.int32, dims, 1) * depth
+            + lax.broadcasted_iota(jnp.int32, dims, 2)
         )
         added = jnp.where(index == spot - start * (size_y * depth), amplitude, 0.0)
-        fwd_new = 2.0 * fwd - fwd_old_ref[here] + courant * lap_fwd + courant * added
-        back_new = (
-            2.0 * back - back_old_ref[here] + courant * lap_back + courant * inject_ref[here]
-        )
-        fwd_new_ref[here] = fwd_new
+        fwd_new_ref[here] = fwd_ahead_ref[here] + courant * (lap_fwd + added)
+        back_new = back_ahead_ref[here] + courant * lap_back
         back_new_ref[here] = back_new
         if moment == 0:
             lap_ref[here] = lap_fwd
         else:
+            rows = sums_ref.shape[1] // 2
+            n, at = start // rows, start % rows
             lap_old = lap_old_ref[here]
-            sums_ref[i, 0:rows] = lap_old * back + lap_fwd * back_new
-            sums_ref[i, rows : 2 * rows] = lap_old * lap_old + lap_fwd * lap_fwd
-        return carry
-
-    lax.fori_loop(0, size_x // rows, one_block, 0)
-
-    total = None
-    for part in split3(fwd_new_ref[...].reshape(cells, depth)):
-        product = lax.dot_general(
-            part, hit, (((0,), (0,)), ((), ())), preferred_element_type=F32
-        )
-        total = product if total is None else total + product
-    trace_ref[...] = total[RDEPTH : RDEPTH + 1, :]
+            sums_ref[n, at : at + 4] = lap_old * back_ref[here] + lap_fwd * back_new
+            sums_ref[n, rows + at : rows + at + 4] = lap_old * lap_old + lap_fwd * lap_fwd
 
     if moment == 0:
         x_up_ref[0:4] = fwd_new_ref[size_x - 4 : size_x]
         x_up_ref[4:8] = back_new_ref[size_x - 4 : size_x]
         x_down_ref[0:4] = fwd_new_ref[0:4]
         x_down_ref[4:8] = back_new_ref[0:4]
-        y_up_ref[:, 0:4] = fwd_new_ref[:, size_y - 4 : size_y]
-        y_up_ref[:, 4:8] = back_new_ref[:, size_y - 4 : size_y]
-        y_down_ref[:, 0:4] = fwd_new_ref[:, 0:4]
-        y_down_ref[:, 4:8] = back_new_ref[:, 0:4]
+        pack_waves(fwd_new_ref, back_new_ref, True, y_up_ref, 0, edge_ref, rest_ref)
+        pack_waves(fwd_new_ref, back_new_ref, False, y_down_ref, 0, edge_ref, rest_ref)
 
 
 def gradient_body(
@@ -456,34 +555,33 @@
         [lax.axis_index("gx") * size_x, lax.axis_index("gy") * size_y, sources[0]]
     ).astype(jnp.int32)
 
-    def edge(last):
-        return pl.BlockSpec((4, size_y, depth), lambda i: ((size_x // 4 - 1) * last, 0, 0))
-
-    def feature_edge(last):
-        return pl.BlockSpec(
-            (channels, 1, size_y, depth), lambda i: (0, (size_x - 1) * last, 0, 0)
-        )
-
     x_shape = shape(8 + channels, size_y, depth)
     with jax.named_scope("pack_x"):
         x_up, x_down = call(
             pack_x_body,
             [x_shape, x_shape],
-            (features, features, fwd_now, fwd_now, back_now, back_now),
-            [feature_edge(0), feature_edge(1), edge(0), edge(1), edge(0), edge(1)],
+            (features, fwd_now, back_now),
+            [pl.BlockSpec(memory_space=pltpu.HBM)] * 3,
+            scratch=[
+                pltpu.VMEM((2 * channels, size_y, depth), BF16),
+                pltpu.SemaphoreType.DMA((2 * (2 + channels),)),
+            ],
             name="pack_x",
-            grid=(1,),
         )
     with jax.named_scope("halo_x"):
         x_low, x_high = neighbours(x_up, x_down, "gx")
-    y_shape = shape(channels * size_x + 16, depth, dtype=BF16)
+    packing = [
+        pltpu.VMEM((size_x, 8, depth), F32),
+        pltpu.VMEM((size_x // 4, 16, depth), F32),
+    ]
+    y_shape = shape(channels * size_x + 16 + wave_rows(size_x), depth, dtype=BF16)
     with jax.named_scope("pack_y"):
         y_up, y_down = call(
             pack_y_body,
             [y_shape, y_shape],
-            (features, x_low, x_high),
-            [VM] * 3,
-            scratch=[pltpu.VMEM(grid, F32)],
+            (features, fwd_now, back_now, x_low, x_high),
+            [VM] * 5,
+            scratch=[pltpu.VMEM(grid, F32)] + packing,
             name="pack_y",
         )
     with jax.named_scope("halo_y"):
@@ -507,19 +605,8 @@
             scratch=[pltpu.VMEM((size_x + 16, depth), F32)],
             name="conv_edge",
         )
-    wave_shape = shape(size_x, 8, depth)
-    with jax.named_scope("pack_waves"):
-        wave_up, wave_down = call(
-            pack_waves_body,
-            [wave_shape, wave_shape],
-            (fwd_now, back_now),
-            [VM] * 2,
-            name="pack_waves",
-        )
-        part, wave_up, wave_down = lax.optimization_barrier((part, wave_up, wave_down))
     with jax.named_scope("squash"):
         parts = lax.all_to_all(part, "shot", 0, 0, tiled=True)
-        wave_low, wave_high = neighbours(wave_up, wave_down, "gy")
         squashed = call(
             squash_body,
             [shape(shots, rows, size_y, depth)],
@@ -529,73 +616,88 @@
         )
         squashed = lax.all_to_all(squashed.reshape(grid), "shot", 0, 0, tiled=True)
 
-    scratch = [
+    full = shape(*grid)
+    inner_scratch = [
         pltpu.VMEM((size_x + 8, size_y, depth), F32),
-        pltpu.VMEM((size_x + 8, size_y, depth), F32),
-        pltpu.VMEM((size_x, size_y + 16, depth), F32),
         pltpu.VMEM((size_x, size_y + 16, depth), F32),
         pltpu.VMEM(grid, F32),
     ]
-    full = shape(*grid)
-    specs = [VM] * 9 + [SM, SM, VM, VM]
-
-    def step_1(*refs):
-        step_body(0, plane_y, rows, refs)
-
-    def step_2(*refs):
-        step_body(1, plane_y, rows, refs)
-
+    step_scratch = packing + [pltpu.VMEM((size_x, 16, depth), F32)] * 4
+    work = 60 * size_x * size_y * depth
+    with jax.named_scope("inner_1"):
+        fwd_ahead, back_ahead, lap_fwd, lap_back = call(
+            functools.partial(inner_body, 0, plane_y),
+            [full] * 4,
+            (fwd_now, back_now, fwd_prev, back_prev, place, receivers, residual, x_low, x_high),
+            [VM] * 4 + [SM] + [VM] * 4,
+            scratch=inner_scratch,
+            flops=work,
+            name="inner_1",
+        )
     with jax.named_scope("step_1"):
-        fwd_1, back_1, lap_1, trace_1, x_up, x_down, y_up, y_down = call(
-            step_1,
-            [full, full, full, shape(1, count)]
+        fwd_1, back_1, lap_1, x_up, x_down, y_up, y_down = call(
+            functools.partial(step_body, 0, plane_y),
+            [full] * 3
             + [shape(8, size_y, depth)] * 2
-            + [shape(size_x, 8, depth)] * 2,
+            + [shape(wave_rows(size_x), depth, dtype=BF16)] * 2,
             (
-                fwd_now,
-                back_now,
-                fwd_prev,
-                back_prev,
+                fwd_ahead,
+                back_ahead,
+                lap_fwd,
+                lap_back,
                 squashed,
-                x_low,
-                x_high,
-                wave_low,
-                wave_high,
+                y_low,
+                y_high,
                 place,
                 wavelet,
-                receivers,
-                residual,
             ),
-            specs,
-            scratch=scratch,
+            [VM] * 7 + [SM] * 2,
+            scratch=step_scratch,
             name="step_1",
         )
     with jax.named_scope("halo_2"):
         x_low_2, x_high_2 = neighbours(x_up, x_down, "gx")
         y_low_2, y_high_2 = neighbours(y_up, y_down, "gy")
+    with jax.named_scope("inner_2"):
+        fwd_ahead, back_ahead, lap_fwd, lap_back, trace_1 = call(
+            functools.partial(inner_body, 1, plane_y),
+            [full] * 4 + [shape(1, count)],
+            (fwd_1, back_1, fwd_now, back_now, place, receivers, residual),
+            [VM] * 4 + [SM] + [VM] * 2,
+            scratch=inner_scratch,
+            flops=work,
+            name="inner_2",
+        )
     with jax.named_scope("step_2"):
-        fwd_2, back_2, sums, trace_2 = call(
-            step_2,
-            [full, full, shape(shots, 2 * rows, size_y, depth), shape(1, count)],
+        fwd_2, back_2, sums = call(
+            functools.partial(step_body, 1, plane_y),
+            [full, full, shape(shots, 2 * rows, size_y, depth)],
             (
-                fwd_1,
-                back_1,
-                fwd_now,
-                back_now,
+                fwd_ahead,
+                back_ahead,
+                lap_fwd,
+                lap_back,
                 squashed,
-                x_low_2,
-                x_high_2,
                 y_low_2,
                 y_high_2,
                 place,
                 wavelet,
-                receivers,
-                residual,
+                x_low_2,
+                x_high_2,
                 lap_1,
+                back_1,
             ),
-            specs + [VM],
-            scratch=scratch,
+            [VM] * 7 + [SM] * 2 + [VM] * 4,
+            scratch=step_scratch,
             name="step_2",
+        )
+    with jax.named_scope("traces"):
+        trace_2 = call(
+            functools.partial(trace_body, plane_y),
+            [shape(1, count)],
+            (fwd_2, place, receivers),
+            [VM, SM, VM],
+            name="trace_2",
         )
     with jax.named_scope("update"):
         sums = lax.all_to_all(

time: 202 us -> 177 us (0.88)
  waiting for transfers between devices: 68.2 us -> 47.1 us
  blocking collectives: 54.1 us -> 45.1 us
  Pallas kernels: 21 us -> 25.5 us
    ppermute x5 -> x4, waiting for transfers between devices: 50.5 us -> 23.1 us  [neighbours(): high = lax.ppermute(down, axis, [(i + 1, i) for i in range(count - 1)])]
    all_to_all x1 -> x0, blocking collectives: 9.95 us -> none  [per_device(): update = lax.all_to_all(update.reshape(grid), 'shot', 0, 0, tiled=True)]
    all_to_all x0 -> x1, waiting for transfers between devices: none -> 6.47 us  [per_device(): update = lax.all_to_all(update.reshape(grid), 'shot', 0, 0, tiled=True)]
    pallas_call x11 -> x13, Pallas kernels: 21 us -> 25.5 us  [call(): pl.pallas_call(body, grid=grid, out_shape=outs[0] if single else tuple(ou...]
    ppermute x5 -> x4, starting transfers between devices: 15.1 us -> 11.4 us  [neighbours(): high = lax.ppermute(down, axis, [(i + 1, i) for i in range(count - 1)])]
    all_to_all x0 -> x1, starting transfers between devices: none -> 3.54 us  [per_device(): update = lax.all_to_all(update.reshape(grid), 'shot', 0, 0, tiled=True)]
    all_to_all x1, waiting for transfers between devices: 0.01 us -> 2.63 us  [per_device(): squashed = lax.all_to_all(squashed.reshape(grid), 'shot', 0, 0, tiled=True)]
    ppermute x5 -> x4, waiting for transfers between devices: 7.95 us -> 5.35 us  [neighbours(): low = lax.ppermute(up, axis, [(i, i + 1) for i in range(count - 1)])]
  transfers between devices with their start and end apart: 12 -> 11, of which waited for: 8 -> 8; matrix products, arithmetic and copies ran while one was open for 0% -> 0% of each run, Pallas kernels for 2% -> 7%
where the time goes in v3:
time: 177 us; the launch traced here: 176 us
  starting transfers between devices  51.3 us (29%)
  waiting for transfers between devices  47.1 us (27%)
  blocking collectives  45.1 us (25%)
  Pallas kernels  25.5 us (14%)
  local copies, waits for them, and re-layouts  4.98 us (3%)
  between operations  2.17 us (1%)
    all_to_all x1, blocking collectives, per_device(): shares = lax.all_to_all(share, ('gx', 'gy'), 0, 0, tiled=True)  33.5 us
    ppermute x4, starting transfers between devices, neighbours(): low = lax.ppermute(up, axis, [(i, i + 1) for i in range(count - 1)])  29.3 us
    pallas_call x13, Pallas kernels, call(): pl.pallas_call(body, grid=grid, out_shape=outs[0] if single else tuple(ou...  25.5 us
    ppermute x4, waiting for transfers between devices, neighbours(): high = lax.ppermute(down, axis, [(i + 1, i) for i in range(count - 1)])  23.1 us
    all_to_all x1, blocking collectives, per_device(): parts = lax.all_to_all(part, 'shot', 0, 0, tiled=True)  11.6 us
    ppermute x4, starting transfers between devices, neighbours(): high = lax.ppermute(down, axis, [(i + 1, i) for i in range(count - 1)])  11.4 us
    all_to_all x1, waiting for transfers between devices, per_device(): lax.all_to_all(sums.reshape(shots * 2 * rows, size_y, depth), 'shot', 0,...  9.62 us
    all_to_all x1, waiting for transfers between devices, per_device(): update = lax.all_to_all(update.reshape(grid), 'shot', 0, 0, tiled=True)  6.47 us
  transfers between devices with their start and end apart: 11, of which 8 were waited for; matrix products, arithmetic and copies ran while one was open for 0% of the time, Pallas kernels for 7%

profile of v3, /device:TPU:32, one launch (start us, length us, event | category | flops | bytes accessed | tf_op | source)
XLA Modules:
  0.0 176.3 jit_solution(6805363033508121470)
XLA Ops:
  0.6 0.0 copy-start
  0.6 1.0 copy-done
  1.7 0.0 copy-start.2
  1.7 0.9 copy-done.2
  2.6 0.0 copy-start.4
  2.6 0.9 copy-done.4
  3.6 0.3 pack_x.1
  3.9 3.8 %collective-permute-start = (f32[12,16,128]{2,1,0:T(8,128)S(1)}, f32[12,16,128]{2,1,0:T(8,128)S(1)}, u32[]{:S(2)}, u32[]{:S(2)}) collective-permute-start(f32[12,16,128]{2,1,0:T(8,128)S(1)} %get-tuple-element.30), channel_id=1, source_target_pairs={{0,8},{8,16},{16,24},{24,32},{32,40},{40,48},{48,56},{1,9},{9,17},... | collective-permute-start | bytes 294920 | tf_op jit(solution)/shard_map/halo_x/ppermute | solution.py:526
  7.7 4.9 %collective-permute-start.1 = (f32[12,16,128]{2,1,0:T(8,128)S(1)}, f32[12,16,128]{2,1,0:T(8,128)S(1)}, u32[]{:S(2)}, u32[]{:S(2)}) collective-permute-start(f32[12,16,128]{2,1,0:T(8,128)S(1)} %get-tuple-element.31), channel_id=1, source_target_pairs={{8,0},{16,8},{24,16},{32,24},{40,32},{48,40},{56,48},{9,1},{17,9},... | collective-permute-start | bytes 294920 | tf_op jit(solution)/shard_map/halo_x/ppermute | solution.py:527
  12.6 0.7 collective-permute-done.refs_7_.low_ref.x_low_ref
  13.2 1.5 collective-permute-done.1.refs_8_.high_ref.x_high_ref
  14.8 0.3 pack_y.1
  15.1 0.0 copy-start.11
  15.1 13.4 %collective-permute-start.2 = (bf16[528,128]{1,0:T(8,128)(2,1)S(1)}, bf16[528,128]{1,0:T(8,128)(2,1)S(1)}, u32[]{:S(2)}, u32[]{:S(2)}) collective-permute-start(bf16[528,128]{1,0:T(8,128)(2,1)S(1)} %get-tuple-element.36), channel_id=1, source_target_pairs={{0,1},{1,2},{2,3},{3,4},{4,5},{5,6},{6,7},{8,9},{9,10},{10,11},{11... | collective-permute-start | bytes 405512 | tf_op jit(solution)/shard_map/halo_y/ppermute | solution.py:526
  28.5 1.3 collective-permute-start.3
  29.8 0.0 copy-done.11
  29.8 4.6 %conv.1.main_ref = f32[32,16,128]{2,1,0:T(8,128)S(1)} custom-call(bf16[4,32,16,128]{3,2,1,0:T(8,128)(2,1)S(1)} %copy-done, f32[12,16,128]{2,1,0:T(8,128)S(1)} %collective-permute-done.refs_7_.low_ref.x_low_ref, f32[12,16,128]{2,1,0:T(8,128)S(1)} %collective-permute-done.1.refs_8_.high_ref.x_high_ref, f32[4,27]{1,0:T(4,128)S(1)} %copy-done.11), custom_call_target="tpu_custom_call" | custom-call | flops 14155776 | bytes 983472 | tf_op jit(solution)/shard_map/conv/conv/pallas_call | solution.py:25
  34.5 4.7 %collective-permute-done.2.low_ref.refs_5_.y_low_ref = bf16[528,128]{1,0:T(8,128)(2,1)S(1)} collective-permute-done((bf16[528,128]{1,0:T(8,128)(2,1)S(1)}, bf16[528,128]{1,0:T(8,128)(2,1)S(1)}, u32[]{:S(2)}, u32[]{:S(2)}) %collective-permute-start.2) | collective-permute-done | bytes 135200 | tf_op jit(solution)/shard_map/halo_y/ppermute | solution.py:526
  39.2 15.1 %collective-permute-done.3.high_ref.refs_6_.y_high_ref = bf16[528,128]{1,0:T(8,128)(2,1)S(1)} collective-permute-done((bf16[528,128]{1,0:T(8,128)(2,1)S(1)}, bf16[528,128]{1,0:T(8,128)(2,1)S(1)}, u32[]{:S(2)}, u32[]{:S(2)}) %collective-permute-start.3) | collective-permute-done | bytes 135200 | tf_op jit(solution)/shard_map/halo_y/ppermute | solution.py:527
  54.3 0.7 conv_edge.1
  55.0 11.6 %all_to_all.25 = f32[32,16,128]{2,1,0:T(8,128)S(1)} all-to-all(f32[32,16,128]{2,1,0:T(8,128)S(1)} %conv_edge.1), channel_id=1, replica_groups=mesh['shot'=8,'gx'=8,'gy'=8] {'shot'}, dimensions={0} | all-to-all | bytes 524288 | tf_op jit(solution)/shard_map/squash/all_to_all | solution.py:609
  66.7 0.0 copy-start.7
  66.7 0.0 copy-start.8
  66.7 0.7 squash.1
  67.4 0.0 copy-start.3
  67.4 3.5 %all-to-all-start.1 = ((f32[32,16,128]{2,1,0:T(8,128)}), f32[32,16,128]{2,1,0:T(8,128)S(1)}, u32[]{:S(2)}, u32[]{:S(2)}) async-start(f32[32,16,128]{2,1,0:T(8,128)} %bitcast.7), calls=%async_computation.1 | async-start | bytes 524288 | tf_op jit(solution)/shard_map/squash/all_to_all | solution.py:617
  71.6 0.0 copy-start.10
  71.6 0.1 pad_add_fusion.refs_4_.refs_7_.place_ref
  71.7 0.0 copy-start.9
  71.7 0.0 copy-done.7
  71.7 0.0 copy-done.8
  71.7 0.0 copy-done.3
  71.7 0.0 copy-done.5
  71.7 0.6 copy-done.10
  72.3 0.1 copy-done.9
  72.4 3.4 %inner_1.1 = (f32[32,16,128]{2,1,0:T(8,128)S(1)}, f32[32,16,128]{2,1,0:T(8,128)S(1)}, f32[32,16,128]{2,1,0:T(8,128)S(1)}, f32[32,16,128]{2,1,0:T(8,128)S(1)}) custom-call(f32[32,16,128]{2,1,0:T(8,128)S(1)} %bitcast.15, f32[32,16,128]{2,1,0:T(8,128)S(1)} %bitcast.19, f32[32,16,128]{2,1,0:T(8,128)S(1)} %bitcast.24, f32[32,16,128]{2,1,0:T(8,128)S(1)} %bitcast.25, ...), custom_call_target="tpu_custom_call" | custom-call | flops 3932160 | bytes 2299916 | tf_op jit(solution)/shard_map/inner_1/inner_1/pallas_call | solution.py:25
  75.8 2.6 %all-to-all-done.1.refs_4_.squashed_ref = f32[32,16,128]{2,1,0:T(8,128)S(1)} async-done(((f32[32,16,128]{2,1,0:T(8,128)}), f32[32,16,128]{2,1,0:T(8,128)S(1)}, u32[]{:S(2)}, u32[]{:S(2)}) %all-to-all-start.1) | async-done | bytes 262176 | tf_op jit(solution)/shard_map/squash/all_to_all | solution.py:617
  78.4 0.0 copy-start.12
  78.4 0.7 copy-done.12
  79.1 1.1 step_1.1
  80.2 10.2 %collective-permute-start.4 = (bf16[384,128]{1,0:T(8,128)(2,1)S(1)}, bf16[384,128]{1,0:T(8,128)(2,1)S(1)}, u32[]{:S(2)}, u32[]{:S(2)}) collective-permute-start(bf16[384,128]{1,0:T(8,128)(2,1)S(1)} %get-tuple-element.44), channel_id=1, source_target_pairs={{0,1},{1,2},{2,3},{3,4},{4,5},{5,6},{6,7},{8,9},{9,10},{10,11},{11... | collective-permute-start | bytes 294920 | tf_op jit(solution)/shard_map/halo_2/ppermute | solution.py:526
  90.4 1.3 collective-permute-start.5
  91.7 1.9 %collective-permute-start.6 = (f32[8,16,128]{2,1,0:T(8,128)S(1)}, f32[8,16,128]{2,1,0:T(8,128)S(1)}, u32[]{:S(2)}, u32[]{:S(2)}) collective-permute-start(f32[8,16,128]{2,1,0:T(8,128)S(1)} %get-tuple-element.46), channel_id=1, source_target_pairs={{0,8},{8,16},{16,24},{24,32},{32,40},{40,48},{48,56},{1,9},{9,17},... | collective-permute-start | bytes 196616 | tf_op jit(solution)/shard_map/halo_2/ppermute | solution.py:526
  93.6 3.9 %collective-permute-start.7 = (f32[8,16,128]{2,1,0:T(8,128)S(1)}, f32[8,16,128]{2,1,0:T(8,128)S(1)}, u32[]{:S(2)}, u32[]{:S(2)}) collective-permute-start(f32[8,16,128]{2,1,0:T(8,128)S(1)} %get-tuple-element.47), channel_id=1, source_target_pairs={{8,0},{16,8},{24,16},{32,24},{40,32},{48,40},{56,48},{9,1},{17,9},... | collective-permute-start | bytes 196616 | tf_op jit(solution)/shard_map/halo_2/ppermute | solution.py:527
  97.6 3.6 %inner_2.1 = (f32[32,16,128]{2,1,0:T(8,128)S(1)}, f32[32,16,128]{2,1,0:T(8,128)S(1)}, f32[32,16,128]{2,1,0:T(8,128)S(1)}, f32[32,16,128]{2,1,0:T(8,128)S(1)}, f32[1,512]{1,0:T(1,128)S(1)}) custom-call(f32[32,16,128]{2,1,0:T(8,128)S(1)} %get-tuple-element.38.refs_0_, f32[32,16,128]{2,1,0:T(8,128)S(1)} %get-tuple-element.39.refs_1_.refs_12_, ...), custom_call_target="tpu_custom_call" | custom-call | flops 3932160 | bytes 2105356 | tf_op jit(solution)/shard_map/inner_2/inner_2/pallas_call | solution.py:25
  101.2 0.0 collective-permute-done.6.refs_9_
  101.2 0.0 collective-permute-done.7.refs_10_
  101.2 0.0 collective-permute-done.4.refs_5_
  101.2 6.4 %collective-permute-done.5.refs_6_ = bf16[384,128]{1,0:T(8,128)(2,1)S(1)} collective-permute-done((bf16[384,128]{1,0:T(8,128)(2,1)S(1)}, bf16[384,128]{1,0:T(8,128)(2,1)S(1)}, u32[]{:S(2)}, u32[]{:S(2)}) %collective-permute-start.5) | collective-permute-done | bytes 98336 | tf_op jit(solution)/shard_map/halo_2/ppermute | solution.py:527
  107.6 1.9 %step_2.1 = (f32[32,16,128]{2,1,0:T(8,128)}, f32[32,16,128]{2,1,0:T(8,128)}, f32[8,8,16,128]{3,2,1,0:T(8,128)}) custom-call(f32[32,16,128]{2,1,0:T(8,128)S(1)} %get-tuple-element.40.refs_0_, f32[32,16,128]{2,1,0:T(8,128)S(1)} %get-tuple-element.41.refs_1_, f32[32,16,128]{2,1,0:T(8,128)S(1)} %get-tuple-element.42.refs_2_, ...), custom_call_target="tpu_custom_call" | custom-call | flops 1000000 | bytes 3211284 | tf_op jit(solution)/shard_map/step_2/step_2/pallas_call | solution.py:25
  109.6 3.5 %all-to-all-start.2 = ((f32[64,16,128]{2,1,0:T(8,128)}), f32[64,16,128]{2,1,0:T(8,128)S(1)}, u32[]{:S(2)}, u32[]{:S(2)}) async-start(f32[64,16,128]{2,1,0:T(8,128)} %bitcast.10), calls=%async_computation.2 | async-start | bytes 1048576 | tf_op jit(solution)/shard_map/update/all_to_all | solution.py:703
  113.7 9.6 %all-to-all-done.2 = f32[64,16,128]{2,1,0:T(8,128)S(1)} async-done(((f32[64,16,128]{2,1,0:T(8,128)}), f32[64,16,128]{2,1,0:T(8,128)S(1)}, u32[]{:S(2)}, u32[]{:S(2)}) %all-to-all-start.2) | async-done | bytes 524320 | tf_op jit(solution)/shard_map/update/all_to_all | solution.py:703
  123.3 0.0 copy-start.6
  123.3 0.7 update.1
  124.1 0.0 copy-start.1
  124.1 3.5 %all-to-all-start.3 = ((f32[32,16,128]{2,1,0:T(8,128)}), f32[32,16,128]{2,1,0:T(8,128)S(1)}, u32[]{:S(2)}, u32[]{:S(2)}) async-start(f32[32,16,128]{2,1,0:T(8,128)} %bitcast.12), calls=%async_computation.3 | async-start | bytes 524288 | tf_op jit(solution)/shard_map/update/all_to_all | solution.py:713
  127.6 0.0 copy-done.6
  127.6 1.0 trace_2.1.second_ref
  128.6 6.5 %all-to-all-done.3.update_ref = f32[32,16,128]{2,1,0:T(8,128)S(1)} async-done(((f32[32,16,128]{2,1,0:T(8,128)}), f32[32,16,128]{2,1,0:T(8,128)S(1)}, u32[]{:S(2)}, u32[]{:S(2)}) %all-to-all-start.3) | async-done | bytes 262176 | tf_op jit(solution)/shard_map/update/all_to_all | solution.py:713
  135.1 0.0 copy-done.1
  135.1 6.3 %gradient.1 = f32[64,1,1152]{2,1,0:T(1,128)S(1)} custom-call(f32[32,16,128]{2,1,0:T(8,128)S(1)} %all-to-all-done.3.update_ref, f32[32,16,128]{2,1,0:T(8,128)S(1)} %all-to-all-done.1.refs_4_.squashed_ref, bf16[4,32,16,128]{3,2,1,0:T(8,128)(2,1)S(1)} %copy-done.1, f32[12,16,128]{2,1,0:T(8,128)S(1)} %collective-permute-done.refs_7_.low_ref.x_low_ref, ...), custom_call_target="tpu_custom_call" | custom-call | flops 14155776 | bytes 1814528 | tf_op jit(solution)/shard_map/gradient/gradient/pallas_call | solution.py:25
  141.4 33.5 %all_to_all.26.shares_ref = f32[64,1,1152]{2,1,0:T(1,128)S(1)} all-to-all(f32[64,1,1152]{2,1,0:T(1,128)S(1)} %gradient.1), channel_id=1, replica_groups=mesh['shot'=8,'gx'=8,'gy'=8] {'gx','gy'}, dimensions={0} | all-to-all | bytes 589824 | tf_op jit(solution)/shard_map/gradient/all_to_all | solution.py:729
  174.8 0.7 total.1
  175.6 0.7 copy.19
  (1 shorter events, 0.0 us)
Async XLA Ops:
  0.6 1.0 copy-start
  1.7 0.9 copy-start.2
  2.6 0.9 copy-start.4
  3.9 9.4 %collective-permute-start = (f32[12,16,128]{2,1,0:T(8,128)S(1)}, f32[12,16,128]{2,1,0:T(8,128)S(1)}, u32[]{:S(2)}, u32[]{:S(2)}) collective-permute-start(f32[12,16,128]{2,1,0:T(8,128)S(1)} %get-tuple-element.30), channel_id=1, source_target_pairs={{0,8},{8,16},{16,24},{24,32},{32,40},{40,48},{48,56},{1,9},{9,17},... | collective-permute-start | bytes 294920 | tf_op jit(solution)/shard_map/halo_x/ppermute | solution.py:526
  7.7 7.1 %collective-permute-start.1 = (f32[12,16,128]{2,1,0:T(8,128)S(1)}, f32[12,16,128]{2,1,0:T(8,128)S(1)}, u32[]{:S(2)}, u32[]{:S(2)}) collective-permute-start(f32[12,16,128]{2,1,0:T(8,128)S(1)} %get-tuple-element.31), channel_id=1, source_target_pairs={{8,0},{16,8},{24,16},{32,24},{40,32},{48,40},{56,48},{9,1},{17,9},... | collective-permute-start | bytes 294920 | tf_op jit(solution)/shard_map/halo_x/ppermute | solution.py:527
  15.1 14.7 %copy-start.11 = (f32[4,27]{1,0:T(4,128)S(1)}, f32[4,27]{1,0:T(4,128)}, u32[]{:S(2)}) copy-start(f32[4,27]{1,0:T(4,128)} %weight_ref.3) | copy-start | bytes 1300
  15.1 24.0 %collective-permute-start.2 = (bf16[528,128]{1,0:T(8,128)(2,1)S(1)}, bf16[528,128]{1,0:T(8,128)(2,1)S(1)}, u32[]{:S(2)}, u32[]{:S(2)}) collective-permute-start(bf16[528,128]{1,0:T(8,128)(2,1)S(1)} %get-tuple-element.36), channel_id=1, source_target_pairs={{0,1},{1,2},{2,3},{3,4},{4,5},{5,6},{6,7},{8,9},{9,10},{10,11},{11... | collective-permute-start | bytes 405512 | tf_op jit(solution)/shard_map/halo_y/ppermute | solution.py:526
  28.5 25.8 %collective-permute-start.3 = (bf16[528,128]{1,0:T(8,128)(2,1)S(1)}, bf16[528,128]{1,0:T(8,128)(2,1)S(1)}, u32[]{:S(2)}, u32[]{:S(2)}) collective-permute-start(bf16[528,128]{1,0:T(8,128)(2,1)S(1)} %get-tuple-element.37), channel_id=1, source_target_pairs={{1,0},{2,1},{3,2},{4,3},{5,4},{6,5},{7,6},{9,8},{10,9},{11,10},{12... | collective-permute-start | bytes 405512 | tf_op jit(solution)/shard_map/halo_y/ppermute | solution.py:527
  66.7 5.0 %copy-start.7 = (f32[1,32,16,128]{3,2,1,0:T(8,128)S(1)}, f32[1,32,16,128]{3,2,1,0:T(8,128)}, u32[]{:S(2)}) copy-start(f32[1,32,16,128]{3,2,1,0:T(8,128)} %param.13) | copy-start | bytes 786436
  66.7 5.0 %copy-start.8 = (f32[1,32,16,128]{3,2,1,0:T(8,128)S(1)}, f32[1,32,16,128]{3,2,1,0:T(8,128)}, u32[]{:S(2)}) copy-start(f32[1,32,16,128]{3,2,1,0:T(8,128)} %param.15) | copy-start | bytes 786436
  67.4 4.3 %copy-start.3 = (f32[1,32,16,128]{3,2,1,0:T(8,128)S(1)}, f32[1,32,16,128]{3,2,1,0:T(8,128)}, u32[]{:S(2)}) copy-start(f32[1,32,16,128]{3,2,1,0:T(8,128)} %param.14) | copy-start | bytes 786436
  67.4 4.3 %copy-start.5 = (f32[1,32,16,128]{3,2,1,0:T(8,128)S(1)}, f32[1,32,16,128]{3,2,1,0:T(8,128)}, u32[]{:S(2)}) copy-start(f32[1,32,16,128]{3,2,1,0:T(8,128)} %param.16) | copy-start | bytes 786436
  67.4 11.0 %all-to-all-start.1 = ((f32[32,16,128]{2,1,0:T(8,128)}), f32[32,16,128]{2,1,0:T(8,128)S(1)}, u32[]{:S(2)}, u32[]{:S(2)}) async-start(f32[32,16,128]{2,1,0:T(8,128)} %bitcast.7), calls=%async_computation.1 | async-start | bytes 524288 | tf_op jit(solution)/shard_map/squash/all_to_all | solution.py:617
  71.6 0.7 copy-start.10
  71.7 0.7 copy-start.9
  78.4 0.7 copy-start.12
  80.2 21.0 %collective-permute-start.4 = (bf16[384,128]{1,0:T(8,128)(2,1)S(1)}, bf16[384,128]{1,0:T(8,128)(2,1)S(1)}, u32[]{:S(2)}, u32[]{:S(2)}) collective-permute-start(bf16[384,128]{1,0:T(8,128)(2,1)S(1)} %get-tuple-element.44), channel_id=1, source_target_pairs={{0,1},{1,2},{2,3},{3,4},{4,5},{5,6},{6,7},{8,9},{9,10},{10,11},{11... | collective-permute-start | bytes 294920 | tf_op jit(solution)/shard_map/halo_2/ppermute | solution.py:526
  90.4 17.2 %collective-permute-start.5 = (bf16[384,128]{1,0:T(8,128)(2,1)S(1)}, bf16[384,128]{1,0:T(8,128)(2,1)S(1)}, u32[]{:S(2)}, u32[]{:S(2)}) collective-permute-start(bf16[384,128]{1,0:T(8,128)(2,1)S(1)} %get-tuple-element.45), channel_id=1, source_target_pairs={{1,0},{2,1},{3,2},{4,3},{5,4},{6,5},{7,6},{9,8},{10,9},{11,10},{12... | collective-permute-start | bytes 294920 | tf_op jit(solution)/shard_map/halo_2/ppermute | solution.py:527
  91.7 9.5 %collective-permute-start.6 = (f32[8,16,128]{2,1,0:T(8,128)S(1)}, f32[8,16,128]{2,1,0:T(8,128)S(1)}, u32[]{:S(2)}, u32[]{:S(2)}) collective-permute-start(f32[8,16,128]{2,1,0:T(8,128)S(1)} %get-tuple-element.46), channel_id=1, source_target_pairs={{0,8},{8,16},{16,24},{24,32},{32,40},{40,48},{48,56},{1,9},{9,17},... | collective-permute-start | bytes 196616 | tf_op jit(solution)/shard_map/halo_2/ppermute | solution.py:526
  93.6 7.6 %collective-permute-start.7 = (f32[8,16,128]{2,1,0:T(8,128)S(1)}, f32[8,16,128]{2,1,0:T(8,128)S(1)}, u32[]{:S(2)}, u32[]{:S(2)}) collective-permute-start(f32[8,16,128]{2,1,0:T(8,128)S(1)} %get-tuple-element.47), channel_id=1, source_target_pairs={{8,0},{16,8},{24,16},{32,24},{40,32},{48,40},{56,48},{9,1},{17,9},... | collective-permute-start | bytes 196616 | tf_op jit(solution)/shard_map/halo_2/ppermute | solution.py:527
  109.6 13.8 %all-to-all-start.2 = ((f32[64,16,128]{2,1,0:T(8,128)}), f32[64,16,128]{2,1,0:T(8,128)S(1)}, u32[]{:S(2)}, u32[]{:S(2)}) async-start(f32[64,16,128]{2,1,0:T(8,128)} %bitcast.10), calls=%async_computation.2 | async-start | bytes 1048576 | tf_op jit(solution)/shard_map/update/all_to_all | solution.py:703
  123.3 4.3 %copy-start.6 = (f32[32,16,128]{2,1,0:T(8,128)S(1)}, f32[32,16,128]{2,1,0:T(8,128)}, u32[]{:S(2)}) copy-start(f32[32,16,128]{2,1,0:T(8,128)} %get-tuple-element.49.fwd_ref) | copy-start | bytes 786436
  124.1 11.0 %copy-start.1 = (bf16[4,32,16,128]{3,2,1,0:T(8,128)(2,1)S(1)}, bf16[4,32,16,128]{3,2,1,0:T(8,128)(2,1)}, u32[]{:S(2)}) copy-start(bf16[4,32,16,128]{3,2,1,0:T(8,128)(2,1)} %feat_ref.7) | copy-start | bytes 1572868
  124.1 11.0 %all-to-all-start.3 = ((f32[32,16,128]{2,1,0:T(8,128)}), f32[32,16,128]{2,1,0:T(8,128)S(1)}, u32[]{:S(2)}, u32[]{:S(2)}) async-start(f32[32,16,128]{2,1,0:T(8,128)} %bitcast.12), calls=%async_computation.3 | async-start | bytes 524288 | tf_op jit(solution)/shard_map/update/all_to_all | solution.py:713

commit v4 on v3

--- a/solution.py
+++ b/solution.py
@@ -12,24 +12,24 @@
 F32 = jnp.float32
 BF16 = jnp.bfloat16
 VMEM_LIMIT = 48 * 1024 * 1024
+VMEM_WHOLE = 63 * 1024 * 1024
 
 VM = pl.BlockSpec(memory_space=pltpu.VMEM)
 SM = pl.BlockSpec(memory_space=pltpu.SMEM)
 
 
-def call(body, outs, ins, specs, scratch=(), flops=1_000_000, name=None, grid=()):
+def call(body, outs, ins, specs, scratch=(), flops=1_000_000, name=None, limit=VMEM_LIMIT):
     moved = sum(a.size * a.dtype.itemsize for a in ins) + sum(
         o.size * jnp.dtype(o.dtype).itemsize for o in outs
     )
     single = len(outs) == 1
     return pl.pallas_call(
         body,
-        grid=grid,
         out_shape=outs[0] if single else tuple(outs),
         in_specs=specs,
         out_specs=VM if single else tuple(VM for _ in outs),
         scratch_shapes=list(scratch),
-        compiler_params=pltpu.CompilerParams(vmem_limit_bytes=VMEM_LIMIT),
+        compiler_params=pltpu.CompilerParams(vmem_limit_bytes=limit),
         cost_estimate=pl.CostEstimate(flops=flops, bytes_accessed=moved, transcendentals=0),
         name=name,
     )(*ins)
@@ -156,7 +156,10 @@
         ext_ref[c, 1 + size_x] = high_ref[8 + c]
 
 
-def conv_body(feat_ref, low_ref, high_ref, weight_ref, out_ref, ext_ref):
+def conv_body(feat_ref, low_ref, high_ref, weight_ref, *refs):
+    small_in, (out_ref, *small_out), ext_ref = refs[:3], refs[3:7], refs[7]
+    for source, target in zip(small_in, small_out):
+        target[...] = source[...]
     channels, size_x = feat_ref.shape[:2]
     fill_features(ext_ref, feat_ref, low_ref, high_ref)
 
@@ -193,10 +196,12 @@
     plane_ref[8 + size_x : 9 + size_x] = tail[2 * c + 1 : 2 * c + 2]
 
 
-def conv_edge_body(main_ref, low_ref, high_ref, weight_ref, out_ref, plane_ref):
+def conv_edge_body(
+    main_ref, low_ref, high_ref, weight_ref, place_ref, keep_ref, give_ref, total_ref, plane_ref
+):
     size_x, size_y, depth = main_ref.shape
     channels = weight_ref.shape[0]
-    out_ref[...] = main_ref[...]
+    total_ref[...] = main_ref[...]
     for buffer_ref, dy, y in ((low_ref, 0, 0), (high_ref, 2, size_y - 1)):
         terms = [None] * 3
         for c in range(channels):
@@ -207,17 +212,24 @@
                     part = weight_ref[c, 9 * dx + 3 * dy + dz] * rows
                     terms[dz] = part if terms[dz] is None else terms[dz] + part
         total = terms[1] + shifted_lanes(terms[0], -1) + shifted_lanes(terms[2], 1)
-        out_ref[:, y : y + 1, :] += total.reshape(size_x, 1, depth)
+        total_ref[:, y : y + 1, :] += total.reshape(size_x, 1, depth)
+    half = size_x // 2
+    core = place_ref[3]
+    keep_ref[...] = total_ref[pl.ds(core * half, half)]
+    give_ref[...] = total_ref[pl.ds((1 - core) * half, half)]
+
+
+def pair_body(keep_ref, got_ref, out_ref):
+    total = keep_ref[...] + got_ref[...]
+    for n in range(out_ref.shape[0]):
+        out_ref[n] = total
 
 
 def squash_body(parts_ref, out_ref):
-    count = parts_ref.shape[0]
     total = parts_ref[0]
-    for n in range(1, count):
+    for n in range(1, parts_ref.shape[0]):
         total = total + parts_ref[n]
-    squashed = jax.nn.sigmoid(total)
-    for n in range(count):
-        out_ref[n] = squashed
+    out_ref[...] = jax.nn.sigmoid(total)
 
 
 def update_body(parts_ref, damping_ref, out_ref):
@@ -328,17 +340,22 @@
 
 
 def step_body(moment, plane_y, *refs):
-    fwd_ahead_ref, back_ahead_ref, lap_fwd_ref, lap_back_ref, squashed_ref = refs[:5]
-    y_low_ref, y_high_ref, place_ref, wavelet_ref = refs[5:9]
-    refs = refs[9:]
+    fwd_ahead_ref, back_ahead_ref, lap_fwd_ref, lap_back_ref = refs[:4]
+    y_low_ref, y_high_ref, place_ref, wavelet_ref = refs[4:8]
+    refs = refs[8:]
     if moment == 0:
-        (fwd_new_ref, back_new_ref, lap_ref) = refs[:3]
-        (x_up_ref, x_down_ref, y_up_ref, y_down_ref) = refs[3:7]
-        refs = refs[7:]
+        own_ref, other_ref = refs[:2]
+        (fwd_new_ref, back_new_ref, lap_ref, squashed_ref) = refs[2:6]
+        (x_up_ref, x_down_ref, y_up_ref, y_down_ref) = refs[6:10]
+        refs = refs[10:]
+        half = own_ref.shape[0]
+        core = place_ref[3]
+        squashed_ref[pl.ds(core * half, half)] = own_ref[...]
+        squashed_ref[pl.ds((1 - core) * half, half)] = other_ref[...]
     else:
-        x_low_ref, x_high_ref, lap_old_ref, back_ref = refs[:4]
-        (fwd_new_ref, back_new_ref, sums_ref) = refs[4:7]
-        refs = refs[7:]
+        squashed_ref, x_low_ref, x_high_ref, lap_old_ref, back_ref = refs[:5]
+        (fwd_new_ref, back_new_ref, sums_ref) = refs[5:8]
+        refs = refs[8:]
     edge_ref, rest_ref, *sides = refs
     size_x, size_y, depth = fwd_ahead_ref.shape
     start_row = y_low_ref.shape[0] - wave_rows(size_x)
@@ -431,51 +448,60 @@
     first_ref,
     second_ref,
     out_ref,
-    ext_ref,
-    moved_ref,
+    left_ref,
+    right_ref,
     plane_ref,
     rows_ref,
 ):
     size_x, size_y, depth = update_ref.shape
     channels = feat_ref.shape[0]
     copies = out_ref.shape[0]
-    fill_features(ext_ref, feat_ref, x_low_ref, x_high_ref)
-
-    def one_row(i, carry):
-        squashed = squashed_ref[i]
-        pulled = update_ref[i] * (0.16 * squashed * (1.0 - squashed))
-        for dz in range(3):
-            along = pulled if dz == 1 else shifted_lanes(pulled, 1 - dz)
+    cells = size_x * size_y
+
+    def one_block(i, carry):
+        for j in range(4):
+            x = 4 * i + j
+            squashed = squashed_ref[x]
+            pulled = update_ref[x] * (0.16 * squashed * (1.0 - squashed))
             for dy in range(3):
-                moved_ref[3 * dy + dz, i] = along if dy == 1 else shifted_rows(along, 1 - dy)
-        edge = pulled[0:1, :], pulled[size_y - 1 : size_y, :]
-        plane_ref[1, pl.ds(i, 1)] = edge[0]
-        plane_ref[2, pl.ds(i, 1)] = edge[1]
+                moved = pulled if dy == 1 else shifted_rows(pulled, 1 - dy)
+                high = moved.astype(BF16)
+                left_ref[2 * dy, x] = high
+                left_ref[2 * dy + 1, x] = (moved - high.astype(F32)).astype(BF16)
+            plane_ref[1, pl.ds(x, 1)] = pulled[0:1, :]
+            plane_ref[2, pl.ds(x, 1)] = pulled[size_y - 1 : size_y, :]
         return carry
 
-    lax.fori_loop(0, size_x, one_row, 0)
-    rows_ref[...] = jnp.zeros_like(rows_ref)
-
+    lax.fori_loop(0, size_x // 4, one_block, 0)
     for c in range(channels):
-
-        def add_row(i, totals):
-            features = [ext_ref[c, i + dx] for dx in range(3)]
-            new = []
+        right_ref[0, 0] = x_low_ref[8 + c].astype(BF16)
+        right_ref[0, 1:size_x] = feat_ref[c, 0 : size_x - 1]
+        right_ref[1] = feat_ref[c]
+        right_ref[2, 0 : size_x - 1] = feat_ref[c, 1:size_x]
+        right_ref[2, size_x - 1] = x_high_ref[8 + c].astype(BF16)
+        right = jnp.concatenate(
+            [right_ref[dx].reshape(cells, depth) for dx in range(3)], axis=1
+        )
+        for dy in range(3):
+            left = jnp.concatenate(
+                [left_ref[2 * dy + part].reshape(cells, depth) for part in range(2)], axis=1
+            )
+            product = lax.dot_general(
+                left, right, (((0,), (0,)), ((), ())), preferred_element_type=F32
+            )
+            ahead = lax.broadcasted_iota(jnp.int32, (depth, depth), 1) - (
+                lax.broadcasted_iota(jnp.int32, (depth, depth), 0)
+            )
             for dx in range(3):
-                for dy in range(3):
-                    for dz in range(3):
-                        product = features[dx] * moved_ref[3 * dy + dz, i]
-                        folded = product[0:8]
-                        for y in range(8, size_y, 8):
-                            folded = folded + product[y : y + 8]
-                        new.append(totals[9 * dx + 3 * dy + dz] + folded)
-            return tuple(new)
-
-        zero = jnp.zeros((8, depth), F32)
-        totals = lax.fori_loop(0, size_x, add_row, (zero,) * 27)
-        for o in range(27):
-            at = c * 27 + o
-            rows_ref[at : at + 1] = jnp.sum(totals[o], axis=0, keepdims=True)
+                lanes = slice(dx * depth, (dx + 1) * depth)
+                block = product[0:depth, lanes] + product[depth : 2 * depth, lanes]
+                for dz in range(3):
+                    at = c * 27 + 9 * dx + 3 * dy + dz
+                    rows_ref[at : at + 1] = jnp.sum(
+                        jnp.where(ahead == dz - 1, block, 0.0), axis=0, keepdims=True
+                    )
+    at = channels * 27
+    rows_ref[at:] = jnp.zeros((rows_ref.shape[0] - at, depth), F32)
 
     for buffer_ref, dy, which in ((y_low_ref, 0, 1), (y_high_ref, 2, 2)):
         pulled = plane_ref[which, 0:size_x]
@@ -519,6 +545,10 @@
     for c in range(channels):
         turned = last if c == 0 else pltpu.roll(last, lanes - c * offsets, 1)
         grad_ref[c : c + 1, :] = turned[0:1, 0:offsets]
+
+
+def keep_body(value_ref, out_ref):
+    out_ref[...] = value_ref[...]
 
 
 def neighbours(up, down, axis):
@@ -552,7 +582,12 @@
         a.reshape(grid) for a in (fwd_prev, fwd_now, back_prev, back_now)
     )
     place = jnp.stack(
-        [lax.axis_index("gx") * size_x, lax.axis_index("gy") * size_y, sources[0]]
+        [
+            lax.axis_index("gx") * size_x,
+            lax.axis_index("gy") * size_y,
+            sources[0],
+            lax.axis_index("shot") % 2,
+        ]
     ).astype(jnp.int32)
 
     x_shape = shape(8 + channels, size_y, depth)
@@ -567,6 +602,7 @@
                 pltpu.SemaphoreType.DMA((2 * (2 + channels),)),
             ],
             name="pack_x",
+            limit=VMEM_WHOLE,
         )
     with jax.named_scope("halo_x"):
         x_low, x_high = neighbours(x_up, x_down, "gx")
@@ -587,35 +623,6 @@
     with jax.named_scope("halo_y"):
         y_low, y_high = neighbours(y_up, y_down, "gy")
     ext = pltpu.VMEM((channels, size_x + 2, size_y, depth), F32)
-    with jax.named_scope("conv"):
-        main = call(
-            conv_body,
-            [shape(*grid)],
-            (features, x_low, x_high, conv_weight),
-            [VM, VM, VM, SM],
-            scratch=[ext],
-            flops=54 * channels * size_x * size_y * depth,
-            name="conv",
-        )
-        part = call(
-            conv_edge_body,
-            [shape(*grid)],
-            (main, y_low, y_high, conv_weight),
-            [VM, VM, VM, SM],
-            scratch=[pltpu.VMEM((size_x + 16, depth), F32)],
-            name="conv_edge",
-        )
-    with jax.named_scope("squash"):
-        parts = lax.all_to_all(part, "shot", 0, 0, tiled=True)
-        squashed = call(
-            squash_body,
-            [shape(shots, rows, size_y, depth)],
-            (parts.reshape(shots, rows, size_y, depth),),
-            [VM],
-            name="squash",
-        )
-        squashed = lax.all_to_all(squashed.reshape(grid), "shot", 0, 0, tiled=True)
-
     full = shape(*grid)
     inner_scratch = [
         pltpu.VMEM((size_x + 8, size_y, depth), F32),
@@ -625,7 +632,7 @@
     step_scratch = packing + [pltpu.VMEM((size_x, 16, depth), F32)] * 4
     work = 60 * size_x * size_y * depth
     with jax.named_scope("inner_1"):
-        fwd_ahead, back_ahead, lap_fwd, lap_back = call(
+        inner_1 = call(
             functools.partial(inner_body, 0, plane_y),
             [full] * 4,
             (fwd_now, back_now, fwd_prev, back_prev, place, receivers, residual, x_low, x_high),
@@ -634,24 +641,73 @@
             flops=work,
             name="inner_1",
         )
+    half = size_x // 2
+    chips = shots // 2
+    half_shape = shape(half, size_y, depth)
+    with jax.named_scope("conv"):
+        small = (receivers, residual, wavelet)
+        main, receivers, residual, wavelet = call(
+            conv_body,
+            [shape(*grid)] + [shape(*a.shape, dtype=a.dtype) for a in small],
+            (features, x_low, x_high, conv_weight) + small,
+            [VM, VM, VM, SM] + [VM] * 3,
+            scratch=[ext],
+            flops=54 * channels * size_x * size_y * depth,
+            name="conv",
+        )
+        main, *inner_1 = lax.optimization_barrier((main, *inner_1))
+        keep, give = call(
+            conv_edge_body,
+            [half_shape] * 2,
+            (main, y_low, y_high, conv_weight, place),
+            [VM, VM, VM, SM, SM],
+            scratch=[pltpu.VMEM(grid, F32), pltpu.VMEM((size_x + 16, depth), F32)],
+            name="conv_edge",
+        )
+    partner = [(i, i ^ 1) for i in range(shots)]
+    with jax.named_scope("squash"):
+        pair = call(
+            pair_body,
+            [shape(chips, half, size_y, depth)],
+            (keep, lax.ppermute(give, "shot", partner)),
+            [VM, VM],
+            name="pair",
+        )
+        if chips > 1:
+            groups = [list(range(core, shots, 2)) for core in range(2)]
+            pair = lax.all_to_all(
+                pair.reshape(chips * half, size_y, depth),
+                "shot",
+                0,
+                0,
+                tiled=True,
+                axis_index_groups=groups,
+            )
+        own = call(
+            squash_body,
+            [half_shape],
+            (pair.reshape(chips, half, size_y, depth),),
+            [VM],
+            name="squash",
+        )
+        other = lax.ppermute(own, "shot", partner)
+
     with jax.named_scope("step_1"):
-        fwd_1, back_1, lap_1, x_up, x_down, y_up, y_down = call(
+        fwd_1, back_1, lap_1, squashed, x_up, x_down, y_up, y_down = call(
             functools.partial(step_body, 0, plane_y),
-            [full] * 3
+            [full] * 4
             + [shape(8, size_y, depth)] * 2
             + [shape(wave_rows(size_x), depth, dtype=BF16)] * 2,
             (
-                fwd_ahead,
-                back_ahead,
-                lap_fwd,
-                lap_back,
-                squashed,
+                *inner_1,
                 y_low,
                 y_high,
                 place,
                 wavelet,
+                own,
+                other,
             ),
-            [VM] * 7 + [SM] * 2,
+            [VM] * 6 + [SM] * 2 + [VM] * 2,
             scratch=step_scratch,
             name="step_1",
         )
@@ -677,17 +733,17 @@
                 back_ahead,
                 lap_fwd,
                 lap_back,
-                squashed,
                 y_low_2,
                 y_high_2,
                 place,
                 wavelet,
+                squashed,
                 x_low_2,
                 x_high_2,
                 lap_1,
                 back_1,
             ),
-            [VM] * 7 + [SM] * 2 + [VM] * 4,
+            [VM] * 6 + [SM] * 2 + [VM] * 5,
             scratch=step_scratch,
             name="step_2",
         )
@@ -718,14 +774,15 @@
             (update, squashed, features, x_low, x_high, y_low, y_high, trace_1, trace_2),
             [VM] * 9,
             scratch=[
-                ext,
-                pltpu.VMEM((9,) + grid, F32),
+                pltpu.VMEM((6,) + grid, BF16),
+                pltpu.VMEM((3,) + grid, BF16),
                 pltpu.VMEM((3, size_x + 16, depth), F32),
                 pltpu.VMEM((128, depth), F32),
             ],
             flops=54 * channels * size_x * size_y * depth,
             name="gradient",
         )
+        share, update = lax.optimization_barrier((share, update))
         shares = lax.all_to_all(share, ("gx", "gy"), 0, 0, tiled=True)
         shares = shares.reshape(blocks, 1, 2 * count + depth)
         traces, weight_grad = call(
@@ -735,6 +792,7 @@
             [VM],
             name="total",
         )
+        update = call(keep_body, [full], (update,), [VM], name="keep")
     return (fwd_2[None], back_2[None], traces, update, weight_grad)
 
 

time: 177 us -> 170 us (0.960)
  blocking collectives: 45.1 us -> 13.9 us
  waiting for transfers between devices: 47.1 us -> 66.6 us
  starting transfers between devices: 51.3 us -> 60.7 us
  local copies, waits for them, and re-layouts: 4.98 us -> 1.65 us
    all_to_all x2 -> x1, blocking collectives: 45.1 us -> 13.9 us  [per_device(): lax.all_to_all(pair.reshape(chips * half, size_y, depth), 'shot', 0, 0, t...]
    all_to_all x1, waiting for transfers between devices: 2.63 us -> 22.8 us  [per_device(): shares = lax.all_to_all(share, ('gx', 'gy'), 0, 0, tiled=True)]
    all_to_all x1, starting transfers between devices: 3.54 us -> 9.11 us  [per_device(): shares = lax.all_to_all(share, ('gx', 'gy'), 0, 0, tiled=True)]
    ppermute x4, waiting for transfers between devices: 5.35 us -> 0.87 us  [neighbours(): low = lax.ppermute(up, axis, [(i, i + 1) for i in range(count - 1)])]
    ppermute x0 -> x2, starting transfers between devices: none -> 3.84 us  [the longest x1 1.92 us: per_device(): lax.ppermute(give, 'shot', partner)]
    unnamed x27 -> x22, local copies, waits for them, and re-layouts: 4.98 us -> 1.65 us
    ppermute x0 -> x2, waiting for transfers between devices: none -> 2.63 us  [the longest x1 1.31 us: per_device(): lax.ppermute(give, 'shot', partner)]
    pallas_call x13 -> x15, Pallas kernels: 25.5 us -> 24 us  [call(): pl.pallas_call(body, out_shape=outs[0] if single else tuple(outs), in_spe...]
  transfers between devices with their start and end apart: 11 -> 13, of which waited for: 8 -> 9; matrix products, arithmetic and copies ran while one was open for 0% -> 0% of each run, Pallas kernels for 7% -> 8%
where the time goes in v4:
time: 170 us; the launch traced here: 169 us
  waiting for transfers between devices  66.6 us (39%)
  starting transfers between devices  60.7 us (36%)
  Pallas kernels  24 us (14%)
  blocking collectives  13.9 us (8%)
  between operations  2.2 us (1%)
    ppermute x4, starting transfers between devices, neighbours(): low = lax.ppermute(up, axis, [(i, i + 1) for i in range(count - 1)])  29.3 us
    ppermute x4, waiting for transfers between devices, neighbours(): high = lax.ppermute(down, axis, [(i + 1, i) for i in range(count - 1)])  24.2 us
    pallas_call x15, Pallas kernels, call(): pl.pallas_call(body, out_shape=outs[0] if single else tuple(outs), in_spe...  24 us
    all_to_all x1, waiting for transfers between devices, per_device(): shares = lax.all_to_all(share, ('gx', 'gy'), 0, 0, tiled=True)  22.8 us
    all_to_all x1, blocking collectives, per_device(): lax.all_to_all(pair.reshape(chips * half, size_y, depth), 'shot', 0, 0, t...  13.9 us
    ppermute x4, starting transfers between devices, neighbours(): high = lax.ppermute(down, axis, [(i + 1, i) for i in range(count - 1)])  11.4 us
    all_to_all x1, waiting for transfers between devices, per_device(): lax.all_to_all(sums.reshape(shots * 2 * rows, size_y, depth), 'shot', 0,...  9.62 us
    all_to_all x1, starting transfers between devices, per_device(): shares = lax.all_to_all(share, ('gx', 'gy'), 0, 0, tiled=True)  9.11 us
  transfers between devices with their start and end apart: 13, of which 9 were waited for; matrix products, arithmetic and copies ran while one was open for 0% of the time, Pallas kernels for 8%

profile of v4, /device:TPU:32, one launch (start us, length us, event | category | flops | bytes accessed | tf_op | source)
XLA Modules:
  0.0 169.0 jit_solution(15031199734768635444)
XLA Ops:
  0.6 0.0 copy-start
  0.6 0.0 copy-start.1
  0.7 1.7 %pack_x.1 = (f32[12,16,128]{2,1,0:T(8,128)}, f32[12,16,128]{2,1,0:T(8,128)}) custom-call(bf16[4,32,16,128]{3,2,1,0:T(8,128)(2,1)} %feat_ref.7, f32[32,16,128]{2,1,0:T(8,128)} %bitcast.14, f32[32,16,128]{2,1,0:T(8,128)} %bitcast.18), custom_call_target="tpu_custom_call" | custom-call | flops 1000000 | bytes 1245184 | tf_op jit(solution)/shard_map/pack_x/pack_x/pallas_call | solution.py:26
  2.4 3.8 %collective-permute-start = (f32[12,16,128]{2,1,0:T(8,128)}, f32[12,16,128]{2,1,0:T(8,128)S(1)}, u32[]{:S(2)}, u32[]{:S(2)}) collective-permute-start(f32[12,16,128]{2,1,0:T(8,128)} %get-tuple-element.44), channel_id=1, source_target_pairs={{0,8},{8,16},{16,24},{24,32},{32,40},{40,48},{48,56},{1,9},{9,17},... | collective-permute-start | bytes 294920 | tf_op jit(solution)/shard_map/halo_x/ppermute | solution.py:556
  6.2 4.9 %collective-permute-start.1 = (f32[12,16,128]{2,1,0:T(8,128)}, f32[12,16,128]{2,1,0:T(8,128)S(1)}, u32[]{:S(2)}, u32[]{:S(2)}) collective-permute-start(f32[12,16,128]{2,1,0:T(8,128)} %get-tuple-element.45), channel_id=1, source_target_pairs={{8,0},{16,8},{24,16},{32,24},{40,32},{48,40},{56,48},{9,1},{17,9},... | collective-permute-start | bytes 294920 | tf_op jit(solution)/shard_map/halo_x/ppermute | solution.py:557
  11.1 0.9 collective-permute-done.low_ref.refs_7_.x_low_ref
  12.0 1.6 collective-permute-done.1.high_ref.refs_8_.x_high_ref
  13.6 0.0 copy-done
  13.6 0.0 copy-done.1
  13.6 0.0 copy-start.2
  13.6 0.9 copy-done.2
  14.6 0.0 copy-start.3
  14.6 0.0 copy-start.5
  14.6 0.0 copy-start.6
  14.6 0.3 pack_y.1
  14.9 13.3 %collective-permute-start.2 = (bf16[528,128]{1,0:T(8,128)(2,1)S(1)}, bf16[528,128]{1,0:T(8,128)(2,1)S(1)}, u32[]{:S(2)}, u32[]{:S(2)}) collective-permute-start(bf16[528,128]{1,0:T(8,128)(2,1)S(1)} %get-tuple-element.55), channel_id=1, source_target_pairs={{0,1},{1,2},{2,3},{3,4},{4,5},{5,6},{6,7},{8,9},{9,10},{10,11},{11... | collective-permute-start | bytes 405512 | tf_op jit(solution)/shard_map/halo_y/ppermute | solution.py:556
  28.2 1.3 collective-permute-start.3
  30.1 0.0 copy-start.7
  30.1 0.1 pad_add_fusion.refs_4_.place_ref.refs_6_
  30.2 0.0 copy-start.8
  30.2 0.0 copy-done.3
  30.2 0.0 copy-done.5
  30.2 0.0 copy-done.6
  30.2 0.6 copy-done.7
  30.8 0.1 copy-done.8
  30.9 0.0 copy-start.9
  30.9 0.0 copy-start.10
  30.9 3.4 %inner_1.1 = (f32[32,16,128]{2,1,0:T(8,128)S(1)}, f32[32,16,128]{2,1,0:T(8,128)S(1)}, f32[32,16,128]{2,1,0:T(8,128)S(1)}, f32[32,16,128]{2,1,0:T(8,128)S(1)}) custom-call(f32[32,16,128]{2,1,0:T(8,128)S(1)} %bitcast.16, f32[32,16,128]{2,1,0:T(8,128)S(1)} %bitcast.20, f32[32,16,128]{2,1,0:T(8,128)S(1)} %bitcast.26, f32[32,16,128]{2,1,0:T(8,128)S(1)} %bitcast.27, ...), custom_call_target="tpu_custom_call" | custom-call | flops 3932160 | bytes 2299920 | tf_op jit(solution)/shard_map/inner_1/inner_1/pallas_call | solution.py:26
  34.3 0.0 copy-done.9
  34.3 0.0 copy-done.10
  34.3 4.6 %conv.1 = (f32[32,16,128]{2,1,0:T(8,128)S(1)}, s32[1,512]{1,0:T(1,128)S(1)}, f32[1,2,512]{2,1,0:T(2,128)S(1)}, f32[1,2]{1,0:T(1,128)S(1)}) custom-call(bf16[4,32,16,128]{3,2,1,0:T(8,128)(2,1)S(1)} %copy-done, f32[12,16,128]{2,1,0:T(8,128)S(1)} %collective-permute-done.low_ref.refs_7_.x_low_ref, ...), custom_call_target="tpu_custom_call" | custom-call | flops 14155776 | bytes 995776 | tf_op jit(solution)/shard_map/conv/conv/pallas_call | solution.py:26
  39.0 0.0 collective-permute-done.2.low_ref.refs_4_.y_low_ref
  39.0 15.0 %collective-permute-done.3.high_ref.refs_5_.y_high_ref = bf16[528,128]{1,0:T(8,128)(2,1)S(1)} collective-permute-done((bf16[528,128]{1,0:T(8,128)(2,1)S(1)}, bf16[528,128]{1,0:T(8,128)(2,1)S(1)}, u32[]{:S(2)}, u32[]{:S(2)}) %collective-permute-start.3) | collective-permute-done | bytes 135200 | tf_op jit(solution)/shard_map/halo_y/ppermute | solution.py:557
  53.9 0.8 conv_edge.1
  54.7 1.9 %collective-permute-start.4 = (f32[16,16,128]{2,1,0:T(8,128)S(1)}, f32[16,16,128]{2,1,0:T(8,128)S(1)}, u32[]{:S(2)}, u32[]{:S(2)}) collective-permute-start(f32[16,16,128]{2,1,0:T(8,128)S(1)} %get-tuple-element.60), channel_id=1, source_target_pairs={{0,64},{64,0},{128,192},{192,128},{256,320},{320,256},{384,448},{4... | collective-permute-start | bytes 393224 | tf_op jit(solution)/shard_map/squash/ppermute | solution.py:672
  56.6 1.3 collective-permute-done.4.got_ref
  58.0 13.9 %all_to_all.20 = f32[64,16,128]{2,1,0:T(8,128)S(1)} all-to-all(f32[64,16,128]{2,1,0:T(8,128)S(1)} %bitcast.24), channel_id=1, replica_groups={{0,128,256,384},{64,192,320,448},{1,129,257,385},{65,193,321,449},{2,13..., dimensions={0} | all-to-all | bytes 1048576 | tf_op jit(solution)/shard_map/squash/all_to_all | solution.py:678
  71.9 1.9 %collective-permute-start.5 = (f32[16,16,128]{2,1,0:T(8,128)S(1)}, f32[16,16,128]{2,1,0:T(8,128)S(1)}, u32[]{:S(2)}, u32[]{:S(2)}) collective-permute-start(f32[16,16,128]{2,1,0:T(8,128)S(1)} %squash.1.refs_8_), channel_id=1, source_target_pairs={{0,64},{64,0},{128,192},{192,128},{256,320},{320,256},{384,448},{4... | collective-permute-start | bytes 393224 | tf_op jit(solution)/shard_map/squash/ppermute | solution.py:693
  73.8 1.3 collective-permute-done.5.refs_9_
  75.2 1.2 step_1.1
  76.3 10.3 %collective-permute-start.6 = (bf16[384,128]{1,0:T(8,128)(2,1)S(1)}, bf16[384,128]{1,0:T(8,128)(2,1)S(1)}, u32[]{:S(2)}, u32[]{:S(2)}) collective-permute-start(bf16[384,128]{1,0:T(8,128)(2,1)S(1)} %get-tuple-element.69), channel_id=1, source_target_pairs={{0,1},{1,2},{2,3},{3,4},{4,5},{5,6},{6,7},{8,9},{9,10},{10,11},{11... | collective-permute-start | bytes 294920 | tf_op jit(solution)/shard_map/halo_2/ppermute | solution.py:556
  86.6 1.3 collective-permute-start.7
  87.9 1.9 %collective-permute-start.8 = (f32[8,16,128]{2,1,0:T(8,128)S(1)}, f32[8,16,128]{2,1,0:T(8,128)S(1)}, u32[]{:S(2)}, u32[]{:S(2)}) collective-permute-start(f32[8,16,128]{2,1,0:T(8,128)S(1)} %get-tuple-element.72), channel_id=1, source_target_pairs={{0,8},{8,16},{16,24},{24,32},{32,40},{40,48},{48,56},{1,9},{9,17},... | collective-permute-start | bytes 196616 | tf_op jit(solution)/shard_map/halo_2/ppermute | solution.py:556
  89.9 3.9 %collective-permute-start.9 = (f32[8,16,128]{2,1,0:T(8,128)S(1)}, f32[8,16,128]{2,1,0:T(8,128)S(1)}, u32[]{:S(2)}, u32[]{:S(2)}) collective-permute-start(f32[8,16,128]{2,1,0:T(8,128)S(1)} %get-tuple-element.73), channel_id=1, source_target_pairs={{8,0},{16,8},{24,16},{32,24},{40,32},{48,40},{56,48},{9,1},{17,9},... | collective-permute-start | bytes 196616 | tf_op jit(solution)/shard_map/halo_2/ppermute | solution.py:557
  93.8 3.6 %inner_2.1 = (f32[32,16,128]{2,1,0:T(8,128)S(1)}, f32[32,16,128]{2,1,0:T(8,128)S(1)}, f32[32,16,128]{2,1,0:T(8,128)S(1)}, f32[32,16,128]{2,1,0:T(8,128)S(1)}, f32[1,512]{1,0:T(1,128)S(1)}) custom-call(f32[32,16,128]{2,1,0:T(8,128)S(1)} %get-tuple-element.61.refs_0_, f32[32,16,128]{2,1,0:T(8,128)S(1)} %get-tuple-element.62.refs_1_.refs_12_, ...), custom_call_target="tpu_custom_call" | custom-call | flops 3932160 | bytes 2105360 | tf_op jit(solution)/shard_map/inner_2/inner_2/pallas_call | solution.py:26
  97.4 0.0 collective-permute-done.8.refs_9_
  97.4 0.0 collective-permute-done.9.refs_10_
  97.4 0.0 collective-permute-done.6.refs_4_
  97.4 7.6 %collective-permute-done.7.refs_5_ = bf16[384,128]{1,0:T(8,128)(2,1)S(1)} collective-permute-done((bf16[384,128]{1,0:T(8,128)(2,1)S(1)}, bf16[384,128]{1,0:T(8,128)(2,1)S(1)}, u32[]{:S(2)}, u32[]{:S(2)}) %collective-permute-start.7) | collective-permute-done | bytes 98336 | tf_op jit(solution)/shard_map/halo_2/ppermute | solution.py:557
  105.0 1.9 %step_2.1 = (f32[32,16,128]{2,1,0:T(8,128)}, f32[32,16,128]{2,1,0:T(8,128)}, f32[8,8,16,128]{3,2,1,0:T(8,128)}) custom-call(f32[32,16,128]{2,1,0:T(8,128)S(1)} %get-tuple-element.65.refs_0_, f32[32,16,128]{2,1,0:T(8,128)S(1)} %get-tuple-element.66.refs_1_, f32[32,16,128]{2,1,0:T(8,128)S(1)} %get-tuple-element.67.refs_2_, ...), custom_call_target="tpu_custom_call" | custom-call | flops 1000000 | bytes 3211288 | tf_op jit(solution)/shard_map/step_2/step_2/pallas_call | solution.py:26
  106.9 3.5 %all-to-all-start.1 = ((f32[64,16,128]{2,1,0:T(8,128)}), f32[64,16,128]{2,1,0:T(8,128)S(1)}, u32[]{:S(2)}, u32[]{:S(2)}) async-start(f32[64,16,128]{2,1,0:T(8,128)} %bitcast.11), calls=%async_computation.1 | async-start | bytes 1048576 | tf_op jit(solution)/shard_map/update/all_to_all | solution.py:759
  111.1 9.6 %all-to-all-done.1 = f32[64,16,128]{2,1,0:T(8,128)S(1)} async-done(((f32[64,16,128]{2,1,0:T(8,128)}), f32[64,16,128]{2,1,0:T(8,128)S(1)}, u32[]{:S(2)}, u32[]{:S(2)}) %all-to-all-start.1) | async-done | bytes 524320 | tf_op jit(solution)/shard_map/update/all_to_all | solution.py:759
  120.7 0.7 update.1
  121.4 0.0 copy-start.4
  121.4 3.5 %all-to-all-start.2 = ((f32[32,16,128]{2,1,0:T(8,128)}), f32[32,16,128]{2,1,0:T(8,128)S(1)}, u32[]{:S(2)}, u32[]{:S(2)}) async-start(f32[32,16,128]{2,1,0:T(8,128)} %bitcast.13), calls=%async_computation.2 | async-start | bytes 524288 | tf_op jit(solution)/shard_map/update/all_to_all | solution.py:769
  125.0 0.0 copy-done.4
  125.0 1.0 trace_2.1.second_ref
  126.0 6.5 %all-to-all-done.2.update_ref.value_ref = f32[32,16,128]{2,1,0:T(8,128)S(1)} async-done(((f32[32,16,128]{2,1,0:T(8,128)}), f32[32,16,128]{2,1,0:T(8,128)S(1)}, u32[]{:S(2)}, u32[]{:S(2)}) %all-to-all-start.2) | async-done | bytes 262176 | tf_op jit(solution)/shard_map/update/all_to_all | solution.py:769
  132.5 3.2 %gradient.1 = f32[64,1,1152]{2,1,0:T(1,128)} custom-call(f32[32,16,128]{2,1,0:T(8,128)S(1)} %all-to-all-done.2.update_ref.value_ref, f32[32,16,128]{2,1,0:T(8,128)S(1)} %get-tuple-element.71.refs_8_.squashed_ref, bf16[4,32,16,128]{3,2,1,0:T(8,128)(2,1)S(1)} %copy-done, f32[12,16,128]{2,1,0:T(8,128)S(1)} %collective-permute-done.low_ref.refs_7_.x_low_ref, ...), custom_call_target="tpu_custom_call" | custom-call | flops 14155776 | bytes 1814528 | tf_op jit(solution)/shard_map/gradient/gradient/pallas_call | solution.py:26
  135.6 9.1 %all-to-all-start.3 = ((f32[64,1,1152]{2,1,0:T(1,128)}), f32[64,1,1152]{2,1,0:T(1,128)S(1)}, u32[]{:S(2)}, u32[]{:S(2)}) async-start(f32[64,1,1152]{2,1,0:T(1,128)} %gradient.1), calls=%async_computation.3 | async-start | bytes 589824 | tf_op jit(solution)/shard_map/gradient/all_to_all | solution.py:786
  144.8 0.7 keep.1
  145.5 22.8 %all-to-all-done.3.shares_ref = f32[64,1,1152]{2,1,0:T(1,128)S(1)} async-done(((f32[64,1,1152]{2,1,0:T(1,128)}), f32[64,1,1152]{2,1,0:T(1,128)S(1)}, u32[]{:S(2)}, u32[]{:S(2)}) %all-to-all-start.3) | async-done | bytes 294944 | tf_op jit(solution)/shard_map/gradient/all_to_all | solution.py:786
  168.3 0.7 total.1
  (2 shorter events, 0.1 us)
Async XLA Ops:
  0.6 13.0 %copy-start = (bf16[4,32,16,128]{3,2,1,0:T(8,128)(2,1)S(1)}, bf16[4,32,16,128]{3,2,1,0:T(8,128)(2,1)}, u32[]{:S(2)}) copy-start(bf16[4,32,16,128]{3,2,1,0:T(8,128)(2,1)} %feat_ref.7) | copy-start | bytes 1572868
  0.6 13.0 %copy-start.1 = (f32[1,32,16,128]{3,2,1,0:T(8,128)S(1)}, f32[1,32,16,128]{3,2,1,0:T(8,128)}, u32[]{:S(2)}) copy-start(f32[1,32,16,128]{3,2,1,0:T(8,128)} %param.14) | copy-start | bytes 786436
  2.4 9.6 %collective-permute-start = (f32[12,16,128]{2,1,0:T(8,128)}, f32[12,16,128]{2,1,0:T(8,128)S(1)}, u32[]{:S(2)}, u32[]{:S(2)}) collective-permute-start(f32[12,16,128]{2,1,0:T(8,128)} %get-tuple-element.44), channel_id=1, source_target_pairs={{0,8},{8,16},{16,24},{24,32},{32,40},{40,48},{48,56},{1,9},{9,17},... | collective-permute-start | bytes 294920 | tf_op jit(solution)/shard_map/halo_x/ppermute | solution.py:556
  6.2 7.4 %collective-permute-start.1 = (f32[12,16,128]{2,1,0:T(8,128)}, f32[12,16,128]{2,1,0:T(8,128)S(1)}, u32[]{:S(2)}, u32[]{:S(2)}) collective-permute-start(f32[12,16,128]{2,1,0:T(8,128)} %get-tuple-element.45), channel_id=1, source_target_pairs={{8,0},{16,8},{24,16},{32,24},{40,32},{48,40},{56,48},{9,1},{17,9},... | collective-permute-start | bytes 294920 | tf_op jit(solution)/shard_map/halo_x/ppermute | solution.py:557
  13.6 1.0 copy-start.2
  14.6 15.7 %copy-start.3 = (f32[1,32,16,128]{3,2,1,0:T(8,128)S(1)}, f32[1,32,16,128]{3,2,1,0:T(8,128)}, u32[]{:S(2)}) copy-start(f32[1,32,16,128]{3,2,1,0:T(8,128)} %param.16) | copy-start | bytes 786436
  14.6 15.7 %copy-start.5 = (f32[1,32,16,128]{3,2,1,0:T(8,128)S(1)}, f32[1,32,16,128]{3,2,1,0:T(8,128)}, u32[]{:S(2)}) copy-start(f32[1,32,16,128]{3,2,1,0:T(8,128)} %param.13) | copy-start | bytes 786436
  14.6 15.7 %copy-start.6 = (f32[1,32,16,128]{3,2,1,0:T(8,128)S(1)}, f32[1,32,16,128]{3,2,1,0:T(8,128)}, u32[]{:S(2)}) copy-start(f32[1,32,16,128]{3,2,1,0:T(8,128)} %param.15) | copy-start | bytes 786436
  14.9 24.1 %collective-permute-start.2 = (bf16[528,128]{1,0:T(8,128)(2,1)S(1)}, bf16[528,128]{1,0:T(8,128)(2,1)S(1)}, u32[]{:S(2)}, u32[]{:S(2)}) collective-permute-start(bf16[528,128]{1,0:T(8,128)(2,1)S(1)} %get-tuple-element.55), channel_id=1, source_target_pairs={{0,1},{1,2},{2,3},{3,4},{4,5},{5,6},{6,7},{8,9},{9,10},{10,11},{11... | collective-permute-start | bytes 405512 | tf_op jit(solution)/shard_map/halo_y/ppermute | solution.py:556
  28.2 25.8 %collective-permute-start.3 = (bf16[528,128]{1,0:T(8,128)(2,1)S(1)}, bf16[528,128]{1,0:T(8,128)(2,1)S(1)}, u32[]{:S(2)}, u32[]{:S(2)}) collective-permute-start(bf16[528,128]{1,0:T(8,128)(2,1)S(1)} %get-tuple-element.56), channel_id=1, source_target_pairs={{1,0},{2,1},{3,2},{4,3},{5,4},{6,5},{7,6},{9,8},{10,9},{11,10},{12... | collective-permute-start | bytes 405512 | tf_op jit(solution)/shard_map/halo_y/ppermute | solution.py:557
  30.1 0.7 copy-start.7
  30.2 0.7 copy-start.8
  30.9 3.4 %copy-start.9 = (f32[4,27]{1,0:T(4,128)S(1)}, f32[4,27]{1,0:T(4,128)}, u32[]{:S(2)}) copy-start(f32[4,27]{1,0:T(4,128)} %weight_ref.3) | copy-start | bytes 1300
  30.9 3.4 %copy-start.10 = (f32[1,2]{1,0:T(1,128)S(1)}, f32[1,2]{1,0:T(1,128)}, u32[]{:S(2)}) copy-start(f32[1,2]{1,0:T(1,128)} %refs_2_.1) | copy-start | bytes 28
  54.7 3.2 %collective-permute-start.4 = (f32[16,16,128]{2,1,0:T(8,128)S(1)}, f32[16,16,128]{2,1,0:T(8,128)S(1)}, u32[]{:S(2)}, u32[]{:S(2)}) collective-permute-start(f32[16,16,128]{2,1,0:T(8,128)S(1)} %get-tuple-element.60), channel_id=1, source_target_pairs={{0,64},{64,0},{128,192},{192,128},{256,320},{320,256},{384,448},{4... | collective-permute-start | bytes 393224 | tf_op jit(solution)/shard_map/squash/ppermute | solution.py:672
  71.9 3.2 %collective-permute-start.5 = (f32[16,16,128]{2,1,0:T(8,128)S(1)}, f32[16,16,128]{2,1,0:T(8,128)S(1)}, u32[]{:S(2)}, u32[]{:S(2)}) collective-permute-start(f32[16,16,128]{2,1,0:T(8,128)S(1)} %squash.1.refs_8_), channel_id=1, source_target_pairs={{0,64},{64,0},{128,192},{192,128},{256,320},{320,256},{384,448},{4... | collective-permute-start | bytes 393224 | tf_op jit(solution)/shard_map/squash/ppermute | solution.py:693
  76.3 21.1 %collective-permute-start.6 = (bf16[384,128]{1,0:T(8,128)(2,1)S(1)}, bf16[384,128]{1,0:T(8,128)(2,1)S(1)}, u32[]{:S(2)}, u32[]{:S(2)}) collective-permute-start(bf16[384,128]{1,0:T(8,128)(2,1)S(1)} %get-tuple-element.69), channel_id=1, source_target_pairs={{0,1},{1,2},{2,3},{3,4},{4,5},{5,6},{6,7},{8,9},{9,10},{10,11},{11... | collective-permute-start | bytes 294920 | tf_op jit(solution)/shard_map/halo_2/ppermute | solution.py:556
  86.6 18.4 %collective-permute-start.7 = (bf16[384,128]{1,0:T(8,128)(2,1)S(1)}, bf16[384,128]{1,0:T(8,128)(2,1)S(1)}, u32[]{:S(2)}, u32[]{:S(2)}) collective-permute-start(bf16[384,128]{1,0:T(8,128)(2,1)S(1)} %get-tuple-element.70), channel_id=1, source_target_pairs={{1,0},{2,1},{3,2},{4,3},{5,4},{6,5},{7,6},{9,8},{10,9},{11,10},{12... | collective-permute-start | bytes 294920 | tf_op jit(solution)/shard_map/halo_2/ppermute | solution.py:557
  87.9 9.5 %collective-permute-start.8 = (f32[8,16,128]{2,1,0:T(8,128)S(1)}, f32[8,16,128]{2,1,0:T(8,128)S(1)}, u32[]{:S(2)}, u32[]{:S(2)}) collective-permute-start(f32[8,16,128]{2,1,0:T(8,128)S(1)} %get-tuple-element.72), channel_id=1, source_target_pairs={{0,8},{8,16},{16,24},{24,32},{32,40},{40,48},{48,56},{1,9},{9,17},... | collective-permute-start | bytes 196616 | tf_op jit(solution)/shard_map/halo_2/ppermute | solution.py:556
  89.9 7.6 %collective-permute-start.9 = (f32[8,16,128]{2,1,0:T(8,128)S(1)}, f32[8,16,128]{2,1,0:T(8,128)S(1)}, u32[]{:S(2)}, u32[]{:S(2)}) collective-permute-start(f32[8,16,128]{2,1,0:T(8,128)S(1)} %get-tuple-element.73), channel_id=1, source_target_pairs={{8,0},{16,8},{24,16},{32,24},{40,32},{48,40},{56,48},{9,1},{17,9},... | collective-permute-start | bytes 196616 | tf_op jit(solution)/shard_map/halo_2/ppermute | solution.py:557
  106.9 13.8 %all-to-all-start.1 = ((f32[64,16,128]{2,1,0:T(8,128)}), f32[64,16,128]{2,1,0:T(8,128)S(1)}, u32[]{:S(2)}, u32[]{:S(2)}) async-start(f32[64,16,128]{2,1,0:T(8,128)} %bitcast.11), calls=%async_computation.1 | async-start | bytes 1048576 | tf_op jit(solution)/shard_map/update/all_to_all | solution.py:759
  121.4 3.6 %copy-start.4 = (f32[32,16,128]{2,1,0:T(8,128)S(1)}, f32[32,16,128]{2,1,0:T(8,128)}, u32[]{:S(2)}) copy-start(f32[32,16,128]{2,1,0:T(8,128)} %get-tuple-element.75.fwd_ref) | copy-start | bytes 786436
  121.4 11.0 %all-to-all-start.2 = ((f32[32,16,128]{2,1,0:T(8,128)}), f32[32,16,128]{2,1,0:T(8,128)S(1)}, u32[]{:S(2)}, u32[]{:S(2)}) async-start(f32[32,16,128]{2,1,0:T(8,128)} %bitcast.13), calls=%async_computation.2 | async-start | bytes 524288 | tf_op jit(solution)/shard_map/update/all_to_all | solution.py:769
  135.6 32.7 %all-to-all-start.3 = ((f32[64,1,1152]{2,1,0:T(1,128)}), f32[64,1,1152]{2,1,0:T(1,128)S(1)}, u32[]{:S(2)}, u32[]{:S(2)}) async-start(f32[64,1,1152]{2,1,0:T(1,128)} %gradient.1), calls=%async_computation.3 | async-start | bytes 589824 | tf_op jit(solution)/shard_map/gradient/all_to_all | solution.py:786

commit v5 on v4

--- a/solution.py
+++ b/solution.py
@@ -156,37 +156,50 @@
         ext_ref[c, 1 + size_x] = high_ref[8 + c]
 
 
-def conv_body(feat_ref, low_ref, high_ref, weight_ref, *refs):
-    small_in, (out_ref, *small_out), ext_ref = refs[:3], refs[3:7], refs[7]
+def conv_body(feat_ref, low_ref, high_ref, weight_ref, place_ref, *refs):
+    small_in, (keep_ref, give_ref, *small_out), (ext_ref, total_ref) = (
+        refs[:3],
+        refs[3:8],
+        refs[8:],
+    )
     for source, target in zip(small_in, small_out):
         target[...] = source[...]
     channels, size_x = feat_ref.shape[:2]
     fill_features(ext_ref, feat_ref, low_ref, high_ref)
-
-    def one_row(i, carry):
-        terms = [[None] * 3 for _ in range(3)]
+    together = 2
+
+    def some_rows(i, carry):
+        start = i * together
+        terms = [[[None] * 3 for _ in range(3)] for _ in range(together)]
         for c in range(channels):
+            inputs = [ext_ref[c, start + r] for r in range(together + 2)]
             for dx in range(3):
-                row = ext_ref[c, i + dx]
                 for dy in range(3):
                     for dz in range(3):
-                        part = weight_ref[c, 9 * dx + 3 * dy + dz] * row
-                        old = terms[dy][dz]
-                        terms[dy][dz] = part if old is None else old + part
-        total = None
-        for dy in range(3):
-            part = (
-                terms[dy][1]
-                + shifted_lanes(terms[dy][0], -1)
-                + shifted_lanes(terms[dy][2], 1)
-            )
-            if dy != 1:
-                part = shifted_rows(part, dy - 1)
-            total = part if total is None else total + part
-        out_ref[i] = total
+                        weight = weight_ref[c, 9 * dx + 3 * dy + dz]
+                        for r in range(together):
+                            part = weight * inputs[r + dx]
+                            old = terms[r][dy][dz]
+                            terms[r][dy][dz] = part if old is None else old + part
+        for r in range(together):
+            total = None
+            for dy in range(3):
+                part = (
+                    terms[r][dy][1]
+                    + shifted_lanes(terms[r][dy][0], -1)
+                    + shifted_lanes(terms[r][dy][2], 1)
+                )
+                if dy != 1:
+                    part = shifted_rows(part, dy - 1)
+                total = part if total is None else total + part
+            total_ref[start + r] = total
         return carry
 
-    lax.fori_loop(0, size_x, one_row, 0)
+    lax.fori_loop(0, size_x // together, some_rows, 0)
+    half = size_x // 2
+    core = place_ref[3]
+    keep_ref[...] = total_ref[pl.ds(core * half, half)]
+    give_ref[...] = total_ref[pl.ds((1 - core) * half, half)]
 
 
 def load_plane(plane_ref, buffer_ref, c, size_x, channels):
@@ -196,13 +209,11 @@
     plane_ref[8 + size_x : 9 + size_x] = tail[2 * c + 1 : 2 * c + 2]
 
 
-def conv_edge_body(
-    main_ref, low_ref, high_ref, weight_ref, place_ref, keep_ref, give_ref, total_ref, plane_ref
-):
-    size_x, size_y, depth = main_ref.shape
+def conv_edge_body(low_ref, high_ref, weight_ref, out_ref, plane_ref):
+    copies, both_x, depth = out_ref.shape
+    size_x = both_x // 2
     channels = weight_ref.shape[0]
-    total_ref[...] = main_ref[...]
-    for buffer_ref, dy, y in ((low_ref, 0, 0), (high_ref, 2, size_y - 1)):
+    for side, (buffer_ref, dy) in enumerate(((low_ref, 0), (high_ref, 2))):
         terms = [None] * 3
         for c in range(channels):
             load_plane(plane_ref, buffer_ref, c, size_x, channels)
@@ -212,11 +223,8 @@
                     part = weight_ref[c, 9 * dx + 3 * dy + dz] * rows
                     terms[dz] = part if terms[dz] is None else terms[dz] + part
         total = terms[1] + shifted_lanes(terms[0], -1) + shifted_lanes(terms[2], 1)
-        total_ref[:, y : y + 1, :] += total.reshape(size_x, 1, depth)
-    half = size_x // 2
-    core = place_ref[3]
-    keep_ref[...] = total_ref[pl.ds(core * half, half)]
-    give_ref[...] = total_ref[pl.ds((1 - core) * half, half)]
+        for n in range(copies):
+            out_ref[n, side * size_x : (side + 1) * size_x] = total
 
 
 def pair_body(keep_ref, got_ref, out_ref):
@@ -225,11 +233,11 @@
         out_ref[n] = total
 
 
-def squash_body(parts_ref, out_ref):
+def sum_body(parts_ref, out_ref):
     total = parts_ref[0]
     for n in range(1, parts_ref.shape[0]):
         total = total + parts_ref[n]
-    out_ref[...] = jax.nn.sigmoid(total)
+    out_ref[...] = total
 
 
 def update_body(parts_ref, damping_ref, out_ref):
@@ -344,14 +352,20 @@
     y_low_ref, y_high_ref, place_ref, wavelet_ref = refs[4:8]
     refs = refs[8:]
     if moment == 0:
-        own_ref, other_ref = refs[:2]
-        (fwd_new_ref, back_new_ref, lap_ref, squashed_ref) = refs[2:6]
-        (x_up_ref, x_down_ref, y_up_ref, y_down_ref) = refs[6:10]
-        refs = refs[10:]
+        own_ref, other_ref, rims_ref = refs[:3]
+        (fwd_new_ref, back_new_ref, lap_ref, squashed_ref) = refs[3:7]
+        (x_up_ref, x_down_ref, y_up_ref, y_down_ref) = refs[7:11]
+        refs = refs[11:]
         half = own_ref.shape[0]
         core = place_ref[3]
         squashed_ref[pl.ds(core * half, half)] = own_ref[...]
         squashed_ref[pl.ds((1 - core) * half, half)] = other_ref[...]
+        size_x, size_y, depth = squashed_ref.shape
+        rims = rims_ref[0]
+        for n in range(1, rims_ref.shape[0]):
+            rims = rims + rims_ref[n]
+        squashed_ref[:, 0:1, :] += rims[:size_x].reshape(size_x, 1, depth)
+        squashed_ref[:, size_y - 1 : size_y, :] += rims[size_x:].reshape(size_x, 1, depth)
     else:
         squashed_ref, x_low_ref, x_high_ref, lap_old_ref, back_ref = refs[:5]
         (fwd_new_ref, back_new_ref, sums_ref) = refs[5:8]
@@ -406,7 +420,11 @@
 
     for start in range(0, size_x, 4):
         here = slice(start, start + 4)
-        courant = 0.02 + 0.16 * squashed_ref[here]
+        squashed = squashed_ref[here]
+        if moment == 0:
+            squashed = jax.nn.sigmoid(squashed)
+            squashed_ref[here] = squashed
+        courant = 0.02 + 0.16 * squashed
         lap_fwd = edges(lap_fwd_ref[here], 0, start)
         lap_back = edges(lap_back_ref[here], 1, start)
         dims = lap_fwd.shape
@@ -644,28 +662,19 @@
     half = size_x // 2
     chips = shots // 2
     half_shape = shape(half, size_y, depth)
+    partner = [(i, i ^ 1) for i in range(shots)]
     with jax.named_scope("conv"):
         small = (receivers, residual, wavelet)
-        main, receivers, residual, wavelet = call(
+        keep, give, receivers, residual, wavelet = call(
             conv_body,
-            [shape(*grid)] + [shape(*a.shape, dtype=a.dtype) for a in small],
-            (features, x_low, x_high, conv_weight) + small,
-            [VM, VM, VM, SM] + [VM] * 3,
-            scratch=[ext],
+            [half_shape] * 2 + [shape(*a.shape, dtype=a.dtype) for a in small],
+            (features, x_low, x_high, conv_weight, place) + small,
+            [VM, VM, VM, SM, SM] + [VM] * 3,
+            scratch=[ext, pltpu.VMEM(grid, F32)],
             flops=54 * channels * size_x * size_y * depth,
             name="conv",
         )
-        main, *inner_1 = lax.optimization_barrier((main, *inner_1))
-        keep, give = call(
-            conv_edge_body,
-            [half_shape] * 2,
-            (main, y_low, y_high, conv_weight, place),
-            [VM, VM, VM, SM, SM],
-            scratch=[pltpu.VMEM(grid, F32), pltpu.VMEM((size_x + 16, depth), F32)],
-            name="conv_edge",
-        )
-    partner = [(i, i ^ 1) for i in range(shots)]
-    with jax.named_scope("squash"):
+    with jax.named_scope("raw"):
         pair = call(
             pair_body,
             [shape(chips, half, size_y, depth)],
@@ -684,13 +693,28 @@
                 axis_index_groups=groups,
             )
         own = call(
-            squash_body,
+            sum_body,
             [half_shape],
             (pair.reshape(chips, half, size_y, depth),),
             [VM],
-            name="squash",
+            name="raw",
         )
         other = lax.ppermute(own, "shot", partner)
+    with jax.named_scope("rims"):
+        weights, own, other, *inner_1 = lax.optimization_barrier(
+            (conv_weight, own, other, *inner_1)
+        )
+        rims = call(
+            conv_edge_body,
+            [shape(shots, 2 * size_x, depth)],
+            (y_low, y_high, weights),
+            [VM, VM, SM],
+            scratch=[pltpu.VMEM((size_x + 16, depth), F32)],
+            name="conv_edge",
+        )
+        rims = lax.all_to_all(
+            rims.reshape(shots * 2 * size_x, depth), "shot", 0, 0, tiled=True
+        ).reshape(shots, 2 * size_x, depth)
 
     with jax.named_scope("step_1"):
         fwd_1, back_1, lap_1, squashed, x_up, x_down, y_up, y_down = call(
@@ -706,8 +730,9 @@
                 wavelet,
                 own,
                 other,
+                rims,
             ),
-            [VM] * 6 + [SM] * 2 + [VM] * 2,
+            [VM] * 6 + [SM] * 2 + [VM] * 3,
             scratch=step_scratch,
             name="step_1",
         )

time: 170 us -> 174 us (1.024)
  starting transfers between devices: 60.7 us -> 66.2 us
  waiting for transfers between devices: 66.6 us -> 69 us
  blocking collectives: 13.9 us -> 11.9 us
    ppermute x4, waiting for transfers between devices: 0.87 us -> 4.81 us  [neighbours(): low = lax.ppermute(up, axis, [(i, i + 1) for i in range(count - 1)])]
    all_to_all x0 -> x1, starting transfers between devices: none -> 3.78 us  [per_device(): lax.all_to_all(pair.reshape(chips * half, size_y, depth), 'shot', 0, 0, t...]
    all_to_all x1, blocking collectives: 13.9 us -> 11.9 us  [per_device(): lax.all_to_all(rims.reshape(shots * 2 * size_x, depth), 'shot', 0, 0, til...]
  transfers between devices with their start and end apart: 13 -> 14, of which waited for: 9 -> 9; matrix products, arithmetic and copies ran while one was open for 0% -> 0% of each run, Pallas kernels for 8% -> 5%
where the time goes in v5:
time: 174 us; the launch traced here: 173 us
  waiting for transfers between devices  69 us (40%)
  starting transfers between devices  66.2 us (38%)
  Pallas kernels  23.3 us (13%)
  blocking collectives  11.9 us (7%)
  between operations  2.24 us (1%)
    ppermute x4, starting transfers between devices, neighbours(): low = lax.ppermute(up, axis, [(i, i + 1) for i in range(count - 1)])  29.4 us
    ppermute x4, waiting for transfers between devices, neighbours(): high = lax.ppermute(down, axis, [(i + 1, i) for i in range(count - 1)])  23.9 us
    pallas_call x15, Pallas kernels, call(): pl.pallas_call(body, out_shape=outs[0] if single else tuple(outs), in_spe...  23.3 us
    all_to_all x1, waiting for transfers between devices, per_device(): shares = lax.all_to_all(share, ('gx', 'gy'), 0, 0, tiled=True)  22.8 us
    all_to_all x1, blocking collectives, per_device(): lax.all_to_all(rims.reshape(shots * 2 * size_x, depth), 'shot', 0, 0, til...  11.9 us
    ppermute x4, starting transfers between devices, neighbours(): high = lax.ppermute(down, axis, [(i + 1, i) for i in range(count - 1)])  11.4 us
    all_to_all x1, starting transfers between devices, per_device(): shares = lax.all_to_all(share, ('gx', 'gy'), 0, 0, tiled=True)  10.7 us
    all_to_all x1, waiting for transfers between devices, per_device(): lax.all_to_all(sums.reshape(shots * 2 * rows, size_y, depth), 'shot', 0,...  9.62 us
  transfers between devices with their start and end apart: 14, of which 9 were waited for; matrix products, arithmetic and copies ran while one was open for 0% of the time, Pallas kernels for 5%

profile of v5, /device:TPU:32, one launch (start us, length us, event | category | flops | bytes accessed | tf_op | source)
XLA Modules:
  0.0 172.8 jit_solution(6004249034344389665)
XLA Ops:
  0.6 0.0 copy-start
  0.6 1.7 pack_x.1
  2.4 3.8 %collective-permute-start = (f32[12,16,128]{2,1,0:T(8,128)}, f32[12,16,128]{2,1,0:T(8,128)S(1)}, u32[]{:S(2)}, u32[]{:S(2)}) collective-permute-start(f32[12,16,128]{2,1,0:T(8,128)} %get-tuple-element.45), channel_id=1, source_target_pairs={{0,8},{8,16},{16,24},{24,32},{32,40},{40,48},{48,56},{1,9},{9,17},... | collective-permute-start | bytes 294920 | tf_op jit(solution)/shard_map/halo_x/ppermute | solution.py:574
  6.2 4.9 %collective-permute-start.1 = (f32[12,16,128]{2,1,0:T(8,128)}, f32[12,16,128]{2,1,0:T(8,128)S(1)}, u32[]{:S(2)}, u32[]{:S(2)}) collective-permute-start(f32[12,16,128]{2,1,0:T(8,128)} %get-tuple-element.46), channel_id=1, source_target_pairs={{8,0},{16,8},{24,16},{32,24},{40,32},{48,40},{56,48},{9,1},{17,9},... | collective-permute-start | bytes 294920 | tf_op jit(solution)/shard_map/halo_x/ppermute | solution.py:575
  11.7 0.0 copy-start.9
  11.7 0.0 copy-start.6
  11.8 0.0 copy-start.7
  11.8 0.0 copy-start.8
  11.8 0.1 pad_add_fusion.place_ref.refs_4_.refs_6_
  11.9 0.1 collective-permute-done.low_ref.refs_7_.x_low_ref
  11.9 1.6 collective-permute-done.1.high_ref.refs_8_.x_high_ref
  13.6 0.0 copy-done
  13.6 0.0 copy-done.9
  13.6 0.0 copy-done.6
  13.6 0.0 copy-done.7
  13.6 0.0 copy-done.8
  13.6 3.2 %conv.1 = (f32[16,16,128]{2,1,0:T(8,128)S(1)}, f32[16,16,128]{2,1,0:T(8,128)S(1)}, s32[1,512]{1,0:T(1,128)S(1)}, f32[1,2,512]{2,1,0:T(2,128)S(1)}, f32[1,2]{1,0:T(1,128)S(1)}) custom-call(bf16[4,32,16,128]{3,2,1,0:T(8,128)(2,1)S(1)} %copy-done, f32[12,16,128]{2,1,0:T(8,128)S(1)} %collective-permute-done.low_ref.refs_7_.x_low_ref, ...), custom_call_target="tpu_custom_call" | custom-call | flops 14155776 | bytes 995792 | tf_op jit(solution)/shard_map/conv/conv/pallas_call | solution.py:26
  16.8 1.9 %collective-permute-start.2 = (f32[16,16,128]{2,1,0:T(8,128)S(1)}, f32[16,16,128]{2,1,0:T(8,128)S(1)}, u32[]{:S(2)}, u32[]{:S(2)}) collective-permute-start(f32[16,16,128]{2,1,0:T(8,128)S(1)} %get-tuple-element.48), channel_id=1, source_target_pairs={{0,64},{64,0},{128,192},{192,128},{256,320},{320,256},{384,448},{4... | collective-permute-start | bytes 393224 | tf_op jit(solution)/shard_map/raw/ppermute | solution.py:681
  18.8 1.3 collective-permute-done.2.got_ref
  20.1 0.8 pair.1
  20.9 0.0 copy-start.1
  20.9 0.0 copy-start.2
  20.9 3.8 %all-to-all-start = ((f32[64,16,128]{2,1,0:T(8,128)}), f32[64,16,128]{2,1,0:T(8,128)S(1)}, u32[]{:S(2)}, u32[]{:S(2)}) async-start(f32[64,16,128]{2,1,0:T(8,128)} %bitcast.5), calls=%async_computation | async-start | bytes 1048576 | tf_op jit(solution)/shard_map/raw/all_to_all | solution.py:687
  24.7 0.0 copy-done.1
  24.7 0.0 copy-done.2
  24.7 0.3 pack_y.1
  25.0 13.9 %collective-permute-start.4 = (bf16[528,128]{1,0:T(8,128)(2,1)S(1)}, bf16[528,128]{1,0:T(8,128)(2,1)S(1)}, u32[]{:S(2)}, u32[]{:S(2)}) collective-permute-start(bf16[528,128]{1,0:T(8,128)(2,1)S(1)} %get-tuple-element.57), channel_id=1, source_target_pairs={{0,1},{1,2},{2,3},{3,4},{4,5},{5,6},{6,7},{8,9},{9,10},{10,11},{11... | collective-permute-start | bytes 405512 | tf_op jit(solution)/shard_map/halo_y/ppermute | solution.py:574
  38.9 1.3 collective-permute-start.5
  40.2 0.0 all-to-all-done
  40.3 0.0 copy-start.4
  40.3 0.0 copy-start.5
  40.3 2.1 %collective-permute-start.3 = (f32[16,16,128]{2,1,0:T(8,128)S(1)}, f32[16,16,128]{2,1,0:T(8,128)S(1)}, u32[]{:S(2)}, u32[]{:S(2)}) collective-permute-start(f32[16,16,128]{2,1,0:T(8,128)S(1)} %raw.1.refs_8_), channel_id=1, source_target_pairs={{0,64},{64,0},{128,192},{192,128},{256,320},{320,256},{384,448},{4... | collective-permute-start | bytes 393224 | tf_op jit(solution)/shard_map/raw/ppermute | solution.py:702
  42.4 0.0 copy-done.4
  42.4 0.0 copy-done.5
  42.4 3.4 %inner_1.1 = (f32[32,16,128]{2,1,0:T(8,128)S(1)}, f32[32,16,128]{2,1,0:T(8,128)S(1)}, f32[32,16,128]{2,1,0:T(8,128)S(1)}, f32[32,16,128]{2,1,0:T(8,128)S(1)}) custom-call(f32[32,16,128]{2,1,0:T(8,128)S(1)} %bitcast.16, f32[32,16,128]{2,1,0:T(8,128)S(1)} %bitcast.20, f32[32,16,128]{2,1,0:T(8,128)S(1)} %bitcast.25, f32[32,16,128]{2,1,0:T(8,128)S(1)} %bitcast.26, ...), custom_call_target="tpu_custom_call" | custom-call | flops 3932160 | bytes 2299920 | tf_op jit(solution)/shard_map/inner_1/inner_1/pallas_call | solution.py:26
  45.8 0.0 collective-permute-done.3.refs_9_
  45.8 4.7 %collective-permute-done.4.low_ref.refs_4_.y_low_ref = bf16[528,128]{1,0:T(8,128)(2,1)S(1)} collective-permute-done((bf16[528,128]{1,0:T(8,128)(2,1)S(1)}, bf16[528,128]{1,0:T(8,128)(2,1)S(1)}, u32[]{:S(2)}, u32[]{:S(2)}) %collective-permute-start.4) | collective-permute-done | bytes 135200 | tf_op jit(solution)/shard_map/halo_y/ppermute | solution.py:574
  50.5 16.0 %collective-permute-done.5.high_ref.refs_5_.y_high_ref = bf16[528,128]{1,0:T(8,128)(2,1)S(1)} collective-permute-done((bf16[528,128]{1,0:T(8,128)(2,1)S(1)}, bf16[528,128]{1,0:T(8,128)(2,1)S(1)}, u32[]{:S(2)}, u32[]{:S(2)}) %collective-permute-start.5) | collective-permute-done | bytes 135200 | tf_op jit(solution)/shard_map/halo_y/ppermute | solution.py:575
  66.5 0.7 conv_edge.1
  67.2 11.9 %all_to_all.26.refs_10_ = f32[8,64,128]{2,1,0:T(8,128)S(1)} all-to-all(f32[8,64,128]{2,1,0:T(8,128)S(1)} %conv_edge.1), channel_id=1, replica_groups=mesh['shot'=8,'gx'=8,'gy'=8] {'shot'}, dimensions={0} | all-to-all | bytes 524288 | tf_op jit(solution)/shard_map/rims/all_to_all | solution.py:715
  79.1 1.2 step_1.1
  80.3 9.7 %collective-permute-start.6 = (bf16[384,128]{1,0:T(8,128)(2,1)S(1)}, bf16[384,128]{1,0:T(8,128)(2,1)S(1)}, u32[]{:S(2)}, u32[]{:S(2)}) collective-permute-start(bf16[384,128]{1,0:T(8,128)(2,1)S(1)} %get-tuple-element.71), channel_id=1, source_target_pairs={{0,1},{1,2},{2,3},{3,4},{4,5},{5,6},{6,7},{8,9},{9,10},{10,11},{11... | collective-permute-start | bytes 294920 | tf_op jit(solution)/shard_map/halo_2/ppermute | solution.py:574
  90.0 1.3 collective-permute-start.7
  91.3 1.9 %collective-permute-start.8 = (f32[8,16,128]{2,1,0:T(8,128)S(1)}, f32[8,16,128]{2,1,0:T(8,128)S(1)}, u32[]{:S(2)}, u32[]{:S(2)}) collective-permute-start(f32[8,16,128]{2,1,0:T(8,128)S(1)} %get-tuple-element.74), channel_id=1, source_target_pairs={{0,8},{8,16},{16,24},{24,32},{32,40},{40,48},{48,56},{1,9},{9,17},... | collective-permute-start | bytes 196616 | tf_op jit(solution)/shard_map/halo_2/ppermute | solution.py:574
  93.2 3.9 %collective-permute-start.9 = (f32[8,16,128]{2,1,0:T(8,128)S(1)}, f32[8,16,128]{2,1,0:T(8,128)S(1)}, u32[]{:S(2)}, u32[]{:S(2)}) collective-permute-start(f32[8,16,128]{2,1,0:T(8,128)S(1)} %get-tuple-element.75), channel_id=1, source_target_pairs={{8,0},{16,8},{24,16},{32,24},{40,32},{48,40},{56,48},{9,1},{17,9},... | collective-permute-start | bytes 196616 | tf_op jit(solution)/shard_map/halo_2/ppermute | solution.py:575
  97.2 3.6 %inner_2.1 = (f32[32,16,128]{2,1,0:T(8,128)S(1)}, f32[32,16,128]{2,1,0:T(8,128)S(1)}, f32[32,16,128]{2,1,0:T(8,128)S(1)}, f32[32,16,128]{2,1,0:T(8,128)S(1)}, f32[1,512]{1,0:T(1,128)S(1)}) custom-call(f32[32,16,128]{2,1,0:T(8,128)S(1)} %get-tuple-element.63.refs_0_, f32[32,16,128]{2,1,0:T(8,128)S(1)} %get-tuple-element.64.refs_1_.refs_12_, ...), custom_call_target="tpu_custom_call" | custom-call | flops 3932160 | bytes 2105360 | tf_op jit(solution)/shard_map/inner_2/inner_2/pallas_call | solution.py:26
  100.8 0.0 collective-permute-done.8.refs_9_
  100.8 0.0 collective-permute-done.9.refs_10_
  100.8 0.0 collective-permute-done.6.refs_4_
  100.8 6.3 %collective-permute-done.7.refs_5_ = bf16[384,128]{1,0:T(8,128)(2,1)S(1)} collective-permute-done((bf16[384,128]{1,0:T(8,128)(2,1)S(1)}, bf16[384,128]{1,0:T(8,128)(2,1)S(1)}, u32[]{:S(2)}, u32[]{:S(2)}) %collective-permute-start.7) | collective-permute-done | bytes 98336 | tf_op jit(solution)/shard_map/halo_2/ppermute | solution.py:575
  107.1 1.9 %step_2.1 = (f32[32,16,128]{2,1,0:T(8,128)}, f32[32,16,128]{2,1,0:T(8,128)}, f32[8,8,16,128]{3,2,1,0:T(8,128)}) custom-call(f32[32,16,128]{2,1,0:T(8,128)S(1)} %get-tuple-element.67.refs_0_, f32[32,16,128]{2,1,0:T(8,128)S(1)} %get-tuple-element.68.refs_1_, f32[32,16,128]{2,1,0:T(8,128)S(1)} %get-tuple-element.69.refs_2_, ...), custom_call_target="tpu_custom_call" | custom-call | flops 1000000 | bytes 3211288 | tf_op jit(solution)/shard_map/step_2/step_2/pallas_call | solution.py:26
  109.1 3.5 %all-to-all-start.2 = ((f32[64,16,128]{2,1,0:T(8,128)}), f32[64,16,128]{2,1,0:T(8,128)S(1)}, u32[]{:S(2)}, u32[]{:S(2)}) async-start(f32[64,16,128]{2,1,0:T(8,128)} %bitcast.11), calls=%async_computation.2 | async-start | bytes 1048576 | tf_op jit(solution)/shard_map/update/all_to_all | solution.py:784
  113.2 9.6 %all-to-all-done.2 = f32[64,16,128]{2,1,0:T(8,128)S(1)} async-done(((f32[64,16,128]{2,1,0:T(8,128)}), f32[64,16,128]{2,1,0:T(8,128)S(1)}, u32[]{:S(2)}, u32[]{:S(2)}) %all-to-all-start.2) | async-done | bytes 524320 | tf_op jit(solution)/shard_map/update/all_to_all | solution.py:784
  122.9 0.7 update.1
  123.6 0.0 copy-start.3
  123.6 3.5 %all-to-all-start.3 = ((f32[32,16,128]{2,1,0:T(8,128)}), f32[32,16,128]{2,1,0:T(8,128)S(1)}, u32[]{:S(2)}, u32[]{:S(2)}) async-start(f32[32,16,128]{2,1,0:T(8,128)} %bitcast.13), calls=%async_computation.3 | async-start | bytes 524288 | tf_op jit(solution)/shard_map/update/all_to_all | solution.py:794
  127.1 0.0 copy-done.3
  127.2 1.0 trace_2.1.second_ref
  128.1 6.5 %all-to-all-done.3.update_ref.value_ref = f32[32,16,128]{2,1,0:T(8,128)S(1)} async-done(((f32[32,16,128]{2,1,0:T(8,128)}), f32[32,16,128]{2,1,0:T(8,128)S(1)}, u32[]{:S(2)}, u32[]{:S(2)}) %all-to-all-start.3) | async-done | bytes 262176 | tf_op jit(solution)/shard_map/update/all_to_all | solution.py:794
  134.6 3.2 %gradient.1 = f32[64,1,1152]{2,1,0:T(1,128)} custom-call(f32[32,16,128]{2,1,0:T(8,128)S(1)} %all-to-all-done.3.update_ref.value_ref, f32[32,16,128]{2,1,0:T(8,128)S(1)} %get-tuple-element.73.refs_8_.squashed_ref, bf16[4,32,16,128]{3,2,1,0:T(8,128)(2,1)S(1)} %copy-done, f32[12,16,128]{2,1,0:T(8,128)S(1)} %collective-permute-done.low_ref.refs_7_.x_low_ref, ...), custom_call_target="tpu_custom_call" | custom-call | flops 14155776 | bytes 1814528 | tf_op jit(solution)/shard_map/gradient/gradient/pallas_call | solution.py:26
  137.8 10.7 %all-to-all-start.4 = ((f32[64,1,1152]{2,1,0:T(1,128)}), f32[64,1,1152]{2,1,0:T(1,128)S(1)}, u32[]{:S(2)}, u32[]{:S(2)}) async-start(f32[64,1,1152]{2,1,0:T(1,128)} %gradient.1), calls=%async_computation.4 | async-start | bytes 589824 | tf_op jit(solution)/shard_map/gradient/all_to_all | solution.py:811
  148.5 0.7 keep.1
  149.2 22.8 %all-to-all-done.4.shares_ref = f32[64,1,1152]{2,1,0:T(1,128)S(1)} async-done(((f32[64,1,1152]{2,1,0:T(1,128)}), f32[64,1,1152]{2,1,0:T(1,128)S(1)}, u32[]{:S(2)}, u32[]{:S(2)}) %all-to-all-start.4) | async-done | bytes 294944 | tf_op jit(solution)/shard_map/gradient/all_to_all | solution.py:811
  172.0 0.7 total.1
  (1 shorter events, 0.0 us)
Async XLA Ops:
  0.6 12.9 %copy-start = (bf16[4,32,16,128]{3,2,1,0:T(8,128)(2,1)S(1)}, bf16[4,32,16,128]{3,2,1,0:T(8,128)(2,1)}, u32[]{:S(2)}) copy-start(bf16[4,32,16,128]{3,2,1,0:T(8,128)(2,1)} %feat_ref.7) | copy-start | bytes 1572868
  2.4 9.6 %collective-permute-start = (f32[12,16,128]{2,1,0:T(8,128)}, f32[12,16,128]{2,1,0:T(8,128)S(1)}, u32[]{:S(2)}, u32[]{:S(2)}) collective-permute-start(f32[12,16,128]{2,1,0:T(8,128)} %get-tuple-element.45), channel_id=1, source_target_pairs={{0,8},{8,16},{16,24},{24,32},{32,40},{40,48},{48,56},{1,9},{9,17},... | collective-permute-start | bytes 294920 | tf_op jit(solution)/shard_map/halo_x/ppermute | solution.py:574
  6.2 7.4 %collective-permute-start.1 = (f32[12,16,128]{2,1,0:T(8,128)}, f32[12,16,128]{2,1,0:T(8,128)S(1)}, u32[]{:S(2)}, u32[]{:S(2)}) collective-permute-start(f32[12,16,128]{2,1,0:T(8,128)} %get-tuple-element.46), channel_id=1, source_target_pairs={{8,0},{16,8},{24,16},{32,24},{40,32},{48,40},{56,48},{9,1},{17,9},... | collective-permute-start | bytes 294920 | tf_op jit(solution)/shard_map/halo_x/ppermute | solution.py:575
  11.7 1.9 %copy-start.9 = (f32[1,2]{1,0:T(1,128)S(1)}, f32[1,2]{1,0:T(1,128)}, u32[]{:S(2)}) copy-start(f32[1,2]{1,0:T(1,128)} %refs_2_.1) | copy-start | bytes 28
  11.7 1.8 %copy-start.6 = (f32[1,2,512]{2,1,0:T(2,128)S(1)}, f32[1,2,512]{2,1,0:T(2,128)}, u32[]{:S(2)}) copy-start(f32[1,2,512]{2,1,0:T(2,128)} %refs_6_.1) | copy-start | bytes 12292
  11.8 1.8 %copy-start.7 = (s32[1,512]{1,0:T(1,128)S(1)}, s32[1,512]{1,0:T(1,128)}, u32[]{:S(2)}) copy-start(s32[1,512]{1,0:T(1,128)} %refs_5_.1) | copy-start | bytes 6148
  11.8 1.8 %copy-start.8 = (f32[4,27]{1,0:T(4,128)S(1)}, f32[4,27]{1,0:T(4,128)}, u32[]{:S(2)}) copy-start(f32[4,27]{1,0:T(4,128)} %weight_ref.2) | copy-start | bytes 1300
  16.8 3.2 %collective-permute-start.2 = (f32[16,16,128]{2,1,0:T(8,128)S(1)}, f32[16,16,128]{2,1,0:T(8,128)S(1)}, u32[]{:S(2)}, u32[]{:S(2)}) collective-permute-start(f32[16,16,128]{2,1,0:T(8,128)S(1)} %get-tuple-element.48), channel_id=1, source_target_pairs={{0,64},{64,0},{128,192},{192,128},{256,320},{320,256},{384,448},{4... | collective-permute-start | bytes 393224 | tf_op jit(solution)/shard_map/raw/ppermute | solution.py:681
  20.9 3.8 %copy-start.1 = (f32[1,32,16,128]{3,2,1,0:T(8,128)S(1)}, f32[1,32,16,128]{3,2,1,0:T(8,128)}, u32[]{:S(2)}) copy-start(f32[1,32,16,128]{3,2,1,0:T(8,128)} %param.14) | copy-start | bytes 786436
  20.9 3.8 %copy-start.2 = (f32[1,32,16,128]{3,2,1,0:T(8,128)S(1)}, f32[1,32,16,128]{3,2,1,0:T(8,128)}, u32[]{:S(2)}) copy-start(f32[1,32,16,128]{3,2,1,0:T(8,128)} %param.16) | copy-start | bytes 786436
  20.9 19.4 %all-to-all-start = ((f32[64,16,128]{2,1,0:T(8,128)}), f32[64,16,128]{2,1,0:T(8,128)S(1)}, u32[]{:S(2)}, u32[]{:S(2)}) async-start(f32[64,16,128]{2,1,0:T(8,128)} %bitcast.5), calls=%async_computation | async-start | bytes 1048576 | tf_op jit(solution)/shard_map/raw/all_to_all | solution.py:687
  25.0 25.5 %collective-permute-start.4 = (bf16[528,128]{1,0:T(8,128)(2,1)S(1)}, bf16[528,128]{1,0:T(8,128)(2,1)S(1)}, u32[]{:S(2)}, u32[]{:S(2)}) collective-permute-start(bf16[528,128]{1,0:T(8,128)(2,1)S(1)} %get-tuple-element.57), channel_id=1, source_target_pairs={{0,1},{1,2},{2,3},{3,4},{4,5},{5,6},{6,7},{8,9},{9,10},{10,11},{11... | collective-permute-start | bytes 405512 | tf_op jit(solution)/shard_map/halo_y/ppermute | solution.py:574
  38.9 27.6 %collective-permute-start.5 = (bf16[528,128]{1,0:T(8,128)(2,1)S(1)}, bf16[528,128]{1,0:T(8,128)(2,1)S(1)}, u32[]{:S(2)}, u32[]{:S(2)}) collective-permute-start(bf16[528,128]{1,0:T(8,128)(2,1)S(1)} %get-tuple-element.58), channel_id=1, source_target_pairs={{1,0},{2,1},{3,2},{4,3},{5,4},{6,5},{7,6},{9,8},{10,9},{11,10},{12... | collective-permute-start | bytes 405512 | tf_op jit(solution)/shard_map/halo_y/ppermute | solution.py:575
  40.3 2.1 %copy-start.4 = (f32[1,32,16,128]{3,2,1,0:T(8,128)S(1)}, f32[1,32,16,128]{3,2,1,0:T(8,128)}, u32[]{:S(2)}) copy-start(f32[1,32,16,128]{3,2,1,0:T(8,128)} %param.13) | copy-start | bytes 786436
  40.3 2.1 %copy-start.5 = (f32[1,32,16,128]{3,2,1,0:T(8,128)S(1)}, f32[1,32,16,128]{3,2,1,0:T(8,128)}, u32[]{:S(2)}) copy-start(f32[1,32,16,128]{3,2,1,0:T(8,128)} %param.15) | copy-start | bytes 786436
  40.3 5.5 %collective-permute-start.3 = (f32[16,16,128]{2,1,0:T(8,128)S(1)}, f32[16,16,128]{2,1,0:T(8,128)S(1)}, u32[]{:S(2)}, u32[]{:S(2)}) collective-permute-start(f32[16,16,128]{2,1,0:T(8,128)S(1)} %raw.1.refs_8_), channel_id=1, source_target_pairs={{0,64},{64,0},{128,192},{192,128},{256,320},{320,256},{384,448},{4... | collective-permute-start | bytes 393224 | tf_op jit(solution)/shard_map/raw/ppermute | solution.py:702
  80.3 20.5 %collective-permute-start.6 = (bf16[384,128]{1,0:T(8,128)(2,1)S(1)}, bf16[384,128]{1,0:T(8,128)(2,1)S(1)}, u32[]{:S(2)}, u32[]{:S(2)}) collective-permute-start(bf16[384,128]{1,0:T(8,128)(2,1)S(1)} %get-tuple-element.71), channel_id=1, source_target_pairs={{0,1},{1,2},{2,3},{3,4},{4,5},{5,6},{6,7},{8,9},{9,10},{10,11},{11... | collective-permute-start | bytes 294920 | tf_op jit(solution)/shard_map/halo_2/ppermute | solution.py:574
  90.0 17.1 %collective-permute-start.7 = (bf16[384,128]{1,0:T(8,128)(2,1)S(1)}, bf16[384,128]{1,0:T(8,128)(2,1)S(1)}, u32[]{:S(2)}, u32[]{:S(2)}) collective-permute-start(bf16[384,128]{1,0:T(8,128)(2,1)S(1)} %get-tuple-element.72), channel_id=1, source_target_pairs={{1,0},{2,1},{3,2},{4,3},{5,4},{6,5},{7,6},{9,8},{10,9},{11,10},{12... | collective-permute-start | bytes 294920 | tf_op jit(solution)/shard_map/halo_2/ppermute | solution.py:575
  91.3 9.5 %collective-permute-start.8 = (f32[8,16,128]{2,1,0:T(8,128)S(1)}, f32[8,16,128]{2,1,0:T(8,128)S(1)}, u32[]{:S(2)}, u32[]{:S(2)}) collective-permute-start(f32[8,16,128]{2,1,0:T(8,128)S(1)} %get-tuple-element.74), channel_id=1, source_target_pairs={{0,8},{8,16},{16,24},{24,32},{32,40},{40,48},{48,56},{1,9},{9,17},... | collective-permute-start | bytes 196616 | tf_op jit(solution)/shard_map/halo_2/ppermute | solution.py:574
  93.2 7.6 %collective-permute-start.9 = (f32[8,16,128]{2,1,0:T(8,128)S(1)}, f32[8,16,128]{2,1,0:T(8,128)S(1)}, u32[]{:S(2)}, u32[]{:S(2)}) collective-permute-start(f32[8,16,128]{2,1,0:T(8,128)S(1)} %get-tuple-element.75), channel_id=1, source_target_pairs={{8,0},{16,8},{24,16},{32,24},{40,32},{48,40},{56,48},{9,1},{17,9},... | collective-permute-start | bytes 196616 | tf_op jit(solution)/shard_map/halo_2/ppermute | solution.py:575
  109.1 13.8 %all-to-all-start.2 = ((f32[64,16,128]{2,1,0:T(8,128)}), f32[64,16,128]{2,1,0:T(8,128)S(1)}, u32[]{:S(2)}, u32[]{:S(2)}) async-start(f32[64,16,128]{2,1,0:T(8,128)} %bitcast.11), calls=%async_computation.2 | async-start | bytes 1048576 | tf_op jit(solution)/shard_map/update/all_to_all | solution.py:784
  123.6 3.6 %copy-start.3 = (f32[32,16,128]{2,1,0:T(8,128)S(1)}, f32[32,16,128]{2,1,0:T(8,128)}, u32[]{:S(2)}) copy-start(f32[32,16,128]{2,1,0:T(8,128)} %get-tuple-element.77.fwd_ref) | copy-start | bytes 786436
  123.6 11.0 %all-to-all-start.3 = ((f32[32,16,128]{2,1,0:T(8,128)}), f32[32,16,128]{2,1,0:T(8,128)S(1)}, u32[]{:S(2)}, u32[]{:S(2)}) async-start(f32[32,16,128]{2,1,0:T(8,128)} %bitcast.13), calls=%async_computation.3 | async-start | bytes 524288 | tf_op jit(solution)/shard_map/update/all_to_all | solution.py:794
  137.8 34.2 %all-to-all-start.4 = ((f32[64,1,1152]{2,1,0:T(1,128)}), f32[64,1,1152]{2,1,0:T(1,128)S(1)}, u32[]{:S(2)}, u32[]{:S(2)}) async-start(f32[64,1,1152]{2,1,0:T(1,128)} %gradient.1), calls=%async_computation.4 | async-start | bytes 589824 | tf_op jit(solution)/shard_map/gradient/all_to_all | solution.py:811

commit v6 on v5

--- a/solution.py
+++ b/solution.py
@@ -89,44 +89,62 @@
 
 
 def wave_rows(size_x):
-    return size_x * 12
+    return size_x * 10
+
+
+def row_mix(value, weights, upward):
+    count = value.shape[0]
+    place = lax.broadcasted_iota(jnp.int32, value.shape, 0) & 3
+    distance = 3 - place if upward else place
+    total = value
+    for j, row in enumerate(weights, 1):
+        factor = jnp.zeros(value.shape, F32)
+        for n, weight in enumerate(row):
+            if weight:
+                factor = jnp.where(distance == n, float(weight), factor)
+        total = total + factor * pltpu.roll(value, count - j if upward else j, 0)
+    return total
 
 
 def pack_waves(fwd_ref, back_ref, upward, out_ref, first, edge_ref, low_ref):
     size_x, size_y, depth = fwd_ref.shape
-    start, near = (size_y - 4, 2) if upward else (0, 0)
+    start, near = (size_y - 4, 3) if upward else (0, 0)
     edge_ref[:, 0:4] = fwd_ref[:, start : start + 4]
     edge_ref[:, 4:8] = back_ref[:, start : start + 4]
     value = edge_ref[...].reshape(size_x * 8, depth)
+    value = row_mix(value, ((0, -1, -2, -2), (0, 0, 1, 1)), upward)
     high = value.astype(BF16)
     out_ref[first : first + size_x * 8] = high
     edge_ref[...] = (value - high.astype(F32)).reshape(size_x, 8, depth)
-    quarter = size_x // 4
-    for q in range(4):
-        part = slice(q * quarter, (q + 1) * quarter)
-        low_ref[:, 4 * q : 4 * q + 2] = edge_ref[part, near : near + 2]
-        low_ref[:, 4 * q + 2 : 4 * q + 4] = edge_ref[part, 4 + near : 6 + near]
-    out_ref[first + size_x * 8 : first + size_x * 12] = (
-        low_ref[...].reshape(size_x * 4, depth).astype(BF16)
+    eighth = size_x // 8
+    for q in range(8):
+        part = slice(q * eighth, (q + 1) * eighth)
+        low_ref[:, 2 * q : 2 * q + 1] = edge_ref[part, near : near + 1]
+        low_ref[:, 2 * q + 1 : 2 * q + 2] = edge_ref[part, 4 + near : 5 + near]
+    out_ref[first + size_x * 8 : first + size_x * 10] = (
+        low_ref[...].reshape(size_x * 2, depth).astype(BF16)
     )
 
 
 def unpack_waves(buffer_ref, upward, first, size_x, edge_ref, low_ref):
     depth = buffer_ref.shape[1]
-    near = 2 if upward else 0
-    quarter = size_x // 4
+    near = 3 if upward else 0
+    eighth = size_x // 8
     edge_ref[...] = (
         buffer_ref[first : first + size_x * 8].astype(F32).reshape(size_x, 8, depth)
     )
     low_ref[...] = (
-        buffer_ref[first + size_x * 8 : first + size_x * 12]
+        buffer_ref[first + size_x * 8 : first + size_x * 10]
         .astype(F32)
-        .reshape(quarter, 16, depth)
-    )
-    for q in range(4):
-        part = slice(q * quarter, (q + 1) * quarter)
-        edge_ref[part, near : near + 2] += low_ref[:, 4 * q : 4 * q + 2]
-        edge_ref[part, 4 + near : 6 + near] += low_ref[:, 4 * q + 2 : 4 * q + 4]
+        .reshape(eighth, 16, depth)
+    )
+    for q in range(8):
+        part = slice(q * eighth, (q + 1) * eighth)
+        edge_ref[part, near : near + 1] += low_ref[:, 2 * q : 2 * q + 1]
+        edge_ref[part, 4 + near : 5 + near] += low_ref[:, 2 * q + 1 : 2 * q + 2]
+    value = edge_ref[...].reshape(size_x * 8, depth)
+    value = row_mix(value, ((0, 1, 2, 2), (0, 0, 1, 3), (0, 0, 0, 1)), upward)
+    edge_ref[...] = value.reshape(size_x, 8, depth)
 
 
 def pack_y_body(
@@ -156,12 +174,8 @@
         ext_ref[c, 1 + size_x] = high_ref[8 + c]
 
 
-def conv_body(feat_ref, low_ref, high_ref, weight_ref, place_ref, *refs):
-    small_in, (keep_ref, give_ref, *small_out), (ext_ref, total_ref) = (
-        refs[:3],
-        refs[3:8],
-        refs[8:],
-    )
+def conv_body(feat_ref, low_ref, high_ref, weight_ref, *refs):
+    small_in, (total_ref, *small_out), ext_ref = refs[:3], refs[3:7], refs[7]
     for source, target in zip(small_in, small_out):
         target[...] = source[...]
     channels, size_x = feat_ref.shape[:2]
@@ -196,10 +210,6 @@
         return carry
 
     lax.fori_loop(0, size_x // together, some_rows, 0)
-    half = size_x // 2
-    core = place_ref[3]
-    keep_ref[...] = total_ref[pl.ds(core * half, half)]
-    give_ref[...] = total_ref[pl.ds((1 - core) * half, half)]
 
 
 def load_plane(plane_ref, buffer_ref, c, size_x, channels):
@@ -209,35 +219,30 @@
     plane_ref[8 + size_x : 9 + size_x] = tail[2 * c + 1 : 2 * c + 2]
 
 
-def conv_edge_body(low_ref, high_ref, weight_ref, out_ref, plane_ref):
-    copies, both_x, depth = out_ref.shape
-    size_x = both_x // 2
+def conv_edge_body(parts_ref, low_ref, high_ref, weight_ref, out_ref, plane_ref):
+    copies, rows, size_y, depth = parts_ref.shape
+    size_x = copies * rows
     channels = weight_ref.shape[0]
+    total = parts_ref[0]
+    for n in range(1, copies):
+        total = total + parts_ref[n]
+    first = rows * size_y
+    total = total.reshape(first, depth)
+    for n in range(copies):
+        out_ref[n, 0:first] = total
     for side, (buffer_ref, dy) in enumerate(((low_ref, 0), (high_ref, 2))):
         terms = [None] * 3
         for c in range(channels):
             load_plane(plane_ref, buffer_ref, c, size_x, channels)
             for dx in range(3):
-                rows = plane_ref[7 + dx : 7 + dx + size_x]
+                plane = plane_ref[7 + dx : 7 + dx + size_x]
                 for dz in range(3):
-                    part = weight_ref[c, 9 * dx + 3 * dy + dz] * rows
+                    part = weight_ref[c, 9 * dx + 3 * dy + dz] * plane
                     terms[dz] = part if terms[dz] is None else terms[dz] + part
         total = terms[1] + shifted_lanes(terms[0], -1) + shifted_lanes(terms[2], 1)
+        at = first + side * size_x
         for n in range(copies):
-            out_ref[n, side * size_x : (side + 1) * size_x] = total
-
-
-def pair_body(keep_ref, got_ref, out_ref):
-    total = keep_ref[...] + got_ref[...]
-    for n in range(out_ref.shape[0]):
-        out_ref[n] = total
-
-
-def sum_body(parts_ref, out_ref):
-    total = parts_ref[0]
-    for n in range(1, parts_ref.shape[0]):
-        total = total + parts_ref[n]
-    out_ref[...] = total
+            out_ref[n, at : at + size_x] = total
 
 
 def update_body(parts_ref, damping_ref, out_ref):
@@ -352,18 +357,21 @@
     y_low_ref, y_high_ref, place_ref, wavelet_ref = refs[4:8]
     refs = refs[8:]
     if moment == 0:
-        own_ref, other_ref, rims_ref = refs[:3]
-        (fwd_new_ref, back_new_ref, lap_ref, squashed_ref) = refs[3:7]
-        (x_up_ref, x_down_ref, y_up_ref, y_down_ref) = refs[7:11]
-        refs = refs[11:]
-        half = own_ref.shape[0]
-        core = place_ref[3]
-        squashed_ref[pl.ds(core * half, half)] = own_ref[...]
-        squashed_ref[pl.ds((1 - core) * half, half)] = other_ref[...]
+        raw_ref = refs[0]
+        (fwd_new_ref, back_new_ref, lap_ref, squashed_ref) = refs[1:5]
+        (x_up_ref, x_down_ref, y_up_ref, y_down_ref) = refs[5:9]
+        refs = refs[9:]
         size_x, size_y, depth = squashed_ref.shape
-        rims = rims_ref[0]
-        for n in range(1, rims_ref.shape[0]):
-            rims = rims + rims_ref[n]
+        shots = raw_ref.shape[0]
+        rows = size_x // shots
+        first = rows * size_y
+        rims = None
+        for n in range(shots):
+            squashed_ref[n * rows : (n + 1) * rows] = raw_ref[n, 0:first].reshape(
+                rows, size_y, depth
+            )
+            part = raw_ref[n, first:]
+            rims = part if rims is None else rims + part
         squashed_ref[:, 0:1, :] += rims[:size_x].reshape(size_x, 1, depth)
         squashed_ref[:, size_y - 1 : size_y, :] += rims[size_x:].reshape(size_x, 1, depth)
     else:
@@ -604,7 +612,6 @@
             lax.axis_index("gx") * size_x,
             lax.axis_index("gy") * size_y,
             sources[0],
-            lax.axis_index("shot") % 2,
         ]
     ).astype(jnp.int32)
 
@@ -626,7 +633,7 @@
         x_low, x_high = neighbours(x_up, x_down, "gx")
     packing = [
         pltpu.VMEM((size_x, 8, depth), F32),
-        pltpu.VMEM((size_x // 4, 16, depth), F32),
+        pltpu.VMEM((size_x // 8, 16, depth), F32),
     ]
     y_shape = shape(channels * size_x + 16 + wave_rows(size_x), depth, dtype=BF16)
     with jax.named_scope("pack_y"):
@@ -659,62 +666,31 @@
             flops=work,
             name="inner_1",
         )
-    half = size_x // 2
-    chips = shots // 2
-    half_shape = shape(half, size_y, depth)
-    partner = [(i, i ^ 1) for i in range(shots)]
     with jax.named_scope("conv"):
         small = (receivers, residual, wavelet)
-        keep, give, receivers, residual, wavelet = call(
+        main, receivers, residual, wavelet = call(
             conv_body,
-            [half_shape] * 2 + [shape(*a.shape, dtype=a.dtype) for a in small],
-            (features, x_low, x_high, conv_weight, place) + small,
-            [VM, VM, VM, SM, SM] + [VM] * 3,
-            scratch=[ext, pltpu.VMEM(grid, F32)],
+            [full] + [shape(*a.shape, dtype=a.dtype) for a in small],
+            (features, x_low, x_high, conv_weight) + small,
+            [VM, VM, VM, SM] + [VM] * 3,
+            scratch=[ext],
             flops=54 * channels * size_x * size_y * depth,
             name="conv",
         )
     with jax.named_scope("raw"):
-        pair = call(
-            pair_body,
-            [shape(chips, half, size_y, depth)],
-            (keep, lax.ppermute(give, "shot", partner)),
-            [VM, VM],
-            name="pair",
-        )
-        if chips > 1:
-            groups = [list(range(core, shots, 2)) for core in range(2)]
-            pair = lax.all_to_all(
-                pair.reshape(chips * half, size_y, depth),
-                "shot",
-                0,
-                0,
-                tiled=True,
-                axis_index_groups=groups,
-            )
-        own = call(
-            sum_body,
-            [half_shape],
-            (pair.reshape(chips, half, size_y, depth),),
-            [VM],
-            name="raw",
-        )
-        other = lax.ppermute(own, "shot", partner)
-    with jax.named_scope("rims"):
-        weights, own, other, *inner_1 = lax.optimization_barrier(
-            (conv_weight, own, other, *inner_1)
-        )
-        rims = call(
+        parts = lax.all_to_all(main, "shot", 0, 0, tiled=True)
+        parts, *inner_1 = lax.optimization_barrier((parts, *inner_1))
+        each = rows * size_y + 2 * size_x
+        raw = call(
             conv_edge_body,
-            [shape(shots, 2 * size_x, depth)],
-            (y_low, y_high, weights),
-            [VM, VM, SM],
+            [shape(shots, each, depth)],
+            (parts.reshape(shots, rows, size_y, depth), y_low, y_high, conv_weight),
+            [VM] * 3 + [SM],
             scratch=[pltpu.VMEM((size_x + 16, depth), F32)],
             name="conv_edge",
         )
-        rims = lax.all_to_all(
-            rims.reshape(shots * 2 * size_x, depth), "shot", 0, 0, tiled=True
-        ).reshape(shots, 2 * size_x, depth)
+        raw = lax.all_to_all(raw.reshape(shots * each, depth), "shot", 0, 0, tiled=True)
+        raw = raw.reshape(shots, each, depth)
 
     with jax.named_scope("step_1"):
         fwd_1, back_1, lap_1, squashed, x_up, x_down, y_up, y_down = call(
@@ -728,11 +704,9 @@
                 y_high,
                 place,
                 wavelet,
-                own,
-                other,
-                rims,
+                raw,
             ),
-            [VM] * 6 + [SM] * 2 + [VM] * 3,
+            [VM] * 6 + [SM] * 2 + [VM],
             scratch=step_scratch,
             name="step_1",
         )

time: 174 us -> 172 us (0.989)
  starting transfers between devices: 66.2 us -> 62.6 us
  blocking collectives: 11.9 us -> 14.6 us
    ppermute x2 -> x0, starting transfers between devices: 3.97 us -> none  [the longest x1 2.05 us: per_device(): other = lax.ppermute(own, 'shot', partner)]
    all_to_all x1, blocking collectives: 11.9 us -> 14.6 us  [per_device(): lax.all_to_all(raw.reshape(shots * each, depth), 'shot', 0, 0, tiled=True)]
    ppermute x4, waiting for transfers between devices: 23.9 us -> 21.9 us  [neighbours(): high = lax.ppermute(down, axis, [(i + 1, i) for i in range(count - 1)])]
    pallas_call x15 -> x13, Pallas kernels: 23.3 us -> 24.6 us  [call(): pl.pallas_call(body, out_shape=outs[0] if single else tuple(outs), in_spe...]
  transfers between devices with their start and end apart: 14 -> 12, of which waited for: 9 -> 8; matrix products, arithmetic and copies ran while one was open for 0% -> 0% of each run, Pallas kernels for 5% -> 6%
where the time goes in v6:
time: 172 us; the launch traced here: 171 us
  waiting for transfers between devices  67.3 us (39%)
  starting transfers between devices  62.6 us (36%)
  Pallas kernels  24.6 us (14%)
  blocking collectives  14.6 us (8%)
  between operations  2.19 us (1%)
    ppermute x4, starting transfers between devices, neighbours(): low = lax.ppermute(up, axis, [(i, i + 1) for i in range(count - 1)])  29.2 us
    pallas_call x13, Pallas kernels, call(): pl.pallas_call(body, out_shape=outs[0] if single else tuple(outs), in_spe...  24.6 us
    all_to_all x1, waiting for transfers between devices, per_device(): shares = lax.all_to_all(share, ('gx', 'gy'), 0, 0, tiled=True)  22.8 us
    ppermute x4, waiting for transfers between devices, neighbours(): high = lax.ppermute(down, axis, [(i + 1, i) for i in range(count - 1)])  21.9 us
    all_to_all x1, blocking collectives, per_device(): lax.all_to_all(raw.reshape(shots * each, depth), 'shot', 0, 0, tiled=True)  14.6 us
    ppermute x4, starting transfers between devices, neighbours(): high = lax.ppermute(down, axis, [(i + 1, i) for i in range(count - 1)])  11.4 us
    all_to_all x1, starting transfers between devices, per_device(): shares = lax.all_to_all(share, ('gx', 'gy'), 0, 0, tiled=True)  11.1 us
    all_to_all x1, waiting for transfers between devices, per_device(): lax.all_to_all(sums.reshape(shots * 2 * rows, size_y, depth), 'shot', 0,...  9.62 us
  transfers between devices with their start and end apart: 12, of which 8 were waited for; matrix products, arithmetic and copies ran while one was open for 0% of the time, Pallas kernels for 6%

profile of v6, /device:TPU:32, one launch (start us, length us, event | category | flops | bytes accessed | tf_op | source)
XLA Modules:
  0.0 171.4 jit_solution(9950698403233038301)
XLA Ops:
  0.6 0.0 copy-start
  0.6 0.0 copy-start.6
  0.7 0.0 copy-start.8
  0.7 1.7 pack_x.1
  2.4 0.0 copy-start.7
  2.4 0.0 copy-start.9
  2.4 3.8 %collective-permute-start = (f32[12,16,128]{2,1,0:T(8,128)}, f32[12,16,128]{2,1,0:T(8,128)S(1)}, u32[]{:S(2)}, u32[]{:S(2)}) collective-permute-start(f32[12,16,128]{2,1,0:T(8,128)} %get-tuple-element.42), channel_id=1, source_target_pairs={{0,8},{8,16},{16,24},{24,32},{32,40},{40,48},{48,56},{1,9},{9,17},... | collective-permute-start | bytes 294920 | tf_op jit(solution)/shard_map/halo_x/ppermute | solution.py:582
  6.2 4.9 %collective-permute-start.1 = (f32[12,16,128]{2,1,0:T(8,128)}, f32[12,16,128]{2,1,0:T(8,128)S(1)}, u32[]{:S(2)}, u32[]{:S(2)}) collective-permute-start(f32[12,16,128]{2,1,0:T(8,128)} %get-tuple-element.43), channel_id=1, source_target_pairs={{8,0},{16,8},{24,16},{32,24},{40,32},{48,40},{56,48},{9,1},{17,9},... | collective-permute-start | bytes 294920 | tf_op jit(solution)/shard_map/halo_x/ppermute | solution.py:583
  11.1 0.9 collective-permute-done.low_ref.refs_7_.x_low_ref
  12.0 1.6 collective-permute-done.1.high_ref.refs_8_.x_high_ref
  13.6 0.0 copy-done
  13.6 0.0 copy-done.6
  13.6 0.0 copy-done.8
  13.6 0.0 copy-done.7
  13.6 0.0 copy-done.9
  13.6 3.9 %conv.1 = (f32[32,16,128]{2,1,0:T(8,128)}, s32[1,512]{1,0:T(1,128)S(1)}, f32[1,2,512]{2,1,0:T(2,128)S(1)}, f32[1,2]{1,0:T(1,128)S(1)}) custom-call(bf16[4,32,16,128]{3,2,1,0:T(8,128)(2,1)S(1)} %copy-done, f32[12,16,128]{2,1,0:T(8,128)S(1)} %collective-permute-done.low_ref.refs_7_.x_low_ref, ...), custom_call_target="tpu_custom_call" | custom-call | flops 14155776 | bytes 995776 | tf_op jit(solution)/shard_map/conv/conv/pallas_call | solution.py:26
  17.5 0.0 copy-start.1
  17.5 0.0 copy-start.2
  17.5 3.8 %all-to-all-start = ((f32[32,16,128]{2,1,0:T(8,128)}), f32[32,16,128]{2,1,0:T(8,128)S(1)}, u32[]{:S(2)}, u32[]{:S(2)}) async-start(f32[32,16,128]{2,1,0:T(8,128)} %get-tuple-element.44), calls=%async_computation | async-start | bytes 524288 | tf_op jit(solution)/shard_map/raw/all_to_all | solution.py:681
  21.3 0.0 copy-done.1
  21.3 0.0 copy-done.2
  21.3 0.0 copy-start.4
  21.3 0.0 copy-start.5
  21.4 1.0 pack_y.1
  22.4 13.9 %collective-permute-start.2 = (bf16[464,128]{1,0:T(8,128)(2,1)}, bf16[464,128]{1,0:T(8,128)(2,1)S(1)}, u32[]{:S(2)}, u32[]{:S(2)}) collective-permute-start(bf16[464,128]{1,0:T(8,128)(2,1)} %get-tuple-element.53), channel_id=1, source_target_pairs={{0,1},{1,2},{2,3},{3,4},{4,5},{5,6},{6,7},{8,9},{9,10},{10,11},{11... | collective-permute-start | bytes 356360 | tf_op jit(solution)/shard_map/halo_y/ppermute | solution.py:582
  36.3 1.3 collective-permute-start.3
  38.3 0.1 pad_add_fusion.refs_4_.refs_6_.place_ref
  38.3 0.0 copy-done.4
  38.3 0.0 copy-done.5
  38.4 3.4 %inner_1.1 = (f32[32,16,128]{2,1,0:T(8,128)S(1)}, f32[32,16,128]{2,1,0:T(8,128)S(1)}, f32[32,16,128]{2,1,0:T(8,128)S(1)}, f32[32,16,128]{2,1,0:T(8,128)S(1)}) custom-call(f32[32,16,128]{2,1,0:T(8,128)S(1)} %bitcast.14, f32[32,16,128]{2,1,0:T(8,128)S(1)} %bitcast.18, f32[32,16,128]{2,1,0:T(8,128)S(1)} %bitcast.23, f32[32,16,128]{2,1,0:T(8,128)S(1)} %bitcast.24, ...), custom_call_target="tpu_custom_call" | custom-call | flops 3932160 | bytes 2299916 | tf_op jit(solution)/shard_map/inner_1/inner_1/pallas_call | solution.py:26
  41.8 0.0 all-to-all-done
  41.8 5.7 %collective-permute-done.2.low_ref.refs_4_.y_low_ref = bf16[464,128]{1,0:T(8,128)(2,1)S(1)} collective-permute-done((bf16[464,128]{1,0:T(8,128)(2,1)}, bf16[464,128]{1,0:T(8,128)(2,1)S(1)}, u32[]{:S(2)}, u32[]{:S(2)}) %collective-permute-start.2) | collective-permute-done | bytes 118816 | tf_op jit(solution)/shard_map/halo_y/ppermute | solution.py:582
  47.4 14.6 %collective-permute-done.3.high_ref.refs_5_.y_high_ref = bf16[464,128]{1,0:T(8,128)(2,1)S(1)} collective-permute-done((bf16[464,128]{1,0:T(8,128)(2,1)S(1)}, bf16[464,128]{1,0:T(8,128)(2,1)S(1)}, u32[]{:S(2)}, u32[]{:S(2)}) %collective-permute-start.3) | collective-permute-done | bytes 118816 | tf_op jit(solution)/shard_map/halo_y/ppermute | solution.py:583
  62.0 0.7 conv_edge.1
  62.8 14.6 %all_to_all.26.refs_8_ = f32[8,128,128]{2,1,0:T(8,128)S(1)} all-to-all(f32[8,128,128]{2,1,0:T(8,128)S(1)} %conv_edge.1), channel_id=1, replica_groups=mesh['shot'=8,'gx'=8,'gy'=8] {'shot'}, dimensions={0} | all-to-all | bytes 1048576 | tf_op jit(solution)/shard_map/raw/all_to_all | solution.py:692
  77.4 1.6 step_1.1
  79.1 9.6 %collective-permute-start.4 = (bf16[320,128]{1,0:T(8,128)(2,1)S(1)}, bf16[320,128]{1,0:T(8,128)(2,1)S(1)}, u32[]{:S(2)}, u32[]{:S(2)}) collective-permute-start(bf16[320,128]{1,0:T(8,128)(2,1)S(1)} %get-tuple-element.65), channel_id=1, source_target_pairs={{0,1},{1,2},{2,3},{3,4},{4,5},{5,6},{6,7},{8,9},{9,10},{10,11},{11... | collective-permute-start | bytes 245768 | tf_op jit(solution)/shard_map/halo_2/ppermute | solution.py:582
  88.7 1.3 collective-permute-start.5
  90.0 1.9 %collective-permute-start.6 = (f32[8,16,128]{2,1,0:T(8,128)S(1)}, f32[8,16,128]{2,1,0:T(8,128)S(1)}, u32[]{:S(2)}, u32[]{:S(2)}) collective-permute-start(f32[8,16,128]{2,1,0:T(8,128)S(1)} %get-tuple-element.68), channel_id=1, source_target_pairs={{0,8},{8,16},{16,24},{24,32},{32,40},{40,48},{48,56},{1,9},{9,17},... | collective-permute-start | bytes 196616 | tf_op jit(solution)/shard_map/halo_2/ppermute | solution.py:582
  91.9 3.9 %collective-permute-start.7 = (f32[8,16,128]{2,1,0:T(8,128)S(1)}, f32[8,16,128]{2,1,0:T(8,128)S(1)}, u32[]{:S(2)}, u32[]{:S(2)}) collective-permute-start(f32[8,16,128]{2,1,0:T(8,128)S(1)} %get-tuple-element.69), channel_id=1, source_target_pairs={{8,0},{16,8},{24,16},{32,24},{40,32},{48,40},{56,48},{9,1},{17,9},... | collective-permute-start | bytes 196616 | tf_op jit(solution)/shard_map/halo_2/ppermute | solution.py:583
  95.8 3.6 %inner_2.1 = (f32[32,16,128]{2,1,0:T(8,128)S(1)}, f32[32,16,128]{2,1,0:T(8,128)S(1)}, f32[32,16,128]{2,1,0:T(8,128)S(1)}, f32[32,16,128]{2,1,0:T(8,128)S(1)}, f32[1,512]{1,0:T(1,128)S(1)}) custom-call(f32[32,16,128]{2,1,0:T(8,128)S(1)} %get-tuple-element.57.refs_0_, f32[32,16,128]{2,1,0:T(8,128)S(1)} %get-tuple-element.58.refs_1_.refs_12_, ...), custom_call_target="tpu_custom_call" | custom-call | flops 3932160 | bytes 2105356 | tf_op jit(solution)/shard_map/inner_2/inner_2/pallas_call | solution.py:26
  99.4 0.0 collective-permute-done.6.refs_9_
  99.5 0.0 collective-permute-done.7.refs_10_
  99.5 0.0 collective-permute-done.4.refs_4_
  99.5 5.6 %collective-permute-done.5.refs_5_ = bf16[320,128]{1,0:T(8,128)(2,1)S(1)} collective-permute-done((bf16[320,128]{1,0:T(8,128)(2,1)S(1)}, bf16[320,128]{1,0:T(8,128)(2,1)S(1)}, u32[]{:S(2)}, u32[]{:S(2)}) %collective-permute-start.5) | collective-permute-done | bytes 81952 | tf_op jit(solution)/shard_map/halo_2/ppermute | solution.py:583
  105.1 2.2 %step_2.1 = (f32[32,16,128]{2,1,0:T(8,128)}, f32[32,16,128]{2,1,0:T(8,128)}, f32[8,8,16,128]{3,2,1,0:T(8,128)}) custom-call(f32[32,16,128]{2,1,0:T(8,128)S(1)} %get-tuple-element.61.refs_0_, f32[32,16,128]{2,1,0:T(8,128)S(1)} %get-tuple-element.62.refs_1_, f32[32,16,128]{2,1,0:T(8,128)S(1)} %get-tuple-element.63.refs_2_, ...), custom_call_target="tpu_custom_call" | custom-call | flops 1000000 | bytes 3178516 | tf_op jit(solution)/shard_map/step_2/step_2/pallas_call | solution.py:26
  107.3 3.5 %all-to-all-start.2 = ((f32[64,16,128]{2,1,0:T(8,128)}), f32[64,16,128]{2,1,0:T(8,128)S(1)}, u32[]{:S(2)}, u32[]{:S(2)}) async-start(f32[64,16,128]{2,1,0:T(8,128)} %bitcast.9), calls=%async_computation.2 | async-start | bytes 1048576 | tf_op jit(solution)/shard_map/update/all_to_all | solution.py:758
  111.4 9.6 %all-to-all-done.2 = f32[64,16,128]{2,1,0:T(8,128)S(1)} async-done(((f32[64,16,128]{2,1,0:T(8,128)}), f32[64,16,128]{2,1,0:T(8,128)S(1)}, u32[]{:S(2)}, u32[]{:S(2)}) %all-to-all-start.2) | async-done | bytes 524320 | tf_op jit(solution)/shard_map/update/all_to_all | solution.py:758
  121.0 0.7 update.1
  121.8 0.0 copy-start.3
  121.8 3.5 %all-to-all-start.3 = ((f32[32,16,128]{2,1,0:T(8,128)}), f32[32,16,128]{2,1,0:T(8,128)S(1)}, u32[]{:S(2)}, u32[]{:S(2)}) async-start(f32[32,16,128]{2,1,0:T(8,128)} %bitcast.11), calls=%async_computation.3 | async-start | bytes 524288 | tf_op jit(solution)/shard_map/update/all_to_all | solution.py:768
  125.3 0.0 copy-done.3
  125.4 1.0 trace_2.1.second_ref
  126.3 6.5 %all-to-all-done.3.update_ref.value_ref = f32[32,16,128]{2,1,0:T(8,128)S(1)} async-done(((f32[32,16,128]{2,1,0:T(8,128)}), f32[32,16,128]{2,1,0:T(8,128)S(1)}, u32[]{:S(2)}, u32[]{:S(2)}) %all-to-all-start.3) | async-done | bytes 262176 | tf_op jit(solution)/shard_map/update/all_to_all | solution.py:768
  132.8 3.2 %gradient.1 = f32[64,1,1152]{2,1,0:T(1,128)} custom-call(f32[32,16,128]{2,1,0:T(8,128)S(1)} %all-to-all-done.3.update_ref.value_ref, f32[32,16,128]{2,1,0:T(8,128)S(1)} %get-tuple-element.67.refs_8_.squashed_ref, bf16[4,32,16,128]{3,2,1,0:T(8,128)(2,1)S(1)} %copy-done, f32[12,16,128]{2,1,0:T(8,128)S(1)} %collective-permute-done.low_ref.refs_7_.x_low_ref, ...), custom_call_target="tpu_custom_call" | custom-call | flops 14155776 | bytes 1781760 | tf_op jit(solution)/shard_map/gradient/gradient/pallas_call | solution.py:26
  136.0 11.1 %all-to-all-start.4 = ((f32[64,1,1152]{2,1,0:T(1,128)}), f32[64,1,1152]{2,1,0:T(1,128)S(1)}, u32[]{:S(2)}, u32[]{:S(2)}) async-start(f32[64,1,1152]{2,1,0:T(1,128)} %gradient.1), calls=%async_computation.4 | async-start | bytes 589824 | tf_op jit(solution)/shard_map/gradient/all_to_all | solution.py:785
  147.1 0.7 keep.1
  147.9 22.8 %all-to-all-done.4.shares_ref = f32[64,1,1152]{2,1,0:T(1,128)S(1)} async-done(((f32[64,1,1152]{2,1,0:T(1,128)}), f32[64,1,1152]{2,1,0:T(1,128)S(1)}, u32[]{:S(2)}, u32[]{:S(2)}) %all-to-all-start.4) | async-done | bytes 294944 | tf_op jit(solution)/shard_map/gradient/all_to_all | solution.py:785
  170.7 0.7 total.1
Async XLA Ops:
  0.6 13.0 %copy-start = (bf16[4,32,16,128]{3,2,1,0:T(8,128)(2,1)S(1)}, bf16[4,32,16,128]{3,2,1,0:T(8,128)(2,1)}, u32[]{:S(2)}) copy-start(bf16[4,32,16,128]{3,2,1,0:T(8,128)(2,1)} %feat_ref.7) | copy-start | bytes 1572868
  0.6 13.0 %copy-start.6 = (f32[1,2,512]{2,1,0:T(2,128)S(1)}, f32[1,2,512]{2,1,0:T(2,128)}, u32[]{:S(2)}) copy-start(f32[1,2,512]{2,1,0:T(2,128)} %refs_6_.1) | copy-start | bytes 12292
  0.7 13.0 %copy-start.8 = (f32[4,27]{1,0:T(4,128)S(1)}, f32[4,27]{1,0:T(4,128)}, u32[]{:S(2)}) copy-start(f32[4,27]{1,0:T(4,128)} %weight_ref.3) | copy-start | bytes 1300
  2.4 11.2 %copy-start.7 = (s32[1,512]{1,0:T(1,128)S(1)}, s32[1,512]{1,0:T(1,128)}, u32[]{:S(2)}) copy-start(s32[1,512]{1,0:T(1,128)} %refs_5_.1) | copy-start | bytes 6148
  2.4 11.2 %copy-start.9 = (f32[1,2]{1,0:T(1,128)S(1)}, f32[1,2]{1,0:T(1,128)}, u32[]{:S(2)}) copy-start(f32[1,2]{1,0:T(1,128)} %refs_2_.1) | copy-start | bytes 28
  2.4 9.6 %collective-permute-start = (f32[12,16,128]{2,1,0:T(8,128)}, f32[12,16,128]{2,1,0:T(8,128)S(1)}, u32[]{:S(2)}, u32[]{:S(2)}) collective-permute-start(f32[12,16,128]{2,1,0:T(8,128)} %get-tuple-element.42), channel_id=1, source_target_pairs={{0,8},{8,16},{16,24},{24,32},{32,40},{40,48},{48,56},{1,9},{9,17},... | collective-permute-start | bytes 294920 | tf_op jit(solution)/shard_map/halo_x/ppermute | solution.py:582
  6.2 7.4 %collective-permute-start.1 = (f32[12,16,128]{2,1,0:T(8,128)}, f32[12,16,128]{2,1,0:T(8,128)S(1)}, u32[]{:S(2)}, u32[]{:S(2)}) collective-permute-start(f32[12,16,128]{2,1,0:T(8,128)} %get-tuple-element.43), channel_id=1, source_target_pairs={{8,0},{16,8},{24,16},{32,24},{40,32},{48,40},{56,48},{9,1},{17,9},... | collective-permute-start | bytes 294920 | tf_op jit(solution)/shard_map/halo_x/ppermute | solution.py:583
  17.5 3.8 %copy-start.1 = (f32[1,32,16,128]{3,2,1,0:T(8,128)S(1)}, f32[1,32,16,128]{3,2,1,0:T(8,128)}, u32[]{:S(2)}) copy-start(f32[1,32,16,128]{3,2,1,0:T(8,128)} %param.14) | copy-start | bytes 786436
  17.5 3.8 %copy-start.2 = (f32[1,32,16,128]{3,2,1,0:T(8,128)S(1)}, f32[1,32,16,128]{3,2,1,0:T(8,128)}, u32[]{:S(2)}) copy-start(f32[1,32,16,128]{3,2,1,0:T(8,128)} %param.16) | copy-start | bytes 786436
  17.5 24.2 %all-to-all-start = ((f32[32,16,128]{2,1,0:T(8,128)}), f32[32,16,128]{2,1,0:T(8,128)S(1)}, u32[]{:S(2)}, u32[]{:S(2)}) async-start(f32[32,16,128]{2,1,0:T(8,128)} %get-tuple-element.44), calls=%async_computation | async-start | bytes 524288 | tf_op jit(solution)/shard_map/raw/all_to_all | solution.py:681
  21.3 17.0 %copy-start.4 = (f32[1,32,16,128]{3,2,1,0:T(8,128)S(1)}, f32[1,32,16,128]{3,2,1,0:T(8,128)}, u32[]{:S(2)}) copy-start(f32[1,32,16,128]{3,2,1,0:T(8,128)} %param.13) | copy-start | bytes 786436
  21.3 17.0 %copy-start.5 = (f32[1,32,16,128]{3,2,1,0:T(8,128)S(1)}, f32[1,32,16,128]{3,2,1,0:T(8,128)}, u32[]{:S(2)}) copy-start(f32[1,32,16,128]{3,2,1,0:T(8,128)} %param.15) | copy-start | bytes 786436
  22.4 25.0 %collective-permute-start.2 = (bf16[464,128]{1,0:T(8,128)(2,1)}, bf16[464,128]{1,0:T(8,128)(2,1)S(1)}, u32[]{:S(2)}, u32[]{:S(2)}) collective-permute-start(bf16[464,128]{1,0:T(8,128)(2,1)} %get-tuple-element.53), channel_id=1, source_target_pairs={{0,1},{1,2},{2,3},{3,4},{4,5},{5,6},{6,7},{8,9},{9,10},{10,11},{11... | collective-permute-start | bytes 356360 | tf_op jit(solution)/shard_map/halo_y/ppermute | solution.py:582
  36.3 25.7 %collective-permute-start.3 = (bf16[464,128]{1,0:T(8,128)(2,1)S(1)}, bf16[464,128]{1,0:T(8,128)(2,1)S(1)}, u32[]{:S(2)}, u32[]{:S(2)}) collective-permute-start(bf16[464,128]{1,0:T(8,128)(2,1)S(1)} %get-tuple-element.54), channel_id=1, source_target_pairs={{1,0},{2,1},{3,2},{4,3},{5,4},{6,5},{7,6},{9,8},{10,9},{11,10},{12... | collective-permute-start | bytes 356360 | tf_op jit(solution)/shard_map/halo_y/ppermute | solution.py:583
  79.1 20.4 %collective-permute-start.4 = (bf16[320,128]{1,0:T(8,128)(2,1)S(1)}, bf16[320,128]{1,0:T(8,128)(2,1)S(1)}, u32[]{:S(2)}, u32[]{:S(2)}) collective-permute-start(bf16[320,128]{1,0:T(8,128)(2,1)S(1)} %get-tuple-element.65), channel_id=1, source_target_pairs={{0,1},{1,2},{2,3},{3,4},{4,5},{5,6},{6,7},{8,9},{9,10},{10,11},{11... | collective-permute-start | bytes 245768 | tf_op jit(solution)/shard_map/halo_2/ppermute | solution.py:582
  88.7 16.4 %collective-permute-start.5 = (bf16[320,128]{1,0:T(8,128)(2,1)S(1)}, bf16[320,128]{1,0:T(8,128)(2,1)S(1)}, u32[]{:S(2)}, u32[]{:S(2)}) collective-permute-start(bf16[320,128]{1,0:T(8,128)(2,1)S(1)} %get-tuple-element.66), channel_id=1, source_target_pairs={{1,0},{2,1},{3,2},{4,3},{5,4},{6,5},{7,6},{9,8},{10,9},{11,10},{12... | collective-permute-start | bytes 245768 | tf_op jit(solution)/shard_map/halo_2/ppermute | solution.py:583
  90.0 9.5 %collective-permute-start.6 = (f32[8,16,128]{2,1,0:T(8,128)S(1)}, f32[8,16,128]{2,1,0:T(8,128)S(1)}, u32[]{:S(2)}, u32[]{:S(2)}) collective-permute-start(f32[8,16,128]{2,1,0:T(8,128)S(1)} %get-tuple-element.68), channel_id=1, source_target_pairs={{0,8},{8,16},{16,24},{24,32},{32,40},{40,48},{48,56},{1,9},{9,17},... | collective-permute-start | bytes 196616 | tf_op jit(solution)/shard_map/halo_2/ppermute | solution.py:582
  91.9 7.6 %collective-permute-start.7 = (f32[8,16,128]{2,1,0:T(8,128)S(1)}, f32[8,16,128]{2,1,0:T(8,128)S(1)}, u32[]{:S(2)}, u32[]{:S(2)}) collective-permute-start(f32[8,16,128]{2,1,0:T(8,128)S(1)} %get-tuple-element.69), channel_id=1, source_target_pairs={{8,0},{16,8},{24,16},{32,24},{40,32},{48,40},{56,48},{9,1},{17,9},... | collective-permute-start | bytes 196616 | tf_op jit(solution)/shard_map/halo_2/ppermute | solution.py:583
  107.3 13.8 %all-to-all-start.2 = ((f32[64,16,128]{2,1,0:T(8,128)}), f32[64,16,128]{2,1,0:T(8,128)S(1)}, u32[]{:S(2)}, u32[]{:S(2)}) async-start(f32[64,16,128]{2,1,0:T(8,128)} %bitcast.9), calls=%async_computation.2 | async-start | bytes 1048576 | tf_op jit(solution)/shard_map/update/all_to_all | solution.py:758
  121.8 3.6 %copy-start.3 = (f32[32,16,128]{2,1,0:T(8,128)S(1)}, f32[32,16,128]{2,1,0:T(8,128)}, u32[]{:S(2)}) copy-start(f32[32,16,128]{2,1,0:T(8,128)} %get-tuple-element.71.fwd_ref) | copy-start | bytes 786436
  121.8 11.0 %all-to-all-start.3 = ((f32[32,16,128]{2,1,0:T(8,128)}), f32[32,16,128]{2,1,0:T(8,128)S(1)}, u32[]{:S(2)}, u32[]{:S(2)}) async-start(f32[32,16,128]{2,1,0:T(8,128)} %bitcast.11), calls=%async_computation.3 | async-start | bytes 524288 | tf_op jit(solution)/shard_map/update/all_to_all | solution.py:768
  136.0 34.7 %all-to-all-start.4 = ((f32[64,1,1152]{2,1,0:T(1,128)}), f32[64,1,1152]{2,1,0:T(1,128)S(1)}, u32[]{:S(2)}, u32[]{:S(2)}) async-start(f32[64,1,1152]{2,1,0:T(1,128)} %gradient.1), calls=%async_computation.4 | async-start | bytes 589824 | tf_op jit(solution)/shard_map/gradient/all_to_all | solution.py:785

commit v7 on v6

--- a/solution.py
+++ b/solution.py
@@ -12,6 +12,7 @@
 F32 = jnp.float32
 BF16 = jnp.bfloat16
 VMEM_LIMIT = 48 * 1024 * 1024
+AHEAD = 50_000_000_000
 VMEM_WHOLE = 63 * 1024 * 1024
 
 VM = pl.BlockSpec(memory_space=pltpu.VMEM)
@@ -89,62 +90,44 @@
 
 
 def wave_rows(size_x):
-    return size_x * 10
-
-
-def row_mix(value, weights, upward):
-    count = value.shape[0]
-    place = lax.broadcasted_iota(jnp.int32, value.shape, 0) & 3
-    distance = 3 - place if upward else place
-    total = value
-    for j, row in enumerate(weights, 1):
-        factor = jnp.zeros(value.shape, F32)
-        for n, weight in enumerate(row):
-            if weight:
-                factor = jnp.where(distance == n, float(weight), factor)
-        total = total + factor * pltpu.roll(value, count - j if upward else j, 0)
-    return total
+    return size_x * 12
 
 
 def pack_waves(fwd_ref, back_ref, upward, out_ref, first, edge_ref, low_ref):
     size_x, size_y, depth = fwd_ref.shape
-    start, near = (size_y - 4, 3) if upward else (0, 0)
+    start, near = (size_y - 4, 2) if upward else (0, 0)
     edge_ref[:, 0:4] = fwd_ref[:, start : start + 4]
     edge_ref[:, 4:8] = back_ref[:, start : start + 4]
     value = edge_ref[...].reshape(size_x * 8, depth)
-    value = row_mix(value, ((0, -1, -2, -2), (0, 0, 1, 1)), upward)
     high = value.astype(BF16)
     out_ref[first : first + size_x * 8] = high
     edge_ref[...] = (value - high.astype(F32)).reshape(size_x, 8, depth)
-    eighth = size_x // 8
-    for q in range(8):
-        part = slice(q * eighth, (q + 1) * eighth)
-        low_ref[:, 2 * q : 2 * q + 1] = edge_ref[part, near : near + 1]
-        low_ref[:, 2 * q + 1 : 2 * q + 2] = edge_ref[part, 4 + near : 5 + near]
-    out_ref[first + size_x * 8 : first + size_x * 10] = (
-        low_ref[...].reshape(size_x * 2, depth).astype(BF16)
+    quarter = size_x // 4
+    for q in range(4):
+        part = slice(q * quarter, (q + 1) * quarter)
+        low_ref[:, 4 * q : 4 * q + 2] = edge_ref[part, near : near + 2]
+        low_ref[:, 4 * q + 2 : 4 * q + 4] = edge_ref[part, 4 + near : 6 + near]
+    out_ref[first + size_x * 8 : first + size_x * 12] = (
+        low_ref[...].reshape(size_x * 4, depth).astype(BF16)
     )
 
 
 def unpack_waves(buffer_ref, upward, first, size_x, edge_ref, low_ref):
     depth = buffer_ref.shape[1]
-    near = 3 if upward else 0
-    eighth = size_x // 8
+    near = 2 if upward else 0
+    quarter = size_x // 4
     edge_ref[...] = (
         buffer_ref[first : first + size_x * 8].astype(F32).reshape(size_x, 8, depth)
     )
     low_ref[...] = (
-        buffer_ref[first + size_x * 8 : first + size_x * 10]
+        buffer_ref[first + size_x * 8 : first + size_x * 12]
         .astype(F32)
-        .reshape(eighth, 16, depth)
-    )
-    for q in range(8):
-        part = slice(q * eighth, (q + 1) * eighth)
-        edge_ref[part, near : near + 1] += low_ref[:, 2 * q : 2 * q + 1]
-        edge_ref[part, 4 + near : 5 + near] += low_ref[:, 2 * q + 1 : 2 * q + 2]
-    value = edge_ref[...].reshape(size_x * 8, depth)
-    value = row_mix(value, ((0, 1, 2, 2), (0, 0, 1, 3), (0, 0, 0, 1)), upward)
-    edge_ref[...] = value.reshape(size_x, 8, depth)
+        .reshape(quarter, 16, depth)
+    )
+    for q in range(4):
+        part = slice(q * quarter, (q + 1) * quarter)
+        edge_ref[part, near : near + 2] += low_ref[:, 4 * q : 4 * q + 2]
+        edge_ref[part, 4 + near : 6 + near] += low_ref[:, 4 * q + 2 : 4 * q + 4]
 
 
 def pack_y_body(
@@ -219,17 +202,9 @@
     plane_ref[8 + size_x : 9 + size_x] = tail[2 * c + 1 : 2 * c + 2]
 
 
-def conv_edge_body(parts_ref, low_ref, high_ref, weight_ref, out_ref, plane_ref):
-    copies, rows, size_y, depth = parts_ref.shape
-    size_x = copies * rows
+def conv_edge_body(low_ref, high_ref, weight_ref, out_ref, plane_ref):
+    size_x = out_ref.shape[0] // 2
     channels = weight_ref.shape[0]
-    total = parts_ref[0]
-    for n in range(1, copies):
-        total = total + parts_ref[n]
-    first = rows * size_y
-    total = total.reshape(first, depth)
-    for n in range(copies):
-        out_ref[n, 0:first] = total
     for side, (buffer_ref, dy) in enumerate(((low_ref, 0), (high_ref, 2))):
         terms = [None] * 3
         for c in range(channels):
@@ -240,9 +215,20 @@
                     part = weight_ref[c, 9 * dx + 3 * dy + dz] * plane
                     terms[dz] = part if terms[dz] is None else terms[dz] + part
         total = terms[1] + shifted_lanes(terms[0], -1) + shifted_lanes(terms[2], 1)
-        at = first + side * size_x
-        for n in range(copies):
-            out_ref[n, at : at + size_x] = total
+        out_ref[side * size_x : (side + 1) * size_x] = total
+
+
+def raw_body(parts_ref, rims_ref, out_ref):
+    copies, rows, size_y, depth = parts_ref.shape
+    total = parts_ref[0]
+    for n in range(1, copies):
+        total = total + parts_ref[n]
+    first = rows * size_y
+    total = total.reshape(first, depth)
+    rims = rims_ref[...]
+    for n in range(copies):
+        out_ref[n, 0:first] = total
+        out_ref[n, first:] = rims
 
 
 def update_body(parts_ref, damping_ref, out_ref):
@@ -633,7 +619,7 @@
         x_low, x_high = neighbours(x_up, x_down, "gx")
     packing = [
         pltpu.VMEM((size_x, 8, depth), F32),
-        pltpu.VMEM((size_x // 8, 16, depth), F32),
+        pltpu.VMEM((size_x // 4, 16, depth), F32),
     ]
     y_shape = shape(channels * size_x + 16 + wave_rows(size_x), depth, dtype=BF16)
     with jax.named_scope("pack_y"):
@@ -679,15 +665,23 @@
         )
     with jax.named_scope("raw"):
         parts = lax.all_to_all(main, "shot", 0, 0, tiled=True)
-        parts, *inner_1 = lax.optimization_barrier((parts, *inner_1))
+        y_low, *inner_1 = lax.optimization_barrier((y_low, *inner_1))
+        rims = call(
+            conv_edge_body,
+            [shape(2 * size_x, depth)],
+            (y_low, y_high, conv_weight),
+            [VM] * 2 + [SM],
+            scratch=[pltpu.VMEM((size_x + 16, depth), F32)],
+            flops=AHEAD,
+            name="conv_edge",
+        )
         each = rows * size_y + 2 * size_x
         raw = call(
-            conv_edge_body,
+            raw_body,
             [shape(shots, each, depth)],
-            (parts.reshape(shots, rows, size_y, depth), y_low, y_high, conv_weight),
-            [VM] * 3 + [SM],
-            scratch=[pltpu.VMEM((size_x + 16, depth), F32)],
-            name="conv_edge",
+            (parts.reshape(shots, rows, size_y, depth), rims),
+            [VM] * 2,
+            name="raw",
         )
         raw = lax.all_to_all(raw.reshape(shots * each, depth), "shot", 0, 0, tiled=True)
         raw = raw.reshape(shots, each, depth)

time: 172 us -> 166 us (0.965)
  waiting for transfers between devices: 67.3 us -> 61 us
    ppermute x4, waiting for transfers between devices: 6.53 us -> 0.87 us  [neighbours(): low = lax.ppermute(up, axis, [(i, i + 1) for i in range(count - 1)])]
    pallas_call x13 -> x14, Pallas kernels: 24.6 us -> 23.8 us  [call(): pl.pallas_call(body, out_shape=outs[0] if single else tuple(outs), in_spe...]
  transfers between devices with their start and end apart: 12 -> 12, of which waited for: 8 -> 7; matrix products, arithmetic and copies ran while one was open for 0% -> 0% of each run, Pallas kernels for 6% -> 8%
where the time goes in v7:
time: 166 us; the launch traced here: 165 us
  starting transfers between devices  61.6 us (37%)
  waiting for transfers between devices  61 us (37%)
  Pallas kernels  23.8 us (14%)
  blocking collectives  14.5 us (9%)
  between operations  2.18 us (1%)
    ppermute x4, starting transfers between devices, neighbours(): low = lax.ppermute(up, axis, [(i, i + 1) for i in range(count - 1)])  29.1 us
    pallas_call x14, Pallas kernels, call(): pl.pallas_call(body, out_shape=outs[0] if single else tuple(outs), in_spe...  23.8 us
    all_to_all x1, waiting for transfers between devices, per_device(): shares = lax.all_to_all(share, ('gx', 'gy'), 0, 0, tiled=True)  22.8 us
    ppermute x4, waiting for transfers between devices, neighbours(): high = lax.ppermute(down, axis, [(i + 1, i) for i in range(count - 1)])  21.2 us
    all_to_all x1, blocking collectives, per_device(): lax.all_to_all(raw.reshape(shots * each, depth), 'shot', 0, 0, tiled=True)  14.5 us
    ppermute x4, starting transfers between devices, neighbours(): high = lax.ppermute(down, axis, [(i + 1, i) for i in range(count - 1)])  11.4 us
    all_to_all x1, waiting for transfers between devices, per_device(): lax.all_to_all(sums.reshape(shots * 2 * rows, size_y, depth), 'shot', 0,...  9.62 us
    all_to_all x1, starting transfers between devices, per_device(): shares = lax.all_to_all(share, ('gx', 'gy'), 0, 0, tiled=True)  9.61 us
  transfers between devices with their start and end apart: 12, of which 7 were waited for; matrix products, arithmetic and copies ran while one was open for 0% of the time, Pallas kernels for 8%

profile of v7, /device:TPU:32, one launch (start us, length us, event | category | flops | bytes accessed | tf_op | source)
XLA Modules:
  0.0 164.7 jit_solution(11153360883099479152)
XLA Ops:
  0.6 0.0 copy-start
  0.6 0.0 copy-start.1
  0.7 1.7 %pack_x.1 = (f32[12,16,128]{2,1,0:T(8,128)}, f32[12,16,128]{2,1,0:T(8,128)}) custom-call(bf16[4,32,16,128]{3,2,1,0:T(8,128)(2,1)} %feat_ref.7, f32[32,16,128]{2,1,0:T(8,128)} %bitcast.12, f32[32,16,128]{2,1,0:T(8,128)} %bitcast.16), custom_call_target="tpu_custom_call" | custom-call | flops 1000000 | bytes 1245184 | tf_op jit(solution)/shard_map/pack_x/pack_x/pallas_call | solution.py:27
  2.4 3.8 %collective-permute-start = (f32[12,16,128]{2,1,0:T(8,128)}, f32[12,16,128]{2,1,0:T(8,128)S(1)}, u32[]{:S(2)}, u32[]{:S(2)}) collective-permute-start(f32[12,16,128]{2,1,0:T(8,128)} %get-tuple-element.42), channel_id=1, source_target_pairs={{0,8},{8,16},{16,24},{24,32},{32,40},{40,48},{48,56},{1,9},{9,17},... | collective-permute-start | bytes 294920 | tf_op jit(solution)/shard_map/halo_x/ppermute | solution.py:568
  6.2 4.9 %collective-permute-start.1 = (f32[12,16,128]{2,1,0:T(8,128)}, f32[12,16,128]{2,1,0:T(8,128)S(1)}, u32[]{:S(2)}, u32[]{:S(2)}) collective-permute-start(f32[12,16,128]{2,1,0:T(8,128)} %get-tuple-element.43), channel_id=1, source_target_pairs={{8,0},{16,8},{24,16},{32,24},{40,32},{48,40},{56,48},{9,1},{17,9},... | collective-permute-start | bytes 294920 | tf_op jit(solution)/shard_map/halo_x/ppermute | solution.py:569
  11.1 0.9 collective-permute-done.low_ref.refs_7_.x_low_ref
  12.0 1.6 collective-permute-done.1.high_ref.refs_8_.x_high_ref
  13.6 0.0 copy-done
  13.6 0.0 copy-done.1
  13.6 0.0 copy-start.2
  13.6 0.9 copy-done.2
  14.6 0.0 copy-start.9
  14.6 0.9 pack_y.1
  15.5 13.3 %collective-permute-start.2 = (bf16[528,128]{1,0:T(8,128)(2,1)}, bf16[528,128]{1,0:T(8,128)(2,1)S(1)}, u32[]{:S(2)}, u32[]{:S(2)}) collective-permute-start(bf16[528,128]{1,0:T(8,128)(2,1)} %get-tuple-element.44), channel_id=1, source_target_pairs={{0,1},{1,2},{2,3},{3,4},{4,5},{5,6},{6,7},{8,9},{9,10},{10,11},{11... | collective-permute-start | bytes 405512 | tf_op jit(solution)/shard_map/halo_y/ppermute | solution.py:568
  28.8 1.3 collective-permute-start.3
  30.7 0.0 copy-start.7
  30.7 0.0 copy-start.8
  30.7 0.0 copy-start.10
  30.8 0.1 pad_add_fusion.refs_4_.refs_6_.place_ref
  30.8 0.0 copy-done.9
  30.8 0.6 copy-done.7
  31.4 0.0 copy-done.8
  31.4 0.0 copy-done.10
  31.4 0.0 copy-start.6
  31.4 3.9 %conv.1 = (f32[32,16,128]{2,1,0:T(8,128)}, s32[1,512]{1,0:T(1,128)S(1)}, f32[1,2,512]{2,1,0:T(2,128)S(1)}, f32[1,2]{1,0:T(1,128)S(1)}) custom-call(bf16[4,32,16,128]{3,2,1,0:T(8,128)(2,1)S(1)} %copy-done, f32[12,16,128]{2,1,0:T(8,128)S(1)} %collective-permute-done.low_ref.refs_7_.x_low_ref, ...), custom_call_target="tpu_custom_call" | custom-call | flops 14155776 | bytes 995776 | tf_op jit(solution)/shard_map/conv/conv/pallas_call | solution.py:27
  35.3 0.0 copy-start.3
  35.3 0.0 copy-start.5
  35.3 4.4 %all-to-all-start = ((f32[32,16,128]{2,1,0:T(8,128)}), f32[32,16,128]{2,1,0:T(8,128)S(1)}, u32[]{:S(2)}, u32[]{:S(2)}) async-start(f32[32,16,128]{2,1,0:T(8,128)} %get-tuple-element.56), calls=%async_computation | async-start | bytes 524288 | tf_op jit(solution)/shard_map/raw/all_to_all | solution.py:667
  39.8 0.0 copy-done.6
  39.8 0.0 copy-done.3
  39.8 0.0 copy-done.5
  39.8 3.4 %inner_1.1 = (f32[32,16,128]{2,1,0:T(8,128)S(1)}, f32[32,16,128]{2,1,0:T(8,128)S(1)}, f32[32,16,128]{2,1,0:T(8,128)S(1)}, f32[32,16,128]{2,1,0:T(8,128)S(1)}) custom-call(f32[32,16,128]{2,1,0:T(8,128)S(1)} %bitcast.14, f32[32,16,128]{2,1,0:T(8,128)S(1)} %bitcast.18, f32[32,16,128]{2,1,0:T(8,128)S(1)} %bitcast.23, f32[32,16,128]{2,1,0:T(8,128)S(1)} %bitcast.24, ...), custom_call_target="tpu_custom_call" | custom-call | flops 3932160 | bytes 2299916 | tf_op jit(solution)/shard_map/inner_1/inner_1/pallas_call | solution.py:27
  43.2 0.0 collective-permute-done.2.low_ref.refs_4_.y_low_ref
  43.2 11.5 %collective-permute-done.3.high_ref.refs_5_.y_high_ref = bf16[528,128]{1,0:T(8,128)(2,1)S(1)} collective-permute-done((bf16[528,128]{1,0:T(8,128)(2,1)S(1)}, bf16[528,128]{1,0:T(8,128)(2,1)S(1)}, u32[]{:S(2)}, u32[]{:S(2)}) %collective-permute-start.3) | collective-permute-done | bytes 135200 | tf_op jit(solution)/shard_map/halo_y/ppermute | solution.py:569
  54.7 0.7 conv_edge.1.rims_ref
  55.5 0.0 all-to-all-done
  55.5 14.5 %all_to_all.26.refs_8_ = f32[8,128,128]{2,1,0:T(8,128)S(1)} all-to-all(f32[8,128,128]{2,1,0:T(8,128)S(1)} %raw.1), channel_id=1, replica_groups=mesh['shot'=8,'gx'=8,'gy'=8] {'shot'}, dimensions={0} | all-to-all | bytes 1048576 | tf_op jit(solution)/shard_map/raw/all_to_all | solution.py:686
  70.0 1.2 step_1.1
  71.2 10.1 %collective-permute-start.4 = (bf16[384,128]{1,0:T(8,128)(2,1)S(1)}, bf16[384,128]{1,0:T(8,128)(2,1)S(1)}, u32[]{:S(2)}, u32[]{:S(2)}) collective-permute-start(bf16[384,128]{1,0:T(8,128)(2,1)S(1)} %get-tuple-element.65), channel_id=1, source_target_pairs={{0,1},{1,2},{2,3},{3,4},{4,5},{5,6},{6,7},{8,9},{9,10},{10,11},{11... | collective-permute-start | bytes 294920 | tf_op jit(solution)/shard_map/halo_2/ppermute | solution.py:568
  81.3 1.3 collective-permute-start.5
  82.6 1.9 %collective-permute-start.6 = (f32[8,16,128]{2,1,0:T(8,128)S(1)}, f32[8,16,128]{2,1,0:T(8,128)S(1)}, u32[]{:S(2)}, u32[]{:S(2)}) collective-permute-start(f32[8,16,128]{2,1,0:T(8,128)S(1)} %get-tuple-element.68), channel_id=1, source_target_pairs={{0,8},{8,16},{16,24},{24,32},{32,40},{40,48},{48,56},{1,9},{9,17},... | collective-permute-start | bytes 196616 | tf_op jit(solution)/shard_map/halo_2/ppermute | solution.py:568
  84.6 3.9 %collective-permute-start.7 = (f32[8,16,128]{2,1,0:T(8,128)S(1)}, f32[8,16,128]{2,1,0:T(8,128)S(1)}, u32[]{:S(2)}, u32[]{:S(2)}) collective-permute-start(f32[8,16,128]{2,1,0:T(8,128)S(1)} %get-tuple-element.69), channel_id=1, source_target_pairs={{8,0},{16,8},{24,16},{32,24},{40,32},{48,40},{56,48},{9,1},{17,9},... | collective-permute-start | bytes 196616 | tf_op jit(solution)/shard_map/halo_2/ppermute | solution.py:569
  88.5 3.6 %inner_2.1 = (f32[32,16,128]{2,1,0:T(8,128)S(1)}, f32[32,16,128]{2,1,0:T(8,128)S(1)}, f32[32,16,128]{2,1,0:T(8,128)S(1)}, f32[32,16,128]{2,1,0:T(8,128)S(1)}, f32[1,512]{1,0:T(1,128)S(1)}) custom-call(f32[32,16,128]{2,1,0:T(8,128)S(1)} %get-tuple-element.57.refs_0_, f32[32,16,128]{2,1,0:T(8,128)S(1)} %get-tuple-element.58.refs_1_.refs_12_, ...), custom_call_target="tpu_custom_call" | custom-call | flops 3932160 | bytes 2105356 | tf_op jit(solution)/shard_map/inner_2/inner_2/pallas_call | solution.py:27
  92.1 0.0 collective-permute-done.6.refs_9_
  92.1 0.0 collective-permute-done.7.refs_10_
  92.1 0.0 collective-permute-done.4.refs_4_
  92.2 8.0 %collective-permute-done.5.refs_5_ = bf16[384,128]{1,0:T(8,128)(2,1)S(1)} collective-permute-done((bf16[384,128]{1,0:T(8,128)(2,1)S(1)}, bf16[384,128]{1,0:T(8,128)(2,1)S(1)}, u32[]{:S(2)}, u32[]{:S(2)}) %collective-permute-start.5) | collective-permute-done | bytes 98336 | tf_op jit(solution)/shard_map/halo_2/ppermute | solution.py:569
  100.2 2.0 %step_2.1 = (f32[32,16,128]{2,1,0:T(8,128)}, f32[32,16,128]{2,1,0:T(8,128)}, f32[8,8,16,128]{3,2,1,0:T(8,128)}) custom-call(f32[32,16,128]{2,1,0:T(8,128)S(1)} %get-tuple-element.61.refs_0_, f32[32,16,128]{2,1,0:T(8,128)S(1)} %get-tuple-element.62.refs_1_, f32[32,16,128]{2,1,0:T(8,128)S(1)} %get-tuple-element.63.refs_2_, ...), custom_call_target="tpu_custom_call" | custom-call | flops 1000000 | bytes 3211284 | tf_op jit(solution)/shard_map/step_2/step_2/pallas_call | solution.py:27
  102.1 3.5 %all-to-all-start.2 = ((f32[64,16,128]{2,1,0:T(8,128)}), f32[64,16,128]{2,1,0:T(8,128)S(1)}, u32[]{:S(2)}, u32[]{:S(2)}) async-start(f32[64,16,128]{2,1,0:T(8,128)} %bitcast.9), calls=%async_computation.2 | async-start | bytes 1048576 | tf_op jit(solution)/shard_map/update/all_to_all | solution.py:752
  106.3 9.6 %all-to-all-done.2 = f32[64,16,128]{2,1,0:T(8,128)S(1)} async-done(((f32[64,16,128]{2,1,0:T(8,128)}), f32[64,16,128]{2,1,0:T(8,128)S(1)}, u32[]{:S(2)}, u32[]{:S(2)}) %all-to-all-start.2) | async-done | bytes 524320 | tf_op jit(solution)/shard_map/update/all_to_all | solution.py:752
  115.9 0.7 update.1
  116.7 0.0 copy-start.4
  116.7 3.5 %all-to-all-start.3 = ((f32[32,16,128]{2,1,0:T(8,128)}), f32[32,16,128]{2,1,0:T(8,128)S(1)}, u32[]{:S(2)}, u32[]{:S(2)}) async-start(f32[32,16,128]{2,1,0:T(8,128)} %bitcast.11), calls=%async_computation.3 | async-start | bytes 524288 | tf_op jit(solution)/shard_map/update/all_to_all | solution.py:762
  120.2 0.0 copy-done.4
  120.2 1.0 trace_2.1.second_ref
  121.2 6.5 %all-to-all-done.3.update_ref.value_ref = f32[32,16,128]{2,1,0:T(8,128)S(1)} async-done(((f32[32,16,128]{2,1,0:T(8,128)}), f32[32,16,128]{2,1,0:T(8,128)S(1)}, u32[]{:S(2)}, u32[]{:S(2)}) %all-to-all-start.3) | async-done | bytes 262176 | tf_op jit(solution)/shard_map/update/all_to_all | solution.py:762
  127.7 3.2 %gradient.1 = f32[64,1,1152]{2,1,0:T(1,128)} custom-call(f32[32,16,128]{2,1,0:T(8,128)S(1)} %all-to-all-done.3.update_ref.value_ref, f32[32,16,128]{2,1,0:T(8,128)S(1)} %get-tuple-element.67.refs_8_.squashed_ref, bf16[4,32,16,128]{3,2,1,0:T(8,128)(2,1)S(1)} %copy-done, f32[12,16,128]{2,1,0:T(8,128)S(1)} %collective-permute-done.low_ref.refs_7_.x_low_ref, ...), custom_call_target="tpu_custom_call" | custom-call | flops 14155776 | bytes 1814528 | tf_op jit(solution)/shard_map/gradient/gradient/pallas_call | solution.py:27
  130.9 9.6 %all-to-all-start.4 = ((f32[64,1,1152]{2,1,0:T(1,128)}), f32[64,1,1152]{2,1,0:T(1,128)S(1)}, u32[]{:S(2)}, u32[]{:S(2)}) async-start(f32[64,1,1152]{2,1,0:T(1,128)} %gradient.1), calls=%async_computation.4 | async-start | bytes 589824 | tf_op jit(solution)/shard_map/gradient/all_to_all | solution.py:779
  140.5 0.7 keep.1
  141.2 22.8 %all-to-all-done.4.shares_ref = f32[64,1,1152]{2,1,0:T(1,128)S(1)} async-done(((f32[64,1,1152]{2,1,0:T(1,128)}), f32[64,1,1152]{2,1,0:T(1,128)S(1)}, u32[]{:S(2)}, u32[]{:S(2)}) %all-to-all-start.4) | async-done | bytes 294944 | tf_op jit(solution)/shard_map/gradient/all_to_all | solution.py:779
  164.0 0.7 total.1
  (1 shorter events, 0.0 us)
Async XLA Ops:
  0.6 13.0 %copy-start = (bf16[4,32,16,128]{3,2,1,0:T(8,128)(2,1)S(1)}, bf16[4,32,16,128]{3,2,1,0:T(8,128)(2,1)}, u32[]{:S(2)}) copy-start(bf16[4,32,16,128]{3,2,1,0:T(8,128)(2,1)} %feat_ref.7) | copy-start | bytes 1572868
  0.6 13.0 %copy-start.1 = (f32[1,32,16,128]{3,2,1,0:T(8,128)S(1)}, f32[1,32,16,128]{3,2,1,0:T(8,128)}, u32[]{:S(2)}) copy-start(f32[1,32,16,128]{3,2,1,0:T(8,128)} %param.14) | copy-start | bytes 786436
  2.4 9.6 %collective-permute-start = (f32[12,16,128]{2,1,0:T(8,128)}, f32[12,16,128]{2,1,0:T(8,128)S(1)}, u32[]{:S(2)}, u32[]{:S(2)}) collective-permute-start(f32[12,16,128]{2,1,0:T(8,128)} %get-tuple-element.42), channel_id=1, source_target_pairs={{0,8},{8,16},{16,24},{24,32},{32,40},{40,48},{48,56},{1,9},{9,17},... | collective-permute-start | bytes 294920 | tf_op jit(solution)/shard_map/halo_x/ppermute | solution.py:568
  6.2 7.4 %collective-permute-start.1 = (f32[12,16,128]{2,1,0:T(8,128)}, f32[12,16,128]{2,1,0:T(8,128)S(1)}, u32[]{:S(2)}, u32[]{:S(2)}) collective-permute-start(f32[12,16,128]{2,1,0:T(8,128)} %get-tuple-element.43), channel_id=1, source_target_pairs={{8,0},{16,8},{24,16},{32,24},{40,32},{48,40},{56,48},{9,1},{17,9},... | collective-permute-start | bytes 294920 | tf_op jit(solution)/shard_map/halo_x/ppermute | solution.py:569
  13.6 1.0 copy-start.2
  14.6 16.3 %copy-start.9 = (f32[4,27]{1,0:T(4,128)S(1)}, f32[4,27]{1,0:T(4,128)}, u32[]{:S(2)}) copy-start(f32[4,27]{1,0:T(4,128)} %weight_ref.3) | copy-start | bytes 1300
  15.5 27.7 %collective-permute-start.2 = (bf16[528,128]{1,0:T(8,128)(2,1)}, bf16[528,128]{1,0:T(8,128)(2,1)S(1)}, u32[]{:S(2)}, u32[]{:S(2)}) collective-permute-start(bf16[528,128]{1,0:T(8,128)(2,1)} %get-tuple-element.44), channel_id=1, source_target_pairs={{0,1},{1,2},{2,3},{3,4},{4,5},{5,6},{6,7},{8,9},{9,10},{10,11},{11... | collective-permute-start | bytes 405512 | tf_op jit(solution)/shard_map/halo_y/ppermute | solution.py:568
  28.8 26.0 %collective-permute-start.3 = (bf16[528,128]{1,0:T(8,128)(2,1)S(1)}, bf16[528,128]{1,0:T(8,128)(2,1)S(1)}, u32[]{:S(2)}, u32[]{:S(2)}) collective-permute-start(bf16[528,128]{1,0:T(8,128)(2,1)S(1)} %get-tuple-element.54), channel_id=1, source_target_pairs={{1,0},{2,1},{3,2},{4,3},{5,4},{6,5},{7,6},{9,8},{10,9},{11,10},{12... | collective-permute-start | bytes 405512 | tf_op jit(solution)/shard_map/halo_y/ppermute | solution.py:569
  30.7 0.7 copy-start.7
  30.7 0.7 copy-start.8
  30.7 0.7 copy-start.10
  31.4 8.3 %copy-start.6 = (f32[1,32,16,128]{3,2,1,0:T(8,128)S(1)}, f32[1,32,16,128]{3,2,1,0:T(8,128)}, u32[]{:S(2)}) copy-start(f32[1,32,16,128]{3,2,1,0:T(8,128)} %param.15) | copy-start | bytes 786436
  35.3 4.4 %copy-start.3 = (f32[1,32,16,128]{3,2,1,0:T(8,128)S(1)}, f32[1,32,16,128]{3,2,1,0:T(8,128)}, u32[]{:S(2)}) copy-start(f32[1,32,16,128]{3,2,1,0:T(8,128)} %param.16) | copy-start | bytes 786436
  35.3 4.5 %copy-start.5 = (f32[1,32,16,128]{3,2,1,0:T(8,128)S(1)}, f32[1,32,16,128]{3,2,1,0:T(8,128)}, u32[]{:S(2)}) copy-start(f32[1,32,16,128]{3,2,1,0:T(8,128)} %param.13) | copy-start | bytes 786436
  35.3 20.1 %all-to-all-start = ((f32[32,16,128]{2,1,0:T(8,128)}), f32[32,16,128]{2,1,0:T(8,128)S(1)}, u32[]{:S(2)}, u32[]{:S(2)}) async-start(f32[32,16,128]{2,1,0:T(8,128)} %get-tuple-element.56), calls=%async_computation | async-start | bytes 524288 | tf_op jit(solution)/shard_map/raw/all_to_all | solution.py:667
  71.2 20.9 %collective-permute-start.4 = (bf16[384,128]{1,0:T(8,128)(2,1)S(1)}, bf16[384,128]{1,0:T(8,128)(2,1)S(1)}, u32[]{:S(2)}, u32[]{:S(2)}) collective-permute-start(bf16[384,128]{1,0:T(8,128)(2,1)S(1)} %get-tuple-element.65), channel_id=1, source_target_pairs={{0,1},{1,2},{2,3},{3,4},{4,5},{5,6},{6,7},{8,9},{9,10},{10,11},{11... | collective-permute-start | bytes 294920 | tf_op jit(solution)/shard_map/halo_2/ppermute | solution.py:568
  81.3 18.9 %collective-permute-start.5 = (bf16[384,128]{1,0:T(8,128)(2,1)S(1)}, bf16[384,128]{1,0:T(8,128)(2,1)S(1)}, u32[]{:S(2)}, u32[]{:S(2)}) collective-permute-start(bf16[384,128]{1,0:T(8,128)(2,1)S(1)} %get-tuple-element.66), channel_id=1, source_target_pairs={{1,0},{2,1},{3,2},{4,3},{5,4},{6,5},{7,6},{9,8},{10,9},{11,10},{12... | collective-permute-start | bytes 294920 | tf_op jit(solution)/shard_map/halo_2/ppermute | solution.py:569
  82.6 9.5 %collective-permute-start.6 = (f32[8,16,128]{2,1,0:T(8,128)S(1)}, f32[8,16,128]{2,1,0:T(8,128)S(1)}, u32[]{:S(2)}, u32[]{:S(2)}) collective-permute-start(f32[8,16,128]{2,1,0:T(8,128)S(1)} %get-tuple-element.68), channel_id=1, source_target_pairs={{0,8},{8,16},{16,24},{24,32},{32,40},{40,48},{48,56},{1,9},{9,17},... | collective-permute-start | bytes 196616 | tf_op jit(solution)/shard_map/halo_2/ppermute | solution.py:568
  84.6 7.6 %collective-permute-start.7 = (f32[8,16,128]{2,1,0:T(8,128)S(1)}, f32[8,16,128]{2,1,0:T(8,128)S(1)}, u32[]{:S(2)}, u32[]{:S(2)}) collective-permute-start(f32[8,16,128]{2,1,0:T(8,128)S(1)} %get-tuple-element.69), channel_id=1, source_target_pairs={{8,0},{16,8},{24,16},{32,24},{40,32},{48,40},{56,48},{9,1},{17,9},... | collective-permute-start | bytes 196616 | tf_op jit(solution)/shard_map/halo_2/ppermute | solution.py:569
  102.1 13.8 %all-to-all-start.2 = ((f32[64,16,128]{2,1,0:T(8,128)}), f32[64,16,128]{2,1,0:T(8,128)S(1)}, u32[]{:S(2)}, u32[]{:S(2)}) async-start(f32[64,16,128]{2,1,0:T(8,128)} %bitcast.9), calls=%async_computation.2 | async-start | bytes 1048576 | tf_op jit(solution)/shard_map/update/all_to_all | solution.py:752
  116.7 3.6 %copy-start.4 = (f32[32,16,128]{2,1,0:T(8,128)S(1)}, f32[32,16,128]{2,1,0:T(8,128)}, u32[]{:S(2)}) copy-start(f32[32,16,128]{2,1,0:T(8,128)} %get-tuple-element.71.fwd_ref) | copy-start | bytes 786436
  116.7 11.0 %all-to-all-start.3 = ((f32[32,16,128]{2,1,0:T(8,128)}), f32[32,16,128]{2,1,0:T(8,128)S(1)}, u32[]{:S(2)}, u32[]{:S(2)}) async-start(f32[32,16,128]{2,1,0:T(8,128)} %bitcast.11), calls=%async_computation.3 | async-start | bytes 524288 | tf_op jit(solution)/shard_map/update/all_to_all | solution.py:762
  130.9 33.2 %all-to-all-start.4 = ((f32[64,1,1152]{2,1,0:T(1,128)}), f32[64,1,1152]{2,1,0:T(1,128)S(1)}, u32[]{:S(2)}, u32[]{:S(2)}) async-start(f32[64,1,1152]{2,1,0:T(1,128)} %gradient.1), calls=%async_computation.4 | async-start | bytes 589824 | tf_op jit(solution)/shard_map/gradient/all_to_all | solution.py:779

commit v8 on v7

--- a/solution.py
+++ b/solution.py
@@ -66,27 +66,25 @@
 
 def pack_x_body(feat_ref, fwd_ref, back_ref, up_ref, down_ref, edge_ref, sems):
     channels, size_x = feat_ref.shape[:2]
-    copies = []
+    pairs = []
     for n, (out_ref, start, row) in enumerate(
         ((up_ref, size_x - 4, size_x - 1), (down_ref, 0, 0))
     ):
-        pairs = [
+        pairs += [
+            (feat_ref.at[:, row], edge_ref.at[n]),
             (fwd_ref.at[pl.ds(start, 4)], out_ref.at[pl.ds(0, 4)]),
             (back_ref.at[pl.ds(start, 4)], out_ref.at[pl.ds(4, 4)]),
         ]
-        for c in range(channels):
-            pairs.append((feat_ref.at[c, row], edge_ref.at[n * channels + c]))
-        for m, (source, target) in enumerate(pairs):
-            copies.append(
-                pltpu.make_async_copy(source, target, sems.at[n * (2 + channels) + m])
-            )
+    copies = [
+        pltpu.make_async_copy(source, target, sems.at[n])
+        for n, (source, target) in enumerate(pairs)
+    ]
     for copy in copies:
         copy.start()
     for copy in copies:
         copy.wait()
-    for c in range(channels):
-        up_ref[8 + c] = edge_ref[c].astype(F32)
-        down_ref[8 + c] = edge_ref[channels + c].astype(F32)
+    up_ref[8 : 8 + channels] = edge_ref[0].astype(F32)
+    down_ref[8 : 8 + channels] = edge_ref[1].astype(F32)
 
 
 def wave_rows(size_x):
@@ -130,23 +128,32 @@
         edge_ref[part, 4 + near : 6 + near] += low_ref[:, 4 * q + 2 : 4 * q + 4]
 
 
-def pack_y_body(
-    feat_ref, fwd_ref, back_ref, low_ref, high_ref, up_ref, down_ref, plane_ref, edge_ref, rest_ref
-):
+def pack_y_body(feat_ref, fwd_ref, back_ref, up_ref, down_ref, plane_ref, edge_ref, rest_ref):
     channels, size_x, size_y, depth = feat_ref.shape
-    row = lax.broadcasted_iota(jnp.int32, (16, depth), 0)
-    tails = [jnp.zeros((16, depth), F32), jnp.zeros((16, depth), F32)]
+    first = channels * size_x
     for c in range(channels):
         plane_ref[...] = feat_ref[c].astype(F32)
-        for n, (out_ref, y) in enumerate(((up_ref, size_y - 1), (down_ref, 0))):
+        for out_ref, y in ((up_ref, size_y - 1), (down_ref, 0)):
             out_ref[c * size_x : (c + 1) * size_x] = plane_ref[:, y, :].astype(BF16)
-            tails[n] = jnp.where(row == 2 * c, low_ref[8 + c, y : y + 1, :], tails[n])
-            tails[n] = jnp.where(row == 2 * c + 1, high_ref[8 + c, y : y + 1, :], tails[n])
+    for out_ref, upward in ((up_ref, True), (down_ref, False)):
+        out_ref[first : first + 16] = jnp.zeros((16, depth), BF16)
+        pack_waves(fwd_ref, back_ref, upward, out_ref, first + 16, edge_ref, rest_ref)
+
+
+def corners_body(up_in_ref, down_in_ref, low_ref, high_ref, up_ref, down_ref):
+    size_y, depth = low_ref.shape[1:]
+    channels = low_ref.shape[0] - 8
+    size_x = (up_ref.shape[0] - 16) // (channels + 12)
     first = channels * size_x
-    for tail, out_ref in zip(tails, (up_ref, down_ref)):
+    row = lax.broadcasted_iota(jnp.int32, (16, depth), 0)
+    for in_ref, out_ref, y in ((up_in_ref, up_ref, size_y - 1), (down_in_ref, down_ref, 0)):
+        out_ref[0:first] = in_ref[0:first]
+        out_ref[first + 16 :] = in_ref[first + 16 :]
+        tail = jnp.zeros((16, depth), F32)
+        for c in range(channels):
+            tail = jnp.where(row == 2 * c, low_ref[8 + c, y : y + 1, :], tail)
+            tail = jnp.where(row == 2 * c + 1, high_ref[8 + c, y : y + 1, :], tail)
         out_ref[first : first + 16] = tail.astype(BF16)
-    pack_waves(fwd_ref, back_ref, True, up_ref, first + 16, edge_ref, rest_ref)
-    pack_waves(fwd_ref, back_ref, False, down_ref, first + 16, edge_ref, rest_ref)
 
 
 def fill_features(ext_ref, feat_ref, low_ref, high_ref):
@@ -271,37 +278,35 @@
     trace_ref[...] = total[RDEPTH : RDEPTH + 1, :]
 
 
-def trace_body(plane_y, fwd_ref, place_ref, receivers_ref, trace_ref):
-    size_x, size_y, _ = fwd_ref.shape
-    sample(fwd_ref, receiver_hits(receivers_ref, place_ref, plane_y, size_x, size_y), trace_ref)
+def trace_body(plane_y, first_ref, second_ref, place_ref, receivers_ref, *out_refs):
+    size_x, size_y, _ = first_ref.shape
+    hit = receiver_hits(receivers_ref, place_ref, plane_y, size_x, size_y)
+    for fwd_ref, trace_ref in zip((first_ref, second_ref), out_refs):
+        sample(fwd_ref, hit, trace_ref)
 
 
 def inner_body(moment, plane_y, *refs):
     fwd_ref, back_ref, fwd_old_ref, back_old_ref = refs[:4]
-    place_ref, receivers_ref, residual_ref = refs[4:7]
-    refs = refs[7:]
-    if moment == 0:
-        x_low_ref, x_high_ref = refs[:2]
-        refs = refs[2:]
-    fwd_ahead_ref, back_ahead_ref, lap_fwd_ref, lap_back_ref = refs[:4]
-    refs = refs[4:]
-    if moment == 1:
-        trace_ref = refs[0]
-        refs = refs[1:]
-    x_ref, y_ref, inject_ref = refs
     size_x, size_y, depth = fwd_ref.shape
     rows = 4
-    hit = receiver_hits(receivers_ref, place_ref, plane_y, size_x, size_y)
-    injected = jnp.where(
-        lax.broadcasted_iota(jnp.int32, (depth, hit.shape[1]), 0) == RDEPTH,
-        residual_ref[0, moment : moment + 1, :],
-        0.0,
-    )
-    inject_ref[...] = exact_product(split3(injected), hit, ((1,), (1,)), False).reshape(
-        size_x, size_y, depth
-    )
-    if moment == 1:
-        sample(fwd_ref, hit, trace_ref)
+    if moment == 0:
+        place_ref, receivers_ref, residual_ref, x_low_ref, x_high_ref = refs[4:9]
+        fwd_ahead_ref, back_ahead_ref, lap_fwd_ref, lap_back_ref, later_ref = refs[9:14]
+        x_ref, y_ref, inject_ref = refs[14:]
+        hit = receiver_hits(receivers_ref, place_ref, plane_y, size_x, size_y)
+        for n, out_ref in enumerate((inject_ref, later_ref)):
+            injected = jnp.where(
+                lax.broadcasted_iota(jnp.int32, (depth, hit.shape[1]), 0) == RDEPTH,
+                residual_ref[0, n : n + 1, :],
+                0.0,
+            )
+            out_ref[...] = exact_product(split3(injected), hit, ((1,), (1,)), False).reshape(
+                size_x, size_y, depth
+            )
+    else:
+        inject_ref = refs[4]
+        fwd_ahead_ref, back_ahead_ref, lap_fwd_ref, lap_back_ref = refs[5:9]
+        x_ref, y_ref = refs[9:]
     zero_x = jnp.zeros((4, size_y, depth), F32)
     y_ref[:, 0:8] = jnp.zeros((size_x, 8, depth), F32)
     y_ref[:, 8 + size_y : 16 + size_y] = jnp.zeros((size_x, 8, depth), F32)
@@ -609,14 +614,12 @@
             (features, fwd_now, back_now),
             [pl.BlockSpec(memory_space=pltpu.HBM)] * 3,
             scratch=[
-                pltpu.VMEM((2 * channels, size_y, depth), BF16),
-                pltpu.SemaphoreType.DMA((2 * (2 + channels),)),
+                pltpu.VMEM((2, channels, size_y, depth), BF16),
+                pltpu.SemaphoreType.DMA((6,)),
             ],
             name="pack_x",
             limit=VMEM_WHOLE,
         )
-    with jax.named_scope("halo_x"):
-        x_low, x_high = neighbours(x_up, x_down, "gx")
     packing = [
         pltpu.VMEM((size_x, 8, depth), F32),
         pltpu.VMEM((size_x // 4, 16, depth), F32),
@@ -626,10 +629,20 @@
         y_up, y_down = call(
             pack_y_body,
             [y_shape, y_shape],
-            (features, fwd_now, back_now, x_low, x_high),
-            [VM] * 5,
+            (features, fwd_now, back_now),
+            [VM] * 3,
             scratch=[pltpu.VMEM(grid, F32)] + packing,
             name="pack_y",
+        )
+    with jax.named_scope("halo_x"):
+        x_low, x_high = neighbours(x_up, x_down, "gx")
+    with jax.named_scope("corners"):
+        y_up, y_down = call(
+            corners_body,
+            [y_shape, y_shape],
+            (y_up, y_down, x_low, x_high),
+            [VM] * 4,
+            name="corners",
         )
     with jax.named_scope("halo_y"):
         y_low, y_high = neighbours(y_up, y_down, "gy")
@@ -645,7 +658,7 @@
     with jax.named_scope("inner_1"):
         inner_1 = call(
             functools.partial(inner_body, 0, plane_y),
-            [full] * 4,
+            [full] * 5,
             (fwd_now, back_now, fwd_prev, back_prev, place, receivers, residual, x_low, x_high),
             [VM] * 4 + [SM] + [VM] * 4,
             scratch=inner_scratch,
@@ -693,7 +706,7 @@
             + [shape(8, size_y, depth)] * 2
             + [shape(wave_rows(size_x), depth, dtype=BF16)] * 2,
             (
-                *inner_1,
+                *inner_1[:4],
                 y_low,
                 y_high,
                 place,
@@ -708,12 +721,12 @@
         x_low_2, x_high_2 = neighbours(x_up, x_down, "gx")
         y_low_2, y_high_2 = neighbours(y_up, y_down, "gy")
     with jax.named_scope("inner_2"):
-        fwd_ahead, back_ahead, lap_fwd, lap_back, trace_1 = call(
+        fwd_ahead, back_ahead, lap_fwd, lap_back = call(
             functools.partial(inner_body, 1, plane_y),
-            [full] * 4 + [shape(1, count)],
-            (fwd_1, back_1, fwd_now, back_now, place, receivers, residual),
-            [VM] * 4 + [SM] + [VM] * 2,
-            scratch=inner_scratch,
+            [full] * 4,
+            (fwd_1, back_1, fwd_now, back_now, inner_1[4]),
+            [VM] * 5,
+            scratch=inner_scratch[:2],
             flops=work,
             name="inner_2",
         )
@@ -741,12 +754,12 @@
             name="step_2",
         )
     with jax.named_scope("traces"):
-        trace_2 = call(
+        trace_1, trace_2 = call(
             functools.partial(trace_body, plane_y),
-            [shape(1, count)],
-            (fwd_2, place, receivers),
-            [VM, SM, VM],
-            name="trace_2",
+            [shape(1, count)] * 2,
+            (fwd_1, fwd_2, place, receivers),
+            [VM, VM, SM, VM],
+            name="traces",
         )
     with jax.named_scope("update"):
         sums = lax.all_to_all(

time: 166 us -> 164 us (0.988)
    pallas_call x14 -> x15, Pallas kernels: 23.8 us -> 23.1 us  [call(): pl.pallas_call(body, out_shape=outs[0] if single else tuple(outs), in_spe...]
  transfers between devices with their start and end apart: 12 -> 12, of which waited for: 7 -> 6; matrix products, arithmetic and copies ran while one was open for 0% -> 0% of each run, Pallas kernels for 8% -> 8%
where the time goes in v8:
time: 164 us
  starting transfers between devices  61.6 us (38%)
  waiting for transfers between devices  59.7 us (36%)
  Pallas kernels  23.1 us (14%)
  blocking collectives  14.6 us (9%)
  local copies, waits for them, and re-layouts  2.27 us (1%)
  between operations  2.21 us (1%)
    ppermute x4, starting transfers between devices, neighbours(): low = lax.ppermute(up, axis, [(i, i + 1) for i in range(count - 1)])  29.1 us
    pallas_call x15, Pallas kernels, call(): pl.pallas_call(body, out_shape=outs[0] if single else tuple(outs), in_spe...  23.1 us
    all_to_all x1, waiting for transfers between devices, per_device(): shares = lax.all_to_all(share, ('gx', 'gy'), 0, 0, tiled=True)  22.8 us
    ppermute x4, waiting for transfers between devices, neighbours(): high = lax.ppermute(down, axis, [(i + 1, i) for i in range(count - 1)])  21 us
    all_to_all x1, blocking collectives, per_device(): lax.all_to_all(raw.reshape(shots * each, depth), 'shot', 0, 0, tiled=True)  14.6 us
    ppermute x4, starting transfers between devices, neighbours(): high = lax.ppermute(down, axis, [(i + 1, i) for i in range(count - 1)])  11.4 us
    all_to_all x1, starting transfers between devices, per_device(): shares = lax.all_to_all(share, ('gx', 'gy'), 0, 0, tiled=True)  9.64 us
    all_to_all x1, waiting for transfers between devices, per_device(): lax.all_to_all(sums.reshape(shots * 2 * rows, size_y, depth), 'shot', 0,...  9.62 us
  transfers between devices with their start and end apart: 12, of which 6 were waited for; matrix products, arithmetic and copies ran while one was open for 0% of the time, Pallas kernels for 8%

profile of v8, /device:TPU:32, one launch (start us, length us, event | category | flops | bytes accessed | tf_op | source)
XLA Modules:
  0.0 163.6 jit_solution(11220226739438092725)
XLA Ops:
  0.6 0.0 copy-start
  0.6 0.0 copy-start.1
  0.7 1.6 %pack_x.1 = (f32[12,16,128]{2,1,0:T(8,128)}, f32[12,16,128]{2,1,0:T(8,128)}) custom-call(bf16[4,32,16,128]{3,2,1,0:T(8,128)(2,1)} %feat_ref.7, f32[32,16,128]{2,1,0:T(8,128)} %bitcast.12, f32[32,16,128]{2,1,0:T(8,128)} %bitcast.16), custom_call_target="tpu_custom_call" | custom-call | flops 1000000 | bytes 1245184 | tf_op jit(solution)/shard_map/pack_x/pack_x/pallas_call | solution.py:27
  2.3 3.8 %collective-permute-start = (f32[12,16,128]{2,1,0:T(8,128)}, f32[12,16,128]{2,1,0:T(8,128)S(1)}, u32[]{:S(2)}, u32[]{:S(2)}) collective-permute-start(f32[12,16,128]{2,1,0:T(8,128)} %get-tuple-element.48), channel_id=1, source_target_pairs={{0,8},{8,16},{16,24},{24,32},{32,40},{40,48},{48,56},{1,9},{9,17},... | collective-permute-start | bytes 294920 | tf_op jit(solution)/shard_map/halo_x/ppermute | solution.py:573
  6.1 4.9 %collective-permute-start.1 = (f32[12,16,128]{2,1,0:T(8,128)}, f32[12,16,128]{2,1,0:T(8,128)S(1)}, u32[]{:S(2)}, u32[]{:S(2)}) collective-permute-start(f32[12,16,128]{2,1,0:T(8,128)} %get-tuple-element.49), channel_id=1, source_target_pairs={{8,0},{16,8},{24,16},{32,24},{40,32},{48,40},{56,48},{9,1},{17,9},... | collective-permute-start | bytes 294920 | tf_op jit(solution)/shard_map/halo_x/ppermute | solution.py:574
  11.0 0.0 copy-done
  11.0 0.0 copy-done.1
  11.0 0.0 copy-start.2
  11.0 0.9 copy-done.2
  12.0 0.3 pack_y.1
  12.3 0.0 collective-permute-done.low_ref.refs_7_.x_low_ref
  12.3 1.2 collective-permute-done.1.high_ref.refs_8_.x_high_ref
  13.5 0.0 copy-start.11
  13.5 0.7 corners.1
  14.2 13.3 %collective-permute-start.2 = (bf16[528,128]{1,0:T(8,128)(2,1)}, bf16[528,128]{1,0:T(8,128)(2,1)S(1)}, u32[]{:S(2)}, u32[]{:S(2)}) collective-permute-start(bf16[528,128]{1,0:T(8,128)(2,1)} %get-tuple-element.50), channel_id=1, source_target_pairs={{0,1},{1,2},{2,3},{3,4},{4,5},{5,6},{6,7},{8,9},{9,10},{10,11},{11... | collective-permute-start | bytes 405512 | tf_op jit(solution)/shard_map/halo_y/ppermute | solution.py:573
  27.5 1.3 collective-permute-start.3
  29.4 0.0 copy-start.9
  29.4 0.0 copy-start.10
  29.4 0.0 copy-start.12
  29.4 0.1 pad_add_fusion.refs_4_.refs_6_.place_ref
  29.5 0.0 copy-done.11
  29.5 0.6 copy-done.9
  30.1 0.0 copy-done.10
  30.1 0.0 copy-done.12
  30.1 0.0 copy-start.8
  30.1 3.9 %conv.1 = (f32[32,16,128]{2,1,0:T(8,128)}, s32[1,512]{1,0:T(1,128)S(1)}, f32[1,2,512]{2,1,0:T(2,128)}, f32[1,2]{1,0:T(1,128)S(1)}) custom-call(bf16[4,32,16,128]{3,2,1,0:T(8,128)(2,1)S(1)} %copy-done, f32[12,16,128]{2,1,0:T(8,128)S(1)} %collective-permute-done.low_ref.refs_7_.x_low_ref, ...), custom_call_target="tpu_custom_call" | custom-call | flops 14155776 | bytes 995776 | tf_op jit(solution)/shard_map/conv/conv/pallas_call | solution.py:27
  34.0 0.0 copy-start.3
  34.0 4.4 %all-to-all-start = ((f32[32,16,128]{2,1,0:T(8,128)}), f32[32,16,128]{2,1,0:T(8,128)S(1)}, u32[]{:S(2)}, u32[]{:S(2)}) async-start(f32[32,16,128]{2,1,0:T(8,128)} %get-tuple-element.63), calls=%async_computation | async-start | bytes 524288 | tf_op jit(solution)/shard_map/raw/all_to_all | solution.py:680
  38.5 0.0 copy-done.8
  38.5 0.0 copy-done.3
  38.5 0.0 copy-done.7
  38.5 3.8 %inner_1.1 = (f32[32,16,128]{2,1,0:T(8,128)S(1)}, f32[32,16,128]{2,1,0:T(8,128)S(1)}, f32[32,16,128]{2,1,0:T(8,128)S(1)}, f32[32,16,128]{2,1,0:T(8,128)S(1)}, f32[32,16,128]{2,1,0:T(8,128)S(1)}) custom-call(f32[32,16,128]{2,1,0:T(8,128)S(1)} %bitcast.14, f32[32,16,128]{2,1,0:T(8,128)S(1)} %bitcast.18, f32[32,16,128]{2,1,0:T(8,128)S(1)} %bitcast.23, ...), custom_call_target="tpu_custom_call" | custom-call | flops 3932160 | bytes 2562060 | tf_op jit(solution)/shard_map/inner_1/inner_1/pallas_call | solution.py:27
  42.3 0.0 copy-start.4
  42.3 0.7 copy-done.4
  43.0 0.0 collective-permute-done.2.low_ref.refs_4_.y_low_ref
  43.0 10.4 %collective-permute-done.3.high_ref.refs_5_.y_high_ref = bf16[528,128]{1,0:T(8,128)(2,1)S(1)} collective-permute-done((bf16[528,128]{1,0:T(8,128)(2,1)S(1)}, bf16[528,128]{1,0:T(8,128)(2,1)S(1)}, u32[]{:S(2)}, u32[]{:S(2)}) %collective-permute-start.3) | collective-permute-done | bytes 135200 | tf_op jit(solution)/shard_map/halo_y/ppermute | solution.py:574
  53.4 0.7 conv_edge.1.rims_ref
  54.2 0.0 all-to-all-done
  54.2 0.0 copy-start.5
  54.2 14.6 %all_to_all.26.refs_8_ = f32[8,128,128]{2,1,0:T(8,128)S(1)} all-to-all(f32[8,128,128]{2,1,0:T(8,128)S(1)} %raw.1), channel_id=1, replica_groups=mesh['shot'=8,'gx'=8,'gy'=8] {'shot'}, dimensions={0} | all-to-all | bytes 1048576 | tf_op jit(solution)/shard_map/raw/all_to_all | solution.py:699
  68.9 0.0 copy-done.5
  68.9 1.2 step_1.1
  70.0 10.1 %collective-permute-start.4 = (bf16[384,128]{1,0:T(8,128)(2,1)S(1)}, bf16[384,128]{1,0:T(8,128)(2,1)S(1)}, u32[]{:S(2)}, u32[]{:S(2)}) collective-permute-start(bf16[384,128]{1,0:T(8,128)(2,1)S(1)} %get-tuple-element.71), channel_id=1, source_target_pairs={{0,1},{1,2},{2,3},{3,4},{4,5},{5,6},{6,7},{8,9},{9,10},{10,11},{11... | collective-permute-start | bytes 294920 | tf_op jit(solution)/shard_map/halo_2/ppermute | solution.py:573
  80.2 1.3 collective-permute-start.5
  81.5 1.9 %collective-permute-start.6 = (f32[8,16,128]{2,1,0:T(8,128)S(1)}, f32[8,16,128]{2,1,0:T(8,128)S(1)}, u32[]{:S(2)}, u32[]{:S(2)}) collective-permute-start(f32[8,16,128]{2,1,0:T(8,128)S(1)} %get-tuple-element.74), channel_id=1, source_target_pairs={{0,8},{8,16},{16,24},{24,32},{32,40},{40,48},{48,56},{1,9},{9,17},... | collective-permute-start | bytes 196616 | tf_op jit(solution)/shard_map/halo_2/ppermute | solution.py:573
  83.4 3.9 %collective-permute-start.7 = (f32[8,16,128]{2,1,0:T(8,128)S(1)}, f32[8,16,128]{2,1,0:T(8,128)S(1)}, u32[]{:S(2)}, u32[]{:S(2)}) collective-permute-start(f32[8,16,128]{2,1,0:T(8,128)S(1)} %get-tuple-element.75), channel_id=1, source_target_pairs={{8,0},{16,8},{24,16},{32,24},{40,32},{48,40},{56,48},{9,1},{17,9},... | collective-permute-start | bytes 196616 | tf_op jit(solution)/shard_map/halo_2/ppermute | solution.py:574
  87.3 2.3 %inner_2.1 = (f32[32,16,128]{2,1,0:T(8,128)S(1)}, f32[32,16,128]{2,1,0:T(8,128)S(1)}, f32[32,16,128]{2,1,0:T(8,128)S(1)}, f32[32,16,128]{2,1,0:T(8,128)S(1)}) custom-call(f32[32,16,128]{2,1,0:T(8,128)S(1)} %get-tuple-element.64.refs_0_.first_ref, f32[32,16,128]{2,1,0:T(8,128)S(1)} %get-tuple-element.65.refs_1_.refs_12_, f32[32,16,128]{2,1,0:T(8,128)S(1)} %bitcast.15, ...), custom_call_target="tpu_custom_call" | custom-call | flops 3932160 | bytes 2359296 | tf_op jit(solution)/shard_map/inner_2/inner_2/pallas_call | solution.py:27
  89.7 0.0 collective-permute-done.6.refs_9_
  89.7 0.0 collective-permute-done.7.refs_10_
  89.7 0.0 collective-permute-done.4.refs_4_
  89.7 9.3 %collective-permute-done.5.refs_5_ = bf16[384,128]{1,0:T(8,128)(2,1)S(1)} collective-permute-done((bf16[384,128]{1,0:T(8,128)(2,1)S(1)}, bf16[384,128]{1,0:T(8,128)(2,1)S(1)}, u32[]{:S(2)}, u32[]{:S(2)}) %collective-permute-start.5) | collective-permute-done | bytes 98336 | tf_op jit(solution)/shard_map/halo_2/ppermute | solution.py:574
  99.0 2.0 %step_2.1 = (f32[32,16,128]{2,1,0:T(8,128)}, f32[32,16,128]{2,1,0:T(8,128)}, f32[8,8,16,128]{3,2,1,0:T(8,128)}) custom-call(f32[32,16,128]{2,1,0:T(8,128)S(1)} %get-tuple-element.67.refs_0_, f32[32,16,128]{2,1,0:T(8,128)S(1)} %get-tuple-element.68.refs_1_, f32[32,16,128]{2,1,0:T(8,128)S(1)} %get-tuple-element.69.refs_2_, ...), custom_call_target="tpu_custom_call" | custom-call | flops 1000000 | bytes 3211284 | tf_op jit(solution)/shard_map/step_2/step_2/pallas_call | solution.py:27
  101.0 3.5 %all-to-all-start.2 = ((f32[64,16,128]{2,1,0:T(8,128)}), f32[64,16,128]{2,1,0:T(8,128)S(1)}, u32[]{:S(2)}, u32[]{:S(2)}) async-start(f32[64,16,128]{2,1,0:T(8,128)} %bitcast.9), calls=%async_computation.2 | async-start | bytes 1048576 | tf_op jit(solution)/shard_map/update/all_to_all | solution.py:765
  105.1 9.6 %all-to-all-done.2 = f32[64,16,128]{2,1,0:T(8,128)S(1)} async-done(((f32[64,16,128]{2,1,0:T(8,128)}), f32[64,16,128]{2,1,0:T(8,128)S(1)}, u32[]{:S(2)}, u32[]{:S(2)}) %all-to-all-start.2) | async-done | bytes 524320 | tf_op jit(solution)/shard_map/update/all_to_all | solution.py:765
  114.7 0.7 update.1
  115.5 3.5 %all-to-all-start.3 = ((f32[32,16,128]{2,1,0:T(8,128)}), f32[32,16,128]{2,1,0:T(8,128)S(1)}, u32[]{:S(2)}, u32[]{:S(2)}) async-start(f32[32,16,128]{2,1,0:T(8,128)} %bitcast.11), calls=%async_computation.3 | async-start | bytes 524288 | tf_op jit(solution)/shard_map/update/all_to_all | solution.py:775
  119.0 0.0 copy-done.6
  119.1 1.2 traces.1
  120.2 6.3 %all-to-all-done.3.update_ref.value_ref = f32[32,16,128]{2,1,0:T(8,128)S(1)} async-done(((f32[32,16,128]{2,1,0:T(8,128)}), f32[32,16,128]{2,1,0:T(8,128)S(1)}, u32[]{:S(2)}, u32[]{:S(2)}) %all-to-all-start.3) | async-done | bytes 262176 | tf_op jit(solution)/shard_map/update/all_to_all | solution.py:775
  126.5 3.2 %gradient.1 = f32[64,1,1152]{2,1,0:T(1,128)} custom-call(f32[32,16,128]{2,1,0:T(8,128)S(1)} %all-to-all-done.3.update_ref.value_ref, f32[32,16,128]{2,1,0:T(8,128)S(1)} %get-tuple-element.73.refs_8_.squashed_ref, bf16[4,32,16,128]{3,2,1,0:T(8,128)(2,1)S(1)} %copy-done, f32[12,16,128]{2,1,0:T(8,128)S(1)} %collective-permute-done.low_ref.refs_7_.x_low_ref, ...), custom_call_target="tpu_custom_call" | custom-call | flops 14155776 | bytes 1814528 | tf_op jit(solution)/shard_map/gradient/gradient/pallas_call | solution.py:27
  129.7 9.6 %all-to-all-start.4 = ((f32[64,1,1152]{2,1,0:T(1,128)}), f32[64,1,1152]{2,1,0:T(1,128)S(1)}, u32[]{:S(2)}, u32[]{:S(2)}) async-start(f32[64,1,1152]{2,1,0:T(1,128)} %gradient.1), calls=%async_computation.4 | async-start | bytes 589824 | tf_op jit(solution)/shard_map/gradient/all_to_all | solution.py:792
  139.3 0.7 keep.1
  140.1 22.8 %all-to-all-done.4.shares_ref = f32[64,1,1152]{2,1,0:T(1,128)S(1)} async-done(((f32[64,1,1152]{2,1,0:T(1,128)}), f32[64,1,1152]{2,1,0:T(1,128)S(1)}, u32[]{:S(2)}, u32[]{:S(2)}) %all-to-all-start.4) | async-done | bytes 294944 | tf_op jit(solution)/shard_map/gradient/all_to_all | solution.py:792
  162.9 0.7 total.1
  (3 shorter events, 0.0 us)
Async XLA Ops:
  0.6 10.4 %copy-start = (bf16[4,32,16,128]{3,2,1,0:T(8,128)(2,1)S(1)}, bf16[4,32,16,128]{3,2,1,0:T(8,128)(2,1)}, u32[]{:S(2)}) copy-start(bf16[4,32,16,128]{3,2,1,0:T(8,128)(2,1)} %feat_ref.7) | copy-start | bytes 1572868
  0.6 10.4 %copy-start.1 = (f32[1,32,16,128]{3,2,1,0:T(8,128)S(1)}, f32[1,32,16,128]{3,2,1,0:T(8,128)}, u32[]{:S(2)}) copy-start(f32[1,32,16,128]{3,2,1,0:T(8,128)} %param.14) | copy-start | bytes 786436
  2.3 10.0 %collective-permute-start = (f32[12,16,128]{2,1,0:T(8,128)}, f32[12,16,128]{2,1,0:T(8,128)S(1)}, u32[]{:S(2)}, u32[]{:S(2)}) collective-permute-start(f32[12,16,128]{2,1,0:T(8,128)} %get-tuple-element.48), channel_id=1, source_target_pairs={{0,8},{8,16},{16,24},{24,32},{32,40},{40,48},{48,56},{1,9},{9,17},... | collective-permute-start | bytes 294920 | tf_op jit(solution)/shard_map/halo_x/ppermute | solution.py:573
  6.1 7.4 %collective-permute-start.1 = (f32[12,16,128]{2,1,0:T(8,128)}, f32[12,16,128]{2,1,0:T(8,128)S(1)}, u32[]{:S(2)}, u32[]{:S(2)}) collective-permute-start(f32[12,16,128]{2,1,0:T(8,128)} %get-tuple-element.49), channel_id=1, source_target_pairs={{8,0},{16,8},{24,16},{32,24},{40,32},{48,40},{56,48},{9,1},{17,9},... | collective-permute-start | bytes 294920 | tf_op jit(solution)/shard_map/halo_x/ppermute | solution.py:574
  11.0 1.0 copy-start.2
  13.5 16.0 %copy-start.11 = (f32[4,27]{1,0:T(4,128)S(1)}, f32[4,27]{1,0:T(4,128)}, u32[]{:S(2)}) copy-start(f32[4,27]{1,0:T(4,128)} %weight_ref.3) | copy-start | bytes 1300
  14.2 28.8 %collective-permute-start.2 = (bf16[528,128]{1,0:T(8,128)(2,1)}, bf16[528,128]{1,0:T(8,128)(2,1)S(1)}, u32[]{:S(2)}, u32[]{:S(2)}) collective-permute-start(bf16[528,128]{1,0:T(8,128)(2,1)} %get-tuple-element.50), channel_id=1, source_target_pairs={{0,1},{1,2},{2,3},{3,4},{4,5},{5,6},{6,7},{8,9},{9,10},{10,11},{11... | collective-permute-start | bytes 405512 | tf_op jit(solution)/shard_map/halo_y/ppermute | solution.py:573
  27.5 26.0 %collective-permute-start.3 = (bf16[528,128]{1,0:T(8,128)(2,1)S(1)}, bf16[528,128]{1,0:T(8,128)(2,1)S(1)}, u32[]{:S(2)}, u32[]{:S(2)}) collective-permute-start(bf16[528,128]{1,0:T(8,128)(2,1)S(1)} %get-tuple-element.61), channel_id=1, source_target_pairs={{1,0},{2,1},{3,2},{4,3},{5,4},{6,5},{7,6},{9,8},{10,9},{11,10},{12... | collective-permute-start | bytes 405512 | tf_op jit(solution)/shard_map/halo_y/ppermute | solution.py:574
  29.4 0.7 copy-start.9
  29.4 0.7 copy-start.10
  29.4 0.7 copy-start.12
  30.1 8.3 %copy-start.8 = (f32[1,32,16,128]{3,2,1,0:T(8,128)S(1)}, f32[1,32,16,128]{3,2,1,0:T(8,128)}, u32[]{:S(2)}) copy-start(f32[1,32,16,128]{3,2,1,0:T(8,128)} %param.15) | copy-start | bytes 786436
  34.0 4.4 %copy-start.3 = (f32[1,32,16,128]{3,2,1,0:T(8,128)S(1)}, f32[1,32,16,128]{3,2,1,0:T(8,128)}, u32[]{:S(2)}) copy-start(f32[1,32,16,128]{3,2,1,0:T(8,128)} %param.16) | copy-start | bytes 786436
  34.0 4.5 %copy-start.7 = (f32[1,32,16,128]{3,2,1,0:T(8,128)S(1)}, f32[1,32,16,128]{3,2,1,0:T(8,128)}, u32[]{:S(2)}) copy-start(f32[1,32,16,128]{3,2,1,0:T(8,128)} %param.13) | copy-start | bytes 786436
  34.0 20.1 %all-to-all-start = ((f32[32,16,128]{2,1,0:T(8,128)}), f32[32,16,128]{2,1,0:T(8,128)S(1)}, u32[]{:S(2)}, u32[]{:S(2)}) async-start(f32[32,16,128]{2,1,0:T(8,128)} %get-tuple-element.63), calls=%async_computation | async-start | bytes 524288 | tf_op jit(solution)/shard_map/raw/all_to_all | solution.py:680
  42.3 0.7 copy-start.4
  54.2 14.6 %copy-start.5 = (f32[32,16,128]{2,1,0:T(8,128)S(1)}, f32[32,16,128]{2,1,0:T(8,128)}, u32[]{:S(2)}) copy-start(f32[32,16,128]{2,1,0:T(8,128)} %copy-done.4) | copy-start | bytes 786436
  70.0 19.7 %collective-permute-start.4 = (bf16[384,128]{1,0:T(8,128)(2,1)S(1)}, bf16[384,128]{1,0:T(8,128)(2,1)S(1)}, u32[]{:S(2)}, u32[]{:S(2)}) collective-permute-start(bf16[384,128]{1,0:T(8,128)(2,1)S(1)} %get-tuple-element.71), channel_id=1, source_target_pairs={{0,1},{1,2},{2,3},{3,4},{4,5},{5,6},{6,7},{8,9},{9,10},{10,11},{11... | collective-permute-start | bytes 294920 | tf_op jit(solution)/shard_map/halo_2/ppermute | solution.py:573
  80.2 18.9 %collective-permute-start.5 = (bf16[384,128]{1,0:T(8,128)(2,1)S(1)}, bf16[384,128]{1,0:T(8,128)(2,1)S(1)}, u32[]{:S(2)}, u32[]{:S(2)}) collective-permute-start(bf16[384,128]{1,0:T(8,128)(2,1)S(1)} %get-tuple-element.72), channel_id=1, source_target_pairs={{1,0},{2,1},{3,2},{4,3},{5,4},{6,5},{7,6},{9,8},{10,9},{11,10},{12... | collective-permute-start | bytes 294920 | tf_op jit(solution)/shard_map/halo_2/ppermute | solution.py:574
  81.5 8.2 %collective-permute-start.6 = (f32[8,16,128]{2,1,0:T(8,128)S(1)}, f32[8,16,128]{2,1,0:T(8,128)S(1)}, u32[]{:S(2)}, u32[]{:S(2)}) collective-permute-start(f32[8,16,128]{2,1,0:T(8,128)S(1)} %get-tuple-element.74), channel_id=1, source_target_pairs={{0,8},{8,16},{16,24},{24,32},{32,40},{40,48},{48,56},{1,9},{9,17},... | collective-permute-start | bytes 196616 | tf_op jit(solution)/shard_map/halo_2/ppermute | solution.py:573
  83.4 6.3 %collective-permute-start.7 = (f32[8,16,128]{2,1,0:T(8,128)S(1)}, f32[8,16,128]{2,1,0:T(8,128)S(1)}, u32[]{:S(2)}, u32[]{:S(2)}) collective-permute-start(f32[8,16,128]{2,1,0:T(8,128)S(1)} %get-tuple-element.75), channel_id=1, source_target_pairs={{8,0},{16,8},{24,16},{32,24},{40,32},{48,40},{56,48},{9,1},{17,9},... | collective-permute-start | bytes 196616 | tf_op jit(solution)/shard_map/halo_2/ppermute | solution.py:574
  101.0 13.8 %all-to-all-start.2 = ((f32[64,16,128]{2,1,0:T(8,128)}), f32[64,16,128]{2,1,0:T(8,128)S(1)}, u32[]{:S(2)}, u32[]{:S(2)}) async-start(f32[64,16,128]{2,1,0:T(8,128)} %bitcast.9), calls=%async_computation.2 | async-start | bytes 1048576 | tf_op jit(solution)/shard_map/update/all_to_all | solution.py:765
  115.5 3.6 %copy-start.6 = (f32[32,16,128]{2,1,0:T(8,128)S(1)}, f32[32,16,128]{2,1,0:T(8,128)}, u32[]{:S(2)}) copy-start(f32[32,16,128]{2,1,0:T(8,128)} %get-tuple-element.77.second_ref) | copy-start | bytes 786436
  115.5 11.0 %all-to-all-start.3 = ((f32[32,16,128]{2,1,0:T(8,128)}), f32[32,16,128]{2,1,0:T(8,128)S(1)}, u32[]{:S(2)}, u32[]{:S(2)}) async-start(f32[32,16,128]{2,1,0:T(8,128)} %bitcast.11), calls=%async_computation.3 | async-start | bytes 524288 | tf_op jit(solution)/shard_map/update/all_to_all | solution.py:775
  129.7 33.2 %all-to-all-start.4 = ((f32[64,1,1152]{2,1,0:T(1,128)}), f32[64,1,1152]{2,1,0:T(1,128)S(1)}, u32[]{:S(2)}, u32[]{:S(2)}) async-start(f32[64,1,1152]{2,1,0:T(1,128)} %gradient.1), calls=%async_computation.4 | async-start | bytes 589824 | tf_op jit(solution)/shard_map/gradient/all_to_all | solution.py:792

commit v9 on v8

--- a/solution.py
+++ b/solution.py
@@ -19,7 +19,16 @@
 SM = pl.BlockSpec(memory_space=pltpu.SMEM)
 
 
-def call(body, outs, ins, specs, scratch=(), flops=1_000_000, name=None, limit=VMEM_LIMIT):
+def call(
+    body,
+    outs,
+    ins,
+    specs,
+    scratch=(),
+    flops=1_000_000,
+    name=None,
+    limit=VMEM_LIMIT,
+):
     moved = sum(a.size * a.dtype.itemsize for a in ins) + sum(
         o.size * jnp.dtype(o.dtype).itemsize for o in outs
     )
@@ -164,10 +173,7 @@
         ext_ref[c, 1 + size_x] = high_ref[8 + c]
 
 
-def conv_body(feat_ref, low_ref, high_ref, weight_ref, *refs):
-    small_in, (total_ref, *small_out), ext_ref = refs[:3], refs[3:7], refs[7]
-    for source, target in zip(small_in, small_out):
-        target[...] = source[...]
+def conv_body(feat_ref, low_ref, high_ref, weight_ref, total_ref, ext_ref):
     channels, size_x = feat_ref.shape[:2]
     fill_features(ext_ref, feat_ref, low_ref, high_ref)
     together = 2
@@ -215,9 +221,10 @@
     for side, (buffer_ref, dy) in enumerate(((low_ref, 0), (high_ref, 2))):
         terms = [None] * 3
         for c in range(channels):
-            load_plane(plane_ref, buffer_ref, c, size_x, channels)
+            held_ref = plane_ref.at[side * channels + c]
+            load_plane(held_ref, buffer_ref, c, size_x, channels)
             for dx in range(3):
-                plane = plane_ref[7 + dx : 7 + dx + size_x]
+                plane = held_ref[7 + dx : 7 + dx + size_x]
                 for dz in range(3):
                     part = weight_ref[c, 9 * dx + 3 * dy + dz] * plane
                     terms[dz] = part if terms[dz] is None else terms[dz] + part
@@ -290,9 +297,10 @@
     size_x, size_y, depth = fwd_ref.shape
     rows = 4
     if moment == 0:
-        place_ref, receivers_ref, residual_ref, x_low_ref, x_high_ref = refs[4:9]
-        fwd_ahead_ref, back_ahead_ref, lap_fwd_ref, lap_back_ref, later_ref = refs[9:14]
-        x_ref, y_ref, inject_ref = refs[14:]
+        place_ref, receivers_ref, residual_ref, wavelet_ref, x_low_ref, x_high_ref = refs[4:10]
+        fwd_ahead_ref, back_ahead_ref, lap_fwd_ref, lap_back_ref = refs[10:14]
+        later_ref, wavelet_out_ref, x_ref, y_ref, inject_ref = refs[14:]
+        wavelet_out_ref[...] = wavelet_ref[...]
         hit = receiver_hits(receivers_ref, place_ref, plane_y, size_x, size_y)
         for n, out_ref in enumerate((inject_ref, later_ref)):
             injected = jnp.where(
@@ -490,27 +498,28 @@
         return carry
 
     lax.fori_loop(0, size_x // 4, one_block, 0)
+    last = cells - size_y
     for c in range(channels):
-        right_ref[0, 0] = x_low_ref[8 + c].astype(BF16)
-        right_ref[0, 1:size_x] = feat_ref[c, 0 : size_x - 1]
-        right_ref[1] = feat_ref[c]
-        right_ref[2, 0 : size_x - 1] = feat_ref[c, 1:size_x]
-        right_ref[2, size_x - 1] = x_high_ref[8 + c].astype(BF16)
-        right = jnp.concatenate(
-            [right_ref[dx].reshape(cells, depth) for dx in range(3)], axis=1
-        )
-        for dy in range(3):
-            left = jnp.concatenate(
-                [left_ref[2 * dy + part].reshape(cells, depth) for part in range(2)], axis=1
-            )
-            product = lax.dot_general(
-                left, right, (((0,), (0,)), ((), ())), preferred_element_type=F32
-            )
-            ahead = lax.broadcasted_iota(jnp.int32, (depth, depth), 1) - (
-                lax.broadcasted_iota(jnp.int32, (depth, depth), 0)
-            )
+        lanes = [slice((3 * c + dx) * depth, (3 * c + dx + 1) * depth) for dx in range(3)]
+        own = feat_ref[c].reshape(cells, depth)
+        right_ref[0:size_y, lanes[0]] = x_low_ref[8 + c].astype(BF16)
+        right_ref[size_y:cells, lanes[0]] = own[0:last]
+        right_ref[:, lanes[1]] = own
+        right_ref[0:last, lanes[2]] = own[size_y:cells]
+        right_ref[last:cells, lanes[2]] = x_high_ref[8 + c].astype(BF16)
+    ahead = lax.broadcasted_iota(jnp.int32, (depth, depth), 1) - (
+        lax.broadcasted_iota(jnp.int32, (depth, depth), 0)
+    )
+    for dy in range(3):
+        left = jnp.concatenate(
+            [left_ref[2 * dy + part].reshape(cells, depth) for part in range(2)], axis=1
+        )
+        product = lax.dot_general(
+            left, right_ref[...], (((0,), (0,)), ((), ())), preferred_element_type=F32
+        )
+        for c in range(channels):
             for dx in range(3):
-                lanes = slice(dx * depth, (dx + 1) * depth)
+                lanes = slice((3 * c + dx) * depth, (3 * c + dx + 1) * depth)
                 block = product[0:depth, lanes] + product[depth : 2 * depth, lanes]
                 for dz in range(3):
                     at = c * 27 + 9 * dx + 3 * dy + dz
@@ -658,20 +667,20 @@
     with jax.named_scope("inner_1"):
         inner_1 = call(
             functools.partial(inner_body, 0, plane_y),
-            [full] * 5,
-            (fwd_now, back_now, fwd_prev, back_prev, place, receivers, residual, x_low, x_high),
-            [VM] * 4 + [SM] + [VM] * 4,
+            [full] * 5 + [shape(*wavelet.shape)],
+            (fwd_now, back_now, fwd_prev, back_prev)
+            + (place, receivers, residual, wavelet, x_low, x_high),
+            [VM] * 4 + [SM] + [VM] * 5,
             scratch=inner_scratch,
             flops=work,
             name="inner_1",
         )
     with jax.named_scope("conv"):
-        small = (receivers, residual, wavelet)
-        main, receivers, residual, wavelet = call(
+        main = call(
             conv_body,
-            [full] + [shape(*a.shape, dtype=a.dtype) for a in small],
-            (features, x_low, x_high, conv_weight) + small,
-            [VM, VM, VM, SM] + [VM] * 3,
+            [full],
+            (features, x_low, x_high, conv_weight),
+            [VM, VM, VM, SM],
             scratch=[ext],
             flops=54 * channels * size_x * size_y * depth,
             name="conv",
@@ -684,7 +693,7 @@
             [shape(2 * size_x, depth)],
             (y_low, y_high, conv_weight),
             [VM] * 2 + [SM],
-            scratch=[pltpu.VMEM((size_x + 16, depth), F32)],
+            scratch=[pltpu.VMEM((2 * channels, size_x + 16, depth), F32)],
             flops=AHEAD,
             name="conv_edge",
         )
@@ -699,6 +708,7 @@
         raw = lax.all_to_all(raw.reshape(shots * each, depth), "shot", 0, 0, tiled=True)
         raw = raw.reshape(shots, each, depth)
 
+    later, wavelet = inner_1[4:]
     with jax.named_scope("step_1"):
         fwd_1, back_1, lap_1, squashed, x_up, x_down, y_up, y_down = call(
             functools.partial(step_body, 0, plane_y),
@@ -724,7 +734,7 @@
         fwd_ahead, back_ahead, lap_fwd, lap_back = call(
             functools.partial(inner_body, 1, plane_y),
             [full] * 4,
-            (fwd_1, back_1, fwd_now, back_now, inner_1[4]),
+            (fwd_1, back_1, fwd_now, back_now, later),
             [VM] * 5,
             scratch=inner_scratch[:2],
             flops=work,
@@ -781,7 +791,7 @@
             [VM] * 9,
             scratch=[
                 pltpu.VMEM((6,) + grid, BF16),
-                pltpu.VMEM((3,) + grid, BF16),
+                pltpu.VMEM((size_x * size_y, 3 * channels * depth), BF16),
                 pltpu.VMEM((3, size_x + 16, depth), F32),
                 pltpu.VMEM((128, depth), F32),
             ],

time: 164 us -> 164 us (level)
  no operation moved by 1% of the time
where the time goes in v9:
time: 164 us
  starting transfers between devices  61.6 us (38%)
  waiting for transfers between devices  59.5 us (36%)
  Pallas kernels  22.6 us (14%)
  blocking collectives  14.6 us (9%)
  local copies, waits for them, and re-layouts  2.91 us (2%)
  between operations  2.23 us (1%)
    ppermute x4, starting transfers between devices, neighbours(): low = lax.ppermute(up, axis, [(i, i + 1) for i in range(count - 1)])  29.1 us
    all_to_all x1, waiting for transfers between devices, per_device(): shares = lax.all_to_all(share, ('gx', 'gy'), 0, 0, tiled=True)  22.8 us
    pallas_call x15, Pallas kernels, call(): pl.pallas_call(body, out_shape=outs[0] if single else tuple(outs), in_spe...  22.6 us
    ppermute x4, waiting for transfers between devices, neighbours(): high = lax.ppermute(down, axis, [(i + 1, i) for i in range(count - 1)])  20.8 us
    all_to_all x1, blocking collectives, per_device(): lax.all_to_all(raw.reshape(shots * each, depth), 'shot', 0, 0, tiled=True)  14.6 us
    ppermute x4, starting transfers between devices, neighbours(): high = lax.ppermute(down, axis, [(i + 1, i) for i in range(count - 1)])  11.4 us
    all_to_all x1, waiting for transfers between devices, per_device(): lax.all_to_all(sums.reshape(shots * 2 * rows, size_y, depth), 'shot', 0,...  9.62 us
    all_to_all x1, starting transfers between devices, per_device(): shares = lax.all_to_all(share, ('gx', 'gy'), 0, 0, tiled=True)  9.6 us
  transfers between devices with their start and end apart: 12, of which 6 were waited for; matrix products, arithmetic and copies ran while one was open for 0% of the time, Pallas kernels for 8%

profile of v9, /device:TPU:32, one launch (start us, length us, event | category | flops | bytes accessed | tf_op | source)
XLA Modules:
  0.0 163.5 jit_solution(2139806440488523082)
XLA Ops:
  0.6 0.0 copy-start
  0.6 0.0 copy-start.1
  0.7 1.6 %pack_x.1 = (f32[12,16,128]{2,1,0:T(8,128)}, f32[12,16,128]{2,1,0:T(8,128)}) custom-call(bf16[4,32,16,128]{3,2,1,0:T(8,128)(2,1)} %feat_ref.7, f32[32,16,128]{2,1,0:T(8,128)} %bitcast.12, f32[32,16,128]{2,1,0:T(8,128)} %bitcast.16), custom_call_target="tpu_custom_call" | custom-call | flops 1000000 | bytes 1245184 | tf_op jit(solution)/shard_map/pack_x/pack_x/pallas_call | solution.py:36
  2.3 3.8 %collective-permute-start = (f32[12,16,128]{2,1,0:T(8,128)}, f32[12,16,128]{2,1,0:T(8,128)S(1)}, u32[]{:S(2)}, u32[]{:S(2)}) collective-permute-start(f32[12,16,128]{2,1,0:T(8,128)} %get-tuple-element.47), channel_id=1, source_target_pairs={{0,8},{8,16},{16,24},{24,32},{32,40},{40,48},{48,56},{1,9},{9,17},... | collective-permute-start | bytes 294920 | tf_op jit(solution)/shard_map/halo_x/ppermute | solution.py:582
  6.1 4.9 %collective-permute-start.1 = (f32[12,16,128]{2,1,0:T(8,128)}, f32[12,16,128]{2,1,0:T(8,128)S(1)}, u32[]{:S(2)}, u32[]{:S(2)}) collective-permute-start(f32[12,16,128]{2,1,0:T(8,128)} %get-tuple-element.48), channel_id=1, source_target_pairs={{8,0},{16,8},{24,16},{32,24},{40,32},{48,40},{56,48},{9,1},{17,9},... | collective-permute-start | bytes 294920 | tf_op jit(solution)/shard_map/halo_x/ppermute | solution.py:583
  11.0 0.0 copy-done
  11.0 0.0 copy-done.1
  11.0 0.0 copy-start.2
  11.0 0.9 copy-done.2
  12.0 0.3 pack_y.1
  12.3 0.0 collective-permute-done.low_ref.refs_8_.x_low_ref
  12.3 1.2 collective-permute-done.1.high_ref.refs_9_.x_high_ref
  13.5 0.7 corners.1
  14.2 13.3 %collective-permute-start.2 = (bf16[528,128]{1,0:T(8,128)(2,1)}, bf16[528,128]{1,0:T(8,128)(2,1)S(1)}, u32[]{:S(2)}, u32[]{:S(2)}) collective-permute-start(bf16[528,128]{1,0:T(8,128)(2,1)} %get-tuple-element.49), channel_id=1, source_target_pairs={{0,1},{1,2},{2,3},{3,4},{4,5},{5,6},{6,7},{8,9},{9,10},{10,11},{11... | collective-permute-start | bytes 405512 | tf_op jit(solution)/shard_map/halo_y/ppermute | solution.py:582
  27.5 1.3 collective-permute-start.3
  29.4 0.0 copy-start.11
  29.4 0.1 pad_add_fusion.refs_4_.refs_6_.place_ref
  29.5 0.6 copy-done.11
  30.1 0.0 copy-start.8
  30.1 0.0 copy-start.10
  30.1 3.9 %conv.1 = f32[32,16,128]{2,1,0:T(8,128)} custom-call(bf16[4,32,16,128]{3,2,1,0:T(8,128)(2,1)S(1)} %copy-done, f32[12,16,128]{2,1,0:T(8,128)S(1)} %collective-permute-done.low_ref.refs_8_.x_low_ref, f32[12,16,128]{2,1,0:T(8,128)S(1)} %collective-permute-done.1.high_ref.refs_9_.x_high_ref, f32[4,27]{1,0:T(4,128)S(1)} %copy-done.11), custom_call_target="tpu_custom_call" | custom-call | flops 14155776 | bytes 983472 | tf_op jit(solution)/shard_map/conv/conv/pallas_call | solution.py:36
  34.0 0.0 copy-start.3
  34.0 4.4 %all-to-all-start = ((f32[32,16,128]{2,1,0:T(8,128)}), f32[32,16,128]{2,1,0:T(8,128)S(1)}, u32[]{:S(2)}, u32[]{:S(2)}) async-start(f32[32,16,128]{2,1,0:T(8,128)} %conv.1), calls=%async_computation | async-start | bytes 524288 | tf_op jit(solution)/shard_map/raw/all_to_all | solution.py:689
  38.4 0.0 copy-start.9
  38.4 0.0 copy-start.12
  38.5 0.0 copy-done.8
  38.5 0.0 copy-done.10
  38.5 0.0 copy-done.3
  38.5 0.0 copy-done.7
  38.5 0.6 copy-done.9
  39.1 0.0 copy-done.12
  39.1 3.8 %inner_1.1 = (f32[32,16,128]{2,1,0:T(8,128)S(1)}, f32[32,16,128]{2,1,0:T(8,128)S(1)}, f32[32,16,128]{2,1,0:T(8,128)S(1)}, f32[32,16,128]{2,1,0:T(8,128)S(1)}, f3...) custom-call(f32[32,16,128]{2,1,0:T(8,128)S(1)} %bitcast.14, f32[32,16,128]{2,1,0:T(8,128)S(1)} %bitcast.18, ...), custom_call_target="tpu_custom_call" | custom-call | flops 3932160 | bytes 2562076 | tf_op jit(solution)/shard_map/inner_1/inner_1/pallas_call | solution.py:36
  42.9 0.0 copy-start.4
  42.9 0.7 copy-done.4
  43.6 0.0 collective-permute-done.2.low_ref.refs_4_.y_low_ref
  43.6 9.8 %collective-permute-done.3.high_ref.refs_5_.y_high_ref = bf16[528,128]{1,0:T(8,128)(2,1)S(1)} collective-permute-done((bf16[528,128]{1,0:T(8,128)(2,1)S(1)}, bf16[528,128]{1,0:T(8,128)(2,1)S(1)}, u32[]{:S(2)}, u32[]{:S(2)}) %collective-permute-start.3) | collective-permute-done | bytes 135200 | tf_op jit(solution)/shard_map/halo_y/ppermute | solution.py:583
  53.4 0.7 conv_edge.1.rims_ref
  54.1 0.0 all-to-all-done
  54.2 0.0 copy-start.5
  54.2 14.6 %all_to_all.26.refs_8_ = f32[8,128,128]{2,1,0:T(8,128)S(1)} all-to-all(f32[8,128,128]{2,1,0:T(8,128)S(1)} %raw.1), channel_id=1, replica_groups=mesh['shot'=8,'gx'=8,'gy'=8] {'shot'}, dimensions={0} | all-to-all | bytes 1048576 | tf_op jit(solution)/shard_map/raw/all_to_all | solution.py:708
  68.8 0.0 copy-done.5
  68.9 1.2 step_1.1
  70.0 10.1 %collective-permute-start.4 = (bf16[384,128]{1,0:T(8,128)(2,1)S(1)}, bf16[384,128]{1,0:T(8,128)(2,1)S(1)}, u32[]{:S(2)}, u32[]{:S(2)}) collective-permute-start(bf16[384,128]{1,0:T(8,128)(2,1)S(1)} %get-tuple-element.70), channel_id=1, source_target_pairs={{0,1},{1,2},{2,3},{3,4},{4,5},{5,6},{6,7},{8,9},{9,10},{10,11},{11... | collective-permute-start | bytes 294920 | tf_op jit(solution)/shard_map/halo_2/ppermute | solution.py:582
  80.2 1.3 collective-permute-start.5
  81.5 1.9 %collective-permute-start.6 = (f32[8,16,128]{2,1,0:T(8,128)S(1)}, f32[8,16,128]{2,1,0:T(8,128)S(1)}, u32[]{:S(2)}, u32[]{:S(2)}) collective-permute-start(f32[8,16,128]{2,1,0:T(8,128)S(1)} %get-tuple-element.73), channel_id=1, source_target_pairs={{0,8},{8,16},{16,24},{24,32},{32,40},{40,48},{48,56},{1,9},{9,17},... | collective-permute-start | bytes 196616 | tf_op jit(solution)/shard_map/halo_2/ppermute | solution.py:582
  83.4 3.9 %collective-permute-start.7 = (f32[8,16,128]{2,1,0:T(8,128)S(1)}, f32[8,16,128]{2,1,0:T(8,128)S(1)}, u32[]{:S(2)}, u32[]{:S(2)}) collective-permute-start(f32[8,16,128]{2,1,0:T(8,128)S(1)} %get-tuple-element.74), channel_id=1, source_target_pairs={{8,0},{16,8},{24,16},{32,24},{40,32},{48,40},{56,48},{9,1},{17,9},... | collective-permute-start | bytes 196616 | tf_op jit(solution)/shard_map/halo_2/ppermute | solution.py:583
  87.3 2.3 %inner_2.1 = (f32[32,16,128]{2,1,0:T(8,128)S(1)}, f32[32,16,128]{2,1,0:T(8,128)S(1)}, f32[32,16,128]{2,1,0:T(8,128)S(1)}, f32[32,16,128]{2,1,0:T(8,128)S(1)}) custom-call(f32[32,16,128]{2,1,0:T(8,128)S(1)} %get-tuple-element.63.refs_0_.first_ref, f32[32,16,128]{2,1,0:T(8,128)S(1)} %get-tuple-element.64.refs_1_.refs_12_, f32[32,16,128]{2,1,0:T(8,128)S(1)} %bitcast.15, ...), custom_call_target="tpu_custom_call" | custom-call | flops 3932160 | bytes 2359296 | tf_op jit(solution)/shard_map/inner_2/inner_2/pallas_call | solution.py:36
  89.7 0.0 collective-permute-done.6.refs_9_
  89.7 0.0 collective-permute-done.7.refs_10_
  89.7 0.0 collective-permute-done.4.refs_4_
  89.7 9.8 %collective-permute-done.5.refs_5_ = bf16[384,128]{1,0:T(8,128)(2,1)S(1)} collective-permute-done((bf16[384,128]{1,0:T(8,128)(2,1)S(1)}, bf16[384,128]{1,0:T(8,128)(2,1)S(1)}, u32[]{:S(2)}, u32[]{:S(2)}) %collective-permute-start.5) | collective-permute-done | bytes 98336 | tf_op jit(solution)/shard_map/halo_2/ppermute | solution.py:583
  99.5 2.0 %step_2.1 = (f32[32,16,128]{2,1,0:T(8,128)}, f32[32,16,128]{2,1,0:T(8,128)}, f32[8,8,16,128]{3,2,1,0:T(8,128)}) custom-call(f32[32,16,128]{2,1,0:T(8,128)S(1)} %get-tuple-element.66.refs_0_, f32[32,16,128]{2,1,0:T(8,128)S(1)} %get-tuple-element.67.refs_1_, f32[32,16,128]{2,1,0:T(8,128)S(1)} %get-tuple-element.68.refs_2_, ...), custom_call_target="tpu_custom_call" | custom-call | flops 1000000 | bytes 3211284 | tf_op jit(solution)/shard_map/step_2/step_2/pallas_call | solution.py:36
  101.4 3.5 %all-to-all-start.2 = ((f32[64,16,128]{2,1,0:T(8,128)}), f32[64,16,128]{2,1,0:T(8,128)S(1)}, u32[]{:S(2)}, u32[]{:S(2)}) async-start(f32[64,16,128]{2,1,0:T(8,128)} %bitcast.9), calls=%async_computation.2 | async-start | bytes 1048576 | tf_op jit(solution)/shard_map/update/all_to_all | solution.py:775
  105.6 9.6 %all-to-all-done.2 = f32[64,16,128]{2,1,0:T(8,128)S(1)} async-done(((f32[64,16,128]{2,1,0:T(8,128)}), f32[64,16,128]{2,1,0:T(8,128)S(1)}, u32[]{:S(2)}, u32[]{:S(2)}) %all-to-all-start.2) | async-done | bytes 524320 | tf_op jit(solution)/shard_map/update/all_to_all | solution.py:775
  115.2 0.7 update.1
  116.0 3.5 %all-to-all-start.3 = ((f32[32,16,128]{2,1,0:T(8,128)}), f32[32,16,128]{2,1,0:T(8,128)S(1)}, u32[]{:S(2)}, u32[]{:S(2)}) async-start(f32[32,16,128]{2,1,0:T(8,128)} %bitcast.11), calls=%async_computation.3 | async-start | bytes 524288 | tf_op jit(solution)/shard_map/update/all_to_all | solution.py:785
  119.5 0.0 copy-done.6
  119.5 1.2 traces.1
  120.7 6.3 %all-to-all-done.3.update_ref.value_ref = f32[32,16,128]{2,1,0:T(8,128)S(1)} async-done(((f32[32,16,128]{2,1,0:T(8,128)}), f32[32,16,128]{2,1,0:T(8,128)S(1)}, u32[]{:S(2)}, u32[]{:S(2)}) %all-to-all-start.3) | async-done | bytes 262176 | tf_op jit(solution)/shard_map/update/all_to_all | solution.py:785
  127.0 2.7 %gradient.1 = f32[64,1,1152]{2,1,0:T(1,128)} custom-call(f32[32,16,128]{2,1,0:T(8,128)S(1)} %all-to-all-done.3.update_ref.value_ref, f32[32,16,128]{2,1,0:T(8,128)S(1)} %get-tuple-element.72.refs_8_.squashed_ref, bf16[4,32,16,128]{3,2,1,0:T(8,128)(2,1)S(1)} %copy-done, f32[12,16,128]{2,1,0:T(8,128)S(1)} %collective-permute-done.low_ref.refs_8_.x_low_ref, ...), custom_call_target="tpu_custom_call" | custom-call | flops 14155776 | bytes 1814528 | tf_op jit(solution)/shard_map/gradient/gradient/pallas_call | solution.py:36
  129.7 9.6 %all-to-all-start.4 = ((f32[64,1,1152]{2,1,0:T(1,128)}), f32[64,1,1152]{2,1,0:T(1,128)S(1)}, u32[]{:S(2)}, u32[]{:S(2)}) async-start(f32[64,1,1152]{2,1,0:T(1,128)} %gradient.1), calls=%async_computation.4 | async-start | bytes 589824 | tf_op jit(solution)/shard_map/gradient/all_to_all | solution.py:802
  139.3 0.7 keep.1
  140.0 22.8 %all-to-all-done.4.shares_ref = f32[64,1,1152]{2,1,0:T(1,128)S(1)} async-done(((f32[64,1,1152]{2,1,0:T(1,128)}), f32[64,1,1152]{2,1,0:T(1,128)S(1)}, u32[]{:S(2)}, u32[]{:S(2)}) %all-to-all-start.4) | async-done | bytes 294944 | tf_op jit(solution)/shard_map/gradient/all_to_all | solution.py:802
  162.8 0.7 total.1
  (3 shorter events, 0.0 us)
Async XLA Ops:
  0.6 10.4 %copy-start = (bf16[4,32,16,128]{3,2,1,0:T(8,128)(2,1)S(1)}, bf16[4,32,16,128]{3,2,1,0:T(8,128)(2,1)}, u32[]{:S(2)}) copy-start(bf16[4,32,16,128]{3,2,1,0:T(8,128)(2,1)} %feat_ref.7) | copy-start | bytes 1572868
  0.6 10.4 %copy-start.1 = (f32[1,32,16,128]{3,2,1,0:T(8,128)S(1)}, f32[1,32,16,128]{3,2,1,0:T(8,128)}, u32[]{:S(2)}) copy-start(f32[1,32,16,128]{3,2,1,0:T(8,128)} %param.14) | copy-start | bytes 786436
  2.3 10.0 %collective-permute-start = (f32[12,16,128]{2,1,0:T(8,128)}, f32[12,16,128]{2,1,0:T(8,128)S(1)}, u32[]{:S(2)}, u32[]{:S(2)}) collective-permute-start(f32[12,16,128]{2,1,0:T(8,128)} %get-tuple-element.47), channel_id=1, source_target_pairs={{0,8},{8,16},{16,24},{24,32},{32,40},{40,48},{48,56},{1,9},{9,17},... | collective-permute-start | bytes 294920 | tf_op jit(solution)/shard_map/halo_x/ppermute | solution.py:582
  6.1 7.4 %collective-permute-start.1 = (f32[12,16,128]{2,1,0:T(8,128)}, f32[12,16,128]{2,1,0:T(8,128)S(1)}, u32[]{:S(2)}, u32[]{:S(2)}) collective-permute-start(f32[12,16,128]{2,1,0:T(8,128)} %get-tuple-element.48), channel_id=1, source_target_pairs={{8,0},{16,8},{24,16},{32,24},{40,32},{48,40},{56,48},{9,1},{17,9},... | collective-permute-start | bytes 294920 | tf_op jit(solution)/shard_map/halo_x/ppermute | solution.py:583
  11.0 1.0 copy-start.2
  14.2 29.5 %collective-permute-start.2 = (bf16[528,128]{1,0:T(8,128)(2,1)}, bf16[528,128]{1,0:T(8,128)(2,1)S(1)}, u32[]{:S(2)}, u32[]{:S(2)}) collective-permute-start(bf16[528,128]{1,0:T(8,128)(2,1)} %get-tuple-element.49), channel_id=1, source_target_pairs={{0,1},{1,2},{2,3},{3,4},{4,5},{5,6},{6,7},{8,9},{9,10},{10,11},{11... | collective-permute-start | bytes 405512 | tf_op jit(solution)/shard_map/halo_y/ppermute | solution.py:582
  27.5 26.0 %collective-permute-start.3 = (bf16[528,128]{1,0:T(8,128)(2,1)S(1)}, bf16[528,128]{1,0:T(8,128)(2,1)S(1)}, u32[]{:S(2)}, u32[]{:S(2)}) collective-permute-start(bf16[528,128]{1,0:T(8,128)(2,1)S(1)} %get-tuple-element.61), channel_id=1, source_target_pairs={{1,0},{2,1},{3,2},{4,3},{5,4},{6,5},{7,6},{9,8},{10,9},{11,10},{12... | collective-permute-start | bytes 405512 | tf_op jit(solution)/shard_map/halo_y/ppermute | solution.py:583
  29.4 0.7 copy-start.11
  30.1 8.4 %copy-start.8 = (f32[1,32,16,128]{3,2,1,0:T(8,128)S(1)}, f32[1,32,16,128]{3,2,1,0:T(8,128)}, u32[]{:S(2)}) copy-start(f32[1,32,16,128]{3,2,1,0:T(8,128)} %param.15) | copy-start | bytes 786436
  30.1 8.4 %copy-start.10 = (f32[1,2,512]{2,1,0:T(2,128)S(1)}, f32[1,2,512]{2,1,0:T(2,128)}, u32[]{:S(2)}) copy-start(f32[1,2,512]{2,1,0:T(2,128)} %refs_6_.1) | copy-start | bytes 12292
  34.0 4.5 %copy-start.3 = (f32[1,32,16,128]{3,2,1,0:T(8,128)S(1)}, f32[1,32,16,128]{3,2,1,0:T(8,128)}, u32[]{:S(2)}) copy-start(f32[1,32,16,128]{3,2,1,0:T(8,128)} %param.16) | copy-start | bytes 786436
  34.0 4.5 %copy-start.7 = (f32[1,32,16,128]{3,2,1,0:T(8,128)S(1)}, f32[1,32,16,128]{3,2,1,0:T(8,128)}, u32[]{:S(2)}) copy-start(f32[1,32,16,128]{3,2,1,0:T(8,128)} %param.13) | copy-start | bytes 786436
  34.0 20.1 %all-to-all-start = ((f32[32,16,128]{2,1,0:T(8,128)}), f32[32,16,128]{2,1,0:T(8,128)S(1)}, u32[]{:S(2)}, u32[]{:S(2)}) async-start(f32[32,16,128]{2,1,0:T(8,128)} %conv.1), calls=%async_computation | async-start | bytes 524288 | tf_op jit(solution)/shard_map/raw/all_to_all | solution.py:689
  38.4 0.7 copy-start.9
  38.4 0.7 copy-start.12
  42.9 0.7 copy-start.4
  54.2 14.6 %copy-start.5 = (f32[32,16,128]{2,1,0:T(8,128)S(1)}, f32[32,16,128]{2,1,0:T(8,128)}, u32[]{:S(2)}) copy-start(f32[32,16,128]{2,1,0:T(8,128)} %copy-done.4) | copy-start | bytes 786436
  70.0 19.7 %collective-permute-start.4 = (bf16[384,128]{1,0:T(8,128)(2,1)S(1)}, bf16[384,128]{1,0:T(8,128)(2,1)S(1)}, u32[]{:S(2)}, u32[]{:S(2)}) collective-permute-start(bf16[384,128]{1,0:T(8,128)(2,1)S(1)} %get-tuple-element.70), channel_id=1, source_target_pairs={{0,1},{1,2},{2,3},{3,4},{4,5},{5,6},{6,7},{8,9},{9,10},{10,11},{11... | collective-permute-start | bytes 294920 | tf_op jit(solution)/shard_map/halo_2/ppermute | solution.py:582
  80.2 19.3 %collective-permute-start.5 = (bf16[384,128]{1,0:T(8,128)(2,1)S(1)}, bf16[384,128]{1,0:T(8,128)(2,1)S(1)}, u32[]{:S(2)}, u32[]{:S(2)}) collective-permute-start(bf16[384,128]{1,0:T(8,128)(2,1)S(1)} %get-tuple-element.71), channel_id=1, source_target_pairs={{1,0},{2,1},{3,2},{4,3},{5,4},{6,5},{7,6},{9,8},{10,9},{11,10},{12... | collective-permute-start | bytes 294920 | tf_op jit(solution)/shard_map/halo_2/ppermute | solution.py:583
  81.5 8.2 %collective-permute-start.6 = (f32[8,16,128]{2,1,0:T(8,128)S(1)}, f32[8,16,128]{2,1,0:T(8,128)S(1)}, u32[]{:S(2)}, u32[]{:S(2)}) collective-permute-start(f32[8,16,128]{2,1,0:T(8,128)S(1)} %get-tuple-element.73), channel_id=1, source_target_pairs={{0,8},{8,16},{16,24},{24,32},{32,40},{40,48},{48,56},{1,9},{9,17},... | collective-permute-start | bytes 196616 | tf_op jit(solution)/shard_map/halo_2/ppermute | solution.py:582
  83.4 6.3 %collective-permute-start.7 = (f32[8,16,128]{2,1,0:T(8,128)S(1)}, f32[8,16,128]{2,1,0:T(8,128)S(1)}, u32[]{:S(2)}, u32[]{:S(2)}) collective-permute-start(f32[8,16,128]{2,1,0:T(8,128)S(1)} %get-tuple-element.74), channel_id=1, source_target_pairs={{8,0},{16,8},{24,16},{32,24},{40,32},{48,40},{56,48},{9,1},{17,9},... | collective-permute-start | bytes 196616 | tf_op jit(solution)/shard_map/halo_2/ppermute | solution.py:583
  101.4 13.8 %all-to-all-start.2 = ((f32[64,16,128]{2,1,0:T(8,128)}), f32[64,16,128]{2,1,0:T(8,128)S(1)}, u32[]{:S(2)}, u32[]{:S(2)}) async-start(f32[64,16,128]{2,1,0:T(8,128)} %bitcast.9), calls=%async_computation.2 | async-start | bytes 1048576 | tf_op jit(solution)/shard_map/update/all_to_all | solution.py:775
  116.0 3.6 %copy-start.6 = (f32[32,16,128]{2,1,0:T(8,128)S(1)}, f32[32,16,128]{2,1,0:T(8,128)}, u32[]{:S(2)}) copy-start(f32[32,16,128]{2,1,0:T(8,128)} %get-tuple-element.76.second_ref) | copy-start | bytes 786436
  116.0 11.0 %all-to-all-start.3 = ((f32[32,16,128]{2,1,0:T(8,128)}), f32[32,16,128]{2,1,0:T(8,128)S(1)}, u32[]{:S(2)}, u32[]{:S(2)}) async-start(f32[32,16,128]{2,1,0:T(8,128)} %bitcast.11), calls=%async_computation.3 | async-start | bytes 524288 | tf_op jit(solution)/shard_map/update/all_to_all | solution.py:785
  129.7 33.2 %all-to-all-start.4 = ((f32[64,1,1152]{2,1,0:T(1,128)}), f32[64,1,1152]{2,1,0:T(1,128)S(1)}, u32[]{:S(2)}, u32[]{:S(2)}) async-start(f32[64,1,1152]{2,1,0:T(1,128)} %gradient.1), calls=%async_computation.4 | async-start | bytes 589824 | tf_op jit(solution)/shard_map/gradient/all_to_all | solution.py:802

commit v10 on v9

--- a/solution.py
+++ b/solution.py
@@ -173,13 +173,12 @@
         ext_ref[c, 1 + size_x] = high_ref[8 + c]
 
 
-def conv_body(feat_ref, low_ref, high_ref, weight_ref, total_ref, ext_ref):
+def conv_body(feat_ref, low_ref, high_ref, weight_ref, total_ref, wide_ref, ext_ref):
     channels, size_x = feat_ref.shape[:2]
     fill_features(ext_ref, feat_ref, low_ref, high_ref)
     together = 2
 
-    def some_rows(i, carry):
-        start = i * together
+    def some_rows(start):
         terms = [[[None] * 3 for _ in range(3)] for _ in range(together)]
         for c in range(channels):
             inputs = [ext_ref[c, start + r] for r in range(together + 2)]
@@ -203,9 +202,17 @@
                     part = shifted_rows(part, dy - 1)
                 total = part if total is None else total + part
             total_ref[start + r] = total
-        return carry
-
-    lax.fori_loop(0, size_x // together, some_rows, 0)
+
+    for start in range(0, size_x, together):
+        some_rows(start)
+    at = 0
+    for dy in (0, 2):
+        for c in range(channels):
+            for dx in range(3):
+                for dz in range(3):
+                    weight = weight_ref[c, 9 * dx + 3 * dy + dz]
+                    wide_ref[at : at + 1] = jnp.full((1, wide_ref.shape[1]), weight, F32)
+                    at += 1
 
 
 def load_plane(plane_ref, buffer_ref, c, size_x, channels):
@@ -215,10 +222,11 @@
     plane_ref[8 + size_x : 9 + size_x] = tail[2 * c + 1 : 2 * c + 2]
 
 
-def conv_edge_body(low_ref, high_ref, weight_ref, out_ref, plane_ref):
+def conv_edge_body(low_ref, high_ref, wide_ref, out_ref, plane_ref):
     size_x = out_ref.shape[0] // 2
-    channels = weight_ref.shape[0]
-    for side, (buffer_ref, dy) in enumerate(((low_ref, 0), (high_ref, 2))):
+    channels = wide_ref.shape[0] // 18
+    at = 0
+    for side, buffer_ref in enumerate((low_ref, high_ref)):
         terms = [None] * 3
         for c in range(channels):
             held_ref = plane_ref.at[side * channels + c]
@@ -226,8 +234,9 @@
             for dx in range(3):
                 plane = held_ref[7 + dx : 7 + dx + size_x]
                 for dz in range(3):
-                    part = weight_ref[c, 9 * dx + 3 * dy + dz] * plane
+                    part = wide_ref[at : at + 1] * plane
                     terms[dz] = part if terms[dz] is None else terms[dz] + part
+                    at += 1
         total = terms[1] + shifted_lanes(terms[0], -1) + shifted_lanes(terms[2], 1)
         out_ref[side * size_x : (side + 1) * size_x] = total
 
@@ -299,8 +308,19 @@
     if moment == 0:
         place_ref, receivers_ref, residual_ref, wavelet_ref, x_low_ref, x_high_ref = refs[4:10]
         fwd_ahead_ref, back_ahead_ref, lap_fwd_ref, lap_back_ref = refs[10:14]
-        later_ref, wavelet_out_ref, x_ref, y_ref, inject_ref = refs[14:]
-        wavelet_out_ref[...] = wavelet_ref[...]
+        later_ref, spot_ref, amplitude_ref, x_ref, y_ref, inject_ref = refs[14:]
+        anchor_x, anchor_y, source = place_ref[0], place_ref[1], place_ref[2]
+        shift_y = plane_y.bit_length() - 1
+        shift_z = depth.bit_length() - 1
+        column = lax.shift_right_logical(source, shift_z)
+        source_x = lax.shift_right_logical(column, shift_y) - anchor_x
+        source_y = (column & (plane_y - 1)) - anchor_y
+        source_z = source & (depth - 1)
+        here = (source_x >= 0) & (source_x < size_x) & (source_y >= 0) & (source_y < size_y)
+        spot = jnp.where(here, (source_x * size_y + source_y) * depth + source_z, -1)
+        spot_ref[...] = jnp.full(spot_ref.shape, spot, jnp.int32)
+        for n in range(2):
+            amplitude_ref[n] = jnp.full(amplitude_ref.shape[1:], wavelet_ref[0, n], F32)
         hit = receiver_hits(receivers_ref, place_ref, plane_y, size_x, size_y)
         for n, out_ref in enumerate((inject_ref, later_ref)):
             injected = jnp.where(
@@ -348,12 +368,13 @@
             ahead_ref[here] = 2.0 * centre - old_ref[here]
             return carry
 
-        lax.fori_loop(0, size_x // rows, one_block, 0)
+        for i in range(size_x // rows):
+            one_block(i, 0)
 
 
 def step_body(moment, plane_y, *refs):
     fwd_ahead_ref, back_ahead_ref, lap_fwd_ref, lap_back_ref = refs[:4]
-    y_low_ref, y_high_ref, place_ref, wavelet_ref = refs[4:8]
+    y_low_ref, y_high_ref, spot_ref, amplitude_ref = refs[4:8]
     refs = refs[8:]
     if moment == 0:
         raw_ref = refs[0]
@@ -388,16 +409,7 @@
             side_ref[:, empty : empty + 8] = jnp.zeros((size_x, 8, depth), F32)
             side_ref[:, at : at + 4] = edge_ref[:, 4 * m : 4 * m + 4]
 
-    anchor_x, anchor_y, source = place_ref[0], place_ref[1], place_ref[2]
-    shift_y = plane_y.bit_length() - 1
-    shift_z = depth.bit_length() - 1
-    column = lax.shift_right_logical(source, shift_z)
-    source_x = lax.shift_right_logical(column, shift_y) - anchor_x
-    source_y = (column & (plane_y - 1)) - anchor_y
-    source_z = source & (depth - 1)
-    here = (source_x >= 0) & (source_x < size_x) & (source_y >= 0) & (source_y < size_y)
-    spot = jnp.where(here, (source_x * size_y + source_y) * depth + source_z, -1)
-    amplitude = wavelet_ref[0, moment]
+    spot, amplitude = spot_ref[0:1, :], amplitude_ref[moment, 0:1, :]
 
     def edges(lap, m, start):
         block = slice(start, start + 4)
@@ -483,21 +495,16 @@
     copies = out_ref.shape[0]
     cells = size_x * size_y
 
-    def one_block(i, carry):
-        for j in range(4):
-            x = 4 * i + j
-            squashed = squashed_ref[x]
-            pulled = update_ref[x] * (0.16 * squashed * (1.0 - squashed))
-            for dy in range(3):
-                moved = pulled if dy == 1 else shifted_rows(pulled, 1 - dy)
-                high = moved.astype(BF16)
-                left_ref[2 * dy, x] = high
-                left_ref[2 * dy + 1, x] = (moved - high.astype(F32)).astype(BF16)
-            plane_ref[1, pl.ds(x, 1)] = pulled[0:1, :]
-            plane_ref[2, pl.ds(x, 1)] = pulled[size_y - 1 : size_y, :]
-        return carry
-
-    lax.fori_loop(0, size_x // 4, one_block, 0)
+    for x in range(size_x):
+        squashed = squashed_ref[x]
+        pulled = update_ref[x] * (0.16 * squashed * (1.0 - squashed))
+        for dy in range(3):
+            moved = pulled if dy == 1 else shifted_rows(pulled, 1 - dy)
+            high = moved.astype(BF16)
+            left_ref[2 * dy, x] = high
+            left_ref[2 * dy + 1, x] = (moved - high.astype(F32)).astype(BF16)
+        plane_ref[1, x : x + 1] = pulled[0:1, :]
+        plane_ref[2, x : x + 1] = pulled[size_y - 1 : size_y, :]
     last = cells - size_y
     for c in range(channels):
         lanes = [slice((3 * c + dx) * depth, (3 * c + dx + 1) * depth) for dx in range(3)]
@@ -667,18 +674,18 @@
     with jax.named_scope("inner_1"):
         inner_1 = call(
             functools.partial(inner_body, 0, plane_y),
-            [full] * 5 + [shape(*wavelet.shape)],
+            [full] * 5 + [shape(8, depth, dtype=jnp.int32), shape(2, 8, depth)],
             (fwd_now, back_now, fwd_prev, back_prev)
             + (place, receivers, residual, wavelet, x_low, x_high),
-            [VM] * 4 + [SM] + [VM] * 5,
+            [VM] * 4 + [SM] + [VM] * 2 + [SM] + [VM] * 2,
             scratch=inner_scratch,
             flops=work,
             name="inner_1",
         )
     with jax.named_scope("conv"):
-        main = call(
+        main, wide = call(
             conv_body,
-            [full],
+            [full, shape(18 * channels, depth)],
             (features, x_low, x_high, conv_weight),
             [VM, VM, VM, SM],
             scratch=[ext],
@@ -691,8 +698,8 @@
         rims = call(
             conv_edge_body,
             [shape(2 * size_x, depth)],
-            (y_low, y_high, conv_weight),
-            [VM] * 2 + [SM],
+            (y_low, y_high, wide),
+            [VM] * 3,
             scratch=[pltpu.VMEM((2 * channels, size_x + 16, depth), F32)],
             flops=AHEAD,
             name="conv_edge",
@@ -708,7 +715,7 @@
         raw = lax.all_to_all(raw.reshape(shots * each, depth), "shot", 0, 0, tiled=True)
         raw = raw.reshape(shots, each, depth)
 
-    later, wavelet = inner_1[4:]
+    later, spot, amplitude = inner_1[4:]
     with jax.named_scope("step_1"):
         fwd_1, back_1, lap_1, squashed, x_up, x_down, y_up, y_down = call(
             functools.partial(step_body, 0, plane_y),
@@ -719,11 +726,11 @@
                 *inner_1[:4],
                 y_low,
                 y_high,
-                place,
-                wavelet,
+                spot,
+                amplitude,
                 raw,
             ),
-            [VM] * 6 + [SM] * 2 + [VM],
+            [VM] * 9,
             scratch=step_scratch,
             name="step_1",
         )
@@ -751,15 +758,15 @@
                 lap_back,
                 y_low_2,
                 y_high_2,
-                place,
-                wavelet,
+                spot,
+                amplitude,
                 squashed,
                 x_low_2,
                 x_high_2,
                 lap_1,
                 back_1,
             ),
-            [VM] * 6 + [SM] * 2 + [VM] * 5,
+            [VM] * 13,
             scratch=step_scratch,
             name="step_2",
         )

time: 164 us -> 162 us (0.988)
  Pallas kernels: 22.6 us -> 17.5 us
  waiting for transfers between devices: 59.5 us -> 62.5 us
    pallas_call x15, Pallas kernels: 22.6 us -> 17.5 us  [call(): pl.pallas_call(body, out_shape=outs[0] if single else tuple(outs), in_spe...]
    ppermute x4, waiting for transfers between devices: 20.8 us -> 22.9 us  [neighbours(): high = lax.ppermute(down, axis, [(i + 1, i) for i in range(count - 1)])]
  transfers between devices with their start and end apart: 12 -> 12, of which waited for: 6 -> 8; matrix products, arithmetic and copies ran while one was open for 0% -> 0% of each run, Pallas kernels for 8% -> 6%
where the time goes in v10:
time: 162 us
  waiting for transfers between devices  62.5 us (39%)
  starting transfers between devices  61.7 us (38%)
  Pallas kernels  17.5 us (11%)
  blocking collectives  14.6 us (9%)
  local copies, waits for them, and re-layouts  2.92 us (2%)
  between operations  2.23 us (1%)
    ppermute x4, starting transfers between devices, neighbours(): low = lax.ppermute(up, axis, [(i, i + 1) for i in range(count - 1)])  29.1 us
    ppermute x4, waiting for transfers between devices, neighbours(): high = lax.ppermute(down, axis, [(i + 1, i) for i in range(count - 1)])  22.9 us
    all_to_all x1, waiting for transfers between devices, per_device(): shares = lax.all_to_all(share, ('gx', 'gy'), 0, 0, tiled=True)  22.8 us
    pallas_call x15, Pallas kernels, call(): pl.pallas_call(body, out_shape=outs[0] if single else tuple(outs), in_spe...  17.5 us
    all_to_all x1, blocking collectives, per_device(): lax.all_to_all(raw.reshape(shots * each, depth), 'shot', 0, 0, tiled=True)  14.6 us
    ppermute x4, starting transfers between devices, neighbours(): high = lax.ppermute(down, axis, [(i + 1, i) for i in range(count - 1)])  11.4 us
    all_to_all x1, starting transfers between devices, per_device(): shares = lax.all_to_all(share, ('gx', 'gy'), 0, 0, tiled=True)  9.76 us
    all_to_all x1, waiting for transfers between devices, per_device(): lax.all_to_all(sums.reshape(shots * 2 * rows, size_y, depth), 'shot', 0,...  9.62 us
  transfers between devices with their start and end apart: 12, of which 8 were waited for; matrix products, arithmetic and copies ran while one was open for 0% of the time, Pallas kernels for 6%

profile of v10, /device:TPU:32, one launch (start us, length us, event | category | flops | bytes accessed | tf_op | source)
XLA Modules:
  0.0 161.6 jit_solution(4434668510648100865)
XLA Ops:
  0.6 0.0 copy-start
  0.6 0.0 copy-start.1
  0.7 1.6 %pack_x.1 = (f32[12,16,128]{2,1,0:T(8,128)}, f32[12,16,128]{2,1,0:T(8,128)}) custom-call(bf16[4,32,16,128]{3,2,1,0:T(8,128)(2,1)} %feat_ref.7, f32[32,16,128]{2,1,0:T(8,128)} %bitcast.12, f32[32,16,128]{2,1,0:T(8,128)} %bitcast.16), custom_call_target="tpu_custom_call" | custom-call | flops 1000000 | bytes 1245184 | tf_op jit(solution)/shard_map/pack_x/pack_x/pallas_call | solution.py:36
  2.3 3.8 %collective-permute-start = (f32[12,16,128]{2,1,0:T(8,128)}, f32[12,16,128]{2,1,0:T(8,128)S(1)}, u32[]{:S(2)}, u32[]{:S(2)}) collective-permute-start(f32[12,16,128]{2,1,0:T(8,128)} %get-tuple-element.51), channel_id=1, source_target_pairs={{0,8},{8,16},{16,24},{24,32},{32,40},{40,48},{48,56},{1,9},{9,17},... | collective-permute-start | bytes 294920 | tf_op jit(solution)/shard_map/halo_x/ppermute | solution.py:589
  6.1 4.9 %collective-permute-start.1 = (f32[12,16,128]{2,1,0:T(8,128)}, f32[12,16,128]{2,1,0:T(8,128)S(1)}, u32[]{:S(2)}, u32[]{:S(2)}) collective-permute-start(f32[12,16,128]{2,1,0:T(8,128)} %get-tuple-element.52), channel_id=1, source_target_pairs={{8,0},{16,8},{24,16},{32,24},{40,32},{48,40},{56,48},{9,1},{17,9},... | collective-permute-start | bytes 294920 | tf_op jit(solution)/shard_map/halo_x/ppermute | solution.py:590
  11.0 0.0 copy-done
  11.0 0.0 copy-done.1
  11.0 0.0 copy-start.2
  11.0 0.9 copy-done.2
  12.0 0.3 pack_y.1
  12.3 0.0 collective-permute-done.low_ref.refs_8_.x_low_ref
  12.3 1.2 collective-permute-done.1.high_ref.refs_9_.x_high_ref
  13.5 0.7 corners.1
  14.2 13.3 %collective-permute-start.2 = (bf16[528,128]{1,0:T(8,128)(2,1)}, bf16[528,128]{1,0:T(8,128)(2,1)S(1)}, u32[]{:S(2)}, u32[]{:S(2)}) collective-permute-start(bf16[528,128]{1,0:T(8,128)(2,1)} %get-tuple-element.53), channel_id=1, source_target_pairs={{0,1},{1,2},{2,3},{3,4},{4,5},{5,6},{6,7},{8,9},{9,10},{10,11},{11... | collective-permute-start | bytes 405512 | tf_op jit(solution)/shard_map/halo_y/ppermute | solution.py:589
  27.4 1.3 collective-permute-start.3
  29.4 0.0 copy-start.13
  29.4 0.1 pad_add_fusion.refs_4_.place_ref
  29.5 0.6 copy-done.13
  30.1 0.0 copy-start.10
  30.1 3.5 %conv.1 = (f32[32,16,128]{2,1,0:T(8,128)}, f32[72,128]{1,0:T(8,128)S(1)}) custom-call(bf16[4,32,16,128]{3,2,1,0:T(8,128)(2,1)S(1)} %copy-done, f32[12,16,128]{2,1,0:T(8,128)S(1)} %collective-permute-done.low_ref.refs_8_.x_low_ref, f32[12,16,128]{2,1,0:T(8,128)S(1)} %collective-permute-done.1.high_ref.refs_9_.x_high_ref, f32[4,27]{1,0:T(4,128)S(1)} %copy-done.13), custom_call_target="tpu_custom_call" | custom-call | flops 14155776 | bytes 1020336 | tf_op jit(solution)/shard_map/conv/conv/pallas_call | solution.py:36
  33.6 4.4 %all-to-all-start = ((f32[32,16,128]{2,1,0:T(8,128)}), f32[32,16,128]{2,1,0:T(8,128)S(1)}, u32[]{:S(2)}, u32[]{:S(2)}) async-start(f32[32,16,128]{2,1,0:T(8,128)} %get-tuple-element.69), calls=%async_computation | async-start | bytes 524288 | tf_op jit(solution)/shard_map/raw/all_to_all | solution.py:696
  38.0 0.0 copy-start.14
  38.0 0.0 copy-done.10
  38.0 0.0 copy-done.12
  38.1 0.0 copy-done.3
  38.1 0.0 copy-done.9
  38.1 0.6 copy-done.11
  38.7 0.0 copy-done.14
  38.7 1.9 %inner_1.1 = (f32[32,16,128]{2,1,0:T(8,128)S(1)}, f32[32,16,128]{2,1,0:T(8,128)S(1)}, f32[32,16,128]{2,1,0:T(8,128)S(1)}, f32[32,16,128]{2,1,0:T(8,128)S(1)}, f3...) custom-call(f32[32,16,128]{2,1,0:T(8,128)S(1)} %bitcast.14, f32[32,16,128]{2,1,0:T(8,128)S(1)} %bitcast.18, ...), custom_call_target="tpu_custom_call" | custom-call | flops 3932160 | bytes 2574356 | tf_op jit(solution)/shard_map/inner_1/inner_1/pallas_call | solution.py:36
  40.6 0.0 copy-start.4
  40.6 0.7 copy-done.4
  41.3 0.0 collective-permute-done.2.low_ref.refs_4_.y_low_ref
  41.3 12.1 %collective-permute-done.3.high_ref.refs_5_.y_high_ref = bf16[528,128]{1,0:T(8,128)(2,1)S(1)} collective-permute-done((bf16[528,128]{1,0:T(8,128)(2,1)S(1)}, bf16[528,128]{1,0:T(8,128)(2,1)S(1)}, u32[]{:S(2)}, u32[]{:S(2)}) %collective-permute-start.3) | collective-permute-done | bytes 135200 | tf_op jit(solution)/shard_map/halo_y/ppermute | solution.py:590
  53.4 0.1 conv_edge.1.rims_ref
  53.6 0.0 copy-done.6
  53.6 0.0 all-to-all-done
  53.7 0.0 copy-start.5
  53.7 0.0 copy-start.7
  53.7 14.6 %all_to_all.26.refs_8_ = f32[8,128,128]{2,1,0:T(8,128)S(1)} all-to-all(f32[8,128,128]{2,1,0:T(8,128)S(1)} %raw.1), channel_id=1, replica_groups=mesh['shot'=8,'gx'=8,'gy'=8] {'shot'}, dimensions={0} | all-to-all | bytes 1048576 | tf_op jit(solution)/shard_map/raw/all_to_all | solution.py:715
  68.3 0.0 copy-done.5
  68.3 0.0 copy-done.7
  68.3 0.6 step_1.1
  68.9 10.1 %collective-permute-start.4 = (bf16[384,128]{1,0:T(8,128)(2,1)S(1)}, bf16[384,128]{1,0:T(8,128)(2,1)S(1)}, u32[]{:S(2)}, u32[]{:S(2)}) collective-permute-start(bf16[384,128]{1,0:T(8,128)(2,1)S(1)} %get-tuple-element.78), channel_id=1, source_target_pairs={{0,1},{1,2},{2,3},{3,4},{4,5},{5,6},{6,7},{8,9},{9,10},{10,11},{11... | collective-permute-start | bytes 294920 | tf_op jit(solution)/shard_map/halo_2/ppermute | solution.py:589
  79.1 1.3 collective-permute-start.5
  80.4 1.9 %collective-permute-start.6 = (f32[8,16,128]{2,1,0:T(8,128)S(1)}, f32[8,16,128]{2,1,0:T(8,128)S(1)}, u32[]{:S(2)}, u32[]{:S(2)}) collective-permute-start(f32[8,16,128]{2,1,0:T(8,128)S(1)} %get-tuple-element.81), channel_id=1, source_target_pairs={{0,8},{8,16},{16,24},{24,32},{32,40},{40,48},{48,56},{1,9},{9,17},... | collective-permute-start | bytes 196616 | tf_op jit(solution)/shard_map/halo_2/ppermute | solution.py:589
  82.3 3.9 %collective-permute-start.7 = (f32[8,16,128]{2,1,0:T(8,128)S(1)}, f32[8,16,128]{2,1,0:T(8,128)S(1)}, u32[]{:S(2)}, u32[]{:S(2)}) collective-permute-start(f32[8,16,128]{2,1,0:T(8,128)S(1)} %get-tuple-element.82), channel_id=1, source_target_pairs={{8,0},{16,8},{24,16},{32,24},{40,32},{48,40},{56,48},{9,1},{17,9},... | collective-permute-start | bytes 196616 | tf_op jit(solution)/shard_map/halo_2/ppermute | solution.py:590
  86.2 1.2 inner_2.1
  87.4 0.9 collective-permute-done.6.refs_9_
  88.4 0.2 collective-permute-done.7.refs_10_
  88.6 0.0 collective-permute-done.4.refs_4_
  88.6 9.3 %collective-permute-done.5.refs_5_ = bf16[384,128]{1,0:T(8,128)(2,1)S(1)} collective-permute-done((bf16[384,128]{1,0:T(8,128)(2,1)S(1)}, bf16[384,128]{1,0:T(8,128)(2,1)S(1)}, u32[]{:S(2)}, u32[]{:S(2)}) %collective-permute-start.5) | collective-permute-done | bytes 98336 | tf_op jit(solution)/shard_map/halo_2/ppermute | solution.py:590
  97.9 1.4 step_2.1
  99.4 3.5 %all-to-all-start.2 = ((f32[64,16,128]{2,1,0:T(8,128)}), f32[64,16,128]{2,1,0:T(8,128)S(1)}, u32[]{:S(2)}, u32[]{:S(2)}) async-start(f32[64,16,128]{2,1,0:T(8,128)} %bitcast.9), calls=%async_computation.2 | async-start | bytes 1048576 | tf_op jit(solution)/shard_map/update/all_to_all | solution.py:782
  103.5 9.6 %all-to-all-done.2 = f32[64,16,128]{2,1,0:T(8,128)S(1)} async-done(((f32[64,16,128]{2,1,0:T(8,128)}), f32[64,16,128]{2,1,0:T(8,128)S(1)}, u32[]{:S(2)}, u32[]{:S(2)}) %all-to-all-start.2) | async-done | bytes 524320 | tf_op jit(solution)/shard_map/update/all_to_all | solution.py:782
  113.2 0.7 update.1
  113.9 3.5 %all-to-all-start.3 = ((f32[32,16,128]{2,1,0:T(8,128)}), f32[32,16,128]{2,1,0:T(8,128)S(1)}, u32[]{:S(2)}, u32[]{:S(2)}) async-start(f32[32,16,128]{2,1,0:T(8,128)} %bitcast.11), calls=%async_computation.3 | async-start | bytes 524288 | tf_op jit(solution)/shard_map/update/all_to_all | solution.py:792
  117.5 0.0 copy-done.8
  117.5 1.2 traces.1
  118.7 6.3 %all-to-all-done.3.update_ref.value_ref = f32[32,16,128]{2,1,0:T(8,128)S(1)} async-done(((f32[32,16,128]{2,1,0:T(8,128)}), f32[32,16,128]{2,1,0:T(8,128)S(1)}, u32[]{:S(2)}, u32[]{:S(2)}) %all-to-all-start.3) | async-done | bytes 262176 | tf_op jit(solution)/shard_map/update/all_to_all | solution.py:792
  124.9 2.6 %gradient.1 = f32[64,1,1152]{2,1,0:T(1,128)} custom-call(f32[32,16,128]{2,1,0:T(8,128)S(1)} %all-to-all-done.3.update_ref.value_ref, f32[32,16,128]{2,1,0:T(8,128)S(1)} %get-tuple-element.80.refs_8_.squashed_ref, bf16[4,32,16,128]{3,2,1,0:T(8,128)(2,1)S(1)} %copy-done, f32[12,16,128]{2,1,0:T(8,128)S(1)} %collective-permute-done.low_ref.refs_8_.x_low_ref, ...), custom_call_target="tpu_custom_call" | custom-call | flops 14155776 | bytes 1814528 | tf_op jit(solution)/shard_map/gradient/gradient/pallas_call | solution.py:36
  127.5 9.8 %all-to-all-start.4 = ((f32[64,1,1152]{2,1,0:T(1,128)}), f32[64,1,1152]{2,1,0:T(1,128)S(1)}, u32[]{:S(2)}, u32[]{:S(2)}) async-start(f32[64,1,1152]{2,1,0:T(1,128)} %gradient.1), calls=%async_computation.4 | async-start | bytes 589824 | tf_op jit(solution)/shard_map/gradient/all_to_all | solution.py:809
  137.3 0.7 keep.1
  138.0 22.8 %all-to-all-done.4.shares_ref = f32[64,1,1152]{2,1,0:T(1,128)S(1)} async-done(((f32[64,1,1152]{2,1,0:T(1,128)}), f32[64,1,1152]{2,1,0:T(1,128)S(1)}, u32[]{:S(2)}, u32[]{:S(2)}) %all-to-all-start.4) | async-done | bytes 294944 | tf_op jit(solution)/shard_map/gradient/all_to_all | solution.py:809
  160.8 0.7 total.1
  (7 shorter events, 0.1 us)
Async XLA Ops:
  0.6 10.4 %copy-start = (bf16[4,32,16,128]{3,2,1,0:T(8,128)(2,1)S(1)}, bf16[4,32,16,128]{3,2,1,0:T(8,128)(2,1)}, u32[]{:S(2)}) copy-start(bf16[4,32,16,128]{3,2,1,0:T(8,128)(2,1)} %feat_ref.7) | copy-start | bytes 1572868
  0.6 10.4 %copy-start.1 = (f32[1,32,16,128]{3,2,1,0:T(8,128)S(1)}, f32[1,32,16,128]{3,2,1,0:T(8,128)}, u32[]{:S(2)}) copy-start(f32[1,32,16,128]{3,2,1,0:T(8,128)} %param.14) | copy-start | bytes 786436
  2.3 10.0 %collective-permute-start = (f32[12,16,128]{2,1,0:T(8,128)}, f32[12,16,128]{2,1,0:T(8,128)S(1)}, u32[]{:S(2)}, u32[]{:S(2)}) collective-permute-start(f32[12,16,128]{2,1,0:T(8,128)} %get-tuple-element.51), channel_id=1, source_target_pairs={{0,8},{8,16},{16,24},{24,32},{32,40},{40,48},{48,56},{1,9},{9,17},... | collective-permute-start | bytes 294920 | tf_op jit(solution)/shard_map/halo_x/ppermute | solution.py:589
  6.1 7.4 %collective-permute-start.1 = (f32[12,16,128]{2,1,0:T(8,128)}, f32[12,16,128]{2,1,0:T(8,128)S(1)}, u32[]{:S(2)}, u32[]{:S(2)}) collective-permute-start(f32[12,16,128]{2,1,0:T(8,128)} %get-tuple-element.52), channel_id=1, source_target_pairs={{8,0},{16,8},{24,16},{32,24},{40,32},{48,40},{56,48},{9,1},{17,9},... | collective-permute-start | bytes 294920 | tf_op jit(solution)/shard_map/halo_x/ppermute | solution.py:590
  11.0 1.0 copy-start.2
  14.2 27.1 %collective-permute-start.2 = (bf16[528,128]{1,0:T(8,128)(2,1)}, bf16[528,128]{1,0:T(8,128)(2,1)S(1)}, u32[]{:S(2)}, u32[]{:S(2)}) collective-permute-start(bf16[528,128]{1,0:T(8,128)(2,1)} %get-tuple-element.53), channel_id=1, source_target_pairs={{0,1},{1,2},{2,3},{3,4},{4,5},{5,6},{6,7},{8,9},{9,10},{10,11},{11... | collective-permute-start | bytes 405512 | tf_op jit(solution)/shard_map/halo_y/ppermute | solution.py:589
  27.4 26.0 %collective-permute-start.3 = (bf16[528,128]{1,0:T(8,128)(2,1)S(1)}, bf16[528,128]{1,0:T(8,128)(2,1)S(1)}, u32[]{:S(2)}, u32[]{:S(2)}) collective-permute-start(bf16[528,128]{1,0:T(8,128)(2,1)S(1)} %get-tuple-element.66), channel_id=1, source_target_pairs={{1,0},{2,1},{3,2},{4,3},{5,4},{6,5},{7,6},{9,8},{10,9},{11,10},{12... | collective-permute-start | bytes 405512 | tf_op jit(solution)/shard_map/halo_y/ppermute | solution.py:590
  29.4 0.7 copy-start.13
  30.1 8.0 %copy-start.10 = (f32[1,32,16,128]{3,2,1,0:T(8,128)S(1)}, f32[1,32,16,128]{3,2,1,0:T(8,128)}, u32[]{:S(2)}) copy-start(f32[1,32,16,128]{3,2,1,0:T(8,128)} %param.15) | copy-start | bytes 786436
  30.1 8.0 %copy-start.12 = (f32[1,2,512]{2,1,0:T(2,128)S(1)}, f32[1,2,512]{2,1,0:T(2,128)}, u32[]{:S(2)}) copy-start(f32[1,2,512]{2,1,0:T(2,128)} %refs_6_.1) | copy-start | bytes 12292
  33.6 4.5 %copy-start.3 = (f32[1,32,16,128]{3,2,1,0:T(8,128)S(1)}, f32[1,32,16,128]{3,2,1,0:T(8,128)}, u32[]{:S(2)}) copy-start(f32[1,32,16,128]{3,2,1,0:T(8,128)} %param.16) | copy-start | bytes 786436
  33.6 4.5 %copy-start.9 = (f32[1,32,16,128]{3,2,1,0:T(8,128)S(1)}, f32[1,32,16,128]{3,2,1,0:T(8,128)}, u32[]{:S(2)}) copy-start(f32[1,32,16,128]{3,2,1,0:T(8,128)} %param.13) | copy-start | bytes 786436
  33.6 20.0 %all-to-all-start = ((f32[32,16,128]{2,1,0:T(8,128)}), f32[32,16,128]{2,1,0:T(8,128)S(1)}, u32[]{:S(2)}, u32[]{:S(2)}) async-start(f32[32,16,128]{2,1,0:T(8,128)} %get-tuple-element.69), calls=%async_computation | async-start | bytes 524288 | tf_op jit(solution)/shard_map/raw/all_to_all | solution.py:696
  38.0 0.7 copy-start.11
  38.0 0.7 copy-start.14
  40.6 0.7 copy-start.4
  41.3 12.3 %copy-start.6 = (f32[32,16,128]{2,1,0:T(8,128)}, f32[32,16,128]{2,1,0:T(8,128)S(1)}, u32[]{:S(2)}) copy-start(f32[32,16,128]{2,1,0:T(8,128)S(1)} %get-tuple-element.64.refs_3_) | copy-start | bytes 786436
  53.7 14.7 %copy-start.5 = (f32[32,16,128]{2,1,0:T(8,128)S(1)}, f32[32,16,128]{2,1,0:T(8,128)}, u32[]{:S(2)}) copy-start(f32[32,16,128]{2,1,0:T(8,128)} %copy-done.4) | copy-start | bytes 786436
  53.7 14.6 %copy-start.7 = (f32[32,16,128]{2,1,0:T(8,128)S(1)}, f32[32,16,128]{2,1,0:T(8,128)}, u32[]{:S(2)}) copy-start(f32[32,16,128]{2,1,0:T(8,128)} %copy-done.6) | copy-start | bytes 786436
  68.9 19.7 %collective-permute-start.4 = (bf16[384,128]{1,0:T(8,128)(2,1)S(1)}, bf16[384,128]{1,0:T(8,128)(2,1)S(1)}, u32[]{:S(2)}, u32[]{:S(2)}) collective-permute-start(bf16[384,128]{1,0:T(8,128)(2,1)S(1)} %get-tuple-element.78), channel_id=1, source_target_pairs={{0,1},{1,2},{2,3},{3,4},{4,5},{5,6},{6,7},{8,9},{9,10},{10,11},{11... | collective-permute-start | bytes 294920 | tf_op jit(solution)/shard_map/halo_2/ppermute | solution.py:589
  79.1 18.9 %collective-permute-start.5 = (bf16[384,128]{1,0:T(8,128)(2,1)S(1)}, bf16[384,128]{1,0:T(8,128)(2,1)S(1)}, u32[]{:S(2)}, u32[]{:S(2)}) collective-permute-start(bf16[384,128]{1,0:T(8,128)(2,1)S(1)} %get-tuple-element.79), channel_id=1, source_target_pairs={{1,0},{2,1},{3,2},{4,3},{5,4},{6,5},{7,6},{9,8},{10,9},{11,10},{12... | collective-permute-start | bytes 294920 | tf_op jit(solution)/shard_map/halo_2/ppermute | solution.py:590
  80.4 8.0 %collective-permute-start.6 = (f32[8,16,128]{2,1,0:T(8,128)S(1)}, f32[8,16,128]{2,1,0:T(8,128)S(1)}, u32[]{:S(2)}, u32[]{:S(2)}) collective-permute-start(f32[8,16,128]{2,1,0:T(8,128)S(1)} %get-tuple-element.81), channel_id=1, source_target_pairs={{0,8},{8,16},{16,24},{24,32},{32,40},{40,48},{48,56},{1,9},{9,17},... | collective-permute-start | bytes 196616 | tf_op jit(solution)/shard_map/halo_2/ppermute | solution.py:589
  82.3 6.3 %collective-permute-start.7 = (f32[8,16,128]{2,1,0:T(8,128)S(1)}, f32[8,16,128]{2,1,0:T(8,128)S(1)}, u32[]{:S(2)}, u32[]{:S(2)}) collective-permute-start(f32[8,16,128]{2,1,0:T(8,128)S(1)} %get-tuple-element.82), channel_id=1, source_target_pairs={{8,0},{16,8},{24,16},{32,24},{40,32},{48,40},{56,48},{9,1},{17,9},... | collective-permute-start | bytes 196616 | tf_op jit(solution)/shard_map/halo_2/ppermute | solution.py:590
  99.4 13.8 %all-to-all-start.2 = ((f32[64,16,128]{2,1,0:T(8,128)}), f32[64,16,128]{2,1,0:T(8,128)S(1)}, u32[]{:S(2)}, u32[]{:S(2)}) async-start(f32[64,16,128]{2,1,0:T(8,128)} %bitcast.9), calls=%async_computation.2 | async-start | bytes 1048576 | tf_op jit(solution)/shard_map/update/all_to_all | solution.py:782
  113.9 3.6 %copy-start.8 = (f32[32,16,128]{2,1,0:T(8,128)S(1)}, f32[32,16,128]{2,1,0:T(8,128)}, u32[]{:S(2)}) copy-start(f32[32,16,128]{2,1,0:T(8,128)} %get-tuple-element.84.second_ref) | copy-start | bytes 786436
  113.9 11.0 %all-to-all-start.3 = ((f32[32,16,128]{2,1,0:T(8,128)}), f32[32,16,128]{2,1,0:T(8,128)S(1)}, u32[]{:S(2)}, u32[]{:S(2)}) async-start(f32[32,16,128]{2,1,0:T(8,128)} %bitcast.11), calls=%async_computation.3 | async-start | bytes 524288 | tf_op jit(solution)/shard_map/update/all_to_all | solution.py:792
  127.5 33.3 %all-to-all-start.4 = ((f32[64,1,1152]{2,1,0:T(1,128)}), f32[64,1,1152]{2,1,0:T(1,128)S(1)}, u32[]{:S(2)}, u32[]{:S(2)}) async-start(f32[64,1,1152]{2,1,0:T(1,128)} %gradient.1), calls=%async_computation.4 | async-start | bytes 589824 | tf_op jit(solution)/shard_map/gradient/all_to_all | solution.py:809

commit v11 on v10

--- a/solution.py
+++ b/solution.py
@@ -301,6 +301,18 @@
         sample(fwd_ref, hit, trace_ref)
 
 
+def spread(sums, out_ref):
+    size_x, size_y, depth = out_ref.shape
+    top, middle, low = (part.astype(F32) for part in split3(sums))
+    row = lax.broadcasted_iota(jnp.int32, (16, sums.shape[1]), 0)
+    parts = jnp.where(row == 0, top, jnp.where(row == 1, middle, jnp.where(row == 2, low, 0.0)))
+    lane = lax.broadcasted_iota(jnp.int32, (16, depth), 1)
+    plane = (lane == RDEPTH).astype(F32).astype(BF16)
+    out_ref[...] = lax.dot_general(
+        parts.astype(BF16), plane, (((0,), (0,)), ((), ())), preferred_element_type=F32
+    ).reshape(size_x, size_y, depth)
+
+
 def inner_body(moment, plane_y, *refs):
     fwd_ref, back_ref, fwd_old_ref, back_old_ref = refs[:4]
     size_x, size_y, depth = fwd_ref.shape
@@ -322,19 +334,17 @@
         for n in range(2):
             amplitude_ref[n] = jnp.full(amplitude_ref.shape[1:], wavelet_ref[0, n], F32)
         hit = receiver_hits(receivers_ref, place_ref, plane_y, size_x, size_y)
-        for n, out_ref in enumerate((inject_ref, later_ref)):
-            injected = jnp.where(
-                lax.broadcasted_iota(jnp.int32, (depth, hit.shape[1]), 0) == RDEPTH,
-                residual_ref[0, n : n + 1, :],
-                0.0,
-            )
-            out_ref[...] = exact_product(split3(injected), hit, ((1,), (1,)), False).reshape(
-                size_x, size_y, depth
-            )
+        sums = []
+        for n in range(2):
+            injected = jnp.broadcast_to(residual_ref[0, n : n + 1, :], (16, hit.shape[1]))
+            sums.append(exact_product(split3(injected), hit, ((1,), (1,)), True)[0:1, :])
+        later_ref[...] = sums[1]
+        spread(sums[0], inject_ref)
     else:
-        inject_ref = refs[4]
+        later_ref = refs[4]
         fwd_ahead_ref, back_ahead_ref, lap_fwd_ref, lap_back_ref = refs[5:9]
-        x_ref, y_ref = refs[9:]
+        x_ref, y_ref, inject_ref = refs[9:]
+        spread(later_ref[...], inject_ref)
     zero_x = jnp.zeros((4, size_y, depth), F32)
     y_ref[:, 0:8] = jnp.zeros((size_x, 8, depth), F32)
     y_ref[:, 8 + size_y : 16 + size_y] = jnp.zeros((size_x, 8, depth), F32)
@@ -674,7 +684,8 @@
     with jax.named_scope("inner_1"):
         inner_1 = call(
             functools.partial(inner_body, 0, plane_y),
-            [full] * 5 + [shape(8, depth, dtype=jnp.int32), shape(2, 8, depth)],
+            [full] * 4
+            + [shape(1, size_x * size_y), shape(8, depth, dtype=jnp.int32), shape(2, 8, depth)],
             (fwd_now, back_now, fwd_prev, back_prev)
             + (place, receivers, residual, wavelet, x_low, x_high),
             [VM] * 4 + [SM] + [VM] * 2 + [SM] + [VM] * 2,
@@ -743,7 +754,7 @@
             [full] * 4,
             (fwd_1, back_1, fwd_now, back_now, later),
             [VM] * 5,
-            scratch=inner_scratch[:2],
+            scratch=inner_scratch,
             flops=work,
             name="inner_2",
         )

time: 162 us -> 162 us (level)
  no operation moved by 1% of the time
where the time goes in v11:
time: 162 us
  waiting for transfers between devices  63.1 us (39%)
  starting transfers between devices  61.7 us (38%)
  Pallas kernels  17.6 us (11%)
  blocking collectives  14.6 us (9%)
  local copies, waits for them, and re-layouts  2.22 us (1%)
  between operations  2.22 us (1%)
    ppermute x4, starting transfers between devices, neighbours(): low = lax.ppermute(up, axis, [(i, i + 1) for i in range(count - 1)])  29.1 us
    ppermute x4, waiting for transfers between devices, neighbours(): high = lax.ppermute(down, axis, [(i + 1, i) for i in range(count - 1)])  23.5 us
    all_to_all x1, waiting for transfers between devices, per_device(): shares = lax.all_to_all(share, ('gx', 'gy'), 0, 0, tiled=True)  22.8 us
    pallas_call x15, Pallas kernels, call(): pl.pallas_call(body, out_shape=outs[0] if single else tuple(outs), in_spe...  17.6 us
    all_to_all x1, blocking collectives, per_device(): lax.all_to_all(raw.reshape(shots * each, depth), 'shot', 0, 0, tiled=True)  14.6 us
    ppermute x4, starting transfers between devices, neighbours(): high = lax.ppermute(down, axis, [(i + 1, i) for i in range(count - 1)])  11.4 us
    all_to_all x1, starting transfers between devices, per_device(): shares = lax.all_to_all(share, ('gx', 'gy'), 0, 0, tiled=True)  9.76 us
    all_to_all x1, waiting for transfers between devices, per_device(): lax.all_to_all(sums.reshape(shots * 2 * rows, size_y, depth), 'shot', 0,...  9.62 us
  transfers between devices with their start and end apart: 12, of which 8 were waited for; matrix products, arithmetic and copies ran while one was open for 0% of the time, Pallas kernels for 6%

profile of v11, /device:TPU:32, one launch (start us, length us, event | category | flops | bytes accessed | tf_op | source)
XLA Modules:
  0.0 161.6 jit_solution(7452386518609621461)
XLA Ops:
  0.6 0.0 copy-start
  0.6 0.0 copy-start.1
  0.7 1.6 %pack_x.1 = (f32[12,16,128]{2,1,0:T(8,128)}, f32[12,16,128]{2,1,0:T(8,128)}) custom-call(bf16[4,32,16,128]{3,2,1,0:T(8,128)(2,1)} %feat_ref.7, f32[32,16,128]{2,1,0:T(8,128)} %bitcast.12, f32[32,16,128]{2,1,0:T(8,128)} %bitcast.16), custom_call_target="tpu_custom_call" | custom-call | flops 1000000 | bytes 1245184 | tf_op jit(solution)/shard_map/pack_x/pack_x/pallas_call | solution.py:36
  2.3 3.8 %collective-permute-start = (f32[12,16,128]{2,1,0:T(8,128)}, f32[12,16,128]{2,1,0:T(8,128)S(1)}, u32[]{:S(2)}, u32[]{:S(2)}) collective-permute-start(f32[12,16,128]{2,1,0:T(8,128)} %get-tuple-element.51), channel_id=1, source_target_pairs={{0,8},{8,16},{16,24},{24,32},{32,40},{40,48},{48,56},{1,9},{9,17},... | collective-permute-start | bytes 294920 | tf_op jit(solution)/shard_map/halo_x/ppermute | solution.py:599
  6.1 4.9 %collective-permute-start.1 = (f32[12,16,128]{2,1,0:T(8,128)}, f32[12,16,128]{2,1,0:T(8,128)S(1)}, u32[]{:S(2)}, u32[]{:S(2)}) collective-permute-start(f32[12,16,128]{2,1,0:T(8,128)} %get-tuple-element.52), channel_id=1, source_target_pairs={{8,0},{16,8},{24,16},{32,24},{40,32},{48,40},{56,48},{9,1},{17,9},... | collective-permute-start | bytes 294920 | tf_op jit(solution)/shard_map/halo_x/ppermute | solution.py:600
  11.0 0.0 copy-done
  11.0 0.0 copy-done.1
  11.0 0.0 copy-start.2
  11.0 0.9 copy-done.2
  12.0 0.3 pack_y.1
  12.3 0.0 collective-permute-done.low_ref.refs_8_.x_low_ref
  12.3 1.2 collective-permute-done.1.high_ref.refs_9_.x_high_ref
  13.5 0.7 corners.1
  14.2 13.3 %collective-permute-start.2 = (bf16[528,128]{1,0:T(8,128)(2,1)}, bf16[528,128]{1,0:T(8,128)(2,1)S(1)}, u32[]{:S(2)}, u32[]{:S(2)}) collective-permute-start(bf16[528,128]{1,0:T(8,128)(2,1)} %get-tuple-element.53), channel_id=1, source_target_pairs={{0,1},{1,2},{2,3},{3,4},{4,5},{5,6},{6,7},{8,9},{9,10},{10,11},{11... | collective-permute-start | bytes 405512 | tf_op jit(solution)/shard_map/halo_y/ppermute | solution.py:599
  27.5 1.3 collective-permute-start.3
  29.4 0.0 copy-start.11
  29.4 0.1 pad_add_fusion.refs_4_.place_ref
  29.5 0.6 copy-done.11
  30.1 0.0 copy-start.8
  30.1 0.0 copy-start.10
  30.1 3.5 %conv.1 = (f32[32,16,128]{2,1,0:T(8,128)}, f32[72,128]{1,0:T(8,128)S(1)}) custom-call(bf16[4,32,16,128]{3,2,1,0:T(8,128)(2,1)S(1)} %copy-done, f32[12,16,128]{2,1,0:T(8,128)S(1)} %collective-permute-done.low_ref.refs_8_.x_low_ref, f32[12,16,128]{2,1,0:T(8,128)S(1)} %collective-permute-done.1.high_ref.refs_9_.x_high_ref, f32[4,27]{1,0:T(4,128)S(1)} %copy-done.11), custom_call_target="tpu_custom_call" | custom-call | flops 14155776 | bytes 1020336 | tf_op jit(solution)/shard_map/conv/conv/pallas_call | solution.py:36
  33.6 0.0 copy-start.3
  33.6 0.0 copy-start.7
  33.6 4.4 %all-to-all-start = ((f32[32,16,128]{2,1,0:T(8,128)}), f32[32,16,128]{2,1,0:T(8,128)S(1)}, u32[]{:S(2)}, u32[]{:S(2)}) async-start(f32[32,16,128]{2,1,0:T(8,128)} %get-tuple-element.69), calls=%async_computation | async-start | bytes 524288 | tf_op jit(solution)/shard_map/raw/all_to_all | solution.py:707
  38.0 0.0 copy-start.12
  38.0 0.0 copy-done.8
  38.1 0.0 copy-done.10
  38.1 0.0 copy-done.3
  38.1 0.0 copy-done.7
  38.1 0.6 copy-done.9
  38.7 0.0 copy-done.12
  38.7 1.9 %inner_1.1 = (f32[32,16,128]{2,1,0:T(8,128)S(1)}, f32[32,16,128]{2,1,0:T(8,128)S(1)}, f32[32,16,128]{2,1,0:T(8,128)S(1)}, f32[32,16,128]{2,1,0:T(8,128)S(1)}, f3...) custom-call(f32[32,16,128]{2,1,0:T(8,128)S(1)} %bitcast.14, f32[32,16,128]{2,1,0:T(8,128)S(1)} %bitcast.18, ...), custom_call_target="tpu_custom_call" | custom-call | flops 3932160 | bytes 2314260 | tf_op jit(solution)/shard_map/inner_1/inner_1/pallas_call | solution.py:36
  40.7 0.0 copy-start.4
  40.7 0.0 collective-permute-done.2.low_ref.refs_4_.y_low_ref
  40.7 12.8 %collective-permute-done.3.high_ref.refs_5_.y_high_ref = bf16[528,128]{1,0:T(8,128)(2,1)S(1)} collective-permute-done((bf16[528,128]{1,0:T(8,128)(2,1)S(1)}, bf16[528,128]{1,0:T(8,128)(2,1)S(1)}, u32[]{:S(2)}, u32[]{:S(2)}) %collective-permute-start.3) | collective-permute-done | bytes 135200 | tf_op jit(solution)/shard_map/halo_y/ppermute | solution.py:600
  53.4 0.1 conv_edge.1.rims_ref
  53.6 0.0 copy-done.4
  53.6 0.0 all-to-all-done
  53.7 0.0 copy-start.5
  53.7 14.6 %all_to_all.26.refs_8_ = f32[8,128,128]{2,1,0:T(8,128)S(1)} all-to-all(f32[8,128,128]{2,1,0:T(8,128)S(1)} %raw.1), channel_id=1, replica_groups=mesh['shot'=8,'gx'=8,'gy'=8] {'shot'}, dimensions={0} | all-to-all | bytes 1048576 | tf_op jit(solution)/shard_map/raw/all_to_all | solution.py:726
  68.3 0.0 copy-done.5
  68.3 0.6 step_1.1
  68.9 10.1 %collective-permute-start.4 = (bf16[384,128]{1,0:T(8,128)(2,1)S(1)}, bf16[384,128]{1,0:T(8,128)(2,1)S(1)}, u32[]{:S(2)}, u32[]{:S(2)}) collective-permute-start(bf16[384,128]{1,0:T(8,128)(2,1)S(1)} %get-tuple-element.78), channel_id=1, source_target_pairs={{0,1},{1,2},{2,3},{3,4},{4,5},{5,6},{6,7},{8,9},{9,10},{10,11},{11... | collective-permute-start | bytes 294920 | tf_op jit(solution)/shard_map/halo_2/ppermute | solution.py:599
  79.1 1.3 collective-permute-start.5
  80.4 1.9 %collective-permute-start.6 = (f32[8,16,128]{2,1,0:T(8,128)S(1)}, f32[8,16,128]{2,1,0:T(8,128)S(1)}, u32[]{:S(2)}, u32[]{:S(2)}) collective-permute-start(f32[8,16,128]{2,1,0:T(8,128)S(1)} %get-tuple-element.81), channel_id=1, source_target_pairs={{0,8},{8,16},{16,24},{24,32},{32,40},{40,48},{48,56},{1,9},{9,17},... | collective-permute-start | bytes 196616 | tf_op jit(solution)/shard_map/halo_2/ppermute | solution.py:599
  82.3 3.9 %collective-permute-start.7 = (f32[8,16,128]{2,1,0:T(8,128)S(1)}, f32[8,16,128]{2,1,0:T(8,128)S(1)}, u32[]{:S(2)}, u32[]{:S(2)}) collective-permute-start(f32[8,16,128]{2,1,0:T(8,128)S(1)} %get-tuple-element.82), channel_id=1, source_target_pairs={{8,0},{16,8},{24,16},{32,24},{40,32},{48,40},{56,48},{9,1},{17,9},... | collective-permute-start | bytes 196616 | tf_op jit(solution)/shard_map/halo_2/ppermute | solution.py:600
  86.2 1.2 inner_2.1
  87.5 0.9 collective-permute-done.6.refs_9_
  88.4 0.2 collective-permute-done.7.refs_10_
  88.6 0.0 collective-permute-done.4.refs_4_
  88.6 9.3 %collective-permute-done.5.refs_5_ = bf16[384,128]{1,0:T(8,128)(2,1)S(1)} collective-permute-done((bf16[384,128]{1,0:T(8,128)(2,1)S(1)}, bf16[384,128]{1,0:T(8,128)(2,1)S(1)}, u32[]{:S(2)}, u32[]{:S(2)}) %collective-permute-start.5) | collective-permute-done | bytes 98336 | tf_op jit(solution)/shard_map/halo_2/ppermute | solution.py:600
  97.9 1.4 step_2.1
  99.4 3.5 %all-to-all-start.2 = ((f32[64,16,128]{2,1,0:T(8,128)}), f32[64,16,128]{2,1,0:T(8,128)S(1)}, u32[]{:S(2)}, u32[]{:S(2)}) async-start(f32[64,16,128]{2,1,0:T(8,128)} %bitcast.9), calls=%async_computation.2 | async-start | bytes 1048576 | tf_op jit(solution)/shard_map/update/all_to_all | solution.py:793
  103.5 9.6 %all-to-all-done.2 = f32[64,16,128]{2,1,0:T(8,128)S(1)} async-done(((f32[64,16,128]{2,1,0:T(8,128)}), f32[64,16,128]{2,1,0:T(8,128)S(1)}, u32[]{:S(2)}, u32[]{:S(2)}) %all-to-all-start.2) | async-done | bytes 524320 | tf_op jit(solution)/shard_map/update/all_to_all | solution.py:793
  113.1 0.7 update.1
  113.9 3.5 %all-to-all-start.3 = ((f32[32,16,128]{2,1,0:T(8,128)}), f32[32,16,128]{2,1,0:T(8,128)S(1)}, u32[]{:S(2)}, u32[]{:S(2)}) async-start(f32[32,16,128]{2,1,0:T(8,128)} %bitcast.11), calls=%async_computation.3 | async-start | bytes 524288 | tf_op jit(solution)/shard_map/update/all_to_all | solution.py:803
  117.4 0.0 copy-done.6
  117.4 1.2 traces.1
  118.6 6.3 %all-to-all-done.3.update_ref.value_ref = f32[32,16,128]{2,1,0:T(8,128)S(1)} async-done(((f32[32,16,128]{2,1,0:T(8,128)}), f32[32,16,128]{2,1,0:T(8,128)S(1)}, u32[]{:S(2)}, u32[]{:S(2)}) %all-to-all-start.3) | async-done | bytes 262176 | tf_op jit(solution)/shard_map/update/all_to_all | solution.py:803
  124.9 2.6 %gradient.1 = f32[64,1,1152]{2,1,0:T(1,128)} custom-call(f32[32,16,128]{2,1,0:T(8,128)S(1)} %all-to-all-done.3.update_ref.value_ref, f32[32,16,128]{2,1,0:T(8,128)S(1)} %get-tuple-element.80.refs_8_.squashed_ref, bf16[4,32,16,128]{3,2,1,0:T(8,128)(2,1)S(1)} %copy-done, f32[12,16,128]{2,1,0:T(8,128)S(1)} %collective-permute-done.low_ref.refs_8_.x_low_ref, ...), custom_call_target="tpu_custom_call" | custom-call | flops 14155776 | bytes 1814528 | tf_op jit(solution)/shard_map/gradient/gradient/pallas_call | solution.py:36
  127.5 9.8 %all-to-all-start.4 = ((f32[64,1,1152]{2,1,0:T(1,128)}), f32[64,1,1152]{2,1,0:T(1,128)S(1)}, u32[]{:S(2)}, u32[]{:S(2)}) async-start(f32[64,1,1152]{2,1,0:T(1,128)} %gradient.1), calls=%async_computation.4 | async-start | bytes 589824 | tf_op jit(solution)/shard_map/gradient/all_to_all | solution.py:820
  137.3 0.7 keep.1
  138.0 22.8 %all-to-all-done.4.shares_ref = f32[64,1,1152]{2,1,0:T(1,128)S(1)} async-done(((f32[64,1,1152]{2,1,0:T(1,128)}), f32[64,1,1152]{2,1,0:T(1,128)S(1)}, u32[]{:S(2)}, u32[]{:S(2)}) %all-to-all-start.4) | async-done | bytes 294944 | tf_op jit(solution)/shard_map/gradient/all_to_all | solution.py:820
  160.8 0.7 total.1
  (3 shorter events, 0.0 us)
Async XLA Ops:
  0.6 10.4 %copy-start = (bf16[4,32,16,128]{3,2,1,0:T(8,128)(2,1)S(1)}, bf16[4,32,16,128]{3,2,1,0:T(8,128)(2,1)}, u32[]{:S(2)}) copy-start(bf16[4,32,16,128]{3,2,1,0:T(8,128)(2,1)} %feat_ref.7) | copy-start | bytes 1572868
  0.6 10.4 %copy-start.1 = (f32[1,32,16,128]{3,2,1,0:T(8,128)S(1)}, f32[1,32,16,128]{3,2,1,0:T(8,128)}, u32[]{:S(2)}) copy-start(f32[1,32,16,128]{3,2,1,0:T(8,128)} %param.14) | copy-start | bytes 786436
  2.3 10.0 %collective-permute-start = (f32[12,16,128]{2,1,0:T(8,128)}, f32[12,16,128]{2,1,0:T(8,128)S(1)}, u32[]{:S(2)}, u32[]{:S(2)}) collective-permute-start(f32[12,16,128]{2,1,0:T(8,128)} %get-tuple-element.51), channel_id=1, source_target_pairs={{0,8},{8,16},{16,24},{24,32},{32,40},{40,48},{48,56},{1,9},{9,17},... | collective-permute-start | bytes 294920 | tf_op jit(solution)/shard_map/halo_x/ppermute | solution.py:599
  6.1 7.4 %collective-permute-start.1 = (f32[12,16,128]{2,1,0:T(8,128)}, f32[12,16,128]{2,1,0:T(8,128)S(1)}, u32[]{:S(2)}, u32[]{:S(2)}) collective-permute-start(f32[12,16,128]{2,1,0:T(8,128)} %get-tuple-element.52), channel_id=1, source_target_pairs={{8,0},{16,8},{24,16},{32,24},{40,32},{48,40},{56,48},{9,1},{17,9},... | collective-permute-start | bytes 294920 | tf_op jit(solution)/shard_map/halo_x/ppermute | solution.py:600
  11.0 1.0 copy-start.2
  14.2 26.5 %collective-permute-start.2 = (bf16[528,128]{1,0:T(8,128)(2,1)}, bf16[528,128]{1,0:T(8,128)(2,1)S(1)}, u32[]{:S(2)}, u32[]{:S(2)}) collective-permute-start(bf16[528,128]{1,0:T(8,128)(2,1)} %get-tuple-element.53), channel_id=1, source_target_pairs={{0,1},{1,2},{2,3},{3,4},{4,5},{5,6},{6,7},{8,9},{9,10},{10,11},{11... | collective-permute-start | bytes 405512 | tf_op jit(solution)/shard_map/halo_y/ppermute | solution.py:599
  27.5 26.0 %collective-permute-start.3 = (bf16[528,128]{1,0:T(8,128)(2,1)S(1)}, bf16[528,128]{1,0:T(8,128)(2,1)S(1)}, u32[]{:S(2)}, u32[]{:S(2)}) collective-permute-start(bf16[528,128]{1,0:T(8,128)(2,1)S(1)} %get-tuple-element.66), channel_id=1, source_target_pairs={{1,0},{2,1},{3,2},{4,3},{5,4},{6,5},{7,6},{9,8},{10,9},{11,10},{12... | collective-permute-start | bytes 405512 | tf_op jit(solution)/shard_map/halo_y/ppermute | solution.py:600
  29.4 0.7 copy-start.11
  30.1 8.0 %copy-start.8 = (f32[1,32,16,128]{3,2,1,0:T(8,128)S(1)}, f32[1,32,16,128]{3,2,1,0:T(8,128)}, u32[]{:S(2)}) copy-start(f32[1,32,16,128]{3,2,1,0:T(8,128)} %param.15) | copy-start | bytes 786436
  30.1 8.0 %copy-start.10 = (f32[1,2,512]{2,1,0:T(2,128)S(1)}, f32[1,2,512]{2,1,0:T(2,128)}, u32[]{:S(2)}) copy-start(f32[1,2,512]{2,1,0:T(2,128)} %refs_6_.1) | copy-start | bytes 12292
  33.6 4.5 %copy-start.3 = (f32[1,32,16,128]{3,2,1,0:T(8,128)S(1)}, f32[1,32,16,128]{3,2,1,0:T(8,128)}, u32[]{:S(2)}) copy-start(f32[1,32,16,128]{3,2,1,0:T(8,128)} %param.16) | copy-start | bytes 786436
  33.6 4.5 %copy-start.7 = (f32[1,32,16,128]{3,2,1,0:T(8,128)S(1)}, f32[1,32,16,128]{3,2,1,0:T(8,128)}, u32[]{:S(2)}) copy-start(f32[1,32,16,128]{3,2,1,0:T(8,128)} %param.13) | copy-start | bytes 786436
  33.6 20.0 %all-to-all-start = ((f32[32,16,128]{2,1,0:T(8,128)}), f32[32,16,128]{2,1,0:T(8,128)S(1)}, u32[]{:S(2)}, u32[]{:S(2)}) async-start(f32[32,16,128]{2,1,0:T(8,128)} %get-tuple-element.69), calls=%async_computation | async-start | bytes 524288 | tf_op jit(solution)/shard_map/raw/all_to_all | solution.py:707
  38.0 0.7 copy-start.9
  38.0 0.7 copy-start.12
  40.7 12.9 %copy-start.4 = (f32[32,16,128]{2,1,0:T(8,128)}, f32[32,16,128]{2,1,0:T(8,128)S(1)}, u32[]{:S(2)}) copy-start(f32[32,16,128]{2,1,0:T(8,128)S(1)} %get-tuple-element.64.refs_3_) | copy-start | bytes 786436
  53.7 14.6 %copy-start.5 = (f32[32,16,128]{2,1,0:T(8,128)S(1)}, f32[32,16,128]{2,1,0:T(8,128)}, u32[]{:S(2)}) copy-start(f32[32,16,128]{2,1,0:T(8,128)} %copy-done.4) | copy-start | bytes 786436
  68.9 19.7 %collective-permute-start.4 = (bf16[384,128]{1,0:T(8,128)(2,1)S(1)}, bf16[384,128]{1,0:T(8,128)(2,1)S(1)}, u32[]{:S(2)}, u32[]{:S(2)}) collective-permute-start(bf16[384,128]{1,0:T(8,128)(2,1)S(1)} %get-tuple-element.78), channel_id=1, source_target_pairs={{0,1},{1,2},{2,3},{3,4},{4,5},{5,6},{6,7},{8,9},{9,10},{10,11},{11... | collective-permute-start | bytes 294920 | tf_op jit(solution)/shard_map/halo_2/ppermute | solution.py:599
  79.1 18.9 %collective-permute-start.5 = (bf16[384,128]{1,0:T(8,128)(2,1)S(1)}, bf16[384,128]{1,0:T(8,128)(2,1)S(1)}, u32[]{:S(2)}, u32[]{:S(2)}) collective-permute-start(bf16[384,128]{1,0:T(8,128)(2,1)S(1)} %get-tuple-element.79), channel_id=1, source_target_pairs={{1,0},{2,1},{3,2},{4,3},{5,4},{6,5},{7,6},{9,8},{10,9},{11,10},{12... | collective-permute-start | bytes 294920 | tf_op jit(solution)/shard_map/halo_2/ppermute | solution.py:600
  80.4 8.0 %collective-permute-start.6 = (f32[8,16,128]{2,1,0:T(8,128)S(1)}, f32[8,16,128]{2,1,0:T(8,128)S(1)}, u32[]{:S(2)}, u32[]{:S(2)}) collective-permute-start(f32[8,16,128]{2,1,0:T(8,128)S(1)} %get-tuple-element.81), channel_id=1, source_target_pairs={{0,8},{8,16},{16,24},{24,32},{32,40},{40,48},{48,56},{1,9},{9,17},... | collective-permute-start | bytes 196616 | tf_op jit(solution)/shard_map/halo_2/ppermute | solution.py:599
  82.3 6.3 %collective-permute-start.7 = (f32[8,16,128]{2,1,0:T(8,128)S(1)}, f32[8,16,128]{2,1,0:T(8,128)S(1)}, u32[]{:S(2)}, u32[]{:S(2)}) collective-permute-start(f32[8,16,128]{2,1,0:T(8,128)S(1)} %get-tuple-element.82), channel_id=1, source_target_pairs={{8,0},{16,8},{24,16},{32,24},{40,32},{48,40},{56,48},{9,1},{17,9},... | collective-permute-start | bytes 196616 | tf_op jit(solution)/shard_map/halo_2/ppermute | solution.py:600
  99.4 13.8 %all-to-all-start.2 = ((f32[64,16,128]{2,1,0:T(8,128)}), f32[64,16,128]{2,1,0:T(8,128)S(1)}, u32[]{:S(2)}, u32[]{:S(2)}) async-start(f32[64,16,128]{2,1,0:T(8,128)} %bitcast.9), calls=%async_computation.2 | async-start | bytes 1048576 | tf_op jit(solution)/shard_map/update/all_to_all | solution.py:793
  113.9 3.6 %copy-start.6 = (f32[32,16,128]{2,1,0:T(8,128)S(1)}, f32[32,16,128]{2,1,0:T(8,128)}, u32[]{:S(2)}) copy-start(f32[32,16,128]{2,1,0:T(8,128)} %get-tuple-element.84.second_ref) | copy-start | bytes 786436
  113.9 11.0 %all-to-all-start.3 = ((f32[32,16,128]{2,1,0:T(8,128)}), f32[32,16,128]{2,1,0:T(8,128)S(1)}, u32[]{:S(2)}, u32[]{:S(2)}) async-start(f32[32,16,128]{2,1,0:T(8,128)} %bitcast.11), calls=%async_computation.3 | async-start | bytes 524288 | tf_op jit(solution)/shard_map/update/all_to_all | solution.py:803
  127.5 33.3 %all-to-all-start.4 = ((f32[64,1,1152]{2,1,0:T(1,128)}), f32[64,1,1152]{2,1,0:T(1,128)S(1)}, u32[]{:S(2)}, u32[]{:S(2)}) async-start(f32[64,1,1152]{2,1,0:T(1,128)} %gradient.1), calls=%async_computation.4 | async-start | bytes 589824 | tf_op jit(solution)/shard_map/gradient/all_to_all | solution.py:820
